TPU v7x, 32 devices: a whole 2x2x4 slice. The times are simulated.
32 devices in a mesh: section: 4 (over y, x), feat: 2 (over core), tensor: 4 (over z).
Axes of the slice: x: 2, y: 2, z: 4, core: 2. Of those that a mesh axis runs over, the one named last changes fastest.
Arguments:
- clean_resid: bfloat16 [32, 8192], P(('section', 'feat'), 'tensor'), may hold values from -6 to 6
- corrupt_resid: bfloat16 [32, 8192], P(('section', 'feat'), 'tensor'), may hold values from -6 to 6
- metric_grad: bfloat16 [32, 8192], P(('section', 'feat'), 'tensor'), may hold values from -0.796875 to 0.796875
- enc_weight: bfloat16 [8192, 4096], P('tensor', ('section', 'feat')), may hold values from -0.0625 to 0.0625
- enc_bias: float32 [4096], P(('section', 'feat')), may hold values from -3 to 3
- dec_weight: bfloat16 [4096, 8192], P(('section', 'feat'), 'tensor'), may hold values from -0.0625 to 0.0625
Outputs:
- feature_effect: float32 [4096], P(('section', 'feat'))
- error_effect: float32 [32], P(('section', 'feat'))
All inputs are finite; a program needn't handle non-finite values.
Results may differ from a plain program's by a relative error of at most 0.0003.
Values may be sent and summed in bfloat16 or wider, within the bound.
No kernel may reach another device: no remote copies, remote signals or barrier semaphores. Data moves between devices by JAX's collectives and lax.ppermute only.
A program may use at most 64 MiB of HBM per device.

v0:
```python
import jax
import jax.numpy as jnp
from jax import lax
from jax.sharding import PartitionSpec as P


def per_device(clean_resid, corrupt_resid, metric_grad, enc_weight, enc_bias, dec_weight):
    stacked = jnp.stack([clean_resid, corrupt_resid, metric_grad])
    rows_piece = lax.all_gather(stacked, ("section", "feat"), axis=1, tiled=True)
    encoded = jnp.einsum(
        "srd,df->srf", rows_piece[:2], enc_weight, preferred_element_type=jnp.float32
    )
    projected = lax.dot_general(
        rows_piece[2], dec_weight, (((1,), (1,)), ((), ())), preferred_element_type=jnp.float32
    )
    preact = jnp.concatenate([encoded, projected[None]], axis=0)
    shifted = corrupt_resid.astype(jnp.float32) - clean_resid.astype(jnp.float32)
    inner_part = jnp.sum(shifted * metric_grad.astype(jnp.float32), axis=1)
    preact, inner_sum = lax.psum((preact, inner_part), "tensor")
    act_clean = jax.nn.relu(preact[0] + enc_bias)
    act_corrupt = jax.nn.relu(preact[1] + enc_bias)
    attribution = (act_corrupt - act_clean) * preact[2]
    feature_effect = jnp.sum(attribution, axis=0)
    token_part = jnp.sum(attribution, axis=1)
    token_total = lax.psum_scatter(token_part, ("section", "feat"), scatter_dimension=0, tiled=True)
    error_sum = inner_sum - token_total
    return (feature_effect, error_sum)


def solution(mesh):
    in_specs = (
        P(("section", "feat"), "tensor"),
        P(("section", "feat"), "tensor"),
        P(("section", "feat"), "tensor"),
        P("tensor", ("section", "feat")),
        P(("section", "feat")),
        P(("section", "feat"), "tensor"),
    )
    out_specs = (P(("section", "feat")), P(("section", "feat")))
    return jax.shard_map(
        per_device, mesh=mesh, in_specs=in_specs, out_specs=out_specs, check_vma=False
    )
```

profile of v0, /device:TPU:0, one launch (start us, length us, event | category | flops | bytes accessed | tf_op | source)
XLA Modules:
  0.0 79.6 jit_solution(15813069101225594271)
XLA Ops:
  7.2 0.0 copy-start
  7.2 0.0 all-reduce.3.cloned.1.call-start
  7.2 0.9 %pad_maximum_fusion.1 = bf16[3,4,2048]{2,1,0:T(4,128)(2,1)S(1)} fusion(bf16[1,4,2048]{2,1,0:T(4,128)(2,1)} %bitcast.35, bf16[1,4,2048]{2,1,0:T(4,128)(2,1)} %bitcast.36, bf16[1,4,2048]{2,1,0:T(4,128)(2,1)} %bitcast.37), kind=kLoop, calls=%fused_computation.15 | loop fusion | flops 49152 | bytes 98304 | tf_op jit(solution)/shard_map/stack | solution.py:8
  8.2 11.3 %all_gather.3 = bf16[3,32,2048]{2,0,1:T(4,128)(2,1)S(1)} all-gather(bf16[3,4,2048]{2,0,1:T(4,128)(2,1)S(1)} %copy.9), channel_id=1, replica_groups=mesh['section'=4,'feat'=2,'tensor'=4] {'section','feat'}, dimensions={1}, use_global_device_ids=true | all-gather | bytes 442368 | tf_op jit(solution)/shard_map/all_gather | solution.py:9
  19.5 0.3 slice.21
  19.8 0.2 slice.20
  20.0 2.3 %convolution_bitcast_fusion = f32[1,32,512]{2,1,0:T(8,128)S(1)} fusion(bf16[512,2048]{1,0:T(8,128)(2,1)} %param.11, bf16[1,32,2048]{2,0,1:T(2,128)(2,1)S(1)} %slice.21), kind=kOutput, calls=%fused_computation.2 | convolution fusion | flops 67108864 | bytes 2293760 | tf_op jit(solution)/shard_map/dot_general | solution.py:13
  22.4 0.0 copy-done
  22.4 0.0 copy-start.1
  22.4 0.0 copy-start.2
  22.4 0.0 copy-start.3
  22.4 0.0 copy-start.5
  22.4 0.0 copy-start.4
  22.4 0.5 fusion
  22.9 0.7 pad_maximum_fusion
  23.6 0.0 all-reduce.3.cloned.1.call-update
  23.6 0.0 copy-done.1
  23.6 0.1 multiply_reduce_fusion
  23.8 12.0 %psum.15 = f32[4]{0:T(128)S(1)} all-reduce(f32[4]{0:T(128)S(1)} %multiply_reduce_fusion), channel_id=1, replica_groups=mesh['section'=4,'feat'=2,'tensor'=4] {'tensor'}, use_global_device_ids=true, to_apply=%region_3.4 | all-reduce | flops 4 | bytes 32 | tf_op jit(solution)/shard_map/psum | solution.py:19
  35.8 0.6 dynamic-slice
  37.0 21.9 %all-reduce.3.cloned.1.call-done = f32[3,32,512]{2,1,0:T(8,128)} async-done(((f32[3,32,512]{2,1,0:T(8,128)}), f32[3,32,512]{2,1,0:T(8,128)}) %all-reduce.3.cloned.1.call-update) | async-done | bytes 196624 | tf_op jit(solution)/shard_map/psum | solution.py:19
  58.9 1.5 %fusion.9 = (f32[32]{0:T(128)S(1)}, f32[512]{0:T(512)}) fusion(f32[3,32,512]{2,1,0:T(8,128)} %all-reduce.3.cloned.1.call-done, f32[512]{0:T(512)S(1)} %copy-done.4), kind=kLoop, calls=%fused_computation.18 | loop fusion | flops 130528 | bytes 200832 | tf_op jit(solution)/shard_map/reduce_sum | solution.py:24
  60.4 11.8 %all-reduce = f32[32]{0:T(128)S(1)} all-reduce(f32[32]{0:T(128)S(1)} %get-tuple-element.2), channel_id=2, replica_groups=mesh['section'=4,'feat'=2,'tensor'=4] {'section','feat'}, use_global_device_ids=true, to_apply=%region_5.6.clone | all-reduce | flops 32 | bytes 256
  72.2 0.6 dynamic-slice_subtract_fusion
  (5 shorter events, 0.1 us)
Async XLA Ops:
  7.2 15.2 %copy-start = (bf16[2048,512]{1,0:T(8,128)(2,1)S(1)}, bf16[2048,512]{1,0:T(8,128)(2,1)}, u32[]{:S(2)}) copy-start(bf16[2048,512]{1,0:T(8,128)(2,1)} %param.9) | copy-start | bytes 6291460
  7.2 51.7 %all-reduce.3.cloned.1.call-start = ((), (), s32[]{:S(2)}) async-start(), calls=%async_computation | async-start | bytes 393216 | tf_op jit(solution)/shard_map/psum | solution.py:19
  22.4 1.2 %copy-start.1 = (bf16[4,2048]{1,0:T(4,128)(2,1)S(1)}, bf16[4,2048]{1,0:T(4,128)(2,1)}, u32[]{:S(2)}) copy-start(bf16[4,2048]{1,0:T(4,128)(2,1)} %param.8) | copy-start | bytes 49156
  22.4 1.2 %copy-start.2 = (bf16[4,2048]{1,0:T(4,128)(2,1)S(1)}, bf16[4,2048]{1,0:T(4,128)(2,1)}, u32[]{:S(2)}) copy-start(bf16[4,2048]{1,0:T(4,128)(2,1)} %param.7) | copy-start | bytes 49156
  22.4 1.2 %copy-start.3 = (bf16[4,2048]{1,0:T(4,128)(2,1)S(1)}, bf16[4,2048]{1,0:T(4,128)(2,1)}, u32[]{:S(2)}) copy-start(bf16[4,2048]{1,0:T(4,128)(2,1)} %param.6) | copy-start | bytes 49156
  22.4 13.4 %copy-start.5 = (u32[32]{0:T(128)S(1)}, u32[32]{0:T(128)}, u32[]{:S(2)}) copy-start(u32[32]{0:T(128)} %constant.10) | copy-start | bytes 388
  22.4 36.5 %copy-start.4 = (f32[512]{0:T(512)S(1)}, f32[512]{0:T(512)}, u32[]{:S(2)}) copy-start(f32[512]{0:T(512)} %param.10) | copy-start | bytes 6148
Sparse Core Ops, SparseCore 0:
  23.7 35.1 all-reduce.2
where the time goes:
time: 79.9 us; the launch traced here: 79.6 us
  blocking collectives  35.1 us (44%)
  waiting for transfers between devices  21.9 us (27%)
  between operations  14.8 us (19%)
  other arithmetic  3.86 us (5%)
  matrix products  2.79 us (3%)
  local copies, waits for them, and re-layouts  1.16 us (1%)
    psum x1, waiting for transfers between devices, per_device(): preact, inner_sum = lax.psum((preact, inner_part), 'tensor')  21.9 us
    psum x1, blocking collectives, per_device(): preact, inner_sum = lax.psum((preact, inner_part), 'tensor')  12 us
    unnamed x1, blocking collectives  11.8 us
    all_gather x1, blocking collectives, per_device(): lax.all_gather(stacked, ('section', 'feat'), axis=1, tiled=True)  11.3 us
    dot_general x1, matrix products, per_device(): lax.dot_general(rows_piece[2], dec_weight, (((1,), (1,)), ((), ())), pref...  2.33 us
  transfers between devices with their start and end apart: 1, of which 1 were waited for; matrix products, arithmetic and copies ran while one was open for 1% of the time, Pallas kernels for 0%

commit v1 on v0

v1 whole, which is shorter than its diff:
```python
import jax
import jax.numpy as jnp
from jax import lax
from jax.sharding import PartitionSpec as P

OWNERS = ("section", "feat")
EVERY = ("section", "feat", "tensor")


def add_up(values):
    while len(values) > 1:
        values = [a + b for a, b in zip(values[::2], values[1::2])]
    return values[0]


def per_device(groups, parts, clean_resid, corrupt_resid, metric_grad, enc_weight, enc_bias, dec_weight):
    tokens = clean_resid.shape[0]
    features = enc_weight.shape[1]
    run = groups // parts
    me = lax.axis_index("tensor")

    stacked = jnp.stack([clean_resid, corrupt_resid, metric_grad])
    blocks = [stacked] + [
        lax.ppermute(stacked, OWNERS, [(g, g ^ k) for g in range(groups)]) for k in range(1, groups)
    ]
    rows = jnp.concatenate(blocks, axis=1)
    encoded = jnp.einsum("srd,df->srf", rows[:2], enc_weight, preferred_element_type=jnp.float32)
    projected = lax.dot_general(
        rows[2], dec_weight, (((1,), (1,)), ((), ())), preferred_element_type=jnp.float32
    )
    preact = jnp.concatenate([encoded, projected[None]], axis=0)
    preact = preact.reshape(3, parts, run * tokens, features)

    terms = [lax.dynamic_index_in_dim(preact, me, 1, keepdims=False)]
    for m in range(1, parts):
        chunk = lax.dynamic_index_in_dim(preact, me ^ m, 1, keepdims=False)
        terms.append(lax.ppermute(chunk, "tensor", [(t, t ^ m) for t in range(parts)]))
    total = add_up(terms)

    act_clean = jax.nn.relu(total[0] + enc_bias)
    act_corrupt = jax.nn.relu(total[1] + enc_bias)
    attribution = (act_corrupt - act_clean) * total[2]
    feature_part = jnp.sum(attribution, axis=0)
    token_part = jnp.sum(attribution, axis=1).reshape(run, tokens)
    shifted = corrupt_resid.astype(jnp.float32) - clean_resid.astype(jnp.float32)
    inner_part = jnp.sum(shifted * metric_grad.astype(jnp.float32), axis=1)

    both = jnp.concatenate([feature_part, inner_part])
    sums = [both] + [
        lax.ppermute(both, "tensor", [(t, t ^ m) for t in range(parts)]) for m in range(1, parts)
    ]
    sums = add_up(sums)
    feature_effect, inner_sum = sums[:features], sums[features:]
    totals = []
    for m in range(parts):
        arrived = []
        for j in range(run):
            pairs = [
                (g * parts + t, (g ^ (t * run + j)) * parts + (t ^ m))
                for g in range(groups)
                for t in range(parts)
            ]
            arrived.append(lax.ppermute(token_part[j], EVERY, pairs))
        totals.append(sum(arrived))
    error_sum = inner_sum - add_up(totals)
    return (feature_effect, error_sum)


def solution(mesh):
    groups = mesh.shape["section"] * mesh.shape["feat"]
    parts = mesh.shape["tensor"]
    in_specs = (
        P(("section", "feat"), "tensor"),
        P(("section", "feat"), "tensor"),
        P(("section", "feat"), "tensor"),
        P("tensor", ("section", "feat")),
        P(("section", "feat")),
        P(("section", "feat"), "tensor"),
    )
    out_specs = (P(("section", "feat")), P(("section", "feat")))

    def run(*args):
        return per_device(groups, parts, *args)

    return jax.shard_map(run, mesh=mesh, in_specs=in_specs, out_specs=out_specs, check_vma=False)
```

time: 79.9 us -> 50.8 us (0.64)
  blocking collectives: 35.1 us -> 0 us
  starting transfers between devices: 0.04 us -> 28.7 us
  between operations: 14.8 us -> 0.77 us
  waiting for transfers between devices: 21.9 us -> 16.1 us
  other arithmetic: 3.86 us -> 1.76 us
  matrix products: 2.79 us -> 1.18 us
  local copies, waits for them, and re-layouts: 1.16 us -> 2.03 us
    ppermute x0 -> x21, starting transfers between devices: none -> 28.7 us  [the longest x8 12.1 us: per_device(): arrived.append(lax.ppermute(token_part[j], EVERY, pairs))]
    psum x1 -> x0, waiting for transfers between devices: 21.9 us -> none  [per_device(): preact, inner_sum = lax.psum((preact, inner_part), 'tensor')]
    ppermute x0 -> x21, waiting for transfers between devices: none -> 16.1 us  [the longest x8 6.06 us: per_device(): arrived.append(lax.ppermute(token_part[j], EVERY, pairs))]
    psum x1 -> x0, blocking collectives: 12 us -> none  [per_device(): preact, inner_sum = lax.psum((preact, inner_part), 'tensor')]
    unnamed x1 -> x0, blocking collectives: 11.8 us -> none
    all_gather x1 -> x0, blocking collectives: 11.3 us -> none  [per_device(): lax.all_gather(stacked, ('section', 'feat'), axis=1, tiled=True)]
    dot_general x2, matrix products: 2.79 us -> 1.18 us  [the longest x1 0.71 us: per_device(): lax.dot_general(rows[2], dec_weight, (((1,), (1,)), ((), ())), preferred_...]
    reduce_sum x1, other arithmetic: 1.51 us -> 0.12 us  [per_device(): token_part = jnp.sum(attribution, axis=1).reshape(run, tokens)]
  transfers between devices with their start and end apart: 1 -> 21, of which waited for: 1 -> 7; matrix products, arithmetic and copies ran while one was open for 1% -> 2% of each run, Pallas kernels for 0% -> 0%
where the time goes in v1:
time: 50.8 us; the launch traced here: 50.5 us
  starting transfers between devices  28.7 us (56%)
  waiting for transfers between devices  16.1 us (32%)
  local copies, waits for them, and re-layouts  2.03 us (4%)
  other arithmetic  1.76 us (3%)
  matrix products  1.18 us (2%)
  between operations  0.77 us (2%)
    ppermute x8, starting transfers between devices, per_device(): arrived.append(lax.ppermute(token_part[j], EVERY, pairs))  12.1 us
    ppermute x7, starting transfers between devices, per_device(): lax.ppermute(stacked, OWNERS, [(g, g ^ k) for g in range(groups)])  7.65 us
    ppermute x8, waiting for transfers between devices, per_device(): arrived.append(lax.ppermute(token_part[j], EVERY, pairs))  6.06 us
    ppermute x3, waiting for transfers between devices, per_device(): lax.ppermute(chunk, 'tensor', [(t, t ^ m) for t in range(parts)])  5.52 us
    ppermute x7, waiting for transfers between devices, per_device(): lax.ppermute(stacked, OWNERS, [(g, g ^ k) for g in range(groups)])  4.48 us
    ppermute x3, starting transfers between devices, per_device(): lax.ppermute(chunk, 'tensor', [(t, t ^ m) for t in range(parts)])  4.45 us
    ppermute x3, starting transfers between devices, per_device(): lax.ppermute(both, 'tensor', [(t, t ^ m) for t in range(parts)])  4.44 us
    unnamed x12, local copies, waits for them, and re-layouts  1.11 us
  transfers between devices with their start and end apart: 21, of which 7 were waited for; matrix products, arithmetic and copies ran while one was open for 2% of the time, Pallas kernels for 0%

profile of v1, /device:TPU:0, one launch (start us, length us, event | category | flops | bytes accessed | tf_op | source)
XLA Modules:
  0.0 50.5 jit_solution(14733339454710134843)
XLA Ops:
  0.6 0.9 %pad_maximum_fusion = bf16[3,4,2048]{2,1,0:T(4,128)(2,1)S(1)} fusion(bf16[1,4,2048]{2,1,0:T(4,128)(2,1)} %bitcast.55, bf16[1,4,2048]{2,1,0:T(4,128)(2,1)} %bitcast.57, bf16[1,4,2048]{2,1,0:T(4,128)(2,1)} %bitcast.56), kind=kLoop, calls=%fused_computation.25 | loop fusion | flops 49152 | bytes 98304 | tf_op jit(solution)/shard_map/stack | solution.py:22
  2.1 2.6 %collective-permute-start.1 = (bf16[3,4,2048]{2,1,0:T(4,128)(2,1)S(1)}, bf16[3,4,2048]{2,1,0:T(4,128)(2,1)S(1)}, u32[]{:S(2)}, u32[]{:S(2)}) collective-permute-start(bf16[3,4,2048]{2,1,0:T(4,128)(2,1)S(1)} %pad_maximum_fusion), channel_id=1, source_target_pairs={{0,8},{4,12},{8,0},{12,4},{16,24},{20,28},{24,16},{28,20},{1,9},{5... | collective-permute-start | bytes 147464 | tf_op jit(solution)/shard_map/ppermute | solution.py:24
  4.7 1.8 %collective-permute-start.3 = (bf16[3,4,2048]{2,1,0:T(4,128)(2,1)S(1)}, bf16[3,4,2048]{2,1,0:T(4,128)(2,1)S(1)}, u32[]{:S(2)}, u32[]{:S(2)}) collective-permute-start(bf16[3,4,2048]{2,1,0:T(4,128)(2,1)S(1)} %pad_maximum_fusion), channel_id=1, source_target_pairs={{0,16},{4,20},{8,24},{12,28},{16,0},{20,4},{24,8},{28,12},{1,17},{... | collective-permute-start | bytes 147464 | tf_op jit(solution)/shard_map/ppermute | solution.py:24
  6.5 2.6 %collective-permute-start.5 = (bf16[3,4,2048]{2,1,0:T(4,128)(2,1)S(1)}, bf16[3,4,2048]{2,1,0:T(4,128)(2,1)S(1)}, u32[]{:S(2)}, u32[]{:S(2)}) collective-permute-start(bf16[3,4,2048]{2,1,0:T(4,128)(2,1)S(1)} %pad_maximum_fusion), channel_id=1, source_target_pairs={{0,24},{4,28},{8,16},{12,20},{16,8},{20,12},{24,0},{28,4},{1,25},{... | collective-permute-start | bytes 147464 | tf_op jit(solution)/shard_map/ppermute | solution.py:24
  9.3 1.1 %collective-permute-done.4 = bf16[3,4,2048]{2,1,0:T(4,128)(2,1)S(1)} collective-permute-done((bf16[3,4,2048]{2,1,0:T(4,128)(2,1)S(1)}, bf16[3,4,2048]{2,1,0:T(4,128)(2,1)S(1)}, u32[]{:S(2)}, u32[]{:S(2)}) %collective-permute-start.4) | collective-permute-done | bytes 49184 | tf_op jit(solution)/shard_map/ppermute | solution.py:24
  10.3 1.3 %collective-permute-done.5 = bf16[3,4,2048]{2,1,0:T(4,128)(2,1)S(1)} collective-permute-done((bf16[3,4,2048]{2,1,0:T(4,128)(2,1)S(1)}, bf16[3,4,2048]{2,1,0:T(4,128)(2,1)S(1)}, u32[]{:S(2)}, u32[]{:S(2)}) %collective-permute-start.5) | collective-permute-done | bytes 49184 | tf_op jit(solution)/shard_map/ppermute | solution.py:24
  11.6 2.1 %collective-permute-done.6 = bf16[3,4,2048]{2,1,0:T(4,128)(2,1)S(1)} collective-permute-done((bf16[3,4,2048]{2,1,0:T(4,128)(2,1)S(1)}, bf16[3,4,2048]{2,1,0:T(4,128)(2,1)S(1)}, u32[]{:S(2)}, u32[]{:S(2)}) %collective-permute-start.6) | collective-permute-done | bytes 49184 | tf_op jit(solution)/shard_map/ppermute | solution.py:24
  14.5 1.1 %copy-done.1 = bf16[512,2048]{1,0:T(8,128)(2,1)S(1)} copy-done((bf16[512,2048]{1,0:T(8,128)(2,1)S(1)}, bf16[512,2048]{1,0:T(8,128)(2,1)}, u32[]{:S(2)}) %copy-start.1) | copy-done | bytes 2097176
  15.6 0.7 %fusion.7 = f32[1,4,8,512]{3,2,1,0:T(8,128)S(1)} fusion(bf16[512,2048]{1,0:T(8,128)(2,1)S(1)} %copy-done.1, bf16[3,32,2048]{2,1,0:T(8,128)(2,1)S(1)} %concatenate.12), kind=kOutput, calls=%fused_computation.5 | convolution fusion | flops 67108864 | bytes 2293760 | tf_op jit(solution)/shard_map/dot_general | solution.py:28
  16.3 1.6 %collective-permute-start.7 = (f32[3,8,512]{2,1,0:T(8,128)S(1)}, f32[3,8,512]{2,1,0:T(8,128)S(1)}, u32[]{:S(2)}, u32[]{:S(2)}) collective-permute-start(f32[3,8,512]{2,1,0:T(8,128)S(1)} %get-tuple-element.5), channel_id=1, source_target_pairs={{0,1},{1,0},{2,3},{3,2},{4,5},{5,4},{6,7},{7,6},{8,9},{9,8},{10,11... | collective-permute-start | bytes 147464 | tf_op jit(solution)/shard_map/ppermute | solution.py:37
  18.0 2.6 %collective-permute-start.8 = (f32[3,8,512]{2,1,0:T(8,128)S(1)}, f32[3,8,512]{2,1,0:T(8,128)S(1)}, u32[]{:S(2)}, u32[]{:S(2)}) collective-permute-start(f32[3,8,512]{2,1,0:T(8,128)S(1)} %get-tuple-element.6), channel_id=1, source_target_pairs={{0,2},{1,3},{2,0},{3,1},{4,6},{5,7},{6,4},{7,5},{8,10},{9,11},{10,... | collective-permute-start | bytes 147464 | tf_op jit(solution)/shard_map/ppermute | solution.py:37
  20.9 2.9 %collective-permute-done.8 = f32[3,8,512]{2,1,0:T(8,128)S(1)} collective-permute-done((f32[3,8,512]{2,1,0:T(8,128)S(1)}, f32[3,8,512]{2,1,0:T(8,128)S(1)}, u32[]{:S(2)}, u32[]{:S(2)}) %collective-permute-start.8) | collective-permute-done | bytes 49184 | tf_op jit(solution)/shard_map/ppermute | solution.py:37
  23.9 2.6 %collective-permute-done.9 = f32[3,8,512]{2,1,0:T(8,128)S(1)} collective-permute-done((f32[3,8,512]{2,1,0:T(8,128)S(1)}, f32[3,8,512]{2,1,0:T(8,128)S(1)}, u32[]{:S(2)}, u32[]{:S(2)}) %collective-permute-start.9) | collective-permute-done | bytes 49184 | tf_op jit(solution)/shard_map/ppermute | solution.py:37
  26.7 1.6 %collective-permute-start.11 = (f32[516]{0:T(1024)S(1)}, f32[516]{0:T(1024)S(1)}, u32[]{:S(2)}, u32[]{:S(2)}) collective-permute-start(f32[516]{0:T(1024)S(1)} %pad_maximum_fusion.1), channel_id=1, source_target_pairs={{0,2},{1,3},{2,0},{3,1},{4,6},{5,7},{6,4},{7,5},{8,10},{9,11},{10,... | collective-permute-start | bytes 6200 | tf_op jit(solution)/shard_map/ppermute | solution.py:50
  28.3 2.8 %collective-permute-start.12 = (f32[516]{0:T(1024)S(1)}, f32[516]{0:T(1024)S(1)}, u32[]{:S(2)}, u32[]{:S(2)}) collective-permute-start(f32[516]{0:T(1024)S(1)} %pad_maximum_fusion.1), channel_id=1, source_target_pairs={{0,3},{1,2},{2,1},{3,0},{4,7},{5,6},{6,5},{7,4},{8,11},{9,10},{10,... | collective-permute-start | bytes 6200 | tf_op jit(solution)/shard_map/ppermute | solution.py:50
  31.1 0.6 %collective-permute-start.13 = (f32[4]{0:T(128)S(1)}, f32[4]{0:T(128)S(1)}, u32[]{:S(2)}, u32[]{:S(2)}) collective-permute-start(f32[4]{0:T(128)S(1)} %get-tuple-element.8), channel_id=1, source_target_pairs={{0,0},{1,9},{2,18},{3,27},{4,4},{5,13},{6,22},{7,31},{8,8},{9,1},{... | collective-permute-start | bytes 56 | tf_op jit(solution)/shard_map/ppermute | solution.py:63
  31.8 1.0 %collective-permute-start.15 = (f32[4]{0:T(128)S(1)}, f32[4]{0:T(128)S(1)}, u32[]{:S(2)}, u32[]{:S(2)}) collective-permute-start(f32[4]{0:T(128)S(1)} %get-tuple-element.8), channel_id=1, source_target_pairs={{0,1},{1,8},{2,19},{3,26},{4,5},{5,12},{6,23},{7,30},{8,9},{9,0},{... | collective-permute-start | bytes 56 | tf_op jit(solution)/shard_map/ppermute | solution.py:63
  32.8 2.2 %collective-permute-start.16 = (f32[4]{0:T(128)S(1)}, f32[4]{0:T(128)S(1)}, u32[]{:S(2)}, u32[]{:S(2)}) collective-permute-start(f32[4]{0:T(128)S(1)} %get-tuple-element.7), channel_id=1, source_target_pairs={{0,5},{1,12},{2,23},{3,30},{4,1},{5,8},{6,19},{7,26},{8,13},{9,4},... | collective-permute-start | bytes 56 | tf_op jit(solution)/shard_map/ppermute | solution.py:63
  35.1 3.4 %collective-permute-start.17 = (f32[4]{0:T(128)S(1)}, f32[4]{0:T(128)S(1)}, u32[]{:S(2)}, u32[]{:S(2)}) collective-permute-start(f32[4]{0:T(128)S(1)} %get-tuple-element.8), channel_id=1, source_target_pairs={{0,2},{1,11},{2,16},{3,25},{4,6},{5,15},{6,20},{7,29},{8,10},{9,3}... | collective-permute-start | bytes 56 | tf_op jit(solution)/shard_map/ppermute | solution.py:63
  38.5 0.6 %slice.40 = f32[512]{0:T(512)} slice(f32[516]{0:T(1024)S(1)} %add_add_fusion), slice={[0:512]} | slice | bytes 4096 | tf_op jit(solution)/shard_map/slice | solution.py:53
  39.1 4.3 %collective-permute-start.19 = (f32[4]{0:T(128)S(1)}, f32[4]{0:T(128)S(1)}, u32[]{:S(2)}, u32[]{:S(2)}) collective-permute-start(f32[4]{0:T(128)S(1)} %get-tuple-element.8), channel_id=1, source_target_pairs={{0,3},{1,10},{2,17},{3,24},{4,7},{5,14},{6,21},{7,28},{8,11},{9,2}... | collective-permute-start | bytes 56 | tf_op jit(solution)/shard_map/ppermute | solution.py:63
  43.9 2.4 %collective-permute-done.19 = f32[4]{0:T(128)S(1)} collective-permute-done((f32[4]{0:T(128)S(1)}, f32[4]{0:T(128)S(1)}, u32[]{:S(2)}, u32[]{:S(2)}) %collective-permute-start.19) | collective-permute-done | bytes 48 | tf_op jit(solution)/shard_map/ppermute | solution.py:63
  46.3 3.7 %collective-permute-done.20 = f32[4]{0:T(128)S(1)} collective-permute-done((f32[4]{0:T(128)S(1)}, f32[4]{0:T(128)S(1)}, u32[]{:S(2)}, u32[]{:S(2)}) %collective-permute-start.20) | collective-permute-done | bytes 48 | tf_op jit(solution)/shard_map/ppermute | solution.py:63
  50.0 0.5 %add_subtract_fusion = f32[4]{0:T(128)} fusion(f32[4]{0:T(128)S(1)} %collective-permute-done.19, f32[4]{0:T(128)S(1)} %collective-permute-done.20, f32[4]{0:T(128)S(1)} %collective-permute-done.17, f32[4]{0:T(128)S(1)} %collective-permute-done.18, f32[4]{0:T(128)S(1)} %collective-permute-done.15, f32[4]{0:T(128)S(1)} %collective-permute-done.16, ...), kind=kLoop, calls=%fused_computation.38 | loop fusion | flops 32 | bytes 160 | tf_op jit(solution)/shard_map/sub | solution.py:65
  (43 shorter events, 2.7 us)
Async XLA Ops:
  0.6 13.4 %copy-start = (bf16[2048,512]{1,0:T(8,128)(2,1)S(1)}, bf16[2048,512]{1,0:T(8,128)(2,1)}, u32[]{:S(2)}) copy-start(bf16[2048,512]{1,0:T(8,128)(2,1)} %param.9) | copy-start | bytes 6291460
  1.6 4.9 %collective-permute-start = (bf16[3,4,2048]{2,1,0:T(4,128)(2,1)S(1)}, bf16[3,4,2048]{2,1,0:T(4,128)(2,1)S(1)}, u32[]{:S(2)}, u32[]{:S(2)}) collective-permute-start(bf16[3,4,2048]{2,1,0:T(4,128)(2,1)S(1)} %pad_maximum_fusion), channel_id=1, source_target_pairs={{0,4},{4,0},{8,12},{12,8},{16,20},{20,16},{24,28},{28,24},{1,5},{5... | collective-permute-start | bytes 147464 | tf_op jit(solution)/shard_map/ppermute | solution.py:24
  2.1 7.0 %collective-permute-start.1 = (bf16[3,4,2048]{2,1,0:T(4,128)(2,1)S(1)}, bf16[3,4,2048]{2,1,0:T(4,128)(2,1)S(1)}, u32[]{:S(2)}, u32[]{:S(2)}) collective-permute-start(bf16[3,4,2048]{2,1,0:T(4,128)(2,1)S(1)} %pad_maximum_fusion), channel_id=1, source_target_pairs={{0,8},{4,12},{8,0},{12,4},{16,24},{20,28},{24,16},{28,20},{1,9},{5... | collective-permute-start | bytes 147464 | tf_op jit(solution)/shard_map/ppermute | solution.py:24
  4.7 4.6 %collective-permute-start.2 = (bf16[3,4,2048]{2,1,0:T(4,128)(2,1)S(1)}, bf16[3,4,2048]{2,1,0:T(4,128)(2,1)S(1)}, u32[]{:S(2)}, u32[]{:S(2)}) collective-permute-start(bf16[3,4,2048]{2,1,0:T(4,128)(2,1)S(1)} %pad_maximum_fusion), channel_id=1, source_target_pairs={{0,12},{4,8},{8,4},{12,0},{16,28},{20,24},{24,20},{28,16},{1,13},{... | collective-permute-start | bytes 147464 | tf_op jit(solution)/shard_map/ppermute | solution.py:24
  4.7 4.5 %collective-permute-start.3 = (bf16[3,4,2048]{2,1,0:T(4,128)(2,1)S(1)}, bf16[3,4,2048]{2,1,0:T(4,128)(2,1)S(1)}, u32[]{:S(2)}, u32[]{:S(2)}) collective-permute-start(bf16[3,4,2048]{2,1,0:T(4,128)(2,1)S(1)} %pad_maximum_fusion), channel_id=1, source_target_pairs={{0,16},{4,20},{8,24},{12,28},{16,0},{20,4},{24,8},{28,12},{1,17},{... | collective-permute-start | bytes 147464 | tf_op jit(solution)/shard_map/ppermute | solution.py:24
  6.5 3.8 %collective-permute-start.4 = (bf16[3,4,2048]{2,1,0:T(4,128)(2,1)S(1)}, bf16[3,4,2048]{2,1,0:T(4,128)(2,1)S(1)}, u32[]{:S(2)}, u32[]{:S(2)}) collective-permute-start(bf16[3,4,2048]{2,1,0:T(4,128)(2,1)S(1)} %pad_maximum_fusion), channel_id=1, source_target_pairs={{0,20},{4,16},{8,28},{12,24},{16,4},{20,0},{24,12},{28,8},{1,21},{... | collective-permute-start | bytes 147464 | tf_op jit(solution)/shard_map/ppermute | solution.py:24
  6.5 5.1 %collective-permute-start.5 = (bf16[3,4,2048]{2,1,0:T(4,128)(2,1)S(1)}, bf16[3,4,2048]{2,1,0:T(4,128)(2,1)S(1)}, u32[]{:S(2)}, u32[]{:S(2)}) collective-permute-start(bf16[3,4,2048]{2,1,0:T(4,128)(2,1)S(1)} %pad_maximum_fusion), channel_id=1, source_target_pairs={{0,24},{4,28},{8,16},{12,20},{16,8},{20,12},{24,0},{28,4},{1,25},{... | collective-permute-start | bytes 147464 | tf_op jit(solution)/shard_map/ppermute | solution.py:24
  9.1 4.6 %collective-permute-start.6 = (bf16[3,4,2048]{2,1,0:T(4,128)(2,1)S(1)}, bf16[3,4,2048]{2,1,0:T(4,128)(2,1)S(1)}, u32[]{:S(2)}, u32[]{:S(2)}) collective-permute-start(bf16[3,4,2048]{2,1,0:T(4,128)(2,1)S(1)} %pad_maximum_fusion), channel_id=1, source_target_pairs={{0,28},{4,24},{8,20},{12,16},{16,12},{20,8},{24,4},{28,0},{1,29},{... | collective-permute-start | bytes 147464 | tf_op jit(solution)/shard_map/ppermute | solution.py:24
  14.0 6.8 %copy-start.2 = (bf16[4,2048]{1,0:T(4,128)(2,1)S(1)}, bf16[4,2048]{1,0:T(4,128)(2,1)}, u32[]{:S(2)}) copy-start(bf16[4,2048]{1,0:T(4,128)(2,1)} %param.8) | copy-start | bytes 49156
  15.6 10.9 %copy-start.5 = (f32[512]{0:T(512)S(1)}, f32[512]{0:T(512)}, u32[]{:S(2)}) copy-start(f32[512]{0:T(512)} %param.10) | copy-start | bytes 6148
  16.3 4.6 %collective-permute-start.7 = (f32[3,8,512]{2,1,0:T(8,128)S(1)}, f32[3,8,512]{2,1,0:T(8,128)S(1)}, u32[]{:S(2)}, u32[]{:S(2)}) collective-permute-start(f32[3,8,512]{2,1,0:T(8,128)S(1)} %get-tuple-element.5), channel_id=1, source_target_pairs={{0,1},{1,0},{2,3},{3,2},{4,5},{5,4},{6,7},{7,6},{8,9},{9,8},{10,11... | collective-permute-start | bytes 147464 | tf_op jit(solution)/shard_map/ppermute | solution.py:37
  18.0 5.9 %collective-permute-start.8 = (f32[3,8,512]{2,1,0:T(8,128)S(1)}, f32[3,8,512]{2,1,0:T(8,128)S(1)}, u32[]{:S(2)}, u32[]{:S(2)}) collective-permute-start(f32[3,8,512]{2,1,0:T(8,128)S(1)} %get-tuple-element.6), channel_id=1, source_target_pairs={{0,2},{1,3},{2,0},{3,1},{4,6},{5,7},{6,4},{7,5},{8,10},{9,11},{10,... | collective-permute-start | bytes 147464 | tf_op jit(solution)/shard_map/ppermute | solution.py:37
  20.6 5.9 %collective-permute-start.9 = (f32[3,8,512]{2,1,0:T(8,128)S(1)}, f32[3,8,512]{2,1,0:T(8,128)S(1)}, u32[]{:S(2)}, u32[]{:S(2)}) collective-permute-start(f32[3,8,512]{2,1,0:T(8,128)S(1)} %get-tuple-element.4), channel_id=1, source_target_pairs={{0,3},{1,2},{2,1},{3,0},{4,7},{5,6},{6,5},{7,4},{8,11},{9,10},{10,... | collective-permute-start | bytes 147464 | tf_op jit(solution)/shard_map/ppermute | solution.py:37
  26.6 6.2 %collective-permute-start.10 = (f32[516]{0:T(1024)S(1)}, f32[516]{0:T(1024)S(1)}, u32[]{:S(2)}, u32[]{:S(2)}) collective-permute-start(f32[516]{0:T(1024)S(1)} %pad_maximum_fusion.1), channel_id=1, source_target_pairs={{0,1},{1,0},{2,3},{3,2},{4,5},{5,4},{6,7},{7,6},{8,9},{9,8},{10,11... | collective-permute-start | bytes 6200 | tf_op jit(solution)/shard_map/ppermute | solution.py:50
  26.7 6.1 %collective-permute-start.11 = (f32[516]{0:T(1024)S(1)}, f32[516]{0:T(1024)S(1)}, u32[]{:S(2)}, u32[]{:S(2)}) collective-permute-start(f32[516]{0:T(1024)S(1)} %pad_maximum_fusion.1), channel_id=1, source_target_pairs={{0,2},{1,3},{2,0},{3,1},{4,6},{5,7},{6,4},{7,5},{8,10},{9,11},{10,... | collective-permute-start | bytes 6200 | tf_op jit(solution)/shard_map/ppermute | solution.py:50
  28.3 6.8 %collective-permute-start.12 = (f32[516]{0:T(1024)S(1)}, f32[516]{0:T(1024)S(1)}, u32[]{:S(2)}, u32[]{:S(2)}) collective-permute-start(f32[516]{0:T(1024)S(1)} %pad_maximum_fusion.1), channel_id=1, source_target_pairs={{0,3},{1,2},{2,1},{3,0},{4,7},{5,6},{6,5},{7,4},{8,11},{9,10},{10,... | collective-permute-start | bytes 6200 | tf_op jit(solution)/shard_map/ppermute | solution.py:50
  31.1 7.9 %collective-permute-start.13 = (f32[4]{0:T(128)S(1)}, f32[4]{0:T(128)S(1)}, u32[]{:S(2)}, u32[]{:S(2)}) collective-permute-start(f32[4]{0:T(128)S(1)} %get-tuple-element.8), channel_id=1, source_target_pairs={{0,0},{1,9},{2,18},{3,27},{4,4},{5,13},{6,22},{7,31},{8,8},{9,1},{... | collective-permute-start | bytes 56 | tf_op jit(solution)/shard_map/ppermute | solution.py:63
  31.8 11.6 %collective-permute-start.15 = (f32[4]{0:T(128)S(1)}, f32[4]{0:T(128)S(1)}, u32[]{:S(2)}, u32[]{:S(2)}) collective-permute-start(f32[4]{0:T(128)S(1)} %get-tuple-element.8), channel_id=1, source_target_pairs={{0,1},{1,8},{2,19},{3,26},{4,5},{5,12},{6,23},{7,30},{8,9},{9,0},{... | collective-permute-start | bytes 56 | tf_op jit(solution)/shard_map/ppermute | solution.py:63
  32.8 6.3 %collective-permute-start.14 = (f32[4]{0:T(128)S(1)}, f32[4]{0:T(128)S(1)}, u32[]{:S(2)}, u32[]{:S(2)}) collective-permute-start(f32[4]{0:T(128)S(1)} %get-tuple-element.7), channel_id=1, source_target_pairs={{0,4},{1,13},{2,22},{3,31},{4,0},{5,9},{6,18},{7,27},{8,12},{9,5},... | collective-permute-start | bytes 56 | tf_op jit(solution)/shard_map/ppermute | solution.py:63
  32.8 11.1 %collective-permute-start.16 = (f32[4]{0:T(128)S(1)}, f32[4]{0:T(128)S(1)}, u32[]{:S(2)}, u32[]{:S(2)}) collective-permute-start(f32[4]{0:T(128)S(1)} %get-tuple-element.7), channel_id=1, source_target_pairs={{0,5},{1,12},{2,23},{3,30},{4,1},{5,8},{6,19},{7,26},{8,13},{9,4},... | collective-permute-start | bytes 56 | tf_op jit(solution)/shard_map/ppermute | solution.py:63
  35.1 8.8 %collective-permute-start.17 = (f32[4]{0:T(128)S(1)}, f32[4]{0:T(128)S(1)}, u32[]{:S(2)}, u32[]{:S(2)}) collective-permute-start(f32[4]{0:T(128)S(1)} %get-tuple-element.8), channel_id=1, source_target_pairs={{0,2},{1,11},{2,16},{3,25},{4,6},{5,15},{6,20},{7,29},{8,10},{9,3}... | collective-permute-start | bytes 56 | tf_op jit(solution)/shard_map/ppermute | solution.py:63
  39.1 4.8 %collective-permute-start.18 = (f32[4]{0:T(128)S(1)}, f32[4]{0:T(128)S(1)}, u32[]{:S(2)}, u32[]{:S(2)}) collective-permute-start(f32[4]{0:T(128)S(1)} %get-tuple-element.7), channel_id=1, source_target_pairs={{0,6},{1,15},{2,20},{3,29},{4,2},{5,11},{6,16},{7,25},{8,14},{9,7}... | collective-permute-start | bytes 56 | tf_op jit(solution)/shard_map/ppermute | solution.py:63
  39.1 7.2 %collective-permute-start.19 = (f32[4]{0:T(128)S(1)}, f32[4]{0:T(128)S(1)}, u32[]{:S(2)}, u32[]{:S(2)}) collective-permute-start(f32[4]{0:T(128)S(1)} %get-tuple-element.8), channel_id=1, source_target_pairs={{0,3},{1,10},{2,17},{3,24},{4,7},{5,14},{6,21},{7,28},{8,11},{9,2}... | collective-permute-start | bytes 56 | tf_op jit(solution)/shard_map/ppermute | solution.py:63
  43.4 6.6 %collective-permute-start.20 = (f32[4]{0:T(128)S(1)}, f32[4]{0:T(128)S(1)}, u32[]{:S(2)}, u32[]{:S(2)}) collective-permute-start(f32[4]{0:T(128)S(1)} %get-tuple-element.7), channel_id=1, source_target_pairs={{0,7},{1,14},{2,21},{3,28},{4,3},{5,10},{6,17},{7,24},{8,15},{9,6}... | collective-permute-start | bytes 56 | tf_op jit(solution)/shard_map/ppermute | solution.py:63
  (3 other events, 15.1 us)

commit v2 on v0

v2 whole, which is shorter than its diff:
```python
import jax
import jax.numpy as jnp
from jax import lax
from jax.sharding import PartitionSpec as P

EVERY = ("section", "feat", "tensor")


def add_up(values):
    while len(values) > 1:
        values = [a + b for a, b in zip(values[::2], values[1::2])]
    return values[0]


def swap_all(value, axis, size):
    return [value] + [
        lax.ppermute(value, axis, [(i, i ^ k) for i in range(size)]) for k in range(1, size)
    ]


def per_device(sizes, clean_resid, corrupt_resid, metric_grad, enc_weight, enc_bias, dec_weight):
    sections, feats, parts = sizes
    groups = sections * feats
    tokens = clean_resid.shape[0]
    features = enc_weight.shape[1]
    share = features // parts

    stacked = jnp.stack([clean_resid, corrupt_resid, metric_grad])
    near = jnp.concatenate(swap_all(stacked, "section", sections), axis=1)
    rows = jnp.concatenate(swap_all(near, "feat", feats), axis=1)
    encoded = jnp.einsum("srd,df->srf", rows[:2], enc_weight, preferred_element_type=jnp.float32)
    projected = lax.dot_general(
        rows[2], dec_weight, (((1,), (1,)), ((), ())), preferred_element_type=jnp.float32
    )
    preact = jnp.concatenate([encoded, projected[None]], axis=0)
    preact = preact.reshape(3, groups * tokens, parts, share)

    total = add_up([*lax.all_to_all(preact.transpose(2, 0, 1, 3), "tensor", 0, 0)])
    bias = lax.dynamic_index_in_dim(enc_bias.reshape(parts, share), lax.axis_index("tensor"), 0)

    act_clean = jax.nn.relu(total[0] + bias)
    act_corrupt = jax.nn.relu(total[1] + bias)
    attribution = (act_corrupt - act_clean) * total[2]
    feature_part = jnp.sum(attribution, axis=0)
    token_part = jnp.sum(attribution, axis=1)
    shifted = corrupt_resid.astype(jnp.float32) - clean_resid.astype(jnp.float32)
    inner_part = jnp.sum(shifted * metric_grad.astype(jnp.float32), axis=1)
    token_part = token_part - jnp.pad(inner_part, (0, (groups - 1) * tokens))

    both = jnp.concatenate([feature_part, token_part])
    every = lax.all_to_all(jnp.broadcast_to(both, (groups * parts, both.size)), EVERY, 0, 0)
    section, feat = lax.axis_index("section"), lax.axis_index("feat")
    mine = lax.dynamic_slice_in_dim(every, (section * feats + feat) * parts, parts, 0)
    feature_effect = mine[:, :share].reshape(features)
    arrived = every[:, share:].reshape(sections, feats, parts, feats, sections, tokens)
    wanted = (
        jnp.arange(sections)[:, None, None, None] ^ section == jnp.arange(sections)
    ) & ((jnp.arange(feats)[:, None] ^ feat == jnp.arange(feats))[:, :, None])
    kept = jnp.where(wanted[:, :, None, :, :, None], arrived, 0.0)
    return (feature_effect, -jnp.sum(kept, axis=(0, 1, 2, 3, 4)))


def solution(mesh):
    sizes = [mesh.shape[name] for name in EVERY]
    in_specs = (
        P(("section", "feat"), "tensor"),
        P(("section", "feat"), "tensor"),
        P(("section", "feat"), "tensor"),
        P("tensor", ("section", "feat")),
        P(("section", "feat")),
        P(("section", "feat"), "tensor"),
    )
    out_specs = (P(("section", "feat")), P(("section", "feat")))

    def run(*args):
        return per_device(sizes, *args)

    return jax.shard_map(run, mesh=mesh, in_specs=in_specs, out_specs=out_specs, check_vma=False)
```

time: 79.9 us -> 42.4 us (0.53)
  blocking collectives: 35.1 us -> 0 us
  between operations: 14.8 us -> 0.75 us
  starting transfers between devices: 0.04 us -> 12.1 us
  waiting for transfers between devices: 21.9 us -> 19.5 us
  local copies, waits for them, and re-layouts: 1.16 us -> 2.43 us
    psum x1 -> x0, waiting for transfers between devices: 21.9 us -> none  [per_device(): preact, inner_sum = lax.psum((preact, inner_part), 'tensor')]
    all_to_all x0 -> x2, waiting for transfers between devices: none -> 14.1 us  [the longest x1 7.06 us: per_device(): lax.all_to_all(preact.transpose(2, 0, 1, 3), 'tensor', 0, 0)]
    psum x1 -> x0, blocking collectives: 12 us -> none  [per_device(): preact, inner_sum = lax.psum((preact, inner_part), 'tensor')]
    unnamed x1 -> x0, blocking collectives: 11.8 us -> none
    all_gather x1 -> x0, blocking collectives: 11.3 us -> none  [per_device(): lax.all_gather(stacked, ('section', 'feat'), axis=1, tiled=True)]
    all_to_all x0 -> x2, starting transfers between devices: none -> 7.44 us  [the longest x1 4.87 us: per_device(): lax.all_to_all(preact.transpose(2, 0, 1, 3), 'tensor', 0, 0)]
    ppermute x0 -> x4, waiting for transfers between devices: none -> 5.41 us  [swap_all(): lax.ppermute(value, axis, [(i, i ^ k) for i in range(size)])]
    ppermute x0 -> x4, starting transfers between devices: none -> 4.62 us  [swap_all(): lax.ppermute(value, axis, [(i, i ^ k) for i in range(size)])]
  transfers between devices with their start and end apart: 1 -> 6, of which waited for: 1 -> 5; matrix products, arithmetic and copies ran while one was open for 1% -> 5% of each run, Pallas kernels for 0% -> 0%
where the time goes in v2:
time: 42.4 us; the launch traced here: 41.8 us
  waiting for transfers between devices  19.5 us (46%)
  starting transfers between devices  12.1 us (29%)
  other arithmetic  4.35 us (10%)
  matrix products  2.79 us (7%)
  local copies, waits for them, and re-layouts  2.43 us (6%)
  between operations  0.75 us (2%)
    all_to_all x1, waiting for transfers between devices, per_device(): lax.all_to_all(preact.transpose(2, 0, 1, 3), 'tensor', 0, 0)  7.06 us
    all_to_all x1, waiting for transfers between devices, per_device(): lax.all_to_all(jnp.broadcast_to(both, (groups * parts, both.size)), EVERY...  7 us
    ppermute x4, waiting for transfers between devices, swap_all(): lax.ppermute(value, axis, [(i, i ^ k) for i in range(size)])  5.41 us
    all_to_all x1, starting transfers between devices, per_device(): lax.all_to_all(preact.transpose(2, 0, 1, 3), 'tensor', 0, 0)  4.87 us
    ppermute x4, starting transfers between devices, swap_all(): lax.ppermute(value, axis, [(i, i ^ k) for i in range(size)])  4.62 us
    all_to_all x1, starting transfers between devices, per_device(): lax.all_to_all(jnp.broadcast_to(both, (groups * parts, both.size)), EVERY...  2.57 us
    dot_general x1, matrix products, per_device(): jnp.einsum('srd,df->srf', rows[:2], enc_weight, preferred_element_type=jn...  2.06 us
    another operation x1, other arithmetic, per_device(): stacked = jnp.stack([clean_resid, corrupt_resid, metric_grad])  0.94 us
  transfers between devices with their start and end apart: 6, of which 5 were waited for; matrix products, arithmetic and copies ran while one was open for 5% of the time, Pallas kernels for 0%

profile of v2, /device:TPU:0, one launch (start us, length us, event | category | flops | bytes accessed | tf_op | source)
XLA Modules:
  0.0 41.8 jit_solution(1553266219844635313)
XLA Ops:
  0.6 0.9 %pad_maximum_fusion.1 = bf16[3,4,2048]{2,1,0:T(4,128)(2,1)S(1)} fusion(bf16[1,4,2048]{2,1,0:T(4,128)(2,1)} %bitcast.61, bf16[1,4,2048]{2,1,0:T(4,128)(2,1)} %bitcast.63, bf16[1,4,2048]{2,1,0:T(4,128)(2,1)} %bitcast.65), kind=kLoop, calls=%fused_computation.11 | loop fusion | flops 49152 | bytes 98304 | tf_op jit(solution)/shard_map/stack | solution.py:28
  1.6 3.0 %collective-permute-start = (bf16[3,4,2048]{2,1,0:T(4,128)(2,1)S(1)}, bf16[3,4,2048]{2,1,0:T(4,128)(2,1)S(1)}, u32[]{:S(2)}, u32[]{:S(2)}) collective-permute-start(bf16[3,4,2048]{2,1,0:T(4,128)(2,1)S(1)} %pad_maximum_fusion.1), channel_id=1, source_target_pairs={{0,8},{8,0},{16,24},{24,16},{1,9},{9,1},{17,25},{25,17},{2,10},{10... | collective-permute-start | bytes 147464 | tf_op jit(solution)/shard_map/ppermute | solution.py:17
  4.6 1.5 %collective-permute-start.1 = (bf16[3,4,2048]{2,1,0:T(4,128)(2,1)S(1)}, bf16[3,4,2048]{2,1,0:T(4,128)(2,1)S(1)}, u32[]{:S(2)}, u32[]{:S(2)}) collective-permute-start(bf16[3,4,2048]{2,1,0:T(4,128)(2,1)S(1)} %pad_maximum_fusion.1), channel_id=1, source_target_pairs={{0,16},{8,24},{16,0},{24,8},{1,17},{9,25},{17,1},{25,9},{2,18},{10... | collective-permute-start | bytes 147464 | tf_op jit(solution)/shard_map/ppermute | solution.py:17
  6.1 0.9 %multiply_reduce_fusion = f32[4]{0:T(128)S(1)} fusion(bf16[4,2048]{1,0:T(4,128)(2,1)} %param.8, bf16[4,2048]{1,0:T(4,128)(2,1)} %param.6, bf16[4,2048]{1,0:T(4,128)(2,1)} %param.7), kind=kLoop, calls=%fused_computation.13 | loop fusion | flops 49148 | bytes 49168 | tf_op jit(solution)/shard_map/reduce_sum | solution.py:47
  7.0 1.6 %collective-permute-done.1 = bf16[3,4,2048]{2,1,0:T(4,128)(2,1)S(1)} collective-permute-done((bf16[3,4,2048]{2,1,0:T(4,128)(2,1)S(1)}, bf16[3,4,2048]{2,1,0:T(4,128)(2,1)S(1)}, u32[]{:S(2)}, u32[]{:S(2)}) %collective-permute-start.1) | collective-permute-done | bytes 49184 | tf_op jit(solution)/shard_map/ppermute | solution.py:17
  8.7 2.4 %collective-permute-done.2 = bf16[3,4,2048]{2,1,0:T(4,128)(2,1)S(1)} collective-permute-done((bf16[3,4,2048]{2,1,0:T(4,128)(2,1)S(1)}, bf16[3,4,2048]{2,1,0:T(4,128)(2,1)S(1)}, u32[]{:S(2)}, u32[]{:S(2)}) %collective-permute-start.2) | collective-permute-done | bytes 49184 | tf_op jit(solution)/shard_map/ppermute | solution.py:17
  11.1 0.9 %pad_maximum_fusion = bf16[3,16,2048]{2,1,0:T(8,128)(2,1)S(1)} fusion(bf16[3,4,2048]{2,1,0:T(4,128)(2,1)S(1)} %collective-permute-done.2, bf16[3,4,2048]{2,1,0:T(4,128)(2,1)S(1)} %collective-permute-done.1, bf16[3,4,2048]{2,1,0:T(4,128)(2,1)S(1)} %collective-permute-done, bf16[1,4,2048]{2,1,0:T(4,128)(2,1)} %bitcast.62, bf16[1,4,2048]{2,1,0:T(4,128)(2,1)} %bitcast.64, ...), kind=kLoop, calls=%fused_computation.4 | loop fusion | flops 1179648 | bytes 393216 | tf_op jit(solution)/shard_map/concatenate | solution.py:29
  12.1 1.4 %collective-permute-done.3 = bf16[3,16,2048]{2,1,0:T(8,128)(2,1)S(1)} collective-permute-done((bf16[3,16,2048]{2,1,0:T(8,128)(2,1)S(1)}, bf16[3,16,2048]{2,1,0:T(8,128)(2,1)S(1)}, u32[]{:S(2)}, u32[]{:S(2)}) %collective-permute-start.3) | collective-permute-done | bytes 196640 | tf_op jit(solution)/shard_map/ppermute | solution.py:17
  13.5 0.2 concatenate.17
  13.7 2.1 %fusion.2 = f32[2,4,4,8,128]{4,3,2,1,0:T(8,128)S(1)} fusion(bf16[3,32,2048]{2,1,0:T(8,128)(2,1)S(1)} %concatenate.17, bf16[2048,512]{1,0:T(8,128)(2,1)} %param.9), kind=kOutput, calls=%fused_computation.2 | convolution fusion | flops 134217728 | bytes 2621440 | tf_op jit(solution)/shard_map/srd,df->srf/dot_general | solution.py:31
  15.8 0.7 %convolution_bitcast_fusion = f32[1,32,4,128]{3,1,0,2:T(8,128)S(1)} fusion(bf16[4,128,2048]{2,1,0:T(8,128)(2,1)S(1)} %bitcast.59, bf16[3,32,2048]{2,1,0:T(8,128)(2,1)S(1)} %concatenate.17), kind=kOutput, calls=%fused_computation.3 | convolution fusion | flops 67108864 | bytes 2293760 | tf_op jit(solution)/shard_map/dot_general | solution.py:32
  16.5 0.7 %maximum_bitcast_fusion = f32[4,3,32,128]{3,2,1,0:T(8,128)} fusion(f32[1,32,4,128]{3,1,0,2:T(8,128)S(1)} %convolution_bitcast_fusion, f32[2,32,4,128]{3,1,0,2:T(8,128)S(1)} %bitcast.60), kind=kLoop, calls=%fused_computation.5 | loop fusion | flops 49152 | bytes 393216 | tf_op jit(solution)/shard_map/transpose | solution.py:38
  17.2 4.9 %all-to-all-start = ((f32[4,3,32,128]{3,2,1,0:T(8,128)}), f32[4,3,32,128]{3,2,1,0:T(8,128)S(1)}, u32[]{:S(2)}, u32[]{:S(2)}) async-start(f32[4,3,32,128]{3,2,1,0:T(8,128)} %maximum_bitcast_fusion), calls=%async_computation | async-start | bytes 393216 | tf_op jit(solution)/shard_map/all_to_all | solution.py:38
  22.1 0.7 %dynamic-slice_bitcast_fusion = f32[128]{0:T(128)S(1)} fusion(f32[4,128]{1,0:T(4,128)} %bitcast.69, s32[]{:T(128)S(6)} %select_n.12), kind=kLoop, calls=%fused_computation.34 | loop fusion | bytes 1028 | tf_op jit(solution)/shard_map/add | solution.py:42
  22.9 7.1 %all-to-all-done = f32[4,3,32,128]{3,2,1,0:T(8,128)S(1)} async-done(((f32[4,3,32,128]{3,2,1,0:T(8,128)}), f32[4,3,32,128]{3,2,1,0:T(8,128)S(1)}, u32[]{:S(2)}, u32[]{:S(2)}) %all-to-all-start) | async-done | bytes 196640 | tf_op jit(solution)/shard_map/all_to_all | solution.py:38
  29.9 0.1 fusion.13
  30.1 0.6 %broadcast_in_dim.23 = f32[32,1,160]{2,1,0:T(1,128)} broadcast(f32[160]{0:T(256)S(1)} %pad_maximum_fusion.2), dimensions={2} | broadcast | bytes 21120 | tf_op jit(solution)/shard_map/broadcast_in_dim | solution.py:51
  30.7 2.6 %all-to-all-start.1 = ((f32[32,1,160]{2,1,0:T(1,128)}), f32[32,1,160]{2,1,0:T(1,128)S(1)}, u32[]{:S(2)}, u32[]{:S(2)}) async-start(f32[32,1,160]{2,1,0:T(1,128)} %broadcast_in_dim.23), calls=%async_computation.1 | async-start | bytes 65536 | tf_op jit(solution)/shard_map/all_to_all | solution.py:51
  33.4 0.1 broadcast_in_dim.24
  33.5 0.1 broadcast_in_dim.25
  33.6 7.0 %all-to-all-done.1 = f32[32,1,160]{2,1,0:T(1,128)S(1)} async-done(((f32[32,1,160]{2,1,0:T(1,128)}), f32[32,1,160]{2,1,0:T(1,128)S(1)}, u32[]{:S(2)}, u32[]{:S(2)}) %all-to-all-start.1) | async-done | bytes 20512 | tf_op jit(solution)/shard_map/all_to_all | solution.py:51
  40.6 0.1 reduce_sum.47
  40.7 0.5 %neg.3 = f32[4]{0:T(128)} negate(f32[4]{0:T(128)S(1)} %reduce_sum.48) | non-fusion elementwise | flops 4 | bytes 32 | tf_op jit(solution)/shard_map/neg | solution.py:60
  41.2 0.6 %slice_bitcast_fusion.5 = f32[512]{0:T(512)} fusion(f32[4,160]{1,0:T(4,128)S(1)} %bitcast.68), kind=kLoop, calls=%fused_computation.27 | loop fusion | bytes 4096 | tf_op jit(solution)/shard_map/reshape | solution.py:54
  (19 shorter events, 0.4 us)
Async XLA Ops:
  0.6 15.2 %copy-start = (bf16[512,2048]{1,0:T(8,128)(2,1)S(1)}, bf16[512,2048]{1,0:T(8,128)(2,1)}, u32[]{:S(2)}) copy-start(bf16[512,2048]{1,0:T(8,128)(2,1)} %param.11) | copy-start | bytes 6291460
  1.6 5.5 %collective-permute-start = (bf16[3,4,2048]{2,1,0:T(4,128)(2,1)S(1)}, bf16[3,4,2048]{2,1,0:T(4,128)(2,1)S(1)}, u32[]{:S(2)}, u32[]{:S(2)}) collective-permute-start(bf16[3,4,2048]{2,1,0:T(4,128)(2,1)S(1)} %pad_maximum_fusion.1), channel_id=1, source_target_pairs={{0,8},{8,0},{16,24},{24,16},{1,9},{9,1},{17,25},{25,17},{2,10},{10... | collective-permute-start | bytes 147464 | tf_op jit(solution)/shard_map/ppermute | solution.py:17
  4.6 4.1 %collective-permute-start.1 = (bf16[3,4,2048]{2,1,0:T(4,128)(2,1)S(1)}, bf16[3,4,2048]{2,1,0:T(4,128)(2,1)S(1)}, u32[]{:S(2)}, u32[]{:S(2)}) collective-permute-start(bf16[3,4,2048]{2,1,0:T(4,128)(2,1)S(1)} %pad_maximum_fusion.1), channel_id=1, source_target_pairs={{0,16},{8,24},{16,0},{24,8},{1,17},{9,25},{17,1},{25,9},{2,18},{10... | collective-permute-start | bytes 147464 | tf_op jit(solution)/shard_map/ppermute | solution.py:17
  6.1 5.0 %collective-permute-start.2 = (bf16[3,4,2048]{2,1,0:T(4,128)(2,1)S(1)}, bf16[3,4,2048]{2,1,0:T(4,128)(2,1)S(1)}, u32[]{:S(2)}, u32[]{:S(2)}) collective-permute-start(bf16[3,4,2048]{2,1,0:T(4,128)(2,1)S(1)} %pad_maximum_fusion.1), channel_id=1, source_target_pairs={{0,24},{8,16},{16,8},{24,0},{1,25},{9,17},{17,9},{25,1},{2,26},{10... | collective-permute-start | bytes 147464 | tf_op jit(solution)/shard_map/ppermute | solution.py:17
  12.0 1.5 %collective-permute-start.3 = (bf16[3,16,2048]{2,1,0:T(8,128)(2,1)S(1)}, bf16[3,16,2048]{2,1,0:T(8,128)(2,1)S(1)}, u32[]{:S(2)}, u32[]{:S(2)}) collective-permute-start(bf16[3,16,2048]{2,1,0:T(8,128)(2,1)S(1)} %pad_maximum_fusion), channel_id=1, source_target_pairs={{0,4},{4,0},{1,5},{5,1},{2,6},{6,2},{3,7},{7,3},{8,12},{12,8},{9,1... | collective-permute-start | bytes 589832 | tf_op jit(solution)/shard_map/ppermute | solution.py:17
  17.2 12.7 %all-to-all-start = ((f32[4,3,32,128]{3,2,1,0:T(8,128)}), f32[4,3,32,128]{3,2,1,0:T(8,128)S(1)}, u32[]{:S(2)}, u32[]{:S(2)}) async-start(f32[4,3,32,128]{3,2,1,0:T(8,128)} %maximum_bitcast_fusion), calls=%async_computation | async-start | bytes 393216 | tf_op jit(solution)/shard_map/all_to_all | solution.py:38
  30.7 9.9 %all-to-all-start.1 = ((f32[32,1,160]{2,1,0:T(1,128)}), f32[32,1,160]{2,1,0:T(1,128)S(1)}, u32[]{:S(2)}, u32[]{:S(2)}) async-start(f32[32,1,160]{2,1,0:T(1,128)} %broadcast_in_dim.23), calls=%async_computation.1 | async-start | bytes 65536 | tf_op jit(solution)/shard_map/all_to_all | solution.py:51

commit v3 on v0

v3 whole, which is shorter than its diff:
```python
import functools

import jax
import jax.numpy as jnp
from jax import lax
from jax.experimental import pallas as pl
from jax.experimental.pallas import tpu as pltpu
from jax.sharding import PartitionSpec as P

LANES = 128
TILE = 8


def exchange(value, axis, size, k):
    return lax.ppermute(value, axis, [(i, i ^ k) for i in range(size)])


def pack_kernel(*refs):
    *parts, packed, sems = refs
    copies = [
        pltpu.make_async_copy(part, packed.at[i], sems.at[i]) for i, part in enumerate(parts)
    ]
    for copy in copies:
        copy.start()
    for copy in copies:
        copy.wait()


def pack(*parts):
    tokens, width = parts[0].shape
    return pl.pallas_call(
        pack_kernel,
        out_shape=jax.ShapeDtypeStruct((len(parts), tokens, width), parts[0].dtype),
        in_specs=[pl.BlockSpec(memory_space=pl.ANY)] * len(parts),
        out_specs=pl.BlockSpec(memory_space=pl.ANY),
        scratch_shapes=[pltpu.SemaphoreType.DMA((len(parts),))],
        name="pack_rows",
    )(*parts)


def product_kernel(groups, parts, *refs):
    blocks = refs[:groups]
    enc, dec = refs[groups : groups + 2]
    outs = refs[groups + 2 : groups + 2 + parts]
    inner, rows, held = refs[groups + 2 + parts :]
    tokens = blocks[0].shape[1]
    total = groups * tokens
    share = LANES
    for k, block in enumerate(blocks):
        for a in range(3):
            rows[pl.ds(a * total + k * tokens, tokens), :] = block[a].astype(jnp.float32)
    encoded = jnp.dot(
        rows[pl.ds(0, 2 * total), :].astype(jnp.bfloat16),
        enc[...],
        preferred_element_type=jnp.float32,
    )
    projected = lax.dot_general(
        rows[pl.ds(2 * total, total), :].astype(jnp.bfloat16),
        dec[...],
        (((1,), (1,)), ((), ())),
        preferred_element_type=jnp.float32,
    )
    for c in range(parts):
        held[c, pl.ds(0, 2 * total), :] = encoded[:, c * share : (c + 1) * share]
        held[c, pl.ds(2 * total, total), :] = projected[:, c * share : (c + 1) * share]
    me = lax.axis_index("tensor")
    for m, out in enumerate(outs):
        out[...] = held[me ^ m]
    own = [rows[pl.ds(a * total, tokens), :] for a in range(3)]
    inner_part = jnp.sum((own[1] - own[0]) * own[2], axis=1, keepdims=True)
    inner[pl.ds(0, tokens), :] = jnp.broadcast_to(inner_part, (tokens, LANES))


def products(parts, blocks, enc_weight, dec_weight):
    groups = len(blocks)
    _, tokens, width = blocks[0].shape
    features = enc_weight.shape[1]
    rows = 3 * groups * tokens
    part = jax.ShapeDtypeStruct((rows, features // parts), jnp.float32)
    inner = jax.ShapeDtypeStruct((TILE, LANES), jnp.float32)
    vmem = pl.BlockSpec(memory_space=pltpu.VMEM)
    return pl.pallas_call(
        functools.partial(product_kernel, groups, parts),
        out_shape=[part] * parts + [inner],
        in_specs=[vmem] * (groups + 2),
        out_specs=[vmem] * (parts + 1),
        scratch_shapes=[
            pltpu.VMEM((rows, width), jnp.float32),
            pltpu.VMEM((parts, rows, features // parts), jnp.float32),
        ],
        compiler_params=pltpu.CompilerParams(vmem_limit_bytes=48 * 2**20),
        name="products",
    )(*blocks, enc_weight, dec_weight)


def attribution_kernel(sizes, *refs):
    sections, feats, parts = sizes
    groups = sections * feats
    terms = refs[:parts]
    bias, inner, sums = refs[parts:]
    total = terms[0].shape[0] // 3
    tokens = total // groups
    values = [term[...] for term in terms]
    while len(values) > 1:
        values = [a + b for a, b in zip(values[::2], values[1::2])]
    preact = values[0]
    me = lax.axis_index("tensor")
    b = bias[pl.ds(me, 1), :]
    act_clean = jnp.maximum(preact[:total] + b, 0.0)
    act_corrupt = jnp.maximum(preact[total : 2 * total] + b, 0.0)
    attribution = (act_corrupt - act_clean) * preact[2 * total :]

    head = sums.shape[0] - groups
    sums[pl.ds(0, head), :] = jnp.zeros((head, LANES), jnp.float32)
    sums[pl.ds(me, 1), :] = jnp.sum(attribution, axis=0, keepdims=True)
    token_part = jnp.sum(attribution, axis=1, keepdims=True)
    lane = lax.broadcasted_iota(jnp.int32, (tokens, LANES), 1)
    place = lane == lax.broadcasted_iota(jnp.int32, (tokens, LANES), 0)
    section, feat = lax.axis_index("section"), lax.axis_index("feat")
    for p in range(feats):
        for q in range(sections):
            k = p * sections + q
            column = jnp.broadcast_to(token_part[k * tokens : (k + 1) * tokens], (tokens, LANES))
            if k == 0:
                column = column - inner[pl.ds(0, tokens), :]
            row = jnp.sum(jnp.where(place, column, 0.0), axis=0, keepdims=True)
            owner = (section ^ q) * feats + (feat ^ p)
            sums[pl.ds(head + owner, 1), :] = row


def attributions(sizes, terms, bias, inner):
    sections, feats, parts = sizes
    head = -(-parts // TILE) * TILE
    vmem = pl.BlockSpec(memory_space=pltpu.VMEM)
    return pl.pallas_call(
        functools.partial(attribution_kernel, sizes),
        out_shape=jax.ShapeDtypeStruct((head + sections * feats, LANES), jnp.float32),
        in_specs=[vmem] * (parts + 2),
        out_specs=vmem,
        compiler_params=pltpu.CompilerParams(vmem_limit_bytes=16 * 2**20),
        name="attributions",
    )(*terms, bias, inner)


def per_device(sizes, clean_resid, corrupt_resid, metric_grad, enc_weight, enc_bias, dec_weight):
    sections, feats, parts = sizes
    tokens = clean_resid.shape[0]
    features = enc_weight.shape[1]

    packed = pack(clean_resid, corrupt_resid, metric_grad)
    near = [packed] + [exchange(packed, "section", sections, q) for q in range(1, sections)]
    blocks = near + [exchange(block, "feat", feats, p) for p in range(1, feats) for block in near]

    *terms, inner = products(parts, blocks, enc_weight, dec_weight)
    arrived = [terms[0]] + [exchange(terms[m], "tensor", parts, m) for m in range(1, parts)]
    sums = attributions(sizes, arrived, enc_bias.reshape(parts, features // parts), inner)

    step = 1
    while step < parts:
        sums = sums + exchange(sums, "tensor", parts, step)
        step *= 2
    feature_effect = sums[:parts].reshape(features)
    owed = sums[-sections * feats :]
    for axis, size in (("section", sections), ("feat", feats)):
        step = 1
        while step < size:
            owed = owed + exchange(owed, axis, size, step)
            step *= 2
    owner = lax.axis_index("section") * feats + lax.axis_index("feat")
    return (feature_effect, -lax.dynamic_slice(owed, (owner, 0), (1, tokens)).reshape(tokens))


def solution(mesh):
    sizes = [mesh.shape[name] for name in ("section", "feat", "tensor")]
    in_specs = (
        P(("section", "feat"), "tensor"),
        P(("section", "feat"), "tensor"),
        P(("section", "feat"), "tensor"),
        P("tensor", ("section", "feat")),
        P(("section", "feat")),
        P(("section", "feat"), "tensor"),
    )
    out_specs = (P(("section", "feat")), P(("section", "feat")))
    return jax.shard_map(
        functools.partial(per_device, sizes),
        mesh=mesh,
        in_specs=in_specs,
        out_specs=out_specs,
        check_vma=False,
    )
```

time: 79.9 us -> 47 us (0.59)
  blocking collectives: 35.1 us -> 0 us
  between operations: 14.8 us -> 0.7 us
  starting transfers between devices: 0.04 us -> 10.8 us
  waiting for transfers between devices: 21.9 us -> 26.3 us
  Pallas kernels: 0 us -> 3.86 us
  local copies, waits for them, and re-layouts: 1.16 us -> 4.57 us
  other arithmetic: 3.86 us -> 0.54 us
  matrix products: 2.79 us -> 0 us
    ppermute x0 -> x15, waiting for transfers between devices: none -> 26.3 us  [exchange(): return lax.ppermute(value, axis, [(i, i ^ k) for i in range(size)])]
    psum x1 -> x0, waiting for transfers between devices: 21.9 us -> none  [per_device(): preact, inner_sum = lax.psum((preact, inner_part), 'tensor')]
    psum x1 -> x0, blocking collectives: 12 us -> none  [per_device(): preact, inner_sum = lax.psum((preact, inner_part), 'tensor')]
    unnamed x1 -> x0, blocking collectives: 11.8 us -> none
    all_gather x1 -> x0, blocking collectives: 11.3 us -> none  [per_device(): lax.all_gather(stacked, ('section', 'feat'), axis=1, tiled=True)]
    ppermute x0 -> x15, starting transfers between devices: none -> 10.8 us  [exchange(): return lax.ppermute(value, axis, [(i, i ^ k) for i in range(size)])]
    pallas_call x0 -> x3, Pallas kernels: none -> 3.86 us  [the longest x1 2.62 us: pack(): pl.pallas_call(pack_kernel, out_shape=jax.ShapeDtypeStruct((len(parts), t...]
    unnamed x13 -> x8, local copies, waits for them, and re-layouts: 0.63 us -> 3.98 us
  transfers between devices with their start and end apart: 1 -> 15, of which waited for: 1 -> 11; matrix products, arithmetic and copies ran while one was open for 1% -> 1% of each run, Pallas kernels for 0% -> 0%
where the time goes in v3:
time: 47 us; the launch traced here: 46.8 us
  waiting for transfers between devices  26.3 us (56%)
  starting transfers between devices  10.8 us (23%)
  local copies, waits for them, and re-layouts  4.57 us (10%)
  Pallas kernels  3.86 us (8%)
  between operations  0.7 us (1%)
  other arithmetic  0.54 us (1%)
    ppermute x15, waiting for transfers between devices, exchange(): return lax.ppermute(value, axis, [(i, i ^ k) for i in range(size)])  26.3 us
    ppermute x15, starting transfers between devices, exchange(): return lax.ppermute(value, axis, [(i, i ^ k) for i in range(size)])  10.8 us
    unnamed x8, local copies, waits for them, and re-layouts  3.98 us
    pallas_call x1, Pallas kernels, pack(): pl.pallas_call(pack_kernel, out_shape=jax.ShapeDtypeStruct((len(parts), t...  2.62 us
    pallas_call x1, Pallas kernels, products(): pl.pallas_call(functools.partial(product_kernel, groups, parts), out_shap...  1.14 us
  transfers between devices with their start and end apart: 15, of which 11 were waited for; matrix products, arithmetic and copies ran while one was open for 1% of the time, Pallas kernels for 0%

profile of v3, /device:TPU:0, one launch (start us, length us, event | category | flops | bytes accessed | tf_op | source)
XLA Modules:
  0.0 46.8 jit_solution(17730017293970053202)
XLA Ops:
  0.6 2.6 %pack_rows.1.refs_0_ = bf16[3,4,2048]{2,1,0:T(4,128)(2,1)} custom-call(bf16[4,2048]{1,0:T(4,128)(2,1)} %refs_0_.1, bf16[4,2048]{1,0:T(4,128)(2,1)} %refs_1_.1, bf16[4,2048]{1,0:T(4,128)(2,1)} %refs_2_.1), custom_call_target="tpu_custom_call" | custom-call | tf_op jit(solution)/shard_map/pack_rows/pallas_call | solution.py:31
  3.3 3.0 %collective-permute-start = (bf16[3,4,2048]{2,1,0:T(4,128)(2,1)}, bf16[3,4,2048]{2,1,0:T(4,128)(2,1)S(1)}, u32[]{:S(2)}, u32[]{:S(2)}) collective-permute-start(bf16[3,4,2048]{2,1,0:T(4,128)(2,1)} %pack_rows.1.refs_0_), channel_id=1, source_target_pairs={{0,8},{8,0},{16,24},{24,16},{1,9},{9,1},{17,25},{25,17},{2,10},{10... | collective-permute-start | bytes 147464 | tf_op jit(solution)/shard_map/ppermute | solution.py:15
  6.3 1.5 %collective-permute-start.1 = (bf16[3,4,2048]{2,1,0:T(4,128)(2,1)}, bf16[3,4,2048]{2,1,0:T(4,128)(2,1)S(1)}, u32[]{:S(2)}, u32[]{:S(2)}) collective-permute-start(bf16[3,4,2048]{2,1,0:T(4,128)(2,1)} %pack_rows.1.refs_0_), channel_id=1, source_target_pairs={{0,16},{8,24},{16,0},{24,8},{1,17},{9,25},{17,1},{25,9},{2,18},{10... | collective-permute-start | bytes 147464 | tf_op jit(solution)/shard_map/ppermute | solution.py:15
  7.8 0.8 %collective-permute-done.refs_1_ = bf16[3,4,2048]{2,1,0:T(4,128)(2,1)S(1)} collective-permute-done((bf16[3,4,2048]{2,1,0:T(4,128)(2,1)}, bf16[3,4,2048]{2,1,0:T(4,128)(2,1)S(1)}, u32[]{:S(2)}, u32[]{:S(2)}) %collective-permute-start) | collective-permute-done | bytes 49184 | tf_op jit(solution)/shard_map/ppermute | solution.py:15
  8.6 2.0 %collective-permute-done.1.refs_2_ = bf16[3,4,2048]{2,1,0:T(4,128)(2,1)S(1)} collective-permute-done((bf16[3,4,2048]{2,1,0:T(4,128)(2,1)}, bf16[3,4,2048]{2,1,0:T(4,128)(2,1)S(1)}, u32[]{:S(2)}, u32[]{:S(2)}) %collective-permute-start.1) | collective-permute-done | bytes 49184 | tf_op jit(solution)/shard_map/ppermute | solution.py:15
  10.6 2.4 %collective-permute-done.2.refs_3_ = bf16[3,4,2048]{2,1,0:T(4,128)(2,1)S(1)} collective-permute-done((bf16[3,4,2048]{2,1,0:T(4,128)(2,1)}, bf16[3,4,2048]{2,1,0:T(4,128)(2,1)S(1)}, u32[]{:S(2)}, u32[]{:S(2)}) %collective-permute-start.2) | collective-permute-done | bytes 49184 | tf_op jit(solution)/shard_map/ppermute | solution.py:15
  13.0 1.2 %collective-permute-done.6.refs_7_ = bf16[3,4,2048]{2,1,0:T(4,128)(2,1)S(1)} collective-permute-done((bf16[3,4,2048]{2,1,0:T(4,128)(2,1)S(1)}, bf16[3,4,2048]{2,1,0:T(4,128)(2,1)S(1)}, u32[]{:S(2)}, u32[]{:S(2)}) %collective-permute-start.6) | collective-permute-done | bytes 49184 | tf_op jit(solution)/shard_map/ppermute | solution.py:15
  14.2 1.6 %copy-done = bf16[2048,512]{1,0:T(8,128)(2,1)S(1)} copy-done((bf16[2048,512]{1,0:T(8,128)(2,1)S(1)}, bf16[2048,512]{1,0:T(8,128)(2,1)}, u32[]{:S(2)}) %copy-start) | copy-done | bytes 2097176
  15.8 1.6 %copy-done.1 = bf16[512,2048]{1,0:T(8,128)(2,1)S(1)} copy-done((bf16[512,2048]{1,0:T(8,128)(2,1)S(1)}, bf16[512,2048]{1,0:T(8,128)(2,1)}, u32[]{:S(2)}) %copy-start.1) | copy-done | bytes 2097176
  17.4 0.8 %copy-done.2 = bf16[3,4,2048]{2,1,0:T(4,128)(2,1)S(1)} copy-done((bf16[3,4,2048]{2,1,0:T(4,128)(2,1)S(1)}, bf16[3,4,2048]{2,1,0:T(4,128)(2,1)}, u32[]{:S(2)}) %copy-start.2) | copy-done | bytes 49176
  18.2 1.1 %products.1 = (f32[96,128]{1,0:T(8,128)S(1)}, f32[96,128]{1,0:T(8,128)S(1)}, f32[96,128]{1,0:T(8,128)S(1)}, f32[96,128]{1,0:T(8,128)S(1)}, f32[8,128]{1,0:T(8,128)S(1)}) custom-call(bf16[3,4,2048]{2,1,0:T(4,128)(2,1)S(1)} %copy-done.2, bf16[3,4,2048]{2,1,0:T(4,128)(2,1)S(1)} %collective-permute-done.refs_1_, ...), custom_call_target="tpu_custom_call" | custom-call | tf_op jit(solution)/shard_map/products/pallas_call | solution.py:82
  19.4 1.6 %collective-permute-start.7 = (f32[96,128]{1,0:T(8,128)S(1)}, f32[96,128]{1,0:T(8,128)S(1)}, u32[]{:S(2)}, u32[]{:S(2)}) collective-permute-start(f32[96,128]{1,0:T(8,128)S(1)} %get-tuple-element.8), channel_id=1, source_target_pairs={{0,1},{1,0},{2,3},{3,2},{4,5},{5,4},{6,7},{7,6},{8,9},{9,8},{10,11... | collective-permute-start | bytes 147464 | tf_op jit(solution)/shard_map/ppermute | solution.py:15
  21.0 2.6 %collective-permute-start.8 = (f32[96,128]{1,0:T(8,128)S(1)}, f32[96,128]{1,0:T(8,128)S(1)}, u32[]{:S(2)}, u32[]{:S(2)}) collective-permute-start(f32[96,128]{1,0:T(8,128)S(1)} %get-tuple-element.9), channel_id=1, source_target_pairs={{0,2},{1,3},{2,0},{3,1},{4,6},{5,7},{6,4},{7,5},{8,10},{9,11},{10,... | collective-permute-start | bytes 147464 | tf_op jit(solution)/shard_map/ppermute | solution.py:15
  23.8 3.1 %collective-permute-done.8.refs_2_ = f32[96,128]{1,0:T(8,128)S(1)} collective-permute-done((f32[96,128]{1,0:T(8,128)S(1)}, f32[96,128]{1,0:T(8,128)S(1)}, u32[]{:S(2)}, u32[]{:S(2)}) %collective-permute-start.8) | collective-permute-done | bytes 49184 | tf_op jit(solution)/shard_map/ppermute | solution.py:15
  26.9 2.6 %collective-permute-done.9.refs_3_ = f32[96,128]{1,0:T(8,128)S(1)} collective-permute-done((f32[96,128]{1,0:T(8,128)S(1)}, f32[96,128]{1,0:T(8,128)S(1)}, u32[]{:S(2)}, u32[]{:S(2)}) %collective-permute-start.9) | collective-permute-done | bytes 49184 | tf_op jit(solution)/shard_map/ppermute | solution.py:15
  29.7 3.6 %collective-permute-done.10 = f32[16,128]{1,0:T(8,128)S(1)} collective-permute-done((f32[16,128]{1,0:T(8,128)S(1)}, f32[16,128]{1,0:T(8,128)S(1)}, u32[]{:S(2)}, u32[]{:S(2)}) %collective-permute-start.10) | collective-permute-done | bytes 8224 | tf_op jit(solution)/shard_map/ppermute | solution.py:15
  33.3 0.7 %collective-permute-start.11 = (f32[16,128]{1,0:T(8,128)S(1)}, f32[16,128]{1,0:T(8,128)S(1)}, u32[]{:S(2)}, u32[]{:S(2)}) collective-permute-start(f32[16,128]{1,0:T(8,128)S(1)} %add.21), channel_id=1, source_target_pairs={{0,2},{1,3},{2,0},{3,1},{4,6},{5,7},{6,4},{7,5},{8,10},{9,11},{10,... | collective-permute-start | bytes 24584 | tf_op jit(solution)/shard_map/ppermute | solution.py:15
  34.0 3.9 %collective-permute-done.11 = f32[16,128]{1,0:T(8,128)S(1)} collective-permute-done((f32[16,128]{1,0:T(8,128)S(1)}, f32[16,128]{1,0:T(8,128)S(1)}, u32[]{:S(2)}, u32[]{:S(2)}) %collective-permute-start.11) | collective-permute-done | bytes 8224 | tf_op jit(solution)/shard_map/ppermute | solution.py:15
  37.9 0.5 %collective-permute-start.12 = (f32[8,128]{1,0:T(8,128)S(1)}, f32[8,128]{1,0:T(8,128)S(1)}, u32[]{:S(2)}, u32[]{:S(2)}) collective-permute-start(f32[8,128]{1,0:T(8,128)S(1)} %slice.9), channel_id=1, source_target_pairs={{0,8},{8,0},{16,24},{24,16},{1,9},{9,1},{17,25},{25,17},{2,10},{10... | collective-permute-start | bytes 12296 | tf_op jit(solution)/shard_map/ppermute | solution.py:15
  38.4 3.1 %collective-permute-done.12 = f32[8,128]{1,0:T(8,128)S(1)} collective-permute-done((f32[8,128]{1,0:T(8,128)S(1)}, f32[8,128]{1,0:T(8,128)S(1)}, u32[]{:S(2)}, u32[]{:S(2)}) %collective-permute-start.12) | collective-permute-done | bytes 4128 | tf_op jit(solution)/shard_map/ppermute | solution.py:15
  42.0 3.1 %collective-permute-done.13 = f32[8,128]{1,0:T(8,128)S(1)} collective-permute-done((f32[8,128]{1,0:T(8,128)S(1)}, f32[8,128]{1,0:T(8,128)S(1)}, u32[]{:S(2)}, u32[]{:S(2)}) %collective-permute-start.13) | collective-permute-done | bytes 4128 | tf_op jit(solution)/shard_map/ppermute | solution.py:15
  45.1 0.6 %slice_bitcast_fusion = f32[512]{0:T(512)} fusion(f32[16,128]{1,0:T(8,128)S(1)} %add.22), kind=kLoop, calls=%fused_computation | loop fusion | bytes 4096 | tf_op jit(solution)/shard_map/reshape | solution.py:162
  45.7 0.6 %collective-permute-done.14 = f32[8,128]{1,0:T(8,128)S(1)} collective-permute-done((f32[8,128]{1,0:T(8,128)S(1)}, f32[8,128]{1,0:T(8,128)S(1)}, u32[]{:S(2)}, u32[]{:S(2)}) %collective-permute-start.14) | collective-permute-done | bytes 4128 | tf_op jit(solution)/shard_map/ppermute | solution.py:15
  46.3 0.5 %negate_bitcast_fusion = f32[4]{0:T(128)} fusion(f32[8,128]{1,0:T(8,128)S(1)} %add.25, s32[]{:T(128)S(6)} %select_n.3), kind=kLoop, calls=%fused_computation.1 | loop fusion | flops 4 | bytes 36 | tf_op jit(solution)/shard_map/neg | solution.py:170
  (25 shorter events, 1.0 us)
Async XLA Ops:
  0.6 28.8 %copy-start.3 = (f32[512]{0:T(512)S(1)}, f32[512]{0:T(512)}, u32[]{:S(2)}) copy-start(f32[512]{0:T(512)} %param.10) | copy-start | bytes 6148
  3.3 5.3 %collective-permute-start = (bf16[3,4,2048]{2,1,0:T(4,128)(2,1)}, bf16[3,4,2048]{2,1,0:T(4,128)(2,1)S(1)}, u32[]{:S(2)}, u32[]{:S(2)}) collective-permute-start(bf16[3,4,2048]{2,1,0:T(4,128)(2,1)} %pack_rows.1.refs_0_), channel_id=1, source_target_pairs={{0,8},{8,0},{16,24},{24,16},{1,9},{9,1},{17,25},{25,17},{2,10},{10... | collective-permute-start | bytes 147464 | tf_op jit(solution)/shard_map/ppermute | solution.py:15
  6.3 4.3 %collective-permute-start.1 = (bf16[3,4,2048]{2,1,0:T(4,128)(2,1)}, bf16[3,4,2048]{2,1,0:T(4,128)(2,1)S(1)}, u32[]{:S(2)}, u32[]{:S(2)}) collective-permute-start(bf16[3,4,2048]{2,1,0:T(4,128)(2,1)} %pack_rows.1.refs_0_), channel_id=1, source_target_pairs={{0,16},{8,24},{16,0},{24,8},{1,17},{9,25},{17,1},{25,9},{2,18},{10... | collective-permute-start | bytes 147464 | tf_op jit(solution)/shard_map/ppermute | solution.py:15
  7.8 5.2 %collective-permute-start.2 = (bf16[3,4,2048]{2,1,0:T(4,128)(2,1)}, bf16[3,4,2048]{2,1,0:T(4,128)(2,1)S(1)}, u32[]{:S(2)}, u32[]{:S(2)}) collective-permute-start(bf16[3,4,2048]{2,1,0:T(4,128)(2,1)} %pack_rows.1.refs_0_), channel_id=1, source_target_pairs={{0,24},{8,16},{16,8},{24,0},{1,25},{9,17},{17,9},{25,1},{2,26},{10... | collective-permute-start | bytes 147464 | tf_op jit(solution)/shard_map/ppermute | solution.py:15
  7.8 5.2 %collective-permute-start.3 = (bf16[3,4,2048]{2,1,0:T(4,128)(2,1)}, bf16[3,4,2048]{2,1,0:T(4,128)(2,1)S(1)}, u32[]{:S(2)}, u32[]{:S(2)}) collective-permute-start(bf16[3,4,2048]{2,1,0:T(4,128)(2,1)} %pack_rows.1.refs_0_), channel_id=1, source_target_pairs={{0,4},{4,0},{1,5},{5,1},{2,6},{6,2},{3,7},{7,3},{8,12},{12,8},{9,1... | collective-permute-start | bytes 147464 | tf_op jit(solution)/shard_map/ppermute | solution.py:15
  8.6 4.4 %collective-permute-start.4 = (bf16[3,4,2048]{2,1,0:T(4,128)(2,1)S(1)}, bf16[3,4,2048]{2,1,0:T(4,128)(2,1)S(1)}, u32[]{:S(2)}, u32[]{:S(2)}) collective-permute-start(bf16[3,4,2048]{2,1,0:T(4,128)(2,1)S(1)} %collective-permute-done.refs_1_), channel_id=1, source_target_pairs={{0,4},{4,0},{1,5},{5,1},{2,6},{6,2},{3,7},{7,3},{8,12},{12,8},{9,1... | collective-permute-start | bytes 147464 | tf_op jit(solution)/shard_map/ppermute | solution.py:15
  10.6 2.4 %collective-permute-start.5 = (bf16[3,4,2048]{2,1,0:T(4,128)(2,1)S(1)}, bf16[3,4,2048]{2,1,0:T(4,128)(2,1)S(1)}, u32[]{:S(2)}, u32[]{:S(2)}) collective-permute-start(bf16[3,4,2048]{2,1,0:T(4,128)(2,1)S(1)} %collective-permute-done.1.refs_2_), channel_id=1, source_target_pairs={{0,4},{4,0},{1,5},{5,1},{2,6},{6,2},{3,7},{7,3},{8,12},{12,8},{9,1... | collective-permute-start | bytes 147464 | tf_op jit(solution)/shard_map/ppermute | solution.py:15
  13.0 1.2 %collective-permute-start.6 = (bf16[3,4,2048]{2,1,0:T(4,128)(2,1)S(1)}, bf16[3,4,2048]{2,1,0:T(4,128)(2,1)S(1)}, u32[]{:S(2)}, u32[]{:S(2)}) collective-permute-start(bf16[3,4,2048]{2,1,0:T(4,128)(2,1)S(1)} %collective-permute-done.2.refs_3_), channel_id=1, source_target_pairs={{0,4},{4,0},{1,5},{5,1},{2,6},{6,2},{3,7},{7,3},{8,12},{12,8},{9,1... | collective-permute-start | bytes 147464 | tf_op jit(solution)/shard_map/ppermute | solution.py:15
  14.2 1.6 %copy-start = (bf16[2048,512]{1,0:T(8,128)(2,1)S(1)}, bf16[2048,512]{1,0:T(8,128)(2,1)}, u32[]{:S(2)}) copy-start(bf16[2048,512]{1,0:T(8,128)(2,1)} %refs_8_.1) | copy-start | bytes 6291460
  15.8 1.6 %copy-start.1 = (bf16[512,2048]{1,0:T(8,128)(2,1)S(1)}, bf16[512,2048]{1,0:T(8,128)(2,1)}, u32[]{:S(2)}) copy-start(bf16[512,2048]{1,0:T(8,128)(2,1)} %refs_9_.1) | copy-start | bytes 6291460
  17.4 0.8 %copy-start.2 = (bf16[3,4,2048]{2,1,0:T(4,128)(2,1)S(1)}, bf16[3,4,2048]{2,1,0:T(4,128)(2,1)}, u32[]{:S(2)}) copy-start(bf16[3,4,2048]{2,1,0:T(4,128)(2,1)} %pack_rows.1.refs_0_) | copy-start | bytes 147460
  19.4 4.5 %collective-permute-start.7 = (f32[96,128]{1,0:T(8,128)S(1)}, f32[96,128]{1,0:T(8,128)S(1)}, u32[]{:S(2)}, u32[]{:S(2)}) collective-permute-start(f32[96,128]{1,0:T(8,128)S(1)} %get-tuple-element.8), channel_id=1, source_target_pairs={{0,1},{1,0},{2,3},{3,2},{4,5},{5,4},{6,7},{7,6},{8,9},{9,8},{10,11... | collective-permute-start | bytes 147464 | tf_op jit(solution)/shard_map/ppermute | solution.py:15
  21.0 5.9 %collective-permute-start.8 = (f32[96,128]{1,0:T(8,128)S(1)}, f32[96,128]{1,0:T(8,128)S(1)}, u32[]{:S(2)}, u32[]{:S(2)}) collective-permute-start(f32[96,128]{1,0:T(8,128)S(1)} %get-tuple-element.9), channel_id=1, source_target_pairs={{0,2},{1,3},{2,0},{3,1},{4,6},{5,7},{6,4},{7,5},{8,10},{9,11},{10,... | collective-permute-start | bytes 147464 | tf_op jit(solution)/shard_map/ppermute | solution.py:15
  23.6 5.9 %collective-permute-start.9 = (f32[96,128]{1,0:T(8,128)S(1)}, f32[96,128]{1,0:T(8,128)S(1)}, u32[]{:S(2)}, u32[]{:S(2)}) collective-permute-start(f32[96,128]{1,0:T(8,128)S(1)} %get-tuple-element.10), channel_id=1, source_target_pairs={{0,3},{1,2},{2,1},{3,0},{4,7},{5,6},{6,5},{7,4},{8,11},{9,10},{10,... | collective-permute-start | bytes 147464 | tf_op jit(solution)/shard_map/ppermute | solution.py:15
  29.6 3.7 %collective-permute-start.10 = (f32[16,128]{1,0:T(8,128)S(1)}, f32[16,128]{1,0:T(8,128)S(1)}, u32[]{:S(2)}, u32[]{:S(2)}) collective-permute-start(f32[16,128]{1,0:T(8,128)S(1)} %attributions.1), channel_id=1, source_target_pairs={{0,1},{1,0},{2,3},{3,2},{4,5},{5,4},{6,7},{7,6},{8,9},{9,8},{10,11... | collective-permute-start | bytes 24584 | tf_op jit(solution)/shard_map/ppermute | solution.py:15
  33.3 4.5 %collective-permute-start.11 = (f32[16,128]{1,0:T(8,128)S(1)}, f32[16,128]{1,0:T(8,128)S(1)}, u32[]{:S(2)}, u32[]{:S(2)}) collective-permute-start(f32[16,128]{1,0:T(8,128)S(1)} %add.21), channel_id=1, source_target_pairs={{0,2},{1,3},{2,0},{3,1},{4,6},{5,7},{6,4},{7,5},{8,10},{9,11},{10,... | collective-permute-start | bytes 24584 | tf_op jit(solution)/shard_map/ppermute | solution.py:15
  37.9 3.6 %collective-permute-start.12 = (f32[8,128]{1,0:T(8,128)S(1)}, f32[8,128]{1,0:T(8,128)S(1)}, u32[]{:S(2)}, u32[]{:S(2)}) collective-permute-start(f32[8,128]{1,0:T(8,128)S(1)} %slice.9), channel_id=1, source_target_pairs={{0,8},{8,0},{16,24},{24,16},{1,9},{9,1},{17,25},{25,17},{2,10},{10... | collective-permute-start | bytes 12296 | tf_op jit(solution)/shard_map/ppermute | solution.py:15
  41.5 3.6 %collective-permute-start.13 = (f32[8,128]{1,0:T(8,128)S(1)}, f32[8,128]{1,0:T(8,128)S(1)}, u32[]{:S(2)}, u32[]{:S(2)}) collective-permute-start(f32[8,128]{1,0:T(8,128)S(1)} %slice_add_fusion), channel_id=1, source_target_pairs={{0,16},{8,24},{16,0},{24,8},{1,17},{9,25},{17,1},{25,9},{2,18},{10... | collective-permute-start | bytes 12296 | tf_op jit(solution)/shard_map/ppermute | solution.py:15
  45.1 1.2 %collective-permute-start.14 = (f32[8,128]{1,0:T(8,128)S(1)}, f32[8,128]{1,0:T(8,128)S(1)}, u32[]{:S(2)}, u32[]{:S(2)}) collective-permute-start(f32[8,128]{1,0:T(8,128)S(1)} %add.24), channel_id=1, source_target_pairs={{0,4},{4,0},{1,5},{5,1},{2,6},{6,2},{3,7},{7,3},{8,12},{12,8},{9,1... | collective-permute-start | bytes 12296 | tf_op jit(solution)/shard_map/ppermute | solution.py:15

commit v4 on v3

--- a/solution.py
+++ b/solution.py
@@ -11,31 +11,49 @@
 TILE = 8
 
 
+EVERY = ("section", "feat", "tensor")
+SUMMER = 1
+
+
+def far_first(size, send):
+    sent = {k: send(k) for k in reversed(range(1, size))}
+    return [sent[k] for k in range(1, size)]
+
+
 def exchange(value, axis, size, k):
     return lax.ppermute(value, axis, [(i, i ^ k) for i in range(size)])
 
 
-def pack_kernel(*refs):
-    *parts, packed, sems = refs
-    copies = [
-        pltpu.make_async_copy(part, packed.at[i], sems.at[i]) for i, part in enumerate(parts)
-    ]
+def load_kernel(pieces, *refs):
+    count = (len(refs) - 1) // 2
+    sems = refs[-1]
+    copies = []
+    for i in range(count):
+        source, target = refs[i], refs[count + i]
+        step = source.shape[0] // pieces
+        for j in range(pieces):
+            part = pl.ds(j * step, step)
+            copies.append(
+                pltpu.make_async_copy(source.at[part], target.at[part], sems.at[i, j])
+            )
     for copy in copies:
         copy.start()
     for copy in copies:
         copy.wait()
 
 
-def pack(*parts):
-    tokens, width = parts[0].shape
-    return pl.pallas_call(
-        pack_kernel,
-        out_shape=jax.ShapeDtypeStruct((len(parts), tokens, width), parts[0].dtype),
-        in_specs=[pl.BlockSpec(memory_space=pl.ANY)] * len(parts),
-        out_specs=pl.BlockSpec(memory_space=pl.ANY),
-        scratch_shapes=[pltpu.SemaphoreType.DMA((len(parts),))],
-        name="pack_rows",
-    )(*parts)
+def load(*arrays, pieces=4):
+    size = sum(array.size * array.dtype.itemsize for array in arrays)
+    return pl.pallas_call(
+        functools.partial(load_kernel, pieces),
+        out_shape=[jax.ShapeDtypeStruct(array.shape, array.dtype) for array in arrays],
+        in_specs=[pl.BlockSpec(memory_space=pl.ANY)] * len(arrays),
+        out_specs=[pl.BlockSpec(memory_space=pltpu.VMEM)] * len(arrays),
+        scratch_shapes=[pltpu.SemaphoreType.DMA((len(arrays), pieces))],
+        compiler_params=pltpu.CompilerParams(vmem_limit_bytes=16 * 2**20),
+        cost_estimate=pl.CostEstimate(flops=0, bytes_accessed=2 * size, transcendentals=0),
+        name="load_weights",
+    )(*arrays)
 
 
 def product_kernel(groups, parts, *refs):
@@ -93,6 +111,12 @@
     )(*blocks, enc_weight, dec_weight)
 
 
+def add_up(values):
+    while len(values) > 1:
+        values = [a + b for a, b in zip(values[::2], values[1::2])]
+    return values[0]
+
+
 def attribution_kernel(sizes, *refs):
     sections, feats, parts = sizes
     groups = sections * feats
@@ -100,23 +124,19 @@
     bias, inner, sums = refs[parts:]
     total = terms[0].shape[0] // 3
     tokens = total // groups
-    values = [term[...] for term in terms]
-    while len(values) > 1:
-        values = [a + b for a, b in zip(values[::2], values[1::2])]
-    preact = values[0]
-    me = lax.axis_index("tensor")
-    b = bias[pl.ds(me, 1), :]
+    preact = add_up([term[...] for term in terms])
+    section, feat = lax.axis_index("section"), lax.axis_index("feat")
+    b = bias[pl.ds(lax.axis_index("tensor"), 1), :]
     act_clean = jnp.maximum(preact[:total] + b, 0.0)
     act_corrupt = jnp.maximum(preact[total : 2 * total] + b, 0.0)
     attribution = (act_corrupt - act_clean) * preact[2 * total :]
 
-    head = sums.shape[0] - groups
-    sums[pl.ds(0, head), :] = jnp.zeros((head, LANES), jnp.float32)
-    sums[pl.ds(me, 1), :] = jnp.sum(attribution, axis=0, keepdims=True)
+    tail = sums.shape[0] - groups
+    sums[pl.ds(groups, tail), :] = jnp.zeros((tail, LANES), jnp.float32)
+    sums[pl.ds(groups + feat, 1), :] = jnp.sum(attribution, axis=0, keepdims=True)
     token_part = jnp.sum(attribution, axis=1, keepdims=True)
     lane = lax.broadcasted_iota(jnp.int32, (tokens, LANES), 1)
     place = lane == lax.broadcasted_iota(jnp.int32, (tokens, LANES), 0)
-    section, feat = lax.axis_index("section"), lax.axis_index("feat")
     for p in range(feats):
         for q in range(sections):
             k = p * sections + q
@@ -125,16 +145,21 @@
                 column = column - inner[pl.ds(0, tokens), :]
             row = jnp.sum(jnp.where(place, column, 0.0), axis=0, keepdims=True)
             owner = (section ^ q) * feats + (feat ^ p)
-            sums[pl.ds(head + owner, 1), :] = row
+            sums[pl.ds(owner, 1), :] = row
+
+
+def round_up(size):
+    return -(-size // TILE) * TILE
 
 
 def attributions(sizes, terms, bias, inner):
     sections, feats, parts = sizes
-    head = -(-parts // TILE) * TILE
     vmem = pl.BlockSpec(memory_space=pltpu.VMEM)
     return pl.pallas_call(
         functools.partial(attribution_kernel, sizes),
-        out_shape=jax.ShapeDtypeStruct((head + sections * feats, LANES), jnp.float32),
+        out_shape=jax.ShapeDtypeStruct(
+            (sections * feats + round_up(feats), LANES), jnp.float32
+        ),
         in_specs=[vmem] * (parts + 2),
         out_specs=vmem,
         compiler_params=pltpu.CompilerParams(vmem_limit_bytes=16 * 2**20),
@@ -142,32 +167,89 @@
     )(*terms, bias, inner)
 
 
+def total_kernel(sizes, *refs):
+    sections, feats, parts = sizes
+    groups = sections * feats
+    sums, outs = refs[: sections * parts], refs[sections * parts :]
+    me, section = lax.axis_index("tensor"), lax.axis_index("section")
+    owed = add_up([part[pl.ds(0, groups), :] for part in sums])
+    for f, out in enumerate(outs):
+        for m in range(parts):
+            out[pl.ds(me ^ m, 1), :] = sums[m][pl.ds(groups + f, 1), :]
+        row = lax.broadcasted_iota(jnp.int32, (groups, LANES), 0) == section * feats + f
+        out[pl.ds(parts, 1), :] = -jnp.sum(jnp.where(row, owed, 0.0), axis=0, keepdims=True)
+
+
+def totals(sizes, sums):
+    feats, parts = sizes[1:]
+    vmem = pl.BlockSpec(memory_space=pltpu.VMEM)
+    result = jax.ShapeDtypeStruct((round_up(parts + 1), LANES), jnp.float32)
+    return pl.pallas_call(
+        functools.partial(total_kernel, sizes),
+        out_shape=[result] * feats,
+        in_specs=[vmem] * len(sums),
+        out_specs=[vmem] * feats,
+        compiler_params=pltpu.CompilerParams(vmem_limit_bytes=32 * 2**20),
+        name="totals",
+    )(*sums)
+
+
+def final_kernel(parts, *refs):
+    *results, feature_out, error_out = refs
+    feat = lax.axis_index("feat")
+    value = results[0][...]
+    for f, result in enumerate(results[1:]):
+        value = jnp.where(feat == (f if f < SUMMER else f + 1), result[...], value)
+    for i in range(parts):
+        feature_out[pl.ds(i * LANES, LANES)] = value[i]
+    error_out[...] = value[parts, : error_out.shape[0]]
+
+
+def final(parts, tokens, results):
+    vmem = pl.BlockSpec(memory_space=pltpu.VMEM)
+    return pl.pallas_call(
+        functools.partial(final_kernel, parts),
+        out_shape=[
+            jax.ShapeDtypeStruct((parts * LANES,), jnp.float32),
+            jax.ShapeDtypeStruct((tokens,), jnp.float32),
+        ],
+        in_specs=[vmem] * len(results),
+        out_specs=[vmem] * 2,
+        name="final",
+    )(*results)
+
+
 def per_device(sizes, clean_resid, corrupt_resid, metric_grad, enc_weight, enc_bias, dec_weight):
     sections, feats, parts = sizes
     tokens = clean_resid.shape[0]
     features = enc_weight.shape[1]
 
-    packed = pack(clean_resid, corrupt_resid, metric_grad)
-    near = [packed] + [exchange(packed, "section", sections, q) for q in range(1, sections)]
+    packed = jnp.stack([clean_resid, corrupt_resid, metric_grad])
+    near = [packed] + far_first(sections, lambda q: exchange(packed, "section", sections, q))
+    enc_weight, dec_weight = load(enc_weight, dec_weight)
     blocks = near + [exchange(block, "feat", feats, p) for p in range(1, feats) for block in near]
 
     *terms, inner = products(parts, blocks, enc_weight, dec_weight)
-    arrived = [terms[0]] + [exchange(terms[m], "tensor", parts, m) for m in range(1, parts)]
-    sums = attributions(sizes, arrived, enc_bias.reshape(parts, features // parts), inner)
-
-    step = 1
-    while step < parts:
-        sums = sums + exchange(sums, "tensor", parts, step)
-        step *= 2
-    feature_effect = sums[:parts].reshape(features)
-    owed = sums[-sections * feats :]
-    for axis, size in (("section", sections), ("feat", feats)):
-        step = 1
-        while step < size:
-            owed = owed + exchange(owed, axis, size, step)
-            step *= 2
-    owner = lax.axis_index("section") * feats + lax.axis_index("feat")
-    return (feature_effect, -lax.dynamic_slice(owed, (owner, 0), (1, tokens)).reshape(tokens))
+    arrived = far_first(parts, lambda m: exchange(terms[m], "tensor", parts, m))
+    bias = enc_bias.reshape(parts, features // parts)
+    sums = attributions(sizes, [terms[0]] + arrived, bias, inner)
+
+    device = lambda s, f, t: (s * feats + f) * parts + t
+    places = [(s, t) for s in range(sections) for t in range(parts)]
+    for f in range(1, feats):
+        pairs = [(device(s, f, t), device(s, 0, t)) for s, t in places]
+        sums = sums + lax.ppermute(sums, EVERY, pairs)
+    spread = {}
+    for q, m in reversed(places):
+        pairs = [(device(s, 0, t), device(s ^ q, SUMMER, t ^ m)) for s, t in places]
+        spread[q, m] = lax.ppermute(sums, EVERY, pairs)
+    results = totals(sizes, [spread[place] for place in places])
+    handed = [results[SUMMER]]
+    for f in range(feats):
+        if f != SUMMER:
+            pairs = [(device(s, SUMMER, t), device(s, f, t)) for s, t in places]
+            handed.append(lax.ppermute(results[f], EVERY, pairs))
+    return tuple(final(parts, tokens, handed))
 
 
 def solution(mesh):

time: 47 us -> 60 us (1.28)
  starting transfers between devices: 10.8 us -> 36.4 us
  waiting for transfers between devices: 26.3 us -> 14 us
  Pallas kernels: 3.86 us -> 2.92 us
    ppermute x0 -> x18, starting transfers between devices: none -> 27.3 us  [the longest x16 24.8 us: per_device(): spread[q, m] = lax.ppermute(sums, EVERY, pairs)]
    ppermute x15 -> x10, waiting for transfers between devices: 26.3 us -> 9.62 us  [exchange(): return lax.ppermute(value, axis, [(i, i ^ k) for i in range(size)])]
    ppermute x0 -> x18, waiting for transfers between devices: none -> 4.34 us  [the longest x1 1.77 us: per_device(): sums = sums + lax.ppermute(sums, EVERY, pairs)]
    ppermute x15 -> x10, starting transfers between devices: 10.8 us -> 9.07 us  [exchange(): return lax.ppermute(value, axis, [(i, i ^ k) for i in range(size)])]
    pallas_call x1 -> x3, Pallas kernels: 2.62 us -> 1.67 us  [the longest x1 1.28 us: final(): pl.pallas_call(functools.partial(final_kernel, parts), out_shape=[jax.Sha...]
    another operation x0 -> x1, other arithmetic: none -> 0.79 us  [per_device(): packed = jnp.stack([clean_resid, corrupt_resid, metric_grad])]
    unnamed x8 -> x10, local copies, waits for them, and re-layouts: 3.98 us -> 4.36 us
  transfers between devices with their start and end apart: 15 -> 28, of which waited for: 11 -> 8; matrix products, arithmetic and copies ran while one was open for 1% -> 0% of each run, Pallas kernels for 0% -> 1%
where the time goes in v4:
time: 60 us; the launch traced here: 59.4 us
  starting transfers between devices  36.4 us (61%)
  waiting for transfers between devices  14 us (23%)
  local copies, waits for them, and re-layouts  4.36 us (7%)
  Pallas kernels  2.92 us (5%)
  between operations  0.97 us (2%)
  other arithmetic  0.8 us (1%)
    ppermute x16, starting transfers between devices, per_device(): spread[q, m] = lax.ppermute(sums, EVERY, pairs)  24.8 us
    ppermute x10, waiting for transfers between devices, exchange(): return lax.ppermute(value, axis, [(i, i ^ k) for i in range(size)])  9.62 us
    ppermute x10, starting transfers between devices, exchange(): return lax.ppermute(value, axis, [(i, i ^ k) for i in range(size)])  9.07 us
    unnamed x10, local copies, waits for them, and re-layouts  4.36 us
    ppermute x1, waiting for transfers between devices, per_device(): sums = sums + lax.ppermute(sums, EVERY, pairs)  1.77 us
    ppermute x1, waiting for transfers between devices, per_device(): handed.append(lax.ppermute(results[f], EVERY, pairs))  1.76 us
    ppermute x1, starting transfers between devices, per_device(): sums = sums + lax.ppermute(sums, EVERY, pairs)  1.29 us
    ppermute x1, starting transfers between devices, per_device(): handed.append(lax.ppermute(results[f], EVERY, pairs))  1.28 us
  transfers between devices with their start and end apart: 28, of which 8 were waited for; matrix products, arithmetic and copies ran while one was open for 0% of the time, Pallas kernels for 1%

profile of v4, /device:TPU:0, one launch (start us, length us, event | category | flops | bytes accessed | tf_op | source)
XLA Modules:
  0.0 59.4 jit_solution(15867475379719020642)
XLA Ops:
  1.4 4.0 %collective-permute-start.2 = (bf16[3,4,2048]{2,1,0:T(4,128)(2,1)S(1)}, bf16[3,4,2048]{2,1,0:T(4,128)(2,1)S(1)}, u32[]{:S(2)}, u32[]{:S(2)}) collective-permute-start(bf16[3,4,2048]{2,1,0:T(4,128)(2,1)S(1)} %pad_maximum_fusion.refs_0_), channel_id=1, source_target_pairs={{0,24},{8,16},{16,8},{24,0},{1,25},{9,17},{17,9},{25,1},{2,26},{10... | collective-permute-start | bytes 147464 | tf_op jit(solution)/shard_map/ppermute | solution.py:24
  6.0 1.4 %collective-permute-done.2.refs_3_ = bf16[3,4,2048]{2,1,0:T(4,128)(2,1)S(1)} collective-permute-done((bf16[3,4,2048]{2,1,0:T(4,128)(2,1)S(1)}, bf16[3,4,2048]{2,1,0:T(4,128)(2,1)S(1)}, u32[]{:S(2)}, u32[]{:S(2)}) %collective-permute-start.2) | collective-permute-done | bytes 49184 | tf_op jit(solution)/shard_map/ppermute | solution.py:24
  7.5 2.0 %collective-permute-done.1.refs_2_ = bf16[3,4,2048]{2,1,0:T(4,128)(2,1)S(1)} collective-permute-done((bf16[3,4,2048]{2,1,0:T(4,128)(2,1)S(1)}, bf16[3,4,2048]{2,1,0:T(4,128)(2,1)S(1)}, u32[]{:S(2)}, u32[]{:S(2)}) %collective-permute-start.1) | collective-permute-done | bytes 49184 | tf_op jit(solution)/shard_map/ppermute | solution.py:24
  10.0 1.6 %copy-done = bf16[2048,512]{1,0:T(8,128)(2,1)S(1)} copy-done((bf16[2048,512]{1,0:T(8,128)(2,1)S(1)}, bf16[2048,512]{1,0:T(8,128)(2,1)}, u32[]{:S(2)}) %copy-start) | copy-done | bytes 2097176
  11.6 1.6 %copy-done.1 = bf16[512,2048]{1,0:T(8,128)(2,1)S(1)} copy-done((bf16[512,2048]{1,0:T(8,128)(2,1)S(1)}, bf16[512,2048]{1,0:T(8,128)(2,1)}, u32[]{:S(2)}) %copy-start.1) | copy-done | bytes 2097176
  14.8 1.6 %collective-permute-start.7 = (f32[96,128]{1,0:T(8,128)S(1)}, f32[96,128]{1,0:T(8,128)S(1)}, u32[]{:S(2)}, u32[]{:S(2)}) collective-permute-start(f32[96,128]{1,0:T(8,128)S(1)} %get-tuple-element.14), channel_id=1, source_target_pairs={{0,1},{1,0},{2,3},{3,2},{4,5},{5,4},{6,7},{7,6},{8,9},{9,8},{10,11... | collective-permute-start | bytes 147464 | tf_op jit(solution)/shard_map/ppermute | solution.py:24
  16.4 2.6 %collective-permute-start.8 = (f32[96,128]{1,0:T(8,128)S(1)}, f32[96,128]{1,0:T(8,128)S(1)}, u32[]{:S(2)}, u32[]{:S(2)}) collective-permute-start(f32[96,128]{1,0:T(8,128)S(1)} %get-tuple-element.15), channel_id=1, source_target_pairs={{0,2},{1,3},{2,0},{3,1},{4,6},{5,7},{6,4},{7,5},{8,10},{9,11},{10,... | collective-permute-start | bytes 147464 | tf_op jit(solution)/shard_map/ppermute | solution.py:24
  19.2 3.3 %collective-permute-done.8.refs_2_ = f32[96,128]{1,0:T(8,128)S(1)} collective-permute-done((f32[96,128]{1,0:T(8,128)S(1)}, f32[96,128]{1,0:T(8,128)S(1)}, u32[]{:S(2)}, u32[]{:S(2)}) %collective-permute-start.8) | collective-permute-done | bytes 49184 | tf_op jit(solution)/shard_map/ppermute | solution.py:24
  22.6 2.3 %collective-permute-done.9.refs_3_ = f32[96,128]{1,0:T(8,128)S(1)} collective-permute-done((f32[96,128]{1,0:T(8,128)S(1)}, f32[96,128]{1,0:T(8,128)S(1)}, u32[]{:S(2)}, u32[]{:S(2)}) %collective-permute-start.9) | collective-permute-done | bytes 49184 | tf_op jit(solution)/shard_map/ppermute | solution.py:24
  25.0 1.3 %collective-permute-start.10 = (f32[16,128]{1,0:T(8,128)S(1)}, f32[16,128]{1,0:T(8,128)S(1)}, u32[]{:S(2)}, u32[]{:S(2)}) collective-permute-start(f32[16,128]{1,0:T(8,128)S(1)} %attributions.1), channel_id=1, source_target_pairs={{4,0},{5,1},{6,2},{7,3},{12,8},{13,9},{14,10},{15,11},{20,16},{21,... | collective-permute-start | bytes 24584 | tf_op jit(solution)/shard_map/ppermute | solution.py:241
  26.3 1.8 %collective-permute-done.10 = f32[16,128]{1,0:T(8,128)S(1)} collective-permute-done((f32[16,128]{1,0:T(8,128)S(1)}, f32[16,128]{1,0:T(8,128)S(1)}, u32[]{:S(2)}, u32[]{:S(2)}) %collective-permute-start.10) | collective-permute-done | bytes 8224 | tf_op jit(solution)/shard_map/ppermute | solution.py:241
  28.1 4.0 %collective-permute-start.26 = (f32[16,128]{1,0:T(8,128)S(1)}, f32[16,128]{1,0:T(8,128)S(1)}, u32[]{:S(2)}, u32[]{:S(2)}) collective-permute-start(f32[16,128]{1,0:T(8,128)S(1)} %add.3), channel_id=1, source_target_pairs={{0,31},{1,30},{2,29},{3,28},{8,23},{9,22},{10,21},{11,20},{16,15},... | collective-permute-start | bytes 24584 | tf_op jit(solution)/shard_map/ppermute | solution.py:245
  32.1 1.3 %collective-permute-start.25 = (f32[16,128]{1,0:T(8,128)S(1)}, f32[16,128]{1,0:T(8,128)S(1)}, u32[]{:S(2)}, u32[]{:S(2)}) collective-permute-start(f32[16,128]{1,0:T(8,128)S(1)} %add.3), channel_id=1, source_target_pairs={{0,30},{1,31},{2,28},{3,29},{8,22},{9,23},{10,20},{11,21},{16,14},... | collective-permute-start | bytes 24584 | tf_op jit(solution)/shard_map/ppermute | solution.py:245
  33.4 1.3 %collective-permute-start.24 = (f32[16,128]{1,0:T(8,128)S(1)}, f32[16,128]{1,0:T(8,128)S(1)}, u32[]{:S(2)}, u32[]{:S(2)}) collective-permute-start(f32[16,128]{1,0:T(8,128)S(1)} %add.3), channel_id=1, source_target_pairs={{0,29},{1,28},{2,31},{3,30},{8,21},{9,20},{10,23},{11,22},{16,13},... | collective-permute-start | bytes 24584 | tf_op jit(solution)/shard_map/ppermute | solution.py:245
  34.7 1.3 %collective-permute-start.23 = (f32[16,128]{1,0:T(8,128)S(1)}, f32[16,128]{1,0:T(8,128)S(1)}, u32[]{:S(2)}, u32[]{:S(2)}) collective-permute-start(f32[16,128]{1,0:T(8,128)S(1)} %add.3), channel_id=1, source_target_pairs={{0,28},{1,29},{2,30},{3,31},{8,20},{9,21},{10,22},{11,23},{16,12},... | collective-permute-start | bytes 24584 | tf_op jit(solution)/shard_map/ppermute | solution.py:245
  36.0 1.3 %collective-permute-start.22 = (f32[16,128]{1,0:T(8,128)S(1)}, f32[16,128]{1,0:T(8,128)S(1)}, u32[]{:S(2)}, u32[]{:S(2)}) collective-permute-start(f32[16,128]{1,0:T(8,128)S(1)} %add.3), channel_id=1, source_target_pairs={{0,23},{1,22},{2,21},{3,20},{8,31},{9,30},{10,29},{11,28},{16,7},{... | collective-permute-start | bytes 24584 | tf_op jit(solution)/shard_map/ppermute | solution.py:245
  37.3 1.3 %collective-permute-start.21 = (f32[16,128]{1,0:T(8,128)S(1)}, f32[16,128]{1,0:T(8,128)S(1)}, u32[]{:S(2)}, u32[]{:S(2)}) collective-permute-start(f32[16,128]{1,0:T(8,128)S(1)} %add.3), channel_id=1, source_target_pairs={{0,22},{1,23},{2,20},{3,21},{8,30},{9,31},{10,28},{11,29},{16,6},{... | collective-permute-start | bytes 24584 | tf_op jit(solution)/shard_map/ppermute | solution.py:245
  38.6 2.5 %collective-permute-start.20 = (f32[16,128]{1,0:T(8,128)S(1)}, f32[16,128]{1,0:T(8,128)S(1)}, u32[]{:S(2)}, u32[]{:S(2)}) collective-permute-start(f32[16,128]{1,0:T(8,128)S(1)} %add.3), channel_id=1, source_target_pairs={{0,21},{1,20},{2,23},{3,22},{8,29},{9,28},{10,31},{11,30},{16,5},{... | collective-permute-start | bytes 24584 | tf_op jit(solution)/shard_map/ppermute | solution.py:245
  41.1 1.3 %collective-permute-start.19 = (f32[16,128]{1,0:T(8,128)S(1)}, f32[16,128]{1,0:T(8,128)S(1)}, u32[]{:S(2)}, u32[]{:S(2)}) collective-permute-start(f32[16,128]{1,0:T(8,128)S(1)} %add.3), channel_id=1, source_target_pairs={{0,20},{1,21},{2,22},{3,23},{8,28},{9,29},{10,30},{11,31},{16,4},{... | collective-permute-start | bytes 24584 | tf_op jit(solution)/shard_map/ppermute | solution.py:245
  42.4 1.3 %collective-permute-start.18 = (f32[16,128]{1,0:T(8,128)S(1)}, f32[16,128]{1,0:T(8,128)S(1)}, u32[]{:S(2)}, u32[]{:S(2)}) collective-permute-start(f32[16,128]{1,0:T(8,128)S(1)} %add.3), channel_id=1, source_target_pairs={{0,15},{1,14},{2,13},{3,12},{8,7},{9,6},{10,5},{11,4},{16,31},{17,... | collective-permute-start | bytes 24584 | tf_op jit(solution)/shard_map/ppermute | solution.py:245
  43.7 1.3 %collective-permute-start.17 = (f32[16,128]{1,0:T(8,128)S(1)}, f32[16,128]{1,0:T(8,128)S(1)}, u32[]{:S(2)}, u32[]{:S(2)}) collective-permute-start(f32[16,128]{1,0:T(8,128)S(1)} %add.3), channel_id=1, source_target_pairs={{0,14},{1,15},{2,12},{3,13},{8,6},{9,7},{10,4},{11,5},{16,30},{17,... | collective-permute-start | bytes 24584 | tf_op jit(solution)/shard_map/ppermute | solution.py:245
  47.7 1.4 %collective-permute-start.14 = (f32[16,128]{1,0:T(8,128)S(1)}, f32[16,128]{1,0:T(8,128)S(1)}, u32[]{:S(2)}, u32[]{:S(2)}) collective-permute-start(f32[16,128]{1,0:T(8,128)S(1)} %add.3), channel_id=1, source_target_pairs={{0,7},{1,6},{2,5},{3,4},{8,15},{9,14},{10,13},{11,12},{16,23},{17,... | collective-permute-start | bytes 24584 | tf_op jit(solution)/shard_map/ppermute | solution.py:245
  50.4 1.3 %collective-permute-start.12 = (f32[16,128]{1,0:T(8,128)S(1)}, f32[16,128]{1,0:T(8,128)S(1)}, u32[]{:S(2)}, u32[]{:S(2)}) collective-permute-start(f32[16,128]{1,0:T(8,128)S(1)} %add.3), channel_id=1, source_target_pairs={{0,5},{1,4},{2,7},{3,6},{8,13},{9,12},{10,15},{11,14},{16,21},{17,... | collective-permute-start | bytes 24584 | tf_op jit(solution)/shard_map/ppermute | solution.py:245
  55.8 1.8 %collective-permute-done.27.refs_1_ = f32[8,128]{1,0:T(8,128)S(1)} collective-permute-done((f32[8,128]{1,0:T(8,128)S(1)}, f32[8,128]{1,0:T(8,128)S(1)}, u32[]{:S(2)}, u32[]{:S(2)}) %collective-permute-start.27) | collective-permute-done | bytes 4128 | tf_op jit(solution)/shard_map/ppermute | solution.py:251
  (49 shorter events, 13.5 us)
Async XLA Ops:
  1.4 6.0 %collective-permute-start.2 = (bf16[3,4,2048]{2,1,0:T(4,128)(2,1)S(1)}, bf16[3,4,2048]{2,1,0:T(4,128)(2,1)S(1)}, u32[]{:S(2)}, u32[]{:S(2)}) collective-permute-start(bf16[3,4,2048]{2,1,0:T(4,128)(2,1)S(1)} %pad_maximum_fusion.refs_0_), channel_id=1, source_target_pairs={{0,24},{8,16},{16,8},{24,0},{1,25},{9,17},{17,9},{25,1},{2,26},{10... | collective-permute-start | bytes 147464 | tf_op jit(solution)/shard_map/ppermute | solution.py:24
  5.4 4.1 %collective-permute-start.1 = (bf16[3,4,2048]{2,1,0:T(4,128)(2,1)S(1)}, bf16[3,4,2048]{2,1,0:T(4,128)(2,1)S(1)}, u32[]{:S(2)}, u32[]{:S(2)}) collective-permute-start(bf16[3,4,2048]{2,1,0:T(4,128)(2,1)S(1)} %pad_maximum_fusion.refs_0_), channel_id=1, source_target_pairs={{0,16},{8,24},{16,0},{24,8},{1,17},{9,25},{17,1},{25,9},{2,18},{10... | collective-permute-start | bytes 147464 | tf_op jit(solution)/shard_map/ppermute | solution.py:24
  5.9 4.1 %collective-permute-start = (bf16[3,4,2048]{2,1,0:T(4,128)(2,1)S(1)}, bf16[3,4,2048]{2,1,0:T(4,128)(2,1)S(1)}, u32[]{:S(2)}, u32[]{:S(2)}) collective-permute-start(bf16[3,4,2048]{2,1,0:T(4,128)(2,1)S(1)} %pad_maximum_fusion.refs_0_), channel_id=1, source_target_pairs={{0,8},{8,0},{16,24},{24,16},{1,9},{9,1},{17,25},{25,17},{2,10},{10... | collective-permute-start | bytes 147464 | tf_op jit(solution)/shard_map/ppermute | solution.py:24
  6.0 7.5 %collective-permute-start.3 = (bf16[3,4,2048]{2,1,0:T(4,128)(2,1)S(1)}, bf16[3,4,2048]{2,1,0:T(4,128)(2,1)S(1)}, u32[]{:S(2)}, u32[]{:S(2)}) collective-permute-start(bf16[3,4,2048]{2,1,0:T(4,128)(2,1)S(1)} %pad_maximum_fusion.refs_0_), channel_id=1, source_target_pairs={{0,4},{4,0},{1,5},{5,1},{2,6},{6,2},{3,7},{7,3},{8,12},{12,8},{9,1... | collective-permute-start | bytes 147464 | tf_op jit(solution)/shard_map/ppermute | solution.py:24
  7.5 6.1 %collective-permute-start.6 = (bf16[3,4,2048]{2,1,0:T(4,128)(2,1)S(1)}, bf16[3,4,2048]{2,1,0:T(4,128)(2,1)S(1)}, u32[]{:S(2)}, u32[]{:S(2)}) collective-permute-start(bf16[3,4,2048]{2,1,0:T(4,128)(2,1)S(1)} %collective-permute-done.2.refs_3_), channel_id=1, source_target_pairs={{0,4},{4,0},{1,5},{5,1},{2,6},{6,2},{3,7},{7,3},{8,12},{12,8},{9,1... | collective-permute-start | bytes 147464 | tf_op jit(solution)/shard_map/ppermute | solution.py:24
  9.5 4.1 %collective-permute-start.5 = (bf16[3,4,2048]{2,1,0:T(4,128)(2,1)S(1)}, bf16[3,4,2048]{2,1,0:T(4,128)(2,1)S(1)}, u32[]{:S(2)}, u32[]{:S(2)}) collective-permute-start(bf16[3,4,2048]{2,1,0:T(4,128)(2,1)S(1)} %collective-permute-done.1.refs_2_), channel_id=1, source_target_pairs={{0,4},{4,0},{1,5},{5,1},{2,6},{6,2},{3,7},{7,3},{8,12},{12,8},{9,1... | collective-permute-start | bytes 147464 | tf_op jit(solution)/shard_map/ppermute | solution.py:24
  10.0 3.6 %collective-permute-start.4 = (bf16[3,4,2048]{2,1,0:T(4,128)(2,1)S(1)}, bf16[3,4,2048]{2,1,0:T(4,128)(2,1)S(1)}, u32[]{:S(2)}, u32[]{:S(2)}) collective-permute-start(bf16[3,4,2048]{2,1,0:T(4,128)(2,1)S(1)} %collective-permute-done.refs_1_), channel_id=1, source_target_pairs={{0,4},{4,0},{1,5},{5,1},{2,6},{6,2},{3,7},{7,3},{8,12},{12,8},{9,1... | collective-permute-start | bytes 147464 | tf_op jit(solution)/shard_map/ppermute | solution.py:24
  14.8 4.5 %collective-permute-start.7 = (f32[96,128]{1,0:T(8,128)S(1)}, f32[96,128]{1,0:T(8,128)S(1)}, u32[]{:S(2)}, u32[]{:S(2)}) collective-permute-start(f32[96,128]{1,0:T(8,128)S(1)} %get-tuple-element.14), channel_id=1, source_target_pairs={{0,1},{1,0},{2,3},{3,2},{4,5},{5,4},{6,7},{7,6},{8,9},{9,8},{10,11... | collective-permute-start | bytes 147464 | tf_op jit(solution)/shard_map/ppermute | solution.py:24
  16.4 6.2 %collective-permute-start.8 = (f32[96,128]{1,0:T(8,128)S(1)}, f32[96,128]{1,0:T(8,128)S(1)}, u32[]{:S(2)}, u32[]{:S(2)}) collective-permute-start(f32[96,128]{1,0:T(8,128)S(1)} %get-tuple-element.15), channel_id=1, source_target_pairs={{0,2},{1,3},{2,0},{3,1},{4,6},{5,7},{6,4},{7,5},{8,10},{9,11},{10,... | collective-permute-start | bytes 147464 | tf_op jit(solution)/shard_map/ppermute | solution.py:24
  19.0 5.9 %collective-permute-start.9 = (f32[96,128]{1,0:T(8,128)S(1)}, f32[96,128]{1,0:T(8,128)S(1)}, u32[]{:S(2)}, u32[]{:S(2)}) collective-permute-start(f32[96,128]{1,0:T(8,128)S(1)} %get-tuple-element.16), channel_id=1, source_target_pairs={{0,3},{1,2},{2,1},{3,0},{4,7},{5,6},{6,5},{7,4},{8,11},{9,10},{10,... | collective-permute-start | bytes 147464 | tf_op jit(solution)/shard_map/ppermute | solution.py:24
  28.1 9.2 %collective-permute-start.26 = (f32[16,128]{1,0:T(8,128)S(1)}, f32[16,128]{1,0:T(8,128)S(1)}, u32[]{:S(2)}, u32[]{:S(2)}) collective-permute-start(f32[16,128]{1,0:T(8,128)S(1)} %add.3), channel_id=1, source_target_pairs={{0,31},{1,30},{2,29},{3,28},{8,23},{9,22},{10,21},{11,20},{16,15},... | collective-permute-start | bytes 24584 | tf_op jit(solution)/shard_map/ppermute | solution.py:245
  32.1 6.5 %collective-permute-start.25 = (f32[16,128]{1,0:T(8,128)S(1)}, f32[16,128]{1,0:T(8,128)S(1)}, u32[]{:S(2)}, u32[]{:S(2)}) collective-permute-start(f32[16,128]{1,0:T(8,128)S(1)} %add.3), channel_id=1, source_target_pairs={{0,30},{1,31},{2,28},{3,29},{8,22},{9,23},{10,20},{11,21},{16,14},... | collective-permute-start | bytes 24584 | tf_op jit(solution)/shard_map/ppermute | solution.py:245
  33.4 7.7 %collective-permute-start.24 = (f32[16,128]{1,0:T(8,128)S(1)}, f32[16,128]{1,0:T(8,128)S(1)}, u32[]{:S(2)}, u32[]{:S(2)}) collective-permute-start(f32[16,128]{1,0:T(8,128)S(1)} %add.3), channel_id=1, source_target_pairs={{0,29},{1,28},{2,31},{3,30},{8,21},{9,20},{10,23},{11,22},{16,13},... | collective-permute-start | bytes 24584 | tf_op jit(solution)/shard_map/ppermute | solution.py:245
  34.7 7.8 %collective-permute-start.23 = (f32[16,128]{1,0:T(8,128)S(1)}, f32[16,128]{1,0:T(8,128)S(1)}, u32[]{:S(2)}, u32[]{:S(2)}) collective-permute-start(f32[16,128]{1,0:T(8,128)S(1)} %add.3), channel_id=1, source_target_pairs={{0,28},{1,29},{2,30},{3,31},{8,20},{9,21},{10,22},{11,23},{16,12},... | collective-permute-start | bytes 24584 | tf_op jit(solution)/shard_map/ppermute | solution.py:245
  36.0 7.8 %collective-permute-start.22 = (f32[16,128]{1,0:T(8,128)S(1)}, f32[16,128]{1,0:T(8,128)S(1)}, u32[]{:S(2)}, u32[]{:S(2)}) collective-permute-start(f32[16,128]{1,0:T(8,128)S(1)} %add.3), channel_id=1, source_target_pairs={{0,23},{1,22},{2,21},{3,20},{8,31},{9,30},{10,29},{11,28},{16,7},{... | collective-permute-start | bytes 24584 | tf_op jit(solution)/shard_map/ppermute | solution.py:245
  37.3 7.7 %collective-permute-start.21 = (f32[16,128]{1,0:T(8,128)S(1)}, f32[16,128]{1,0:T(8,128)S(1)}, u32[]{:S(2)}, u32[]{:S(2)}) collective-permute-start(f32[16,128]{1,0:T(8,128)S(1)} %add.3), channel_id=1, source_target_pairs={{0,22},{1,23},{2,20},{3,21},{8,30},{9,31},{10,28},{11,29},{16,6},{... | collective-permute-start | bytes 24584 | tf_op jit(solution)/shard_map/ppermute | solution.py:245
  38.6 7.7 %collective-permute-start.20 = (f32[16,128]{1,0:T(8,128)S(1)}, f32[16,128]{1,0:T(8,128)S(1)}, u32[]{:S(2)}, u32[]{:S(2)}) collective-permute-start(f32[16,128]{1,0:T(8,128)S(1)} %add.3), channel_id=1, source_target_pairs={{0,21},{1,20},{2,23},{3,22},{8,29},{9,28},{10,31},{11,30},{16,5},{... | collective-permute-start | bytes 24584 | tf_op jit(solution)/shard_map/ppermute | solution.py:245
  41.1 6.5 %collective-permute-start.19 = (f32[16,128]{1,0:T(8,128)S(1)}, f32[16,128]{1,0:T(8,128)S(1)}, u32[]{:S(2)}, u32[]{:S(2)}) collective-permute-start(f32[16,128]{1,0:T(8,128)S(1)} %add.3), channel_id=1, source_target_pairs={{0,20},{1,21},{2,22},{3,23},{8,28},{9,29},{10,30},{11,31},{16,4},{... | collective-permute-start | bytes 24584 | tf_op jit(solution)/shard_map/ppermute | solution.py:245
  42.4 6.7 %collective-permute-start.18 = (f32[16,128]{1,0:T(8,128)S(1)}, f32[16,128]{1,0:T(8,128)S(1)}, u32[]{:S(2)}, u32[]{:S(2)}) collective-permute-start(f32[16,128]{1,0:T(8,128)S(1)} %add.3), channel_id=1, source_target_pairs={{0,15},{1,14},{2,13},{3,12},{8,7},{9,6},{10,5},{11,4},{16,31},{17,... | collective-permute-start | bytes 24584 | tf_op jit(solution)/shard_map/ppermute | solution.py:245
  43.7 6.7 %collective-permute-start.17 = (f32[16,128]{1,0:T(8,128)S(1)}, f32[16,128]{1,0:T(8,128)S(1)}, u32[]{:S(2)}, u32[]{:S(2)}) collective-permute-start(f32[16,128]{1,0:T(8,128)S(1)} %add.3), channel_id=1, source_target_pairs={{0,14},{1,15},{2,12},{3,13},{8,6},{9,7},{10,4},{11,5},{16,30},{17,... | collective-permute-start | bytes 24584 | tf_op jit(solution)/shard_map/ppermute | solution.py:245
  45.1 6.7 %collective-permute-start.16 = (f32[16,128]{1,0:T(8,128)S(1)}, f32[16,128]{1,0:T(8,128)S(1)}, u32[]{:S(2)}, u32[]{:S(2)}) collective-permute-start(f32[16,128]{1,0:T(8,128)S(1)} %add.3), channel_id=1, source_target_pairs={{0,13},{1,12},{2,15},{3,14},{8,5},{9,4},{10,7},{11,6},{16,29},{17,... | collective-permute-start | bytes 24584 | tf_op jit(solution)/shard_map/ppermute | solution.py:245
  46.4 6.7 %collective-permute-start.15 = (f32[16,128]{1,0:T(8,128)S(1)}, f32[16,128]{1,0:T(8,128)S(1)}, u32[]{:S(2)}, u32[]{:S(2)}) collective-permute-start(f32[16,128]{1,0:T(8,128)S(1)} %add.3), channel_id=1, source_target_pairs={{0,12},{1,13},{2,14},{3,15},{8,4},{9,5},{10,6},{11,7},{16,28},{17,... | collective-permute-start | bytes 24584 | tf_op jit(solution)/shard_map/ppermute | solution.py:245
  47.7 5.4 %collective-permute-start.14 = (f32[16,128]{1,0:T(8,128)S(1)}, f32[16,128]{1,0:T(8,128)S(1)}, u32[]{:S(2)}, u32[]{:S(2)}) collective-permute-start(f32[16,128]{1,0:T(8,128)S(1)} %add.3), channel_id=1, source_target_pairs={{0,7},{1,6},{2,5},{3,4},{8,15},{9,14},{10,13},{11,12},{16,23},{17,... | collective-permute-start | bytes 24584 | tf_op jit(solution)/shard_map/ppermute | solution.py:245
  49.1 3.9 %collective-permute-start.13 = (f32[16,128]{1,0:T(8,128)S(1)}, f32[16,128]{1,0:T(8,128)S(1)}, u32[]{:S(2)}, u32[]{:S(2)}) collective-permute-start(f32[16,128]{1,0:T(8,128)S(1)} %add.3), channel_id=1, source_target_pairs={{0,6},{1,7},{2,4},{3,5},{8,14},{9,15},{10,12},{11,13},{16,22},{17,... | collective-permute-start | bytes 24584 | tf_op jit(solution)/shard_map/ppermute | solution.py:245
  (9 other events, 26.5 us)

commit v5 on v4

v5 whole, which is shorter than its diff:
```python
import functools

import jax
import jax.numpy as jnp
from jax import lax
from jax.experimental import pallas as pl
from jax.experimental.pallas import tpu as pltpu
from jax.sharding import PartitionSpec as P

LANES = 128
TILE = 8


EVERY = ("section", "feat", "tensor")


def far_first(size, send):
    sent = {k: send(k) for k in reversed(range(1, size))}
    return [sent[k] for k in range(1, size)]


def exchange(value, axis, size, k):
    return lax.ppermute(value, axis, [(i, i ^ k) for i in range(size)])


def inner_kernel(packed, inner):
    tokens = packed.shape[1]
    clean, corrupt, grad = [packed[a].astype(jnp.float32) for a in range(3)]
    part = jnp.sum((corrupt - clean) * grad, axis=1, keepdims=True)
    inner[pl.ds(0, tokens), :] = jnp.broadcast_to(part, (tokens, LANES))


def inner_products(packed):
    vmem = pl.BlockSpec(memory_space=pltpu.VMEM)
    return pl.pallas_call(
        inner_kernel,
        out_shape=jax.ShapeDtypeStruct((TILE, LANES), jnp.float32),
        in_specs=[vmem],
        out_specs=vmem,
        name="inner_products",
    )(packed)


def load_kernel(pieces, *refs):
    count = (len(refs) - 2) // 2
    sems = refs[-1]
    copies = []
    for i in range(count):
        source, target = refs[1 + i], refs[1 + count + i]
        step = source.shape[0] // pieces
        for j in range(pieces):
            part = pl.ds(j * step, step)
            copies.append(
                pltpu.make_async_copy(source.at[part], target.at[part], sems.at[i, j])
            )
    for copy in copies:
        copy.start()
    for copy in copies:
        copy.wait()


def load(after, *arrays, pieces=4):
    size = sum(array.size * array.dtype.itemsize for array in arrays)
    return pl.pallas_call(
        functools.partial(load_kernel, pieces),
        out_shape=[jax.ShapeDtypeStruct(array.shape, array.dtype) for array in arrays],
        in_specs=[pl.BlockSpec(memory_space=pltpu.VMEM)]
        + [pl.BlockSpec(memory_space=pltpu.HBM)] * len(arrays),
        out_specs=[pl.BlockSpec(memory_space=pltpu.VMEM)] * len(arrays),
        scratch_shapes=[pltpu.SemaphoreType.DMA((len(arrays), pieces))],
        compiler_params=pltpu.CompilerParams(vmem_limit_bytes=48 * 2**20),
        cost_estimate=pl.CostEstimate(flops=0, bytes_accessed=2 * size, transcendentals=0),
        name="load_weights",
    )(after, *arrays)


def product_kernel(groups, parts, *refs):
    blocks = refs[:groups]
    enc, dec = refs[groups : groups + 2]
    outs = refs[groups + 2 : groups + 2 + parts]
    rows, held = refs[groups + 2 + parts :]
    tokens = blocks[0].shape[1]
    total = groups * tokens
    share = LANES
    for k, block in enumerate(blocks):
        for a in range(3):
            rows[pl.ds(a * total + k * tokens, tokens), :] = block[a].astype(jnp.float32)
    encoded = jnp.dot(
        rows[pl.ds(0, 2 * total), :].astype(jnp.bfloat16),
        enc[...],
        preferred_element_type=jnp.float32,
    )
    projected = lax.dot_general(
        rows[pl.ds(2 * total, total), :].astype(jnp.bfloat16),
        dec[...],
        (((1,), (1,)), ((), ())),
        preferred_element_type=jnp.float32,
    )
    for c in range(parts):
        held[c, pl.ds(0, 2 * total), :] = encoded[:, c * share : (c + 1) * share]
        held[c, pl.ds(2 * total, total), :] = projected[:, c * share : (c + 1) * share]
    me = lax.axis_index("tensor")
    for m, out in enumerate(outs):
        out[...] = held[me ^ m]


def products(parts, blocks, enc_weight, dec_weight):
    groups = len(blocks)
    _, tokens, width = blocks[0].shape
    features = enc_weight.shape[1]
    rows = 3 * groups * tokens
    part = jax.ShapeDtypeStruct((rows, features // parts), jnp.float32)
    vmem = pl.BlockSpec(memory_space=pltpu.VMEM)
    return pl.pallas_call(
        functools.partial(product_kernel, groups, parts),
        out_shape=[part] * parts,
        in_specs=[vmem] * (groups + 2),
        out_specs=[vmem] * parts,
        scratch_shapes=[
            pltpu.VMEM((rows, width), jnp.float32),
            pltpu.VMEM((parts, rows, features // parts), jnp.float32),
        ],
        compiler_params=pltpu.CompilerParams(vmem_limit_bytes=48 * 2**20),
        name="products",
    )(*blocks, enc_weight, dec_weight)


def add_up(values):
    while len(values) > 1:
        values = [a + b for a, b in zip(values[::2], values[1::2])]
    return values[0]


def attribution_kernel(sizes, *refs):
    sections, feats, parts = sizes
    groups = sections * feats
    terms = refs[:parts]
    bias, inner, sums = refs[parts:]
    total = terms[0].shape[0] // 3
    tokens = total // groups
    preact = add_up([term[...] for term in terms])
    section, feat = lax.axis_index("section"), lax.axis_index("feat")
    b = bias[pl.ds(lax.axis_index("tensor"), 1), :]
    act_clean = jnp.maximum(preact[:total] + b, 0.0)
    act_corrupt = jnp.maximum(preact[total : 2 * total] + b, 0.0)
    attribution = (act_corrupt - act_clean) * preact[2 * total :]

    devices = groups * parts
    feature_part = jnp.sum(attribution, axis=0, keepdims=True)
    sums[:, 0, :] = jnp.broadcast_to(feature_part, (devices, LANES))
    token_part = jnp.sum(attribution, axis=1, keepdims=True)
    lane = lax.broadcasted_iota(jnp.int32, (tokens, LANES), 1)
    place = lane == lax.broadcasted_iota(jnp.int32, (tokens, LANES), 0)
    for p in range(feats):
        for q in range(sections):
            k = p * sections + q
            column = jnp.broadcast_to(token_part[k * tokens : (k + 1) * tokens], (tokens, LANES))
            if k == 0:
                column = column - inner[pl.ds(0, tokens), :]
            row = jnp.sum(jnp.where(place, column, 0.0), axis=0, keepdims=True)
            owner = (section ^ q) * feats + (feat ^ p)
            sums[pl.ds(owner * parts, parts), 1, :] = jnp.broadcast_to(row, (parts, LANES))


def attributions(sizes, terms, bias, inner):
    sections, feats, parts = sizes
    vmem = pl.BlockSpec(memory_space=pltpu.VMEM)
    return pl.pallas_call(
        functools.partial(attribution_kernel, sizes),
        out_shape=jax.ShapeDtypeStruct((sections * feats * parts, 2, LANES), jnp.float32),
        in_specs=[vmem] * (parts + 2),
        out_specs=vmem,
        compiler_params=pltpu.CompilerParams(vmem_limit_bytes=16 * 2**20),
        name="attributions",
    )(*terms, bias, inner)


def final_kernel(sizes, arrived, feature_out, error_out, features, errors, sems):
    sections, feats, parts = sizes
    group = lax.axis_index("section") * feats + lax.axis_index("feat")
    mine = arrived[pl.ds(group * parts, parts), 0, :]
    for i in range(parts):
        features[pl.ds(i * LANES, LANES)] = mine[i]
    feature_copy = pltpu.make_async_copy(features, feature_out, sems.at[0])
    feature_copy.start()
    owed = add_up([arrived[i, 1:2, :] for i in range(sections * feats * parts)])
    errors[...] = -owed[0, : errors.shape[0]]
    error_copy = pltpu.make_async_copy(errors, error_out, sems.at[1])
    error_copy.start()
    feature_copy.wait()
    error_copy.wait()


def final(sizes, tokens, arrived):
    features = (sizes[2] * LANES,)
    return pl.pallas_call(
        functools.partial(final_kernel, sizes),
        out_shape=[
            jax.ShapeDtypeStruct(features, jnp.float32),
            jax.ShapeDtypeStruct((tokens,), jnp.float32),
        ],
        in_specs=[pl.BlockSpec(memory_space=pltpu.VMEM)],
        out_specs=[pl.BlockSpec(memory_space=pltpu.HBM)] * 2,
        scratch_shapes=[
            pltpu.VMEM(features, jnp.float32),
            pltpu.VMEM((tokens,), jnp.float32),
            pltpu.SemaphoreType.DMA((2,)),
        ],
        name="final",
    )(arrived)


def per_device(sizes, clean_resid, corrupt_resid, metric_grad, enc_weight, enc_bias, dec_weight):
    sections, feats, parts = sizes
    tokens = clean_resid.shape[0]
    features = enc_weight.shape[1]

    packed = jnp.stack([clean_resid, corrupt_resid, metric_grad])
    near = [packed] + far_first(sections, lambda q: exchange(packed, "section", sections, q))
    inner = inner_products(packed)
    enc_weight, dec_weight = load(packed, enc_weight, dec_weight)
    blocks = near + [exchange(block, "feat", feats, p) for p in range(1, feats) for block in near]

    terms = products(parts, blocks, enc_weight, dec_weight)
    arrived = far_first(parts, lambda m: exchange(terms[m], "tensor", parts, m))
    bias = enc_bias.reshape(parts, features // parts)
    sums = attributions(sizes, [terms[0]] + arrived, bias, inner)

    return tuple(final(sizes, tokens, lax.all_to_all(sums, EVERY, 0, 0)))


def solution(mesh):
    sizes = [mesh.shape[name] for name in ("section", "feat", "tensor")]
    in_specs = (
        P(("section", "feat"), "tensor"),
        P(("section", "feat"), "tensor"),
        P(("section", "feat"), "tensor"),
        P("tensor", ("section", "feat")),
        P(("section", "feat")),
        P(("section", "feat"), "tensor"),
    )
    out_specs = (P(("section", "feat")), P(("section", "feat")))
    return jax.shard_map(
        functools.partial(per_device, sizes),
        mesh=mesh,
        in_specs=in_specs,
        out_specs=out_specs,
        check_vma=False,
    )
```

time: 60 us -> 36.7 us (0.61)
  starting transfers between devices: 36.4 us -> 9.01 us
  blocking collectives: 0 us -> 9.63 us
  waiting for transfers between devices: 14 us -> 9.15 us
  local copies, waits for them, and re-layouts: 4.36 us -> 0.69 us
  Pallas kernels: 2.92 us -> 6.32 us
    ppermute x18 -> x0, starting transfers between devices: 27.3 us -> none  [the longest x16 24.8 us: per_device(): spread[q, m] = lax.ppermute(sums, EVERY, pairs)]
    all_to_all x0 -> x1, blocking collectives: none -> 9.63 us  [per_device(): return tuple(final(sizes, tokens, lax.all_to_all(sums, EVERY, 0, 0)))]
    ppermute x18 -> x0, waiting for transfers between devices: 4.34 us -> none  [the longest x1 1.77 us: per_device(): sums = sums + lax.ppermute(sums, EVERY, pairs)]
    unnamed x10 -> x6, local copies, waits for them, and re-layouts: 4.36 us -> 0.69 us
    pallas_call x1, Pallas kernels: 0.37 us -> 2.21 us  [load(): pl.pallas_call(functools.partial(load_kernel, pieces), out_shape=[jax.Sha...]
    pallas_call x2, Pallas kernels: 1.3 us -> 2.85 us  [the longest x1 1.49 us: inner_products(): pl.pallas_call(inner_kernel, out_shape=jax.ShapeDtypeStruct((TILE, LANES)...]
  transfers between devices with their start and end apart: 28 -> 10, of which waited for: 8 -> 5; matrix products, arithmetic and copies ran while one was open for 0% -> 0% of each run, Pallas kernels for 1% -> 10%
where the time goes in v5:
time: 36.7 us; the launch traced here: 36.3 us
  blocking collectives  9.63 us (26%)
  waiting for transfers between devices  9.15 us (25%)
  starting transfers between devices  9.01 us (25%)
  Pallas kernels  6.32 us (17%)
  other arithmetic  0.79 us (2%)
  between operations  0.72 us (2%)
  local copies, waits for them, and re-layouts  0.69 us (2%)
    all_to_all x1, blocking collectives, per_device(): return tuple(final(sizes, tokens, lax.all_to_all(sums, EVERY, 0, 0)))  9.63 us
    ppermute x10, waiting for transfers between devices, exchange(): return lax.ppermute(value, axis, [(i, i ^ k) for i in range(size)])  9.15 us
    ppermute x10, starting transfers between devices, exchange(): return lax.ppermute(value, axis, [(i, i ^ k) for i in range(size)])  9.01 us
    pallas_call x1, Pallas kernels, load(): pl.pallas_call(functools.partial(load_kernel, pieces), out_shape=[jax.Sha...  2.21 us
    pallas_call x1, Pallas kernels, inner_products(): pl.pallas_call(inner_kernel, out_shape=jax.ShapeDtypeStruct((TILE, LANES)...  1.49 us
    pallas_call x1, Pallas kernels, final(): pl.pallas_call(functools.partial(final_kernel, sizes), out_shape=[jax.Sha...  1.37 us
    pallas_call x1, Pallas kernels, products(): pl.pallas_call(functools.partial(product_kernel, groups, parts), out_shap...  1.14 us
    another operation x1, other arithmetic, per_device(): packed = jnp.stack([clean_resid, corrupt_resid, metric_grad])  0.79 us
  transfers between devices with their start and end apart: 10, of which 5 were waited for; matrix products, arithmetic and copies ran while one was open for 0% of the time, Pallas kernels for 10%

profile of v5, /device:TPU:0, one launch (start us, length us, event | category | flops | bytes accessed | tf_op | source)
XLA Modules:
  0.0 36.3 jit_solution(13529023714315559390)
XLA Ops:
  0.6 0.8 %pad_maximum_fusion.refs_0_.packed = bf16[3,4,2048]{2,1,0:T(4,128)(2,1)S(1)} fusion(bf16[1,4,2048]{2,1,0:T(4,128)(2,1)} %bitcast.5, bf16[1,4,2048]{2,1,0:T(4,128)(2,1)} %bitcast.6, bf16[1,4,2048]{2,1,0:T(4,128)(2,1)} %bitcast.7), kind=kLoop, calls=%fused_computation | loop fusion | flops 49152 | bytes 98304 | tf_op jit(solution)/shard_map/stack | solution.py:218
  1.4 3.0 %collective-permute-start = (bf16[3,4,2048]{2,1,0:T(4,128)(2,1)S(1)}, bf16[3,4,2048]{2,1,0:T(4,128)(2,1)S(1)}, u32[]{:S(2)}, u32[]{:S(2)}) collective-permute-start(bf16[3,4,2048]{2,1,0:T(4,128)(2,1)S(1)} %pad_maximum_fusion.refs_0_.packed), channel_id=1, source_target_pairs={{0,8},{8,0},{16,24},{24,16},{1,9},{9,1},{17,25},{25,17},{2,10},{10... | collective-permute-start | bytes 147464 | tf_op jit(solution)/shard_map/ppermute | solution.py:23
  4.4 1.5 %collective-permute-start.1 = (bf16[3,4,2048]{2,1,0:T(4,128)(2,1)S(1)}, bf16[3,4,2048]{2,1,0:T(4,128)(2,1)S(1)}, u32[]{:S(2)}, u32[]{:S(2)}) collective-permute-start(bf16[3,4,2048]{2,1,0:T(4,128)(2,1)S(1)} %pad_maximum_fusion.refs_0_.packed), channel_id=1, source_target_pairs={{0,16},{8,24},{16,0},{24,8},{1,17},{9,25},{17,1},{25,9},{2,18},{10... | collective-permute-start | bytes 147464 | tf_op jit(solution)/shard_map/ppermute | solution.py:23
  6.0 0.0 collective-permute-start.2
  6.0 0.0 collective-permute-start.3
  6.0 0.5 %collective-permute-done.refs_1_ = bf16[3,4,2048]{2,1,0:T(4,128)(2,1)S(1)} collective-permute-done((bf16[3,4,2048]{2,1,0:T(4,128)(2,1)S(1)}, bf16[3,4,2048]{2,1,0:T(4,128)(2,1)S(1)}, u32[]{:S(2)}, u32[]{:S(2)}) %collective-permute-start) | collective-permute-done | bytes 49184 | tf_op jit(solution)/shard_map/ppermute | solution.py:23
  6.5 2.0 %collective-permute-done.1.refs_2_ = bf16[3,4,2048]{2,1,0:T(4,128)(2,1)S(1)} collective-permute-done((bf16[3,4,2048]{2,1,0:T(4,128)(2,1)S(1)}, bf16[3,4,2048]{2,1,0:T(4,128)(2,1)S(1)}, u32[]{:S(2)}, u32[]{:S(2)}) %collective-permute-start.1) | collective-permute-done | bytes 49184 | tf_op jit(solution)/shard_map/ppermute | solution.py:23
  8.5 2.4 %collective-permute-done.2.refs_3_ = bf16[3,4,2048]{2,1,0:T(4,128)(2,1)S(1)} collective-permute-done((bf16[3,4,2048]{2,1,0:T(4,128)(2,1)S(1)}, bf16[3,4,2048]{2,1,0:T(4,128)(2,1)S(1)}, u32[]{:S(2)}, u32[]{:S(2)}) %collective-permute-start.2) | collective-permute-done | bytes 49184 | tf_op jit(solution)/shard_map/ppermute | solution.py:23
  10.9 0.0 collective-permute-start.6
  11.0 2.2 %load_weights.1 = (bf16[2048,512]{1,0:T(8,128)(2,1)S(1)}, bf16[512,2048]{1,0:T(8,128)(2,1)S(1)}) custom-call(bf16[3,4,2048]{2,1,0:T(4,128)(2,1)S(1)} %pad_maximum_fusion.refs_0_.packed, bf16[2048,512]{1,0:T(8,128)(2,1)} %refs_1_.1, bf16[512,2048]{1,0:T(8,128)(2,1)} %refs_2_.1), custom_call_target="tpu_custom_call" | custom-call | bytes 8388608 | tf_op jit(solution)/shard_map/load_weights/pallas_call | solution.py:64
  13.2 0.0 collective-permute-done.4.refs_5_
  13.2 0.0 collective-permute-done.5.refs_6_
  13.2 0.0 copy-start.2
  13.2 1.1 %products.1 = (f32[96,128]{1,0:T(8,128)S(1)}, f32[96,128]{1,0:T(8,128)S(1)}, f32[96,128]{1,0:T(8,128)S(1)}, f32[96,128]{1,0:T(8,128)S(1)}) custom-call(bf16[3,4,2048]{2,1,0:T(4,128)(2,1)S(1)} %pad_maximum_fusion.refs_0_.packed, bf16[3,4,2048]{2,1,0:T(4,128)(2,1)S(1)} %collective-permute-done.refs_1_, bf16[3,4,2048]{2,1,0:T(4,128)(2,1)S(1)} %collective-permute-done.1.refs_2_, ...), custom_call_target="tpu_custom_call" | custom-call | tf_op jit(solution)/shard_map/products/pallas_call | solution.py:114
  14.4 1.6 %collective-permute-start.7 = (f32[96,128]{1,0:T(8,128)S(1)}, f32[96,128]{1,0:T(8,128)S(1)}, u32[]{:S(2)}, u32[]{:S(2)}) collective-permute-start(f32[96,128]{1,0:T(8,128)S(1)} %get-tuple-element.11), channel_id=1, source_target_pairs={{0,1},{1,0},{2,3},{3,2},{4,5},{5,4},{6,7},{7,6},{8,9},{9,8},{10,11... | collective-permute-start | bytes 147464 | tf_op jit(solution)/shard_map/ppermute | solution.py:23
  16.0 2.6 %collective-permute-start.8 = (f32[96,128]{1,0:T(8,128)S(1)}, f32[96,128]{1,0:T(8,128)S(1)}, u32[]{:S(2)}, u32[]{:S(2)}) collective-permute-start(f32[96,128]{1,0:T(8,128)S(1)} %get-tuple-element.12), channel_id=1, source_target_pairs={{0,2},{1,3},{2,0},{3,1},{4,6},{5,7},{6,4},{7,5},{8,10},{9,11},{10,... | collective-permute-start | bytes 147464 | tf_op jit(solution)/shard_map/ppermute | solution.py:23
  18.6 0.2 collective-permute-start.9
  18.8 1.5 %inner_products.1.refs_5_ = f32[8,128]{1,0:T(8,128)} custom-call(bf16[3,4,2048]{2,1,0:T(4,128)(2,1)} %copy-done), custom_call_target="tpu_custom_call" | custom-call | tf_op jit(solution)/shard_map/inner_products/pallas_call | solution.py:35
  20.3 1.9 %collective-permute-done.8.refs_2_ = f32[96,128]{1,0:T(8,128)S(1)} collective-permute-done((f32[96,128]{1,0:T(8,128)S(1)}, f32[96,128]{1,0:T(8,128)S(1)}, u32[]{:S(2)}, u32[]{:S(2)}) %collective-permute-start.8) | collective-permute-done | bytes 49184 | tf_op jit(solution)/shard_map/ppermute | solution.py:23
  22.2 2.3 %collective-permute-done.9.refs_3_ = f32[96,128]{1,0:T(8,128)S(1)} collective-permute-done((f32[96,128]{1,0:T(8,128)S(1)}, f32[96,128]{1,0:T(8,128)S(1)}, u32[]{:S(2)}, u32[]{:S(2)}) %collective-permute-start.9) | collective-permute-done | bytes 49184 | tf_op jit(solution)/shard_map/ppermute | solution.py:23
  24.5 0.7 %copy-done.1 = f32[8,128]{1,0:T(8,128)S(1)} copy-done((f32[8,128]{1,0:T(8,128)S(1)}, f32[8,128]{1,0:T(8,128)}, u32[]{:S(2)}) %copy-start.1) | copy-done | bytes 4120
  25.2 0.1 attributions.1
  25.3 9.6 %all_to_all.5.arrived = f32[32,2,128]{2,1,0:T(2,128)} all-to-all(f32[32,2,128]{2,1,0:T(2,128)S(1)} %attributions.1), channel_id=1, replica_groups=mesh['section'=4,'feat'=2,'tensor'=4] {'section','feat','tensor'}, dimensions={0} | all-to-all | bytes 65536 | tf_op jit(solution)/shard_map/all_to_all | solution.py:229
  34.9 1.4 %final.1 = (f32[512]{0:T(512)}, f32[4]{0:T(128)}) custom-call(f32[32,2,128]{2,1,0:T(2,128)} %all_to_all.5.arrived), custom_call_target="tpu_custom_call" | custom-call | tf_op jit(solution)/shard_map/final/pallas_call | solution.py:196
  (9 shorter events, 0.0 us)
Async XLA Ops:
  1.4 11.8 %copy-start = (bf16[3,4,2048]{2,1,0:T(4,128)(2,1)}, bf16[3,4,2048]{2,1,0:T(4,128)(2,1)S(1)}, u32[]{:S(2)}) copy-start(bf16[3,4,2048]{2,1,0:T(4,128)(2,1)S(1)} %pad_maximum_fusion.refs_0_.packed) | copy-start | bytes 147460
  1.4 5.1 %collective-permute-start = (bf16[3,4,2048]{2,1,0:T(4,128)(2,1)S(1)}, bf16[3,4,2048]{2,1,0:T(4,128)(2,1)S(1)}, u32[]{:S(2)}, u32[]{:S(2)}) collective-permute-start(bf16[3,4,2048]{2,1,0:T(4,128)(2,1)S(1)} %pad_maximum_fusion.refs_0_.packed), channel_id=1, source_target_pairs={{0,8},{8,0},{16,24},{24,16},{1,9},{9,1},{17,25},{25,17},{2,10},{10... | collective-permute-start | bytes 147464 | tf_op jit(solution)/shard_map/ppermute | solution.py:23
  4.4 4.1 %collective-permute-start.1 = (bf16[3,4,2048]{2,1,0:T(4,128)(2,1)S(1)}, bf16[3,4,2048]{2,1,0:T(4,128)(2,1)S(1)}, u32[]{:S(2)}, u32[]{:S(2)}) collective-permute-start(bf16[3,4,2048]{2,1,0:T(4,128)(2,1)S(1)} %pad_maximum_fusion.refs_0_.packed), channel_id=1, source_target_pairs={{0,16},{8,24},{16,0},{24,8},{1,17},{9,25},{17,1},{25,9},{2,18},{10... | collective-permute-start | bytes 147464 | tf_op jit(solution)/shard_map/ppermute | solution.py:23
  6.0 5.0 %collective-permute-start.2 = (bf16[3,4,2048]{2,1,0:T(4,128)(2,1)S(1)}, bf16[3,4,2048]{2,1,0:T(4,128)(2,1)S(1)}, u32[]{:S(2)}, u32[]{:S(2)}) collective-permute-start(bf16[3,4,2048]{2,1,0:T(4,128)(2,1)S(1)} %pad_maximum_fusion.refs_0_.packed), channel_id=1, source_target_pairs={{0,24},{8,16},{16,8},{24,0},{1,25},{9,17},{17,9},{25,1},{2,26},{10... | collective-permute-start | bytes 147464 | tf_op jit(solution)/shard_map/ppermute | solution.py:23
  6.0 7.2 %collective-permute-start.3 = (bf16[3,4,2048]{2,1,0:T(4,128)(2,1)S(1)}, bf16[3,4,2048]{2,1,0:T(4,128)(2,1)S(1)}, u32[]{:S(2)}, u32[]{:S(2)}) collective-permute-start(bf16[3,4,2048]{2,1,0:T(4,128)(2,1)S(1)} %pad_maximum_fusion.refs_0_.packed), channel_id=1, source_target_pairs={{0,4},{4,0},{1,5},{5,1},{2,6},{6,2},{3,7},{7,3},{8,12},{12,8},{9,1... | collective-permute-start | bytes 147464 | tf_op jit(solution)/shard_map/ppermute | solution.py:23
  6.5 6.7 %collective-permute-start.4 = (bf16[3,4,2048]{2,1,0:T(4,128)(2,1)S(1)}, bf16[3,4,2048]{2,1,0:T(4,128)(2,1)S(1)}, u32[]{:S(2)}, u32[]{:S(2)}) collective-permute-start(bf16[3,4,2048]{2,1,0:T(4,128)(2,1)S(1)} %collective-permute-done.refs_1_), channel_id=1, source_target_pairs={{0,4},{4,0},{1,5},{5,1},{2,6},{6,2},{3,7},{7,3},{8,12},{12,8},{9,1... | collective-permute-start | bytes 147464 | tf_op jit(solution)/shard_map/ppermute | solution.py:23
  8.5 4.7 %collective-permute-start.5 = (bf16[3,4,2048]{2,1,0:T(4,128)(2,1)S(1)}, bf16[3,4,2048]{2,1,0:T(4,128)(2,1)S(1)}, u32[]{:S(2)}, u32[]{:S(2)}) collective-permute-start(bf16[3,4,2048]{2,1,0:T(4,128)(2,1)S(1)} %collective-permute-done.1.refs_2_), channel_id=1, source_target_pairs={{0,4},{4,0},{1,5},{5,1},{2,6},{6,2},{3,7},{7,3},{8,12},{12,8},{9,1... | collective-permute-start | bytes 147464 | tf_op jit(solution)/shard_map/ppermute | solution.py:23
  10.9 2.3 %collective-permute-start.6 = (bf16[3,4,2048]{2,1,0:T(4,128)(2,1)S(1)}, bf16[3,4,2048]{2,1,0:T(4,128)(2,1)S(1)}, u32[]{:S(2)}, u32[]{:S(2)}) collective-permute-start(bf16[3,4,2048]{2,1,0:T(4,128)(2,1)S(1)} %collective-permute-done.2.refs_3_), channel_id=1, source_target_pairs={{0,4},{4,0},{1,5},{5,1},{2,6},{6,2},{3,7},{7,3},{8,12},{12,8},{9,1... | collective-permute-start | bytes 147464 | tf_op jit(solution)/shard_map/ppermute | solution.py:23
  13.2 11.3 %copy-start.2 = (f32[512]{0:T(512)S(1)}, f32[512]{0:T(512)}, u32[]{:S(2)}) copy-start(f32[512]{0:T(512)} %param.10) | copy-start | bytes 6148
  14.4 5.9 %collective-permute-start.7 = (f32[96,128]{1,0:T(8,128)S(1)}, f32[96,128]{1,0:T(8,128)S(1)}, u32[]{:S(2)}, u32[]{:S(2)}) collective-permute-start(f32[96,128]{1,0:T(8,128)S(1)} %get-tuple-element.11), channel_id=1, source_target_pairs={{0,1},{1,0},{2,3},{3,2},{4,5},{5,4},{6,7},{7,6},{8,9},{9,8},{10,11... | collective-permute-start | bytes 147464 | tf_op jit(solution)/shard_map/ppermute | solution.py:23
  16.0 6.2 %collective-permute-start.8 = (f32[96,128]{1,0:T(8,128)S(1)}, f32[96,128]{1,0:T(8,128)S(1)}, u32[]{:S(2)}, u32[]{:S(2)}) collective-permute-start(f32[96,128]{1,0:T(8,128)S(1)} %get-tuple-element.12), channel_id=1, source_target_pairs={{0,2},{1,3},{2,0},{3,1},{4,6},{5,7},{6,4},{7,5},{8,10},{9,11},{10,... | collective-permute-start | bytes 147464 | tf_op jit(solution)/shard_map/ppermute | solution.py:23
  18.6 5.9 %collective-permute-start.9 = (f32[96,128]{1,0:T(8,128)S(1)}, f32[96,128]{1,0:T(8,128)S(1)}, u32[]{:S(2)}, u32[]{:S(2)}) collective-permute-start(f32[96,128]{1,0:T(8,128)S(1)} %get-tuple-element.13), channel_id=1, source_target_pairs={{0,3},{1,2},{2,1},{3,0},{4,7},{5,6},{6,5},{7,4},{8,11},{9,10},{10,... | collective-permute-start | bytes 147464 | tf_op jit(solution)/shard_map/ppermute | solution.py:23
  24.5 0.7 %copy-start.1 = (f32[8,128]{1,0:T(8,128)S(1)}, f32[8,128]{1,0:T(8,128)}, u32[]{:S(2)}) copy-start(f32[8,128]{1,0:T(8,128)} %inner_products.1.refs_5_) | copy-start | bytes 12292

commit v6 on v5

--- a/solution.py
+++ b/solution.py
@@ -37,6 +37,7 @@
         out_shape=jax.ShapeDtypeStruct((TILE, LANES), jnp.float32),
         in_specs=[vmem],
         out_specs=vmem,
+        compiler_params=pltpu.CompilerParams(vmem_limit_bytes=4 * 2**20),
         name="inner_products",
     )(packed)
 
@@ -47,8 +48,9 @@
     copies = []
     for i in range(count):
         source, target = refs[1 + i], refs[1 + count + i]
-        step = source.shape[0] // pieces
-        for j in range(pieces):
+        count_here = min(pieces, source.shape[0] // 16) or 1
+        step = source.shape[0] // count_here
+        for j in range(count_here):
             part = pl.ds(j * step, step)
             copies.append(
                 pltpu.make_async_copy(source.at[part], target.at[part], sems.at[i, j])
@@ -59,7 +61,7 @@
         copy.wait()
 
 
-def load(after, *arrays, pieces=4):
+def load(after, *arrays, pieces=16):
     size = sum(array.size * array.dtype.itemsize for array in arrays)
     return pl.pallas_call(
         functools.partial(load_kernel, pieces),
@@ -68,7 +70,7 @@
         + [pl.BlockSpec(memory_space=pltpu.HBM)] * len(arrays),
         out_specs=[pl.BlockSpec(memory_space=pltpu.VMEM)] * len(arrays),
         scratch_shapes=[pltpu.SemaphoreType.DMA((len(arrays), pieces))],
-        compiler_params=pltpu.CompilerParams(vmem_limit_bytes=48 * 2**20),
+        compiler_params=pltpu.CompilerParams(vmem_limit_bytes=50 * 2**20),
         cost_estimate=pl.CostEstimate(flops=0, bytes_accessed=2 * size, transcendentals=0),
         name="load_weights",
     )(after, *arrays)
@@ -206,6 +208,7 @@
             pltpu.VMEM((tokens,), jnp.float32),
             pltpu.SemaphoreType.DMA((2,)),
         ],
+        compiler_params=pltpu.CompilerParams(vmem_limit_bytes=4 * 2**20),
         name="final",
     )(arrived)
 
@@ -218,12 +221,19 @@
     packed = jnp.stack([clean_resid, corrupt_resid, metric_grad])
     near = [packed] + far_first(sections, lambda q: exchange(packed, "section", sections, q))
     inner = inner_products(packed)
-    enc_weight, dec_weight = load(packed, enc_weight, dec_weight)
-    blocks = near + [exchange(block, "feat", feats, p) for p in range(1, feats) for block in near]
+    bias = enc_bias.reshape(parts, features // parts)
+    (enc_weight,) = load(packed, enc_weight)
+    far = []
+    for p in range(1, feats):
+        for block in near:
+            if block is packed:
+                block, _ = lax.optimization_barrier((block, enc_weight))
+            far.append(exchange(block, "feat", feats, p))
+    (dec_weight,) = load(near[-1], dec_weight)
+    blocks = near + far
 
     terms = products(parts, blocks, enc_weight, dec_weight)
     arrived = far_first(parts, lambda m: exchange(terms[m], "tensor", parts, m))
-    bias = enc_bias.reshape(parts, features // parts)
     sums = attributions(sizes, [terms[0]] + arrived, bias, inner)
 
     return tuple(final(sizes, tokens, lax.all_to_all(sums, EVERY, 0, 0)))

time: 36.7 us -> 33.9 us (0.924)
  waiting for transfers between devices: 9.15 us -> 7.24 us
  Pallas kernels: 6.32 us -> 5.42 us
  local copies, waits for them, and re-layouts: 0.69 us -> 0.01 us
  starting transfers between devices: 9.01 us -> 9.62 us
    ppermute x10, waiting for transfers between devices: 9.15 us -> 7.24 us  [exchange(): return lax.ppermute(value, axis, [(i, i ^ k) for i in range(size)])]
    pallas_call x1, Pallas kernels: 1.49 us -> 0.1 us  [inner_products(): pl.pallas_call(inner_kernel, out_shape=jax.ShapeDtypeStruct((TILE, LANES)...]
    pallas_call x1 -> x2, Pallas kernels: 2.21 us -> 3.47 us  [load(): pl.pallas_call(functools.partial(load_kernel, pieces), out_shape=[jax.Sha...]
    pallas_call x1, Pallas kernels: 1.37 us -> 0.61 us  [final(): pl.pallas_call(functools.partial(final_kernel, sizes), out_shape=[jax.Sha...]
    unnamed x6 -> x2, local copies, waits for them, and re-layouts: 0.69 us -> 0.01 us
    ppermute x10, starting transfers between devices: 9.01 us -> 9.62 us  [exchange(): return lax.ppermute(value, axis, [(i, i ^ k) for i in range(size)])]
  transfers between devices with their start and end apart: 10 -> 10, of which waited for: 5 -> 4; matrix products, arithmetic and copies ran while one was open for 0% -> 0% of each run, Pallas kernels for 10% -> 11%
where the time goes in v6:
time: 33.9 us; the launch traced here: 33.6 us
  blocking collectives  9.8 us (29%)
  starting transfers between devices  9.62 us (28%)
  waiting for transfers between devices  7.24 us (21%)
  Pallas kernels  5.42 us (16%)
  other arithmetic  0.79 us (2%)
  between operations  0.72 us (2%)
    all_to_all x1, blocking collectives, per_device(): return tuple(final(sizes, tokens, lax.all_to_all(sums, EVERY, 0, 0)))  9.8 us
    ppermute x10, starting transfers between devices, exchange(): return lax.ppermute(value, axis, [(i, i ^ k) for i in range(size)])  9.62 us
    ppermute x10, waiting for transfers between devices, exchange(): return lax.ppermute(value, axis, [(i, i ^ k) for i in range(size)])  7.24 us
    pallas_call x2, Pallas kernels, load(): pl.pallas_call(functools.partial(load_kernel, pieces), out_shape=[jax.Sha...  3.47 us
    pallas_call x1, Pallas kernels, products(): pl.pallas_call(functools.partial(product_kernel, groups, parts), out_shap...  1.14 us
    another operation x1, other arithmetic, per_device(): packed = jnp.stack([clean_resid, corrupt_resid, metric_grad])  0.79 us
  transfers between devices with their start and end apart: 10, of which 4 were waited for; matrix products, arithmetic and copies ran while one was open for 0% of the time, Pallas kernels for 11%

profile of v6, /device:TPU:0, one launch (start us, length us, event | category | flops | bytes accessed | tf_op | source)
XLA Modules:
  0.0 33.6 jit_solution(6049566892232773508)
XLA Ops:
  0.6 0.8 %pad_maximum_fusion.refs_0_.packed = bf16[3,4,2048]{2,1,0:T(4,128)(2,1)S(1)} fusion(bf16[1,4,2048]{2,1,0:T(4,128)(2,1)} %bitcast.5, bf16[1,4,2048]{2,1,0:T(4,128)(2,1)} %bitcast.6, bf16[1,4,2048]{2,1,0:T(4,128)(2,1)} %bitcast.7), kind=kLoop, calls=%fused_computation | loop fusion | flops 49152 | bytes 98304 | tf_op jit(solution)/shard_map/stack | solution.py:221
  1.4 4.0 %collective-permute-start.2 = (bf16[3,4,2048]{2,1,0:T(4,128)(2,1)S(1)}, bf16[3,4,2048]{2,1,0:T(4,128)(2,1)S(1)}, u32[]{:S(2)}, u32[]{:S(2)}) collective-permute-start(bf16[3,4,2048]{2,1,0:T(4,128)(2,1)S(1)} %pad_maximum_fusion.refs_0_.packed), channel_id=1, source_target_pairs={{0,24},{8,16},{16,8},{24,0},{1,25},{9,17},{17,9},{25,1},{2,26},{10... | collective-permute-start | bytes 147464 | tf_op jit(solution)/shard_map/ppermute | solution.py:23
  5.4 0.5 %collective-permute-start = (bf16[3,4,2048]{2,1,0:T(4,128)(2,1)S(1)}, bf16[3,4,2048]{2,1,0:T(4,128)(2,1)S(1)}, u32[]{:S(2)}, u32[]{:S(2)}) collective-permute-start(bf16[3,4,2048]{2,1,0:T(4,128)(2,1)S(1)} %pad_maximum_fusion.refs_0_.packed), channel_id=1, source_target_pairs={{0,8},{8,0},{16,24},{24,16},{1,9},{9,1},{17,25},{25,17},{2,10},{10... | collective-permute-start | bytes 147464 | tf_op jit(solution)/shard_map/ppermute | solution.py:23
  5.9 0.1 collective-permute-start.1
  6.0 1.7 %load_weights.2.refs_8_ = bf16[2048,512]{1,0:T(8,128)(2,1)S(1)} custom-call(bf16[3,4,2048]{2,1,0:T(4,128)(2,1)S(1)} %pad_maximum_fusion.refs_0_.packed, bf16[2048,512]{1,0:T(8,128)(2,1)} %refs_1_.2), custom_call_target="tpu_custom_call" | custom-call | bytes 4194304 | tf_op jit(solution)/shard_map/load_weights/pallas_call | solution.py:66
  7.8 0.1 collective-permute-start.3
  7.9 0.5 %collective-permute-start.6 = (bf16[3,4,2048]{2,1,0:T(4,128)(2,1)S(1)}, bf16[3,4,2048]{2,1,0:T(4,128)(2,1)S(1)}, u32[]{:S(2)}, u32[]{:S(2)}) collective-permute-start(bf16[3,4,2048]{2,1,0:T(4,128)(2,1)S(1)} %collective-permute-done.2.refs_0_.refs_3_), channel_id=1, source_target_pairs={{0,4},{4,0},{1,5},{5,1},{2,6},{6,2},{3,7},{7,3},{8,12},{12,8},{9,1... | collective-permute-start | bytes 147464 | tf_op jit(solution)/shard_map/ppermute | solution.py:23
  8.3 1.1 %collective-permute-done.refs_1_ = bf16[3,4,2048]{2,1,0:T(4,128)(2,1)S(1)} collective-permute-done((bf16[3,4,2048]{2,1,0:T(4,128)(2,1)S(1)}, bf16[3,4,2048]{2,1,0:T(4,128)(2,1)S(1)}, u32[]{:S(2)}, u32[]{:S(2)}) %collective-permute-start) | collective-permute-done | bytes 49184 | tf_op jit(solution)/shard_map/ppermute | solution.py:23
  9.5 0.0 collective-permute-start.4
  9.5 0.5 %collective-permute-done.1.refs_2_ = bf16[3,4,2048]{2,1,0:T(4,128)(2,1)S(1)} collective-permute-done((bf16[3,4,2048]{2,1,0:T(4,128)(2,1)S(1)}, bf16[3,4,2048]{2,1,0:T(4,128)(2,1)S(1)}, u32[]{:S(2)}, u32[]{:S(2)}) %collective-permute-start.1) | collective-permute-done | bytes 49184 | tf_op jit(solution)/shard_map/ppermute | solution.py:23
  10.0 1.7 %load_weights.3.refs_9_ = bf16[512,2048]{1,0:T(8,128)(2,1)S(1)} custom-call(bf16[3,4,2048]{2,1,0:T(4,128)(2,1)S(1)} %collective-permute-done.2.refs_0_.refs_3_, bf16[512,2048]{1,0:T(8,128)(2,1)} %refs_1_.3), custom_call_target="tpu_custom_call" | custom-call | bytes 4194304 | tf_op jit(solution)/shard_map/load_weights/pallas_call | solution.py:66
  11.8 0.0 copy-start
  11.8 0.0 collective-permute-done.6.refs_7_
  11.8 1.1 %products.1 = (f32[96,128]{1,0:T(8,128)S(1)}, f32[96,128]{1,0:T(8,128)S(1)}, f32[96,128]{1,0:T(8,128)S(1)}, f32[96,128]{1,0:T(8,128)S(1)}) custom-call(bf16[3,4,2048]{2,1,0:T(4,128)(2,1)S(1)} %pad_maximum_fusion.refs_0_.packed, bf16[3,4,2048]{2,1,0:T(4,128)(2,1)S(1)} %collective-permute-done.refs_1_, bf16[3,4,2048]{2,1,0:T(4,128)(2,1)S(1)} %collective-permute-done.1.refs_2_, ...), custom_call_target="tpu_custom_call" | custom-call | tf_op jit(solution)/shard_map/products/pallas_call | solution.py:116
  13.0 1.6 %collective-permute-start.7 = (f32[96,128]{1,0:T(8,128)S(1)}, f32[96,128]{1,0:T(8,128)S(1)}, u32[]{:S(2)}, u32[]{:S(2)}) collective-permute-start(f32[96,128]{1,0:T(8,128)S(1)} %get-tuple-element.9), channel_id=1, source_target_pairs={{0,1},{1,0},{2,3},{3,2},{4,5},{5,4},{6,7},{7,6},{8,9},{9,8},{10,11... | collective-permute-start | bytes 147464 | tf_op jit(solution)/shard_map/ppermute | solution.py:23
  14.6 2.6 %collective-permute-start.8 = (f32[96,128]{1,0:T(8,128)S(1)}, f32[96,128]{1,0:T(8,128)S(1)}, u32[]{:S(2)}, u32[]{:S(2)}) collective-permute-start(f32[96,128]{1,0:T(8,128)S(1)} %get-tuple-element.10), channel_id=1, source_target_pairs={{0,2},{1,3},{2,0},{3,1},{4,6},{5,7},{6,4},{7,5},{8,10},{9,11},{10,... | collective-permute-start | bytes 147464 | tf_op jit(solution)/shard_map/ppermute | solution.py:23
  17.2 0.2 collective-permute-start.9
  17.4 0.1 inner_products.1.refs_5_
  17.5 0.0 collective-permute-done.7.refs_1_
  17.5 3.3 %collective-permute-done.8.refs_2_ = f32[96,128]{1,0:T(8,128)S(1)} collective-permute-done((f32[96,128]{1,0:T(8,128)S(1)}, f32[96,128]{1,0:T(8,128)S(1)}, u32[]{:S(2)}, u32[]{:S(2)}) %collective-permute-start.8) | collective-permute-done | bytes 49184 | tf_op jit(solution)/shard_map/ppermute | solution.py:23
  20.8 2.3 %collective-permute-done.9.refs_3_ = f32[96,128]{1,0:T(8,128)S(1)} collective-permute-done((f32[96,128]{1,0:T(8,128)S(1)}, f32[96,128]{1,0:T(8,128)S(1)}, u32[]{:S(2)}, u32[]{:S(2)}) %collective-permute-start.9) | collective-permute-done | bytes 49184 | tf_op jit(solution)/shard_map/ppermute | solution.py:23
  23.1 0.1 attributions.1
  23.2 9.8 %all_to_all.5.arrived = f32[32,2,128]{2,1,0:T(2,128)S(1)} all-to-all(f32[32,2,128]{2,1,0:T(2,128)S(1)} %attributions.1), channel_id=1, replica_groups=mesh['section'=4,'feat'=2,'tensor'=4] {'section','feat','tensor'}, dimensions={0} | all-to-all | bytes 65536 | tf_op jit(solution)/shard_map/all_to_all | solution.py:239
  33.0 0.6 %final.1 = (f32[512]{0:T(512)}, f32[4]{0:T(128)}) custom-call(f32[32,2,128]{2,1,0:T(2,128)S(1)} %all_to_all.5.arrived), custom_call_target="tpu_custom_call" | custom-call | tf_op jit(solution)/shard_map/final/pallas_call | solution.py:198
  (6 shorter events, 0.0 us)
Async XLA Ops:
  1.4 6.4 %collective-permute-start.2 = (bf16[3,4,2048]{2,1,0:T(4,128)(2,1)S(1)}, bf16[3,4,2048]{2,1,0:T(4,128)(2,1)S(1)}, u32[]{:S(2)}, u32[]{:S(2)}) collective-permute-start(bf16[3,4,2048]{2,1,0:T(4,128)(2,1)S(1)} %pad_maximum_fusion.refs_0_.packed), channel_id=1, source_target_pairs={{0,24},{8,16},{16,8},{24,0},{1,25},{9,17},{17,9},{25,1},{2,26},{10... | collective-permute-start | bytes 147464 | tf_op jit(solution)/shard_map/ppermute | solution.py:23
  5.4 4.1 %collective-permute-start = (bf16[3,4,2048]{2,1,0:T(4,128)(2,1)S(1)}, bf16[3,4,2048]{2,1,0:T(4,128)(2,1)S(1)}, u32[]{:S(2)}, u32[]{:S(2)}) collective-permute-start(bf16[3,4,2048]{2,1,0:T(4,128)(2,1)S(1)} %pad_maximum_fusion.refs_0_.packed), channel_id=1, source_target_pairs={{0,8},{8,0},{16,24},{24,16},{1,9},{9,1},{17,25},{25,17},{2,10},{10... | collective-permute-start | bytes 147464 | tf_op jit(solution)/shard_map/ppermute | solution.py:23
  5.9 4.1 %collective-permute-start.1 = (bf16[3,4,2048]{2,1,0:T(4,128)(2,1)S(1)}, bf16[3,4,2048]{2,1,0:T(4,128)(2,1)S(1)}, u32[]{:S(2)}, u32[]{:S(2)}) collective-permute-start(bf16[3,4,2048]{2,1,0:T(4,128)(2,1)S(1)} %pad_maximum_fusion.refs_0_.packed), channel_id=1, source_target_pairs={{0,16},{8,24},{16,0},{24,8},{1,17},{9,25},{17,1},{25,9},{2,18},{10... | collective-permute-start | bytes 147464 | tf_op jit(solution)/shard_map/ppermute | solution.py:23
  7.8 4.0 %collective-permute-start.3 = (bf16[3,4,2048]{2,1,0:T(4,128)(2,1)S(1)}, bf16[3,4,2048]{2,1,0:T(4,128)(2,1)S(1)}, u32[]{:S(2)}, u32[]{:S(2)}) collective-permute-start(bf16[3,4,2048]{2,1,0:T(4,128)(2,1)S(1)} %pad_maximum_fusion.refs_0_.packed), channel_id=1, source_target_pairs={{0,4},{4,0},{1,5},{5,1},{2,6},{6,2},{3,7},{7,3},{8,12},{12,8},{9,1... | collective-permute-start | bytes 147464 | tf_op jit(solution)/shard_map/ppermute | solution.py:23
  7.9 3.9 %collective-permute-start.6 = (bf16[3,4,2048]{2,1,0:T(4,128)(2,1)S(1)}, bf16[3,4,2048]{2,1,0:T(4,128)(2,1)S(1)}, u32[]{:S(2)}, u32[]{:S(2)}) collective-permute-start(bf16[3,4,2048]{2,1,0:T(4,128)(2,1)S(1)} %collective-permute-done.2.refs_0_.refs_3_), channel_id=1, source_target_pairs={{0,4},{4,0},{1,5},{5,1},{2,6},{6,2},{3,7},{7,3},{8,12},{12,8},{9,1... | collective-permute-start | bytes 147464 | tf_op jit(solution)/shard_map/ppermute | solution.py:23
  9.5 2.3 %collective-permute-start.4 = (bf16[3,4,2048]{2,1,0:T(4,128)(2,1)S(1)}, bf16[3,4,2048]{2,1,0:T(4,128)(2,1)S(1)}, u32[]{:S(2)}, u32[]{:S(2)}) collective-permute-start(bf16[3,4,2048]{2,1,0:T(4,128)(2,1)S(1)} %collective-permute-done.refs_1_), channel_id=1, source_target_pairs={{0,4},{4,0},{1,5},{5,1},{2,6},{6,2},{3,7},{7,3},{8,12},{12,8},{9,1... | collective-permute-start | bytes 147464 | tf_op jit(solution)/shard_map/ppermute | solution.py:23
  10.0 1.8 %collective-permute-start.5 = (bf16[3,4,2048]{2,1,0:T(4,128)(2,1)S(1)}, bf16[3,4,2048]{2,1,0:T(4,128)(2,1)S(1)}, u32[]{:S(2)}, u32[]{:S(2)}) collective-permute-start(bf16[3,4,2048]{2,1,0:T(4,128)(2,1)S(1)} %collective-permute-done.1.refs_2_), channel_id=1, source_target_pairs={{0,4},{4,0},{1,5},{5,1},{2,6},{6,2},{3,7},{7,3},{8,12},{12,8},{9,1... | collective-permute-start | bytes 147464 | tf_op jit(solution)/shard_map/ppermute | solution.py:23
  11.8 11.3 %copy-start = (f32[512]{0:T(512)S(1)}, f32[512]{0:T(512)}, u32[]{:S(2)}) copy-start(f32[512]{0:T(512)} %param.10) | copy-start | bytes 6148
  13.0 4.6 %collective-permute-start.7 = (f32[96,128]{1,0:T(8,128)S(1)}, f32[96,128]{1,0:T(8,128)S(1)}, u32[]{:S(2)}, u32[]{:S(2)}) collective-permute-start(f32[96,128]{1,0:T(8,128)S(1)} %get-tuple-element.9), channel_id=1, source_target_pairs={{0,1},{1,0},{2,3},{3,2},{4,5},{5,4},{6,7},{7,6},{8,9},{9,8},{10,11... | collective-permute-start | bytes 147464 | tf_op jit(solution)/shard_map/ppermute | solution.py:23
  14.6 6.2 %collective-permute-start.8 = (f32[96,128]{1,0:T(8,128)S(1)}, f32[96,128]{1,0:T(8,128)S(1)}, u32[]{:S(2)}, u32[]{:S(2)}) collective-permute-start(f32[96,128]{1,0:T(8,128)S(1)} %get-tuple-element.10), channel_id=1, source_target_pairs={{0,2},{1,3},{2,0},{3,1},{4,6},{5,7},{6,4},{7,5},{8,10},{9,11},{10,... | collective-permute-start | bytes 147464 | tf_op jit(solution)/shard_map/ppermute | solution.py:23
  17.2 5.9 %collective-permute-start.9 = (f32[96,128]{1,0:T(8,128)S(1)}, f32[96,128]{1,0:T(8,128)S(1)}, u32[]{:S(2)}, u32[]{:S(2)}) collective-permute-start(f32[96,128]{1,0:T(8,128)S(1)} %get-tuple-element.11), channel_id=1, source_target_pairs={{0,3},{1,2},{2,1},{3,0},{4,7},{5,6},{6,5},{7,4},{8,11},{9,10},{10,... | collective-permute-start | bytes 147464 | tf_op jit(solution)/shard_map/ppermute | solution.py:23

commit v7 on v6

--- a/solution.py
+++ b/solution.py
@@ -14,9 +14,8 @@
 EVERY = ("section", "feat", "tensor")
 
 
-def far_first(size, send):
-    sent = {k: send(k) for k in reversed(range(1, size))}
-    return [sent[k] for k in range(1, size)]
+def far_first(size):
+    return [0, *reversed(range(1, size))]
 
 
 def exchange(value, axis, size, k):
@@ -70,7 +69,7 @@
         + [pl.BlockSpec(memory_space=pltpu.HBM)] * len(arrays),
         out_specs=[pl.BlockSpec(memory_space=pltpu.VMEM)] * len(arrays),
         scratch_shapes=[pltpu.SemaphoreType.DMA((len(arrays), pieces))],
-        compiler_params=pltpu.CompilerParams(vmem_limit_bytes=50 * 2**20),
+        compiler_params=pltpu.CompilerParams(vmem_limit_bytes=48 * 2**20),
         cost_estimate=pl.CostEstimate(flops=0, bytes_accessed=2 * size, transcendentals=0),
         name="load_weights",
     )(after, *arrays)
@@ -136,7 +135,7 @@
 def attribution_kernel(sizes, *refs):
     sections, feats, parts = sizes
     groups = sections * feats
-    terms = refs[:parts]
+    terms = [refs[far_first(parts).index(m)] for m in range(parts)]
     bias, inner, sums = refs[parts:]
     total = terms[0].shape[0] // 3
     tokens = total // groups
@@ -154,8 +153,8 @@
     lane = lax.broadcasted_iota(jnp.int32, (tokens, LANES), 1)
     place = lane == lax.broadcasted_iota(jnp.int32, (tokens, LANES), 0)
     for p in range(feats):
-        for q in range(sections):
-            k = p * sections + q
+        for i, q in enumerate(far_first(sections)):
+            k = p * sections + i
             column = jnp.broadcast_to(token_part[k * tokens : (k + 1) * tokens], (tokens, LANES))
             if k == 0:
                 column = column - inner[pl.ds(0, tokens), :]
@@ -219,23 +218,21 @@
     features = enc_weight.shape[1]
 
     packed = jnp.stack([clean_resid, corrupt_resid, metric_grad])
-    near = [packed] + far_first(sections, lambda q: exchange(packed, "section", sections, q))
+    near = [packed] + [exchange(packed, "section", sections, q) for q in far_first(sections)[1:]]
     inner = inner_products(packed)
     bias = enc_bias.reshape(parts, features // parts)
-    (enc_weight,) = load(packed, enc_weight)
+    enc_weight, dec_weight = load(packed, enc_weight, dec_weight)
     far = []
     for p in range(1, feats):
         for block in near:
             if block is packed:
                 block, _ = lax.optimization_barrier((block, enc_weight))
             far.append(exchange(block, "feat", feats, p))
-    (dec_weight,) = load(near[-1], dec_weight)
     blocks = near + far
 
     terms = products(parts, blocks, enc_weight, dec_weight)
-    arrived = far_first(parts, lambda m: exchange(terms[m], "tensor", parts, m))
+    arrived = [exchange(terms[m], "tensor", parts, m) for m in far_first(parts)[1:]]
     sums = attributions(sizes, [terms[0]] + arrived, bias, inner)
-
     return tuple(final(sizes, tokens, lax.all_to_all(sums, EVERY, 0, 0)))
 
 

time: 33.9 us -> 33.4 us (0.985)
  blocking collectives: 9.8 us -> 11.4 us
  waiting for transfers between devices: 7.24 us -> 6.19 us
  Pallas kernels: 5.42 us -> 4.46 us
    all_to_all x1, blocking collectives: 9.8 us -> 11.4 us  [per_device(): return tuple(final(sizes, tokens, lax.all_to_all(sums, EVERY, 0, 0)))]
    ppermute x10, waiting for transfers between devices: 7.24 us -> 6.19 us  [exchange(): return lax.ppermute(value, axis, [(i, i ^ k) for i in range(size)])]
    pallas_call x2 -> x1, Pallas kernels: 3.47 us -> 2.5 us  [load(): pl.pallas_call(functools.partial(load_kernel, pieces), out_shape=[jax.Sha...]
  transfers between devices with their start and end apart: 10 -> 10, of which waited for: 4 -> 6; matrix products, arithmetic and copies ran while one was open for 0% -> 0% of each run, Pallas kernels for 11% -> 8%
where the time goes in v7:
time: 33.4 us; the launch traced here: 33.1 us
  blocking collectives  11.4 us (34%)
  starting transfers between devices  9.63 us (29%)
  waiting for transfers between devices  6.19 us (19%)
  Pallas kernels  4.46 us (13%)
  other arithmetic  0.79 us (2%)
  between operations  0.68 us (2%)
    all_to_all x1, blocking collectives, per_device(): return tuple(final(sizes, tokens, lax.all_to_all(sums, EVERY, 0, 0)))  11.4 us
    ppermute x10, starting transfers between devices, exchange(): return lax.ppermute(value, axis, [(i, i ^ k) for i in range(size)])  9.63 us
    ppermute x10, waiting for transfers between devices, exchange(): return lax.ppermute(value, axis, [(i, i ^ k) for i in range(size)])  6.19 us
    pallas_call x1, Pallas kernels, load(): pl.pallas_call(functools.partial(load_kernel, pieces), out_shape=[jax.Sha...  2.5 us
    pallas_call x1, Pallas kernels, products(): pl.pallas_call(functools.partial(product_kernel, groups, parts), out_shap...  1.14 us
    another operation x1, other arithmetic, per_device(): packed = jnp.stack([clean_resid, corrupt_resid, metric_grad])  0.79 us
  transfers between devices with their start and end apart: 10, of which 6 were waited for; matrix products, arithmetic and copies ran while one was open for 0% of the time, Pallas kernels for 8%

profile of v7, /device:TPU:0, one launch (start us, length us, event | category | flops | bytes accessed | tf_op | source)
XLA Modules:
  0.0 33.1 jit_solution(5227140546715490627)
XLA Ops:
  0.6 0.8 %pad_maximum_fusion.refs_0_.packed = bf16[3,4,2048]{2,1,0:T(4,128)(2,1)S(1)} fusion(bf16[1,4,2048]{2,1,0:T(4,128)(2,1)} %bitcast.5, bf16[1,4,2048]{2,1,0:T(4,128)(2,1)} %bitcast.6, bf16[1,4,2048]{2,1,0:T(4,128)(2,1)} %bitcast.7), kind=kLoop, calls=%fused_computation | loop fusion | flops 49152 | bytes 98304 | tf_op jit(solution)/shard_map/stack | solution.py:220
  1.4 4.0 %collective-permute-start = (bf16[3,4,2048]{2,1,0:T(4,128)(2,1)S(1)}, bf16[3,4,2048]{2,1,0:T(4,128)(2,1)S(1)}, u32[]{:S(2)}, u32[]{:S(2)}) collective-permute-start(bf16[3,4,2048]{2,1,0:T(4,128)(2,1)S(1)} %pad_maximum_fusion.refs_0_.packed), channel_id=1, source_target_pairs={{0,24},{8,16},{16,8},{24,0},{1,25},{9,17},{17,9},{25,1},{2,26},{10... | collective-permute-start | bytes 147464 | tf_op jit(solution)/shard_map/ppermute | solution.py:22
  5.4 0.5 %collective-permute-start.1 = (bf16[3,4,2048]{2,1,0:T(4,128)(2,1)S(1)}, bf16[3,4,2048]{2,1,0:T(4,128)(2,1)S(1)}, u32[]{:S(2)}, u32[]{:S(2)}) collective-permute-start(bf16[3,4,2048]{2,1,0:T(4,128)(2,1)S(1)} %pad_maximum_fusion.refs_0_.packed), channel_id=1, source_target_pairs={{0,16},{8,24},{16,0},{24,8},{1,17},{9,25},{17,1},{25,9},{2,18},{10... | collective-permute-start | bytes 147464 | tf_op jit(solution)/shard_map/ppermute | solution.py:22
  5.9 0.1 collective-permute-start.2
  6.0 2.5 %load_weights.1 = (bf16[2048,512]{1,0:T(8,128)(2,1)S(1)}, bf16[512,2048]{1,0:T(8,128)(2,1)S(1)}) custom-call(bf16[3,4,2048]{2,1,0:T(4,128)(2,1)S(1)} %pad_maximum_fusion.refs_0_.packed, bf16[2048,512]{1,0:T(8,128)(2,1)} %refs_1_.1, bf16[512,2048]{1,0:T(8,128)(2,1)} %refs_2_.1), custom_call_target="tpu_custom_call" | custom-call | bytes 8388608 | tf_op jit(solution)/shard_map/load_weights/pallas_call | solution.py:65
  8.5 0.1 collective-permute-start.3
  8.6 0.5 %collective-permute-start.4 = (bf16[3,4,2048]{2,1,0:T(4,128)(2,1)S(1)}, bf16[3,4,2048]{2,1,0:T(4,128)(2,1)S(1)}, u32[]{:S(2)}, u32[]{:S(2)}) collective-permute-start(bf16[3,4,2048]{2,1,0:T(4,128)(2,1)S(1)} %collective-permute-done.refs_1_), channel_id=1, source_target_pairs={{0,4},{4,0},{1,5},{5,1},{2,6},{6,2},{3,7},{7,3},{8,12},{12,8},{9,1... | collective-permute-start | bytes 147464 | tf_op jit(solution)/shard_map/ppermute | solution.py:22
  9.1 0.4 %collective-permute-done.1.refs_2_ = bf16[3,4,2048]{2,1,0:T(4,128)(2,1)S(1)} collective-permute-done((bf16[3,4,2048]{2,1,0:T(4,128)(2,1)S(1)}, bf16[3,4,2048]{2,1,0:T(4,128)(2,1)S(1)}, u32[]{:S(2)}, u32[]{:S(2)}) %collective-permute-start.1) | collective-permute-done | bytes 49184 | tf_op jit(solution)/shard_map/ppermute | solution.py:22
  9.5 0.0 collective-permute-start.5
  9.5 0.5 %collective-permute-done.2.refs_3_ = bf16[3,4,2048]{2,1,0:T(4,128)(2,1)S(1)} collective-permute-done((bf16[3,4,2048]{2,1,0:T(4,128)(2,1)S(1)}, bf16[3,4,2048]{2,1,0:T(4,128)(2,1)S(1)}, u32[]{:S(2)}, u32[]{:S(2)}) %collective-permute-start.2) | collective-permute-done | bytes 49184 | tf_op jit(solution)/shard_map/ppermute | solution.py:22
  10.0 0.0 collective-permute-start.6
  10.0 0.0 collective-permute-done.3.refs_4_
  10.0 0.0 collective-permute-done.4.refs_5_
  10.0 0.7 %collective-permute-done.5.refs_6_ = bf16[3,4,2048]{2,1,0:T(4,128)(2,1)S(1)} collective-permute-done((bf16[3,4,2048]{2,1,0:T(4,128)(2,1)S(1)}, bf16[3,4,2048]{2,1,0:T(4,128)(2,1)S(1)}, u32[]{:S(2)}, u32[]{:S(2)}) %collective-permute-start.5) | collective-permute-done | bytes 49184 | tf_op jit(solution)/shard_map/ppermute | solution.py:22
  10.7 0.5 %collective-permute-done.6.refs_7_ = bf16[3,4,2048]{2,1,0:T(4,128)(2,1)S(1)} collective-permute-done((bf16[3,4,2048]{2,1,0:T(4,128)(2,1)S(1)}, bf16[3,4,2048]{2,1,0:T(4,128)(2,1)S(1)}, u32[]{:S(2)}, u32[]{:S(2)}) %collective-permute-start.6) | collective-permute-done | bytes 49184 | tf_op jit(solution)/shard_map/ppermute | solution.py:22
  11.2 1.1 %products.1 = (f32[96,128]{1,0:T(8,128)S(1)}, f32[96,128]{1,0:T(8,128)S(1)}, f32[96,128]{1,0:T(8,128)S(1)}, f32[96,128]{1,0:T(8,128)S(1)}) custom-call(bf16[3,4,2048]{2,1,0:T(4,128)(2,1)S(1)} %pad_maximum_fusion.refs_0_.packed, bf16[3,4,2048]{2,1,0:T(4,128)(2,1)S(1)} %collective-permute-done.refs_1_, bf16[3,4,2048]{2,1,0:T(4,128)(2,1)S(1)} %collective-permute-done.1.refs_2_, ...), custom_call_target="tpu_custom_call" | custom-call | tf_op jit(solution)/shard_map/products/pallas_call | solution.py:115
  12.4 3.7 %collective-permute-start.7 = (f32[96,128]{1,0:T(8,128)S(1)}, f32[96,128]{1,0:T(8,128)S(1)}, u32[]{:S(2)}, u32[]{:S(2)}) collective-permute-start(f32[96,128]{1,0:T(8,128)S(1)} %get-tuple-element.13), channel_id=1, source_target_pairs={{0,3},{1,2},{2,1},{3,0},{4,7},{5,6},{6,5},{7,4},{8,11},{9,10},{10,... | collective-permute-start | bytes 147464 | tf_op jit(solution)/shard_map/ppermute | solution.py:22
  16.0 0.8 %collective-permute-start.9 = (f32[96,128]{1,0:T(8,128)S(1)}, f32[96,128]{1,0:T(8,128)S(1)}, u32[]{:S(2)}, u32[]{:S(2)}) collective-permute-start(f32[96,128]{1,0:T(8,128)S(1)} %get-tuple-element.15), channel_id=1, source_target_pairs={{0,1},{1,0},{2,3},{3,2},{4,5},{5,4},{6,7},{7,6},{8,9},{9,8},{10,11... | collective-permute-start | bytes 147464 | tf_op jit(solution)/shard_map/ppermute | solution.py:22
  16.8 0.1 inner_products.1.refs_5_
  16.9 1.5 %collective-permute-done.7.refs_1_ = f32[96,128]{1,0:T(8,128)S(1)} collective-permute-done((f32[96,128]{1,0:T(8,128)S(1)}, f32[96,128]{1,0:T(8,128)S(1)}, u32[]{:S(2)}, u32[]{:S(2)}) %collective-permute-start.7) | collective-permute-done | bytes 49184 | tf_op jit(solution)/shard_map/ppermute | solution.py:22
  18.4 2.7 %collective-permute-done.8.refs_2_ = f32[96,128]{1,0:T(8,128)S(1)} collective-permute-done((f32[96,128]{1,0:T(8,128)S(1)}, f32[96,128]{1,0:T(8,128)S(1)}, u32[]{:S(2)}, u32[]{:S(2)}) %collective-permute-start.8) | collective-permute-done | bytes 49184 | tf_op jit(solution)/shard_map/ppermute | solution.py:22
  21.0 0.1 attributions.1
  21.1 11.4 %all_to_all.5.arrived = f32[32,2,128]{2,1,0:T(2,128)S(1)} all-to-all(f32[32,2,128]{2,1,0:T(2,128)S(1)} %attributions.1), channel_id=1, replica_groups=mesh['section'=4,'feat'=2,'tensor'=4] {'section','feat','tensor'}, dimensions={0} | all-to-all | bytes 65536 | tf_op jit(solution)/shard_map/all_to_all | solution.py:236
  32.5 0.6 %final.1 = (f32[512]{0:T(512)}, f32[4]{0:T(128)}) custom-call(f32[32,2,128]{2,1,0:T(2,128)S(1)} %all_to_all.5.arrived), custom_call_target="tpu_custom_call" | custom-call | tf_op jit(solution)/shard_map/final/pallas_call | solution.py:197
  (5 shorter events, 0.0 us)
Async XLA Ops:
  1.4 7.2 %collective-permute-start = (bf16[3,4,2048]{2,1,0:T(4,128)(2,1)S(1)}, bf16[3,4,2048]{2,1,0:T(4,128)(2,1)S(1)}, u32[]{:S(2)}, u32[]{:S(2)}) collective-permute-start(bf16[3,4,2048]{2,1,0:T(4,128)(2,1)S(1)} %pad_maximum_fusion.refs_0_.packed), channel_id=1, source_target_pairs={{0,24},{8,16},{16,8},{24,0},{1,25},{9,17},{17,9},{25,1},{2,26},{10... | collective-permute-start | bytes 147464 | tf_op jit(solution)/shard_map/ppermute | solution.py:22
  5.4 4.1 %collective-permute-start.1 = (bf16[3,4,2048]{2,1,0:T(4,128)(2,1)S(1)}, bf16[3,4,2048]{2,1,0:T(4,128)(2,1)S(1)}, u32[]{:S(2)}, u32[]{:S(2)}) collective-permute-start(bf16[3,4,2048]{2,1,0:T(4,128)(2,1)S(1)} %pad_maximum_fusion.refs_0_.packed), channel_id=1, source_target_pairs={{0,16},{8,24},{16,0},{24,8},{1,17},{9,25},{17,1},{25,9},{2,18},{10... | collective-permute-start | bytes 147464 | tf_op jit(solution)/shard_map/ppermute | solution.py:22
  5.9 4.1 %collective-permute-start.2 = (bf16[3,4,2048]{2,1,0:T(4,128)(2,1)S(1)}, bf16[3,4,2048]{2,1,0:T(4,128)(2,1)S(1)}, u32[]{:S(2)}, u32[]{:S(2)}) collective-permute-start(bf16[3,4,2048]{2,1,0:T(4,128)(2,1)S(1)} %pad_maximum_fusion.refs_0_.packed), channel_id=1, source_target_pairs={{0,8},{8,0},{16,24},{24,16},{1,9},{9,1},{17,25},{25,17},{2,10},{10... | collective-permute-start | bytes 147464 | tf_op jit(solution)/shard_map/ppermute | solution.py:22
  8.5 1.5 %collective-permute-start.3 = (bf16[3,4,2048]{2,1,0:T(4,128)(2,1)S(1)}, bf16[3,4,2048]{2,1,0:T(4,128)(2,1)S(1)}, u32[]{:S(2)}, u32[]{:S(2)}) collective-permute-start(bf16[3,4,2048]{2,1,0:T(4,128)(2,1)S(1)} %pad_maximum_fusion.refs_0_.packed), channel_id=1, source_target_pairs={{0,4},{4,0},{1,5},{5,1},{2,6},{6,2},{3,7},{7,3},{8,12},{12,8},{9,1... | collective-permute-start | bytes 147464 | tf_op jit(solution)/shard_map/ppermute | solution.py:22
  8.6 1.4 %collective-permute-start.4 = (bf16[3,4,2048]{2,1,0:T(4,128)(2,1)S(1)}, bf16[3,4,2048]{2,1,0:T(4,128)(2,1)S(1)}, u32[]{:S(2)}, u32[]{:S(2)}) collective-permute-start(bf16[3,4,2048]{2,1,0:T(4,128)(2,1)S(1)} %collective-permute-done.refs_1_), channel_id=1, source_target_pairs={{0,4},{4,0},{1,5},{5,1},{2,6},{6,2},{3,7},{7,3},{8,12},{12,8},{9,1... | collective-permute-start | bytes 147464 | tf_op jit(solution)/shard_map/ppermute | solution.py:22
  9.5 1.2 %collective-permute-start.5 = (bf16[3,4,2048]{2,1,0:T(4,128)(2,1)S(1)}, bf16[3,4,2048]{2,1,0:T(4,128)(2,1)S(1)}, u32[]{:S(2)}, u32[]{:S(2)}) collective-permute-start(bf16[3,4,2048]{2,1,0:T(4,128)(2,1)S(1)} %collective-permute-done.1.refs_2_), channel_id=1, source_target_pairs={{0,4},{4,0},{1,5},{5,1},{2,6},{6,2},{3,7},{7,3},{8,12},{12,8},{9,1... | collective-permute-start | bytes 147464 | tf_op jit(solution)/shard_map/ppermute | solution.py:22
  10.0 1.2 %collective-permute-start.6 = (bf16[3,4,2048]{2,1,0:T(4,128)(2,1)S(1)}, bf16[3,4,2048]{2,1,0:T(4,128)(2,1)S(1)}, u32[]{:S(2)}, u32[]{:S(2)}) collective-permute-start(bf16[3,4,2048]{2,1,0:T(4,128)(2,1)S(1)} %collective-permute-done.2.refs_3_), channel_id=1, source_target_pairs={{0,4},{4,0},{1,5},{5,1},{2,6},{6,2},{3,7},{7,3},{8,12},{12,8},{9,1... | collective-permute-start | bytes 147464 | tf_op jit(solution)/shard_map/ppermute | solution.py:22
  11.2 9.8 %copy-start = (f32[512]{0:T(512)S(1)}, f32[512]{0:T(512)}, u32[]{:S(2)}) copy-start(f32[512]{0:T(512)} %param.10) | copy-start | bytes 6148
  12.4 6.0 %collective-permute-start.7 = (f32[96,128]{1,0:T(8,128)S(1)}, f32[96,128]{1,0:T(8,128)S(1)}, u32[]{:S(2)}, u32[]{:S(2)}) collective-permute-start(f32[96,128]{1,0:T(8,128)S(1)} %get-tuple-element.13), channel_id=1, source_target_pairs={{0,3},{1,2},{2,1},{3,0},{4,7},{5,6},{6,5},{7,4},{8,11},{9,10},{10,... | collective-permute-start | bytes 147464 | tf_op jit(solution)/shard_map/ppermute | solution.py:22
  16.0 5.0 %collective-permute-start.8 = (f32[96,128]{1,0:T(8,128)S(1)}, f32[96,128]{1,0:T(8,128)S(1)}, u32[]{:S(2)}, u32[]{:S(2)}) collective-permute-start(f32[96,128]{1,0:T(8,128)S(1)} %get-tuple-element.14), channel_id=1, source_target_pairs={{0,2},{1,3},{2,0},{3,1},{4,6},{5,7},{6,4},{7,5},{8,10},{9,11},{10,... | collective-permute-start | bytes 147464 | tf_op jit(solution)/shard_map/ppermute | solution.py:22
  16.0 5.0 %collective-permute-start.9 = (f32[96,128]{1,0:T(8,128)S(1)}, f32[96,128]{1,0:T(8,128)S(1)}, u32[]{:S(2)}, u32[]{:S(2)}) collective-permute-start(f32[96,128]{1,0:T(8,128)S(1)} %get-tuple-element.15), channel_id=1, source_target_pairs={{0,1},{1,0},{2,3},{3,2},{4,5},{5,4},{6,7},{7,6},{8,9},{9,8},{10,11... | collective-permute-start | bytes 147464 | tf_op jit(solution)/shard_map/ppermute | solution.py:22

commit v8 on v7

--- a/solution.py
+++ b/solution.py
@@ -37,6 +37,27 @@
         in_specs=[vmem],
         out_specs=vmem,
         compiler_params=pltpu.CompilerParams(vmem_limit_bytes=4 * 2**20),
+        cost_estimate=pl.CostEstimate(flops=2**32, bytes_accessed=2**24, transcendentals=0),
+        name="inner_products",
+    )(packed)
+
+
+def inner_kernel(packed, inner):
+    tokens = packed.shape[1]
+    clean, corrupt, grad = [packed[a].astype(jnp.float32) for a in range(3)]
+    part = jnp.sum((corrupt - clean) * grad, axis=1, keepdims=True)
+    inner[pl.ds(0, tokens), :] = jnp.broadcast_to(part, (tokens, LANES))
+
+
+def inner_products(packed):
+    vmem = pl.BlockSpec(memory_space=pltpu.VMEM)
+    return pl.pallas_call(
+        inner_kernel,
+        out_shape=jax.ShapeDtypeStruct((TILE, LANES), jnp.float32),
+        in_specs=[vmem],
+        out_specs=vmem,
+        compiler_params=pltpu.CompilerParams(vmem_limit_bytes=4 * 2**20),
+        cost_estimate=pl.CostEstimate(flops=2**32, bytes_accessed=2**24, transcendentals=0),
         name="inner_products",
     )(packed)
 
@@ -60,7 +81,7 @@
         copy.wait()
 
 
-def load(after, *arrays, pieces=16):
+def load(after, *arrays, pieces=4):
     size = sum(array.size * array.dtype.itemsize for array in arrays)
     return pl.pallas_call(
         functools.partial(load_kernel, pieces),
@@ -69,7 +90,7 @@
         + [pl.BlockSpec(memory_space=pltpu.HBM)] * len(arrays),
         out_specs=[pl.BlockSpec(memory_space=pltpu.VMEM)] * len(arrays),
         scratch_shapes=[pltpu.SemaphoreType.DMA((len(arrays), pieces))],
-        compiler_params=pltpu.CompilerParams(vmem_limit_bytes=48 * 2**20),
+        compiler_params=pltpu.CompilerParams(vmem_limit_bytes=16 * 2**20),
         cost_estimate=pl.CostEstimate(flops=0, bytes_accessed=2 * size, transcendentals=0),
         name="load_weights",
     )(after, *arrays)
@@ -153,8 +174,8 @@
     lane = lax.broadcasted_iota(jnp.int32, (tokens, LANES), 1)
     place = lane == lax.broadcasted_iota(jnp.int32, (tokens, LANES), 0)
     for p in range(feats):
-        for i, q in enumerate(far_first(sections)):
-            k = p * sections + i
+        for q in range(sections):
+            k = p * sections + q
             column = jnp.broadcast_to(token_part[k * tokens : (k + 1) * tokens], (tokens, LANES))
             if k == 0:
                 column = column - inner[pl.ds(0, tokens), :]
@@ -218,15 +239,14 @@
     features = enc_weight.shape[1]
 
     packed = jnp.stack([clean_resid, corrupt_resid, metric_grad])
-    near = [packed] + [exchange(packed, "section", sections, q) for q in far_first(sections)[1:]]
+    near = [packed] + [exchange(packed, "section", sections, q) for q in range(1, sections)]
     inner = inner_products(packed)
     bias = enc_bias.reshape(parts, features // parts)
-    enc_weight, dec_weight = load(packed, enc_weight, dec_weight)
     far = []
     for p in range(1, feats):
         for block in near:
             if block is packed:
-                block, _ = lax.optimization_barrier((block, enc_weight))
+                block, inner = lax.optimization_barrier((block, inner))
             far.append(exchange(block, "feat", feats, p))
     blocks = near + far
 

time: 33.4 us -> 32.7 us (0.979)
  waiting for transfers between devices: 6.19 us -> 9.26 us
  Pallas kernels: 4.46 us -> 1.96 us
  blocking collectives: 11.4 us -> 10.6 us
  starting transfers between devices: 9.63 us -> 9.07 us
    ppermute x10, waiting for transfers between devices: 6.19 us -> 9.26 us  [exchange(): return lax.ppermute(value, axis, [(i, i ^ k) for i in range(size)])]
    pallas_call x1 -> x0, Pallas kernels: 2.5 us -> none  [load(): pl.pallas_call(functools.partial(load_kernel, pieces), out_shape=[jax.Sha...]
    all_to_all x1, blocking collectives: 11.4 us -> 10.6 us  [per_device(): return tuple(final(sizes, tokens, lax.all_to_all(sums, EVERY, 0, 0)))]
    ppermute x10, starting transfers between devices: 9.63 us -> 9.07 us  [exchange(): return lax.ppermute(value, axis, [(i, i ^ k) for i in range(size)])]
  transfers between devices with their start and end apart: 10 -> 10, of which waited for: 6 -> 7; matrix products, arithmetic and copies ran while one was open for 0% -> 0% of each run, Pallas kernels for 8% -> 0%
where the time goes in v8:
time: 32.7 us; the launch traced here: 32.4 us
  blocking collectives  10.6 us (32%)
  waiting for transfers between devices  9.26 us (28%)
  starting transfers between devices  9.07 us (28%)
  Pallas kernels  1.96 us (6%)
  other arithmetic  0.79 us (2%)
  between operations  0.68 us (2%)
    all_to_all x1, blocking collectives, per_device(): return tuple(final(sizes, tokens, lax.all_to_all(sums, EVERY, 0, 0)))  10.6 us
    ppermute x10, waiting for transfers between devices, exchange(): return lax.ppermute(value, axis, [(i, i ^ k) for i in range(size)])  9.26 us
    ppermute x10, starting transfers between devices, exchange(): return lax.ppermute(value, axis, [(i, i ^ k) for i in range(size)])  9.07 us
    pallas_call x1, Pallas kernels, products(): pl.pallas_call(functools.partial(product_kernel, groups, parts), out_shap...  1.14 us
    another operation x1, other arithmetic, per_device(): packed = jnp.stack([clean_resid, corrupt_resid, metric_grad])  0.79 us
  transfers between devices with their start and end apart: 10, of which 7 were waited for; matrix products, arithmetic and copies ran while one was open for 0% of the time, Pallas kernels for 0%

profile of v8, /device:TPU:0, one launch (start us, length us, event | category | flops | bytes accessed | tf_op | source)
XLA Modules:
  0.0 32.4 jit_solution(16543544032012407074)
XLA Ops:
  0.6 0.8 %pad_maximum_fusion.packed.refs_0_ = bf16[3,4,2048]{2,1,0:T(4,128)(2,1)S(1)} fusion(bf16[1,4,2048]{2,1,0:T(4,128)(2,1)} %bitcast.5, bf16[1,4,2048]{2,1,0:T(4,128)(2,1)} %bitcast.6, bf16[1,4,2048]{2,1,0:T(4,128)(2,1)} %bitcast.7), kind=kLoop, calls=%fused_computation | loop fusion | flops 49152 | bytes 98304 | tf_op jit(solution)/shard_map/stack | solution.py:241
  1.4 0.0 copy-start
  1.4 0.0 copy-start.1
  1.4 4.0 %collective-permute-start.2 = (bf16[3,4,2048]{2,1,0:T(4,128)(2,1)S(1)}, bf16[3,4,2048]{2,1,0:T(4,128)(2,1)S(1)}, u32[]{:S(2)}, u32[]{:S(2)}) collective-permute-start(bf16[3,4,2048]{2,1,0:T(4,128)(2,1)S(1)} %pad_maximum_fusion.packed.refs_0_), channel_id=1, source_target_pairs={{0,24},{8,16},{16,8},{24,0},{1,25},{9,17},{17,9},{25,1},{2,26},{10... | collective-permute-start | bytes 147464 | tf_op jit(solution)/shard_map/ppermute | solution.py:22
  5.4 0.5 %collective-permute-start.1 = (bf16[3,4,2048]{2,1,0:T(4,128)(2,1)S(1)}, bf16[3,4,2048]{2,1,0:T(4,128)(2,1)S(1)}, u32[]{:S(2)}, u32[]{:S(2)}) collective-permute-start(bf16[3,4,2048]{2,1,0:T(4,128)(2,1)S(1)} %pad_maximum_fusion.packed.refs_0_), channel_id=1, source_target_pairs={{0,16},{8,24},{16,0},{24,8},{1,17},{9,25},{17,1},{25,9},{2,18},{10... | collective-permute-start | bytes 147464 | tf_op jit(solution)/shard_map/ppermute | solution.py:22
  5.9 0.1 collective-permute-start
  6.1 0.1 inner_products.1.refs_5_
  6.2 0.0 collective-permute-start.3
  6.2 1.3 %collective-permute-done.2.refs_3_ = bf16[3,4,2048]{2,1,0:T(4,128)(2,1)S(1)} collective-permute-done((bf16[3,4,2048]{2,1,0:T(4,128)(2,1)S(1)}, bf16[3,4,2048]{2,1,0:T(4,128)(2,1)S(1)}, u32[]{:S(2)}, u32[]{:S(2)}) %collective-permute-start.2) | collective-permute-done | bytes 49184 | tf_op jit(solution)/shard_map/ppermute | solution.py:22
  7.5 0.0 collective-permute-start.6
  7.5 2.0 %collective-permute-done.1.refs_2_ = bf16[3,4,2048]{2,1,0:T(4,128)(2,1)S(1)} collective-permute-done((bf16[3,4,2048]{2,1,0:T(4,128)(2,1)S(1)}, bf16[3,4,2048]{2,1,0:T(4,128)(2,1)S(1)}, u32[]{:S(2)}, u32[]{:S(2)}) %collective-permute-start.1) | collective-permute-done | bytes 49184 | tf_op jit(solution)/shard_map/ppermute | solution.py:22
  9.5 0.0 collective-permute-start.5
  9.5 0.5 %collective-permute-done.refs_1_ = bf16[3,4,2048]{2,1,0:T(4,128)(2,1)S(1)} collective-permute-done((bf16[3,4,2048]{2,1,0:T(4,128)(2,1)S(1)}, bf16[3,4,2048]{2,1,0:T(4,128)(2,1)S(1)}, u32[]{:S(2)}, u32[]{:S(2)}) %collective-permute-start) | collective-permute-done | bytes 49184 | tf_op jit(solution)/shard_map/ppermute | solution.py:22
  10.0 0.0 collective-permute-start.4
  10.0 0.7 %collective-permute-done.5.refs_6_ = bf16[3,4,2048]{2,1,0:T(4,128)(2,1)S(1)} collective-permute-done((bf16[3,4,2048]{2,1,0:T(4,128)(2,1)S(1)}, bf16[3,4,2048]{2,1,0:T(4,128)(2,1)S(1)}, u32[]{:S(2)}, u32[]{:S(2)}) %collective-permute-start.5) | collective-permute-done | bytes 49184 | tf_op jit(solution)/shard_map/ppermute | solution.py:22
  10.7 0.5 %collective-permute-done.4.refs_5_ = bf16[3,4,2048]{2,1,0:T(4,128)(2,1)S(1)} collective-permute-done((bf16[3,4,2048]{2,1,0:T(4,128)(2,1)S(1)}, bf16[3,4,2048]{2,1,0:T(4,128)(2,1)S(1)}, u32[]{:S(2)}, u32[]{:S(2)}) %collective-permute-start.4) | collective-permute-done | bytes 49184 | tf_op jit(solution)/shard_map/ppermute | solution.py:22
  11.2 1.1 %products.1 = (f32[96,128]{1,0:T(8,128)S(1)}, f32[96,128]{1,0:T(8,128)S(1)}, f32[96,128]{1,0:T(8,128)S(1)}, f32[96,128]{1,0:T(8,128)S(1)}) custom-call(bf16[3,4,2048]{2,1,0:T(4,128)(2,1)S(1)} %pad_maximum_fusion.packed.refs_0_, bf16[3,4,2048]{2,1,0:T(4,128)(2,1)S(1)} %collective-permute-done.refs_1_, bf16[3,4,2048]{2,1,0:T(4,128)(2,1)S(1)} %collective-permute-done.1.refs_2_, ...), custom_call_target="tpu_custom_call" | custom-call | tf_op jit(solution)/shard_map/products/pallas_call | solution.py:136
  12.4 3.7 %collective-permute-start.7 = (f32[96,128]{1,0:T(8,128)S(1)}, f32[96,128]{1,0:T(8,128)S(1)}, u32[]{:S(2)}, u32[]{:S(2)}) collective-permute-start(f32[96,128]{1,0:T(8,128)S(1)} %get-tuple-element.10), channel_id=1, source_target_pairs={{0,3},{1,2},{2,1},{3,0},{4,7},{5,6},{6,5},{7,4},{8,11},{9,10},{10,... | collective-permute-start | bytes 147464 | tf_op jit(solution)/shard_map/ppermute | solution.py:22
  16.1 0.8 %collective-permute-start.9 = (f32[96,128]{1,0:T(8,128)S(1)}, f32[96,128]{1,0:T(8,128)S(1)}, u32[]{:S(2)}, u32[]{:S(2)}) collective-permute-start(f32[96,128]{1,0:T(8,128)S(1)} %get-tuple-element.12), channel_id=1, source_target_pairs={{0,1},{1,0},{2,3},{3,2},{4,5},{5,4},{6,7},{7,6},{8,9},{9,8},{10,11... | collective-permute-start | bytes 147464 | tf_op jit(solution)/shard_map/ppermute | solution.py:22
  16.8 1.6 %collective-permute-done.7.refs_1_ = f32[96,128]{1,0:T(8,128)S(1)} collective-permute-done((f32[96,128]{1,0:T(8,128)S(1)}, f32[96,128]{1,0:T(8,128)S(1)}, u32[]{:S(2)}, u32[]{:S(2)}) %collective-permute-start.7) | collective-permute-done | bytes 49184 | tf_op jit(solution)/shard_map/ppermute | solution.py:22
  18.4 2.6 %collective-permute-done.8.refs_2_ = f32[96,128]{1,0:T(8,128)S(1)} collective-permute-done((f32[96,128]{1,0:T(8,128)S(1)}, f32[96,128]{1,0:T(8,128)S(1)}, u32[]{:S(2)}, u32[]{:S(2)}) %collective-permute-start.8) | collective-permute-done | bytes 49184 | tf_op jit(solution)/shard_map/ppermute | solution.py:22
  21.1 0.1 attributions.1
  21.2 10.6 %all_to_all.5.arrived = f32[32,2,128]{2,1,0:T(2,128)S(1)} all-to-all(f32[32,2,128]{2,1,0:T(2,128)S(1)} %attributions.1), channel_id=1, replica_groups=mesh['section'=4,'feat'=2,'tensor'=4] {'section','feat','tensor'}, dimensions={0} | all-to-all | bytes 65536 | tf_op jit(solution)/shard_map/all_to_all | solution.py:256
  31.8 0.6 %final.1 = (f32[512]{0:T(512)}, f32[4]{0:T(128)}) custom-call(f32[32,2,128]{2,1,0:T(2,128)S(1)} %all_to_all.5.arrived), custom_call_target="tpu_custom_call" | custom-call | tf_op jit(solution)/shard_map/final/pallas_call | solution.py:218
  (8 shorter events, 0.0 us)
Async XLA Ops:
  1.4 9.8 %copy-start = (bf16[2048,512]{1,0:T(8,128)(2,1)S(1)}, bf16[2048,512]{1,0:T(8,128)(2,1)}, u32[]{:S(2)}) copy-start(bf16[2048,512]{1,0:T(8,128)(2,1)} %refs_8_.1) | copy-start | bytes 6291460
  1.4 9.8 %copy-start.1 = (bf16[512,2048]{1,0:T(8,128)(2,1)S(1)}, bf16[512,2048]{1,0:T(8,128)(2,1)}, u32[]{:S(2)}) copy-start(bf16[512,2048]{1,0:T(8,128)(2,1)} %refs_9_.1) | copy-start | bytes 6291460
  1.4 6.0 %collective-permute-start.2 = (bf16[3,4,2048]{2,1,0:T(4,128)(2,1)S(1)}, bf16[3,4,2048]{2,1,0:T(4,128)(2,1)S(1)}, u32[]{:S(2)}, u32[]{:S(2)}) collective-permute-start(bf16[3,4,2048]{2,1,0:T(4,128)(2,1)S(1)} %pad_maximum_fusion.packed.refs_0_), channel_id=1, source_target_pairs={{0,24},{8,16},{16,8},{24,0},{1,25},{9,17},{17,9},{25,1},{2,26},{10... | collective-permute-start | bytes 147464 | tf_op jit(solution)/shard_map/ppermute | solution.py:22
  5.4 4.1 %collective-permute-start.1 = (bf16[3,4,2048]{2,1,0:T(4,128)(2,1)S(1)}, bf16[3,4,2048]{2,1,0:T(4,128)(2,1)S(1)}, u32[]{:S(2)}, u32[]{:S(2)}) collective-permute-start(bf16[3,4,2048]{2,1,0:T(4,128)(2,1)S(1)} %pad_maximum_fusion.packed.refs_0_), channel_id=1, source_target_pairs={{0,16},{8,24},{16,0},{24,8},{1,17},{9,25},{17,1},{25,9},{2,18},{10... | collective-permute-start | bytes 147464 | tf_op jit(solution)/shard_map/ppermute | solution.py:22
  5.9 4.1 %collective-permute-start = (bf16[3,4,2048]{2,1,0:T(4,128)(2,1)S(1)}, bf16[3,4,2048]{2,1,0:T(4,128)(2,1)S(1)}, u32[]{:S(2)}, u32[]{:S(2)}) collective-permute-start(bf16[3,4,2048]{2,1,0:T(4,128)(2,1)S(1)} %pad_maximum_fusion.packed.refs_0_), channel_id=1, source_target_pairs={{0,8},{8,0},{16,24},{24,16},{1,9},{9,1},{17,25},{25,17},{2,10},{10... | collective-permute-start | bytes 147464 | tf_op jit(solution)/shard_map/ppermute | solution.py:22
  6.2 14.9 %copy-start.2 = (f32[512]{0:T(512)S(1)}, f32[512]{0:T(512)}, u32[]{:S(2)}) copy-start(f32[512]{0:T(512)} %param.10) | copy-start | bytes 6148
  6.2 3.9 %collective-permute-start.3 = (bf16[3,4,2048]{2,1,0:T(4,128)(2,1)S(1)}, bf16[3,4,2048]{2,1,0:T(4,128)(2,1)S(1)}, u32[]{:S(2)}, u32[]{:S(2)}) collective-permute-start(bf16[3,4,2048]{2,1,0:T(4,128)(2,1)S(1)} %pad_maximum_fusion.packed.refs_0_), channel_id=1, source_target_pairs={{0,4},{4,0},{1,5},{5,1},{2,6},{6,2},{3,7},{7,3},{8,12},{12,8},{9,1... | collective-permute-start | bytes 147464 | tf_op jit(solution)/shard_map/ppermute | solution.py:22
  7.5 2.5 %collective-permute-start.6 = (bf16[3,4,2048]{2,1,0:T(4,128)(2,1)S(1)}, bf16[3,4,2048]{2,1,0:T(4,128)(2,1)S(1)}, u32[]{:S(2)}, u32[]{:S(2)}) collective-permute-start(bf16[3,4,2048]{2,1,0:T(4,128)(2,1)S(1)} %collective-permute-done.2.refs_3_), channel_id=1, source_target_pairs={{0,4},{4,0},{1,5},{5,1},{2,6},{6,2},{3,7},{7,3},{8,12},{12,8},{9,1... | collective-permute-start | bytes 147464 | tf_op jit(solution)/shard_map/ppermute | solution.py:22
  9.5 1.2 %collective-permute-start.5 = (bf16[3,4,2048]{2,1,0:T(4,128)(2,1)S(1)}, bf16[3,4,2048]{2,1,0:T(4,128)(2,1)S(1)}, u32[]{:S(2)}, u32[]{:S(2)}) collective-permute-start(bf16[3,4,2048]{2,1,0:T(4,128)(2,1)S(1)} %collective-permute-done.1.refs_2_), channel_id=1, source_target_pairs={{0,4},{4,0},{1,5},{5,1},{2,6},{6,2},{3,7},{7,3},{8,12},{12,8},{9,1... | collective-permute-start | bytes 147464 | tf_op jit(solution)/shard_map/ppermute | solution.py:22
  10.0 1.2 %collective-permute-start.4 = (bf16[3,4,2048]{2,1,0:T(4,128)(2,1)S(1)}, bf16[3,4,2048]{2,1,0:T(4,128)(2,1)S(1)}, u32[]{:S(2)}, u32[]{:S(2)}) collective-permute-start(bf16[3,4,2048]{2,1,0:T(4,128)(2,1)S(1)} %collective-permute-done.refs_1_), channel_id=1, source_target_pairs={{0,4},{4,0},{1,5},{5,1},{2,6},{6,2},{3,7},{7,3},{8,12},{12,8},{9,1... | collective-permute-start | bytes 147464 | tf_op jit(solution)/shard_map/ppermute | solution.py:22
  12.4 6.0 %collective-permute-start.7 = (f32[96,128]{1,0:T(8,128)S(1)}, f32[96,128]{1,0:T(8,128)S(1)}, u32[]{:S(2)}, u32[]{:S(2)}) collective-permute-start(f32[96,128]{1,0:T(8,128)S(1)} %get-tuple-element.10), channel_id=1, source_target_pairs={{0,3},{1,2},{2,1},{3,0},{4,7},{5,6},{6,5},{7,4},{8,11},{9,10},{10,... | collective-permute-start | bytes 147464 | tf_op jit(solution)/shard_map/ppermute | solution.py:22
  16.1 5.0 %collective-permute-start.8 = (f32[96,128]{1,0:T(8,128)S(1)}, f32[96,128]{1,0:T(8,128)S(1)}, u32[]{:S(2)}, u32[]{:S(2)}) collective-permute-start(f32[96,128]{1,0:T(8,128)S(1)} %get-tuple-element.11), channel_id=1, source_target_pairs={{0,2},{1,3},{2,0},{3,1},{4,6},{5,7},{6,4},{7,5},{8,10},{9,11},{10,... | collective-permute-start | bytes 147464 | tf_op jit(solution)/shard_map/ppermute | solution.py:22
  16.1 5.0 %collective-permute-start.9 = (f32[96,128]{1,0:T(8,128)S(1)}, f32[96,128]{1,0:T(8,128)S(1)}, u32[]{:S(2)}, u32[]{:S(2)}) collective-permute-start(f32[96,128]{1,0:T(8,128)S(1)} %get-tuple-element.12), channel_id=1, source_target_pairs={{0,1},{1,0},{2,3},{3,2},{4,5},{5,4},{6,7},{7,6},{8,9},{9,8},{10,11... | collective-permute-start | bytes 147464 | tf_op jit(solution)/shard_map/ppermute | solution.py:22

commit v9 on v8

--- a/solution.py
+++ b/solution.py
@@ -181,7 +181,7 @@
                 column = column - inner[pl.ds(0, tokens), :]
             row = jnp.sum(jnp.where(place, column, 0.0), axis=0, keepdims=True)
             owner = (section ^ q) * feats + (feat ^ p)
-            sums[pl.ds(owner * parts, parts), 1, :] = jnp.broadcast_to(row, (parts, LANES))
+            sums[pl.ds((groups - 1 - owner) * parts, parts), 1, :] = jnp.broadcast_to(row, (parts, LANES))
 
 
 def attributions(sizes, terms, bias, inner):
@@ -200,9 +200,9 @@
 def final_kernel(sizes, arrived, feature_out, error_out, features, errors, sems):
     sections, feats, parts = sizes
     group = lax.axis_index("section") * feats + lax.axis_index("feat")
-    mine = arrived[pl.ds(group * parts, parts), 0, :]
+    mine = arrived[pl.ds((sections * feats - 1 - group) * parts, parts), 0, :]
     for i in range(parts):
-        features[pl.ds(i * LANES, LANES)] = mine[i]
+        features[pl.ds(i * LANES, LANES)] = mine[parts - 1 - i]
     feature_copy = pltpu.make_async_copy(features, feature_out, sems.at[0])
     feature_copy.start()
     owed = add_up([arrived[i, 1:2, :] for i in range(sections * feats * parts)])
@@ -253,7 +253,9 @@
     terms = products(parts, blocks, enc_weight, dec_weight)
     arrived = [exchange(terms[m], "tensor", parts, m) for m in far_first(parts)[1:]]
     sums = attributions(sizes, [terms[0]] + arrived, bias, inner)
-    return tuple(final(sizes, tokens, lax.all_to_all(sums, EVERY, 0, 0)))
+    far_end = [list(reversed(range(sections * feats * parts)))]
+    arrived = lax.all_to_all(sums, EVERY, 0, 0, axis_index_groups=far_end)
+    return tuple(final(sizes, tokens, arrived))
 
 
 def solution(mesh):

time: 32.7 us -> 32.6 us (level)
  no operation moved by 1% of the time
where the time goes in v9:
time: 32.6 us; the launch traced here: 32.3 us
  blocking collectives  10.5 us (32%)
  waiting for transfers between devices  9.26 us (28%)
  starting transfers between devices  9.07 us (28%)
  Pallas kernels  1.96 us (6%)
  other arithmetic  0.79 us (2%)
  between operations  0.68 us (2%)
    all_to_all x1, blocking collectives, per_device(): arrived = lax.all_to_all(sums, EVERY, 0, 0, axis_index_groups=far_end)  10.5 us
    ppermute x10, waiting for transfers between devices, exchange(): return lax.ppermute(value, axis, [(i, i ^ k) for i in range(size)])  9.26 us
    ppermute x10, starting transfers between devices, exchange(): return lax.ppermute(value, axis, [(i, i ^ k) for i in range(size)])  9.07 us
    pallas_call x1, Pallas kernels, products(): pl.pallas_call(functools.partial(product_kernel, groups, parts), out_shap...  1.14 us
    another operation x1, other arithmetic, per_device(): packed = jnp.stack([clean_resid, corrupt_resid, metric_grad])  0.79 us
  transfers between devices with their start and end apart: 10, of which 7 were waited for; matrix products, arithmetic and copies ran while one was open for 0% of the time, Pallas kernels for 0%

profile of v9, /device:TPU:0, one launch (start us, length us, event | category | flops | bytes accessed | tf_op | source)
XLA Modules:
  0.0 32.3 jit_solution(18109438059415837031)
XLA Ops:
  0.6 0.8 %pad_maximum_fusion.packed.refs_0_ = bf16[3,4,2048]{2,1,0:T(4,128)(2,1)S(1)} fusion(bf16[1,4,2048]{2,1,0:T(4,128)(2,1)} %bitcast.5, bf16[1,4,2048]{2,1,0:T(4,128)(2,1)} %bitcast.6, bf16[1,4,2048]{2,1,0:T(4,128)(2,1)} %bitcast.7), kind=kLoop, calls=%fused_computation | loop fusion | flops 49152 | bytes 98304 | tf_op jit(solution)/shard_map/stack | solution.py:241
  1.4 0.0 copy-start
  1.4 0.0 copy-start.1
  1.4 4.0 %collective-permute-start.2 = (bf16[3,4,2048]{2,1,0:T(4,128)(2,1)S(1)}, bf16[3,4,2048]{2,1,0:T(4,128)(2,1)S(1)}, u32[]{:S(2)}, u32[]{:S(2)}) collective-permute-start(bf16[3,4,2048]{2,1,0:T(4,128)(2,1)S(1)} %pad_maximum_fusion.packed.refs_0_), channel_id=1, source_target_pairs={{0,24},{8,16},{16,8},{24,0},{1,25},{9,17},{17,9},{25,1},{2,26},{10... | collective-permute-start | bytes 147464 | tf_op jit(solution)/shard_map/ppermute | solution.py:22
  5.4 0.5 %collective-permute-start.1 = (bf16[3,4,2048]{2,1,0:T(4,128)(2,1)S(1)}, bf16[3,4,2048]{2,1,0:T(4,128)(2,1)S(1)}, u32[]{:S(2)}, u32[]{:S(2)}) collective-permute-start(bf16[3,4,2048]{2,1,0:T(4,128)(2,1)S(1)} %pad_maximum_fusion.packed.refs_0_), channel_id=1, source_target_pairs={{0,16},{8,24},{16,0},{24,8},{1,17},{9,25},{17,1},{25,9},{2,18},{10... | collective-permute-start | bytes 147464 | tf_op jit(solution)/shard_map/ppermute | solution.py:22
  5.9 0.1 collective-permute-start
  6.1 0.1 inner_products.1.refs_5_
  6.2 0.0 collective-permute-start.3
  6.2 1.3 %collective-permute-done.2.refs_3_ = bf16[3,4,2048]{2,1,0:T(4,128)(2,1)S(1)} collective-permute-done((bf16[3,4,2048]{2,1,0:T(4,128)(2,1)S(1)}, bf16[3,4,2048]{2,1,0:T(4,128)(2,1)S(1)}, u32[]{:S(2)}, u32[]{:S(2)}) %collective-permute-start.2) | collective-permute-done | bytes 49184 | tf_op jit(solution)/shard_map/ppermute | solution.py:22
  7.5 0.0 collective-permute-start.6
  7.5 2.0 %collective-permute-done.1.refs_2_ = bf16[3,4,2048]{2,1,0:T(4,128)(2,1)S(1)} collective-permute-done((bf16[3,4,2048]{2,1,0:T(4,128)(2,1)S(1)}, bf16[3,4,2048]{2,1,0:T(4,128)(2,1)S(1)}, u32[]{:S(2)}, u32[]{:S(2)}) %collective-permute-start.1) | collective-permute-done | bytes 49184 | tf_op jit(solution)/shard_map/ppermute | solution.py:22
  9.5 0.0 collective-permute-start.5
  9.5 0.5 %collective-permute-done.refs_1_ = bf16[3,4,2048]{2,1,0:T(4,128)(2,1)S(1)} collective-permute-done((bf16[3,4,2048]{2,1,0:T(4,128)(2,1)S(1)}, bf16[3,4,2048]{2,1,0:T(4,128)(2,1)S(1)}, u32[]{:S(2)}, u32[]{:S(2)}) %collective-permute-start) | collective-permute-done | bytes 49184 | tf_op jit(solution)/shard_map/ppermute | solution.py:22
  10.0 0.0 collective-permute-start.4
  10.0 0.7 %collective-permute-done.5.refs_6_ = bf16[3,4,2048]{2,1,0:T(4,128)(2,1)S(1)} collective-permute-done((bf16[3,4,2048]{2,1,0:T(4,128)(2,1)S(1)}, bf16[3,4,2048]{2,1,0:T(4,128)(2,1)S(1)}, u32[]{:S(2)}, u32[]{:S(2)}) %collective-permute-start.5) | collective-permute-done | bytes 49184 | tf_op jit(solution)/shard_map/ppermute | solution.py:22
  10.7 0.5 %collective-permute-done.4.refs_5_ = bf16[3,4,2048]{2,1,0:T(4,128)(2,1)S(1)} collective-permute-done((bf16[3,4,2048]{2,1,0:T(4,128)(2,1)S(1)}, bf16[3,4,2048]{2,1,0:T(4,128)(2,1)S(1)}, u32[]{:S(2)}, u32[]{:S(2)}) %collective-permute-start.4) | collective-permute-done | bytes 49184 | tf_op jit(solution)/shard_map/ppermute | solution.py:22
  11.2 1.1 %products.1 = (f32[96,128]{1,0:T(8,128)S(1)}, f32[96,128]{1,0:T(8,128)S(1)}, f32[96,128]{1,0:T(8,128)S(1)}, f32[96,128]{1,0:T(8,128)S(1)}) custom-call(bf16[3,4,2048]{2,1,0:T(4,128)(2,1)S(1)} %pad_maximum_fusion.packed.refs_0_, bf16[3,4,2048]{2,1,0:T(4,128)(2,1)S(1)} %collective-permute-done.refs_1_, bf16[3,4,2048]{2,1,0:T(4,128)(2,1)S(1)} %collective-permute-done.1.refs_2_, ...), custom_call_target="tpu_custom_call" | custom-call | tf_op jit(solution)/shard_map/products/pallas_call | solution.py:136
  12.4 3.7 %collective-permute-start.7 = (f32[96,128]{1,0:T(8,128)S(1)}, f32[96,128]{1,0:T(8,128)S(1)}, u32[]{:S(2)}, u32[]{:S(2)}) collective-permute-start(f32[96,128]{1,0:T(8,128)S(1)} %get-tuple-element.10), channel_id=1, source_target_pairs={{0,3},{1,2},{2,1},{3,0},{4,7},{5,6},{6,5},{7,4},{8,11},{9,10},{10,... | collective-permute-start | bytes 147464 | tf_op jit(solution)/shard_map/ppermute | solution.py:22
  16.1 0.8 %collective-permute-start.9 = (f32[96,128]{1,0:T(8,128)S(1)}, f32[96,128]{1,0:T(8,128)S(1)}, u32[]{:S(2)}, u32[]{:S(2)}) collective-permute-start(f32[96,128]{1,0:T(8,128)S(1)} %get-tuple-element.12), channel_id=1, source_target_pairs={{0,1},{1,0},{2,3},{3,2},{4,5},{5,4},{6,7},{7,6},{8,9},{9,8},{10,11... | collective-permute-start | bytes 147464 | tf_op jit(solution)/shard_map/ppermute | solution.py:22
  16.8 1.6 %collective-permute-done.7.refs_1_ = f32[96,128]{1,0:T(8,128)S(1)} collective-permute-done((f32[96,128]{1,0:T(8,128)S(1)}, f32[96,128]{1,0:T(8,128)S(1)}, u32[]{:S(2)}, u32[]{:S(2)}) %collective-permute-start.7) | collective-permute-done | bytes 49184 | tf_op jit(solution)/shard_map/ppermute | solution.py:22
  18.4 2.6 %collective-permute-done.8.refs_2_ = f32[96,128]{1,0:T(8,128)S(1)} collective-permute-done((f32[96,128]{1,0:T(8,128)S(1)}, f32[96,128]{1,0:T(8,128)S(1)}, u32[]{:S(2)}, u32[]{:S(2)}) %collective-permute-start.8) | collective-permute-done | bytes 49184 | tf_op jit(solution)/shard_map/ppermute | solution.py:22
  21.1 0.1 attributions.1
  21.2 10.5 %all_to_all.5.arrived = f32[32,2,128]{2,1,0:T(2,128)S(1)} all-to-all(f32[32,2,128]{2,1,0:T(2,128)S(1)} %attributions.1), channel_id=1, replica_groups={{31,30,29,28,27,26,25,24,23,22,21,20,19,18,17,16,15,14,13,12,11,10,9,8,..., dimensions={0} | all-to-all | bytes 65536 | tf_op jit(solution)/shard_map/all_to_all | solution.py:257
  31.7 0.6 %final.1 = (f32[512]{0:T(512)}, f32[4]{0:T(128)}) custom-call(f32[32,2,128]{2,1,0:T(2,128)S(1)} %all_to_all.5.arrived), custom_call_target="tpu_custom_call" | custom-call | tf_op jit(solution)/shard_map/final/pallas_call | solution.py:218
  (8 shorter events, 0.0 us)
Async XLA Ops:
  1.4 9.8 %copy-start = (bf16[2048,512]{1,0:T(8,128)(2,1)S(1)}, bf16[2048,512]{1,0:T(8,128)(2,1)}, u32[]{:S(2)}) copy-start(bf16[2048,512]{1,0:T(8,128)(2,1)} %refs_8_.1) | copy-start | bytes 6291460
  1.4 9.8 %copy-start.1 = (bf16[512,2048]{1,0:T(8,128)(2,1)S(1)}, bf16[512,2048]{1,0:T(8,128)(2,1)}, u32[]{:S(2)}) copy-start(bf16[512,2048]{1,0:T(8,128)(2,1)} %refs_9_.1) | copy-start | bytes 6291460
  1.4 6.0 %collective-permute-start.2 = (bf16[3,4,2048]{2,1,0:T(4,128)(2,1)S(1)}, bf16[3,4,2048]{2,1,0:T(4,128)(2,1)S(1)}, u32[]{:S(2)}, u32[]{:S(2)}) collective-permute-start(bf16[3,4,2048]{2,1,0:T(4,128)(2,1)S(1)} %pad_maximum_fusion.packed.refs_0_), channel_id=1, source_target_pairs={{0,24},{8,16},{16,8},{24,0},{1,25},{9,17},{17,9},{25,1},{2,26},{10... | collective-permute-start | bytes 147464 | tf_op jit(solution)/shard_map/ppermute | solution.py:22
  5.4 4.1 %collective-permute-start.1 = (bf16[3,4,2048]{2,1,0:T(4,128)(2,1)S(1)}, bf16[3,4,2048]{2,1,0:T(4,128)(2,1)S(1)}, u32[]{:S(2)}, u32[]{:S(2)}) collective-permute-start(bf16[3,4,2048]{2,1,0:T(4,128)(2,1)S(1)} %pad_maximum_fusion.packed.refs_0_), channel_id=1, source_target_pairs={{0,16},{8,24},{16,0},{24,8},{1,17},{9,25},{17,1},{25,9},{2,18},{10... | collective-permute-start | bytes 147464 | tf_op jit(solution)/shard_map/ppermute | solution.py:22
  5.9 4.1 %collective-permute-start = (bf16[3,4,2048]{2,1,0:T(4,128)(2,1)S(1)}, bf16[3,4,2048]{2,1,0:T(4,128)(2,1)S(1)}, u32[]{:S(2)}, u32[]{:S(2)}) collective-permute-start(bf16[3,4,2048]{2,1,0:T(4,128)(2,1)S(1)} %pad_maximum_fusion.packed.refs_0_), channel_id=1, source_target_pairs={{0,8},{8,0},{16,24},{24,16},{1,9},{9,1},{17,25},{25,17},{2,10},{10... | collective-permute-start | bytes 147464 | tf_op jit(solution)/shard_map/ppermute | solution.py:22
  6.2 14.9 %copy-start.2 = (f32[512]{0:T(512)S(1)}, f32[512]{0:T(512)}, u32[]{:S(2)}) copy-start(f32[512]{0:T(512)} %param.10) | copy-start | bytes 6148
  6.2 3.9 %collective-permute-start.3 = (bf16[3,4,2048]{2,1,0:T(4,128)(2,1)S(1)}, bf16[3,4,2048]{2,1,0:T(4,128)(2,1)S(1)}, u32[]{:S(2)}, u32[]{:S(2)}) collective-permute-start(bf16[3,4,2048]{2,1,0:T(4,128)(2,1)S(1)} %pad_maximum_fusion.packed.refs_0_), channel_id=1, source_target_pairs={{0,4},{4,0},{1,5},{5,1},{2,6},{6,2},{3,7},{7,3},{8,12},{12,8},{9,1... | collective-permute-start | bytes 147464 | tf_op jit(solution)/shard_map/ppermute | solution.py:22
  7.5 2.5 %collective-permute-start.6 = (bf16[3,4,2048]{2,1,0:T(4,128)(2,1)S(1)}, bf16[3,4,2048]{2,1,0:T(4,128)(2,1)S(1)}, u32[]{:S(2)}, u32[]{:S(2)}) collective-permute-start(bf16[3,4,2048]{2,1,0:T(4,128)(2,1)S(1)} %collective-permute-done.2.refs_3_), channel_id=1, source_target_pairs={{0,4},{4,0},{1,5},{5,1},{2,6},{6,2},{3,7},{7,3},{8,12},{12,8},{9,1... | collective-permute-start | bytes 147464 | tf_op jit(solution)/shard_map/ppermute | solution.py:22
  9.5 1.2 %collective-permute-start.5 = (bf16[3,4,2048]{2,1,0:T(4,128)(2,1)S(1)}, bf16[3,4,2048]{2,1,0:T(4,128)(2,1)S(1)}, u32[]{:S(2)}, u32[]{:S(2)}) collective-permute-start(bf16[3,4,2048]{2,1,0:T(4,128)(2,1)S(1)} %collective-permute-done.1.refs_2_), channel_id=1, source_target_pairs={{0,4},{4,0},{1,5},{5,1},{2,6},{6,2},{3,7},{7,3},{8,12},{12,8},{9,1... | collective-permute-start | bytes 147464 | tf_op jit(solution)/shard_map/ppermute | solution.py:22
  10.0 1.2 %collective-permute-start.4 = (bf16[3,4,2048]{2,1,0:T(4,128)(2,1)S(1)}, bf16[3,4,2048]{2,1,0:T(4,128)(2,1)S(1)}, u32[]{:S(2)}, u32[]{:S(2)}) collective-permute-start(bf16[3,4,2048]{2,1,0:T(4,128)(2,1)S(1)} %collective-permute-done.refs_1_), channel_id=1, source_target_pairs={{0,4},{4,0},{1,5},{5,1},{2,6},{6,2},{3,7},{7,3},{8,12},{12,8},{9,1... | collective-permute-start | bytes 147464 | tf_op jit(solution)/shard_map/ppermute | solution.py:22
  12.4 6.0 %collective-permute-start.7 = (f32[96,128]{1,0:T(8,128)S(1)}, f32[96,128]{1,0:T(8,128)S(1)}, u32[]{:S(2)}, u32[]{:S(2)}) collective-permute-start(f32[96,128]{1,0:T(8,128)S(1)} %get-tuple-element.10), channel_id=1, source_target_pairs={{0,3},{1,2},{2,1},{3,0},{4,7},{5,6},{6,5},{7,4},{8,11},{9,10},{10,... | collective-permute-start | bytes 147464 | tf_op jit(solution)/shard_map/ppermute | solution.py:22
  16.1 5.0 %collective-permute-start.8 = (f32[96,128]{1,0:T(8,128)S(1)}, f32[96,128]{1,0:T(8,128)S(1)}, u32[]{:S(2)}, u32[]{:S(2)}) collective-permute-start(f32[96,128]{1,0:T(8,128)S(1)} %get-tuple-element.11), channel_id=1, source_target_pairs={{0,2},{1,3},{2,0},{3,1},{4,6},{5,7},{6,4},{7,5},{8,10},{9,11},{10,... | collective-permute-start | bytes 147464 | tf_op jit(solution)/shard_map/ppermute | solution.py:22
  16.1 5.0 %collective-permute-start.9 = (f32[96,128]{1,0:T(8,128)S(1)}, f32[96,128]{1,0:T(8,128)S(1)}, u32[]{:S(2)}, u32[]{:S(2)}) collective-permute-start(f32[96,128]{1,0:T(8,128)S(1)} %get-tuple-element.12), channel_id=1, source_target_pairs={{0,1},{1,0},{2,3},{3,2},{4,5},{5,4},{6,7},{7,6},{8,9},{9,8},{10,11... | collective-permute-start | bytes 147464 | tf_op jit(solution)/shard_map/ppermute | solution.py:22

commit v10 on v8

--- a/solution.py
+++ b/solution.py
@@ -16,6 +16,11 @@
 
 def far_first(size):
     return [0, *reversed(range(1, size))]
+
+
+def row_blocks(sections, feats):
+    places = [(p, q) for p in range(feats) for q in range(sections)]
+    return sorted(places, key=lambda place: (place[0] > 0 and place[1] != 1, place[1], place[0]))
 
 
 def exchange(value, axis, size, k):
@@ -173,15 +178,13 @@
     token_part = jnp.sum(attribution, axis=1, keepdims=True)
     lane = lax.broadcasted_iota(jnp.int32, (tokens, LANES), 1)
     place = lane == lax.broadcasted_iota(jnp.int32, (tokens, LANES), 0)
-    for p in range(feats):
-        for q in range(sections):
-            k = p * sections + q
-            column = jnp.broadcast_to(token_part[k * tokens : (k + 1) * tokens], (tokens, LANES))
-            if k == 0:
-                column = column - inner[pl.ds(0, tokens), :]
-            row = jnp.sum(jnp.where(place, column, 0.0), axis=0, keepdims=True)
-            owner = (section ^ q) * feats + (feat ^ p)
-            sums[pl.ds(owner * parts, parts), 1, :] = jnp.broadcast_to(row, (parts, LANES))
+    for k, (p, q) in enumerate(row_blocks(sections, feats)):
+        column = jnp.broadcast_to(token_part[k * tokens : (k + 1) * tokens], (tokens, LANES))
+        if k == 0:
+            column = column - inner[pl.ds(0, tokens), :]
+        row = jnp.sum(jnp.where(place, column, 0.0), axis=0, keepdims=True)
+        owner = (section ^ q) * feats + (feat ^ p)
+        sums[pl.ds(owner * parts, parts), 1, :] = jnp.broadcast_to(row, (parts, LANES))
 
 
 def attributions(sizes, terms, bias, inner):
@@ -239,16 +242,23 @@
     features = enc_weight.shape[1]
 
     packed = jnp.stack([clean_resid, corrupt_resid, metric_grad])
-    near = [packed] + [exchange(packed, "section", sections, q) for q in range(1, sections)]
     inner = inner_products(packed)
     bias = enc_bias.reshape(parts, features // parts)
-    far = []
-    for p in range(1, feats):
-        for block in near:
-            if block is packed:
+    held = {(0, 0): packed}
+    for p, q in row_blocks(sections, feats):
+        if q > 0 and (p == 0 or q == 1):
+            pairs = [
+                (s * feats + f, (s ^ q) * feats + (f ^ p))
+                for s in range(sections)
+                for f in range(feats)
+            ]
+            held[p, q] = lax.ppermute(packed, ("section", "feat"), pairs)
+        elif p > 0:
+            block = held[0, q]
+            if q == 0:
                 block, inner = lax.optimization_barrier((block, inner))
-            far.append(exchange(block, "feat", feats, p))
-    blocks = near + far
+            held[p, q] = exchange(block, "feat", feats, p)
+    blocks = [held[place] for place in row_blocks(sections, feats)]
 
     terms = products(parts, blocks, enc_weight, dec_weight)
     arrived = [exchange(terms[m], "tensor", parts, m) for m in far_first(parts)[1:]]

time: 32.7 us -> 32.2 us (0.985)
  waiting for transfers between devices: 9.26 us -> 6.97 us
  starting transfers between devices: 9.07 us -> 10.9 us
    ppermute x0 -> x4, starting transfers between devices: none -> 5.37 us  [per_device(): held[p, q] = lax.ppermute(packed, ('section', 'feat'), pairs)]
    ppermute x10 -> x6, waiting for transfers between devices: 9.26 us -> 4.46 us  [exchange(): return lax.ppermute(value, axis, [(i, i ^ k) for i in range(size)])]
    ppermute x10 -> x6, starting transfers between devices: 9.07 us -> 5.5 us  [exchange(): return lax.ppermute(value, axis, [(i, i ^ k) for i in range(size)])]
    ppermute x0 -> x4, waiting for transfers between devices: none -> 2.51 us  [per_device(): held[p, q] = lax.ppermute(packed, ('section', 'feat'), pairs)]
  transfers between devices with their start and end apart: 10 -> 10, of which waited for: 7 -> 5; matrix products, arithmetic and copies ran while one was open for 0% -> 0% of each run, Pallas kernels for 0% -> 0%
where the time goes in v10:
time: 32.2 us; the launch traced here: 31.9 us
  starting transfers between devices  10.9 us (34%)
  blocking collectives  10.7 us (33%)
  waiting for transfers between devices  6.97 us (22%)
  Pallas kernels  1.95 us (6%)
  other arithmetic  0.79 us (2%)
  between operations  0.68 us (2%)
    all_to_all x1, blocking collectives, per_device(): return tuple(final(sizes, tokens, lax.all_to_all(sums, EVERY, 0, 0)))  10.7 us
    ppermute x6, starting transfers between devices, exchange(): return lax.ppermute(value, axis, [(i, i ^ k) for i in range(size)])  5.5 us
    ppermute x4, starting transfers between devices, per_device(): held[p, q] = lax.ppermute(packed, ('section', 'feat'), pairs)  5.37 us
    ppermute x6, waiting for transfers between devices, exchange(): return lax.ppermute(value, axis, [(i, i ^ k) for i in range(size)])  4.46 us
    ppermute x4, waiting for transfers between devices, per_device(): held[p, q] = lax.ppermute(packed, ('section', 'feat'), pairs)  2.51 us
    pallas_call x1, Pallas kernels, products(): pl.pallas_call(functools.partial(product_kernel, groups, parts), out_shap...  1.14 us
    another operation x1, other arithmetic, per_device(): packed = jnp.stack([clean_resid, corrupt_resid, metric_grad])  0.79 us
  transfers between devices with their start and end apart: 10, of which 5 were waited for; matrix products, arithmetic and copies ran while one was open for 0% of the time, Pallas kernels for 0%

profile of v10, /device:TPU:0, one launch (start us, length us, event | category | flops | bytes accessed | tf_op | source)
XLA Modules:
  0.0 31.9 jit_solution(4761795464221554701)
XLA Ops:
  0.6 0.8 %pad_maximum_fusion.packed.refs_0_ = bf16[3,4,2048]{2,1,0:T(4,128)(2,1)S(1)} fusion(bf16[1,4,2048]{2,1,0:T(4,128)(2,1)} %bitcast.5, bf16[1,4,2048]{2,1,0:T(4,128)(2,1)} %bitcast.6, bf16[1,4,2048]{2,1,0:T(4,128)(2,1)} %bitcast.7), kind=kLoop, calls=%fused_computation | loop fusion | flops 49152 | bytes 98304 | tf_op jit(solution)/shard_map/stack | solution.py:244
  1.4 0.0 copy-start
  1.4 0.0 copy-start.1
  1.4 4.0 %collective-permute-start.3 = (bf16[3,4,2048]{2,1,0:T(4,128)(2,1)S(1)}, bf16[3,4,2048]{2,1,0:T(4,128)(2,1)S(1)}, u32[]{:S(2)}, u32[]{:S(2)}) collective-permute-start(bf16[3,4,2048]{2,1,0:T(4,128)(2,1)S(1)} %pad_maximum_fusion.packed.refs_0_), channel_id=1, source_target_pairs={{0,24},{4,28},{8,16},{12,20},{16,8},{20,12},{24,0},{28,4},{1,25},{... | collective-permute-start | bytes 147464 | tf_op jit(solution)/shard_map/ppermute | solution.py:255
  5.4 0.5 %collective-permute-start.2 = (bf16[3,4,2048]{2,1,0:T(4,128)(2,1)S(1)}, bf16[3,4,2048]{2,1,0:T(4,128)(2,1)S(1)}, u32[]{:S(2)}, u32[]{:S(2)}) collective-permute-start(bf16[3,4,2048]{2,1,0:T(4,128)(2,1)S(1)} %pad_maximum_fusion.packed.refs_0_), channel_id=1, source_target_pairs={{0,16},{4,20},{8,24},{12,28},{16,0},{20,4},{24,8},{28,12},{1,17},{... | collective-permute-start | bytes 147464 | tf_op jit(solution)/shard_map/ppermute | solution.py:255
  5.9 0.0 collective-permute-start.1
  5.9 0.9 %collective-permute-start = (bf16[3,4,2048]{2,1,0:T(4,128)(2,1)S(1)}, bf16[3,4,2048]{2,1,0:T(4,128)(2,1)S(1)}, u32[]{:S(2)}, u32[]{:S(2)}) collective-permute-start(bf16[3,4,2048]{2,1,0:T(4,128)(2,1)S(1)} %pad_maximum_fusion.packed.refs_0_), channel_id=1, source_target_pairs={{0,8},{4,12},{8,0},{12,4},{16,24},{20,28},{24,16},{28,20},{1,9},{5... | collective-permute-start | bytes 147464 | tf_op jit(solution)/shard_map/ppermute | solution.py:255
  6.8 0.1 inner_products.1.refs_5_
  6.9 1.0 %collective-permute-start.4 = (bf16[3,4,2048]{2,1,0:T(4,128)(2,1)S(1)}, bf16[3,4,2048]{2,1,0:T(4,128)(2,1)S(1)}, u32[]{:S(2)}, u32[]{:S(2)}) collective-permute-start(bf16[3,4,2048]{2,1,0:T(4,128)(2,1)S(1)} %pad_maximum_fusion.packed.refs_0_), channel_id=1, source_target_pairs={{0,4},{4,0},{1,5},{5,1},{2,6},{6,2},{3,7},{7,3},{8,12},{12,8},{9,1... | collective-permute-start | bytes 147464 | tf_op jit(solution)/shard_map/ppermute | solution.py:27
  7.9 0.0 collective-permute-done.3.refs_4_
  7.9 0.1 collective-permute-start.6
  8.0 1.5 %collective-permute-done.2.refs_3_ = bf16[3,4,2048]{2,1,0:T(4,128)(2,1)S(1)} collective-permute-done((bf16[3,4,2048]{2,1,0:T(4,128)(2,1)S(1)}, bf16[3,4,2048]{2,1,0:T(4,128)(2,1)S(1)}, u32[]{:S(2)}, u32[]{:S(2)}) %collective-permute-start.2) | collective-permute-done | bytes 49184 | tf_op jit(solution)/shard_map/ppermute | solution.py:255
  9.5 1.0 %collective-permute-done.refs_1_ = bf16[3,4,2048]{2,1,0:T(4,128)(2,1)S(1)} collective-permute-done((bf16[3,4,2048]{2,1,0:T(4,128)(2,1)S(1)}, bf16[3,4,2048]{2,1,0:T(4,128)(2,1)S(1)}, u32[]{:S(2)}, u32[]{:S(2)}) %collective-permute-start) | collective-permute-done | bytes 49184 | tf_op jit(solution)/shard_map/ppermute | solution.py:255
  10.5 0.0 collective-permute-done.6.refs_7_
  10.5 0.2 collective-permute-done.5.refs_6_
  10.7 1.1 %products.1 = (f32[96,128]{1,0:T(8,128)S(1)}, f32[96,128]{1,0:T(8,128)S(1)}, f32[96,128]{1,0:T(8,128)S(1)}, f32[96,128]{1,0:T(8,128)S(1)}) custom-call(bf16[3,4,2048]{2,1,0:T(4,128)(2,1)S(1)} %pad_maximum_fusion.packed.refs_0_, bf16[3,4,2048]{2,1,0:T(4,128)(2,1)S(1)} %collective-permute-done.refs_1_, bf16[3,4,2048]{2,1,0:T(4,128)(2,1)S(1)} %collective-permute-done.1.refs_2_, ...), custom_call_target="tpu_custom_call" | custom-call | tf_op jit(solution)/shard_map/products/pallas_call | solution.py:141
  11.9 3.7 %collective-permute-start.7 = (f32[96,128]{1,0:T(8,128)S(1)}, f32[96,128]{1,0:T(8,128)S(1)}, u32[]{:S(2)}, u32[]{:S(2)}) collective-permute-start(f32[96,128]{1,0:T(8,128)S(1)} %get-tuple-element.10), channel_id=1, source_target_pairs={{0,3},{1,2},{2,1},{3,0},{4,7},{5,6},{6,5},{7,4},{8,11},{9,10},{10,... | collective-permute-start | bytes 147464 | tf_op jit(solution)/shard_map/ppermute | solution.py:27
  15.6 0.8 %collective-permute-start.9 = (f32[96,128]{1,0:T(8,128)S(1)}, f32[96,128]{1,0:T(8,128)S(1)}, u32[]{:S(2)}, u32[]{:S(2)}) collective-permute-start(f32[96,128]{1,0:T(8,128)S(1)} %get-tuple-element.12), channel_id=1, source_target_pairs={{0,1},{1,0},{2,3},{3,2},{4,5},{5,4},{6,7},{7,6},{8,9},{9,8},{10,11... | collective-permute-start | bytes 147464 | tf_op jit(solution)/shard_map/ppermute | solution.py:27
  16.3 1.6 %collective-permute-done.7.refs_1_ = f32[96,128]{1,0:T(8,128)S(1)} collective-permute-done((f32[96,128]{1,0:T(8,128)S(1)}, f32[96,128]{1,0:T(8,128)S(1)}, u32[]{:S(2)}, u32[]{:S(2)}) %collective-permute-start.7) | collective-permute-done | bytes 49184 | tf_op jit(solution)/shard_map/ppermute | solution.py:27
  17.9 2.7 %collective-permute-done.8.refs_2_ = f32[96,128]{1,0:T(8,128)S(1)} collective-permute-done((f32[96,128]{1,0:T(8,128)S(1)}, f32[96,128]{1,0:T(8,128)S(1)}, u32[]{:S(2)}, u32[]{:S(2)}) %collective-permute-start.8) | collective-permute-done | bytes 49184 | tf_op jit(solution)/shard_map/ppermute | solution.py:27
  20.5 0.0 collective-permute-done.9.refs_3_
  20.5 0.1 attributions.1
  20.7 10.7 %all_to_all.5.arrived = f32[32,2,128]{2,1,0:T(2,128)S(1)} all-to-all(f32[32,2,128]{2,1,0:T(2,128)S(1)} %attributions.1), channel_id=1, replica_groups=mesh['section'=4,'feat'=2,'tensor'=4] {'section','feat','tensor'}, dimensions={0} | all-to-all | bytes 65536 | tf_op jit(solution)/shard_map/all_to_all | solution.py:266
  31.3 0.6 %final.1 = (f32[512]{0:T(512)}, f32[4]{0:T(128)}) custom-call(f32[32,2,128]{2,1,0:T(2,128)S(1)} %all_to_all.5.arrived), custom_call_target="tpu_custom_call" | custom-call | tf_op jit(solution)/shard_map/final/pallas_call | solution.py:221
  (8 shorter events, 0.0 us)
Async XLA Ops:
  1.4 9.3 %copy-start = (bf16[2048,512]{1,0:T(8,128)(2,1)S(1)}, bf16[2048,512]{1,0:T(8,128)(2,1)}, u32[]{:S(2)}) copy-start(bf16[2048,512]{1,0:T(8,128)(2,1)} %refs_8_.1) | copy-start | bytes 6291460
  1.4 9.3 %copy-start.1 = (bf16[512,2048]{1,0:T(8,128)(2,1)S(1)}, bf16[512,2048]{1,0:T(8,128)(2,1)}, u32[]{:S(2)}) copy-start(bf16[512,2048]{1,0:T(8,128)(2,1)} %refs_9_.1) | copy-start | bytes 6291460
  1.4 6.4 %collective-permute-start.3 = (bf16[3,4,2048]{2,1,0:T(4,128)(2,1)S(1)}, bf16[3,4,2048]{2,1,0:T(4,128)(2,1)S(1)}, u32[]{:S(2)}, u32[]{:S(2)}) collective-permute-start(bf16[3,4,2048]{2,1,0:T(4,128)(2,1)S(1)} %pad_maximum_fusion.packed.refs_0_), channel_id=1, source_target_pairs={{0,24},{4,28},{8,16},{12,20},{16,8},{20,12},{24,0},{28,4},{1,25},{... | collective-permute-start | bytes 147464 | tf_op jit(solution)/shard_map/ppermute | solution.py:255
  5.4 4.1 %collective-permute-start.2 = (bf16[3,4,2048]{2,1,0:T(4,128)(2,1)S(1)}, bf16[3,4,2048]{2,1,0:T(4,128)(2,1)S(1)}, u32[]{:S(2)}, u32[]{:S(2)}) collective-permute-start(bf16[3,4,2048]{2,1,0:T(4,128)(2,1)S(1)} %pad_maximum_fusion.packed.refs_0_), channel_id=1, source_target_pairs={{0,16},{4,20},{8,24},{12,28},{16,0},{20,4},{24,8},{28,12},{1,17},{... | collective-permute-start | bytes 147464 | tf_op jit(solution)/shard_map/ppermute | solution.py:255
  5.9 3.6 %collective-permute-start.1 = (bf16[3,4,2048]{2,1,0:T(4,128)(2,1)S(1)}, bf16[3,4,2048]{2,1,0:T(4,128)(2,1)S(1)}, u32[]{:S(2)}, u32[]{:S(2)}) collective-permute-start(bf16[3,4,2048]{2,1,0:T(4,128)(2,1)S(1)} %pad_maximum_fusion.packed.refs_0_), channel_id=1, source_target_pairs={{0,12},{4,8},{8,4},{12,0},{16,28},{20,24},{24,20},{28,16},{1,13},{... | collective-permute-start | bytes 147464 | tf_op jit(solution)/shard_map/ppermute | solution.py:255
  5.9 4.6 %collective-permute-start = (bf16[3,4,2048]{2,1,0:T(4,128)(2,1)S(1)}, bf16[3,4,2048]{2,1,0:T(4,128)(2,1)S(1)}, u32[]{:S(2)}, u32[]{:S(2)}) collective-permute-start(bf16[3,4,2048]{2,1,0:T(4,128)(2,1)S(1)} %pad_maximum_fusion.packed.refs_0_), channel_id=1, source_target_pairs={{0,8},{4,12},{8,0},{12,4},{16,24},{20,28},{24,16},{28,20},{1,9},{5... | collective-permute-start | bytes 147464 | tf_op jit(solution)/shard_map/ppermute | solution.py:255
  6.9 13.6 %copy-start.2 = (f32[512]{0:T(512)S(1)}, f32[512]{0:T(512)}, u32[]{:S(2)}) copy-start(f32[512]{0:T(512)} %param.10) | copy-start | bytes 6148
  6.9 2.6 %collective-permute-start.4 = (bf16[3,4,2048]{2,1,0:T(4,128)(2,1)S(1)}, bf16[3,4,2048]{2,1,0:T(4,128)(2,1)S(1)}, u32[]{:S(2)}, u32[]{:S(2)}) collective-permute-start(bf16[3,4,2048]{2,1,0:T(4,128)(2,1)S(1)} %pad_maximum_fusion.packed.refs_0_), channel_id=1, source_target_pairs={{0,4},{4,0},{1,5},{5,1},{2,6},{6,2},{3,7},{7,3},{8,12},{12,8},{9,1... | collective-permute-start | bytes 147464 | tf_op jit(solution)/shard_map/ppermute | solution.py:27
  7.9 2.6 %collective-permute-start.6 = (bf16[3,4,2048]{2,1,0:T(4,128)(2,1)S(1)}, bf16[3,4,2048]{2,1,0:T(4,128)(2,1)S(1)}, u32[]{:S(2)}, u32[]{:S(2)}) collective-permute-start(bf16[3,4,2048]{2,1,0:T(4,128)(2,1)S(1)} %collective-permute-done.3.refs_4_), channel_id=1, source_target_pairs={{0,4},{4,0},{1,5},{5,1},{2,6},{6,2},{3,7},{7,3},{8,12},{12,8},{9,1... | collective-permute-start | bytes 147464 | tf_op jit(solution)/shard_map/ppermute | solution.py:27
  9.5 1.2 %collective-permute-start.5 = (bf16[3,4,2048]{2,1,0:T(4,128)(2,1)S(1)}, bf16[3,4,2048]{2,1,0:T(4,128)(2,1)S(1)}, u32[]{:S(2)}, u32[]{:S(2)}) collective-permute-start(bf16[3,4,2048]{2,1,0:T(4,128)(2,1)S(1)} %collective-permute-done.2.refs_3_), channel_id=1, source_target_pairs={{0,4},{4,0},{1,5},{5,1},{2,6},{6,2},{3,7},{7,3},{8,12},{12,8},{9,1... | collective-permute-start | bytes 147464 | tf_op jit(solution)/shard_map/ppermute | solution.py:27
  11.9 6.0 %collective-permute-start.7 = (f32[96,128]{1,0:T(8,128)S(1)}, f32[96,128]{1,0:T(8,128)S(1)}, u32[]{:S(2)}, u32[]{:S(2)}) collective-permute-start(f32[96,128]{1,0:T(8,128)S(1)} %get-tuple-element.10), channel_id=1, source_target_pairs={{0,3},{1,2},{2,1},{3,0},{4,7},{5,6},{6,5},{7,4},{8,11},{9,10},{10,... | collective-permute-start | bytes 147464 | tf_op jit(solution)/shard_map/ppermute | solution.py:27
  15.6 5.0 %collective-permute-start.8 = (f32[96,128]{1,0:T(8,128)S(1)}, f32[96,128]{1,0:T(8,128)S(1)}, u32[]{:S(2)}, u32[]{:S(2)}) collective-permute-start(f32[96,128]{1,0:T(8,128)S(1)} %get-tuple-element.11), channel_id=1, source_target_pairs={{0,2},{1,3},{2,0},{3,1},{4,6},{5,7},{6,4},{7,5},{8,10},{9,11},{10,... | collective-permute-start | bytes 147464 | tf_op jit(solution)/shard_map/ppermute | solution.py:27
  15.6 5.0 %collective-permute-start.9 = (f32[96,128]{1,0:T(8,128)S(1)}, f32[96,128]{1,0:T(8,128)S(1)}, u32[]{:S(2)}, u32[]{:S(2)}) collective-permute-start(f32[96,128]{1,0:T(8,128)S(1)} %get-tuple-element.12), channel_id=1, source_target_pairs={{0,1},{1,0},{2,3},{3,2},{4,5},{5,4},{6,7},{7,6},{8,9},{9,8},{10,11... | collective-permute-start | bytes 147464 | tf_op jit(solution)/shard_map/ppermute | solution.py:27

commit v11 on v10

--- a/solution.py
+++ b/solution.py
@@ -9,13 +9,26 @@
 
 LANES = 128
 TILE = 8
+STEPS = 4
 
 
 EVERY = ("section", "feat", "tensor")
 
 
-def far_first(size):
-    return [0, *reversed(range(1, size))]
+def rotations(size):
+    return sorted(range(1, size), key=lambda r: (r != size // 2, r))
+
+
+def turned(index, r, size):
+    place = jnp.where(index % 2 == 0, index // 2, size - 1 - index // 2)
+    place = (place + r) % size
+    return jnp.where(place < size // 2, 2 * place, 2 * (size - 1 - place) + 1)
+
+
+def turn(value, axis, size, r):
+    ring = [*range(0, size, 2), *reversed(range(1, size, 2))]
+    pairs = [(ring[i], ring[(i + r) % size]) for i in range(size)]
+    return lax.ppermute(value, axis, pairs)
 
 
 def row_blocks(sections, feats):
@@ -108,27 +121,32 @@
     rows, held = refs[groups + 2 + parts :]
     tokens = blocks[0].shape[1]
     total = groups * tokens
-    share = LANES
-    for k, block in enumerate(blocks):
-        for a in range(3):
-            rows[pl.ds(a * total + k * tokens, tokens), :] = block[a].astype(jnp.float32)
-    encoded = jnp.dot(
-        rows[pl.ds(0, 2 * total), :].astype(jnp.bfloat16),
-        enc[...],
-        preferred_element_type=jnp.float32,
-    )
-    projected = lax.dot_general(
-        rows[pl.ds(2 * total, total), :].astype(jnp.bfloat16),
-        dec[...],
-        (((1,), (1,)), ((), ())),
-        preferred_element_type=jnp.float32,
-    )
+    steps, _, depth = rows.shape
+    encoded = projected = 0.0
+    for j in range(steps):
+        part = pl.ds(j * depth, depth)
+        for k, block in enumerate(blocks):
+            for a in range(3):
+                piece = block[a, :, part].astype(jnp.float32)
+                rows[j, pl.ds(a * total + k * tokens, tokens), :] = piece
+        encoded += jnp.dot(
+            rows[j, pl.ds(0, 2 * total), :].astype(jnp.bfloat16),
+            enc[part, :],
+            preferred_element_type=jnp.float32,
+        )
+        projected += lax.dot_general(
+            rows[j, pl.ds(2 * total, total), :].astype(jnp.bfloat16),
+            dec[:, part],
+            (((1,), (1,)), ((), ())),
+            preferred_element_type=jnp.float32,
+        )
     for c in range(parts):
-        held[c, pl.ds(0, 2 * total), :] = encoded[:, c * share : (c + 1) * share]
-        held[c, pl.ds(2 * total, total), :] = projected[:, c * share : (c + 1) * share]
+        held[c, pl.ds(0, 2 * total), :] = encoded[:, c * LANES : (c + 1) * LANES]
+        held[c, pl.ds(2 * total, total), :] = projected[:, c * LANES : (c + 1) * LANES]
     me = lax.axis_index("tensor")
-    for m, out in enumerate(outs):
-        out[...] = held[me ^ m]
+    outs[0][...] = held[me]
+    for r, out in zip(rotations(parts), outs[1:]):
+        out[...] = held[turned(me, r, parts)]
 
 
 def products(parts, blocks, enc_weight, dec_weight):
@@ -144,7 +162,7 @@
         in_specs=[vmem] * (groups + 2),
         out_specs=[vmem] * parts,
         scratch_shapes=[
-            pltpu.VMEM((rows, width), jnp.float32),
+            pltpu.VMEM((STEPS, rows, width // STEPS), jnp.float32),
             pltpu.VMEM((parts, rows, features // parts), jnp.float32),
         ],
         compiler_params=pltpu.CompilerParams(vmem_limit_bytes=48 * 2**20),
@@ -161,7 +179,7 @@
 def attribution_kernel(sizes, *refs):
     sections, feats, parts = sizes
     groups = sections * feats
-    terms = [refs[far_first(parts).index(m)] for m in range(parts)]
+    terms = refs[:parts]
     bias, inner, sums = refs[parts:]
     total = terms[0].shape[0] // 3
     tokens = total // groups
@@ -261,7 +279,7 @@
     blocks = [held[place] for place in row_blocks(sections, feats)]
 
     terms = products(parts, blocks, enc_weight, dec_weight)
-    arrived = [exchange(terms[m], "tensor", parts, m) for m in far_first(parts)[1:]]
+    arrived = [turn(term, "tensor", parts, r) for r, term in zip(rotations(parts), terms[1:])]
     sums = attributions(sizes, [terms[0]] + arrived, bias, inner)
     return tuple(final(sizes, tokens, lax.all_to_all(sums, EVERY, 0, 0)))
 

time: 32.2 us -> 32.8 us (1.019)
  waiting for transfers between devices: 6.97 us -> 5.72 us
  starting transfers between devices: 10.9 us -> 12.1 us
  blocking collectives: 10.7 us -> 11.2 us
    ppermute x0 -> x3, starting transfers between devices: none -> 5.69 us  [turn(): return lax.ppermute(value, axis, pairs)]
    ppermute x6 -> x3, starting transfers between devices: 5.5 us -> 1.04 us  [exchange(): return lax.ppermute(value, axis, [(i, i ^ k) for i in range(size)])]
    ppermute x6 -> x3, waiting for transfers between devices: 4.46 us -> 0.25 us  [exchange(): return lax.ppermute(value, axis, [(i, i ^ k) for i in range(size)])]
    ppermute x0 -> x3, waiting for transfers between devices: none -> 2.96 us  [turn(): return lax.ppermute(value, axis, pairs)]
    all_to_all x1, blocking collectives: 10.7 us -> 11.2 us  [per_device(): return tuple(final(sizes, tokens, lax.all_to_all(sums, EVERY, 0, 0)))]
  transfers between devices with their start and end apart: 10 -> 10, of which waited for: 5 -> 6; matrix products, arithmetic and copies ran while one was open for 0% -> 0% of each run, Pallas kernels for 0% -> 0%
where the time goes in v11:
time: 32.8 us; the launch traced here: 32.5 us
  starting transfers between devices  12.1 us (37%)
  blocking collectives  11.2 us (34%)
  waiting for transfers between devices  5.72 us (17%)
  Pallas kernels  1.96 us (6%)
  other arithmetic  0.79 us (2%)
  between operations  0.68 us (2%)
    all_to_all x1, blocking collectives, per_device(): return tuple(final(sizes, tokens, lax.all_to_all(sums, EVERY, 0, 0)))  11.2 us
    ppermute x3, starting transfers between devices, turn(): return lax.ppermute(value, axis, pairs)  5.69 us
    ppermute x4, starting transfers between devices, per_device(): held[p, q] = lax.ppermute(packed, ('section', 'feat'), pairs)  5.37 us
    ppermute x3, waiting for transfers between devices, turn(): return lax.ppermute(value, axis, pairs)  2.96 us
    ppermute x4, waiting for transfers between devices, per_device(): held[p, q] = lax.ppermute(packed, ('section', 'feat'), pairs)  2.51 us
    pallas_call x1, Pallas kernels, products(): pl.pallas_call(functools.partial(product_kernel, groups, parts), out_shap...  1.14 us
    ppermute x3, starting transfers between devices, exchange(): return lax.ppermute(value, axis, [(i, i ^ k) for i in range(size)])  1.04 us
    another operation x1, other arithmetic, per_device(): packed = jnp.stack([clean_resid, corrupt_resid, metric_grad])  0.79 us
  transfers between devices with their start and end apart: 10, of which 6 were waited for; matrix products, arithmetic and copies ran while one was open for 0% of the time, Pallas kernels for 0%

profile of v11, /device:TPU:0, one launch (start us, length us, event | category | flops | bytes accessed | tf_op | source)
XLA Modules:
  0.0 32.5 jit_solution(5035022135846815956)
XLA Ops:
  0.6 0.8 %pad_maximum_fusion.packed.refs_0_ = bf16[3,4,2048]{2,1,0:T(4,128)(2,1)S(1)} fusion(bf16[1,4,2048]{2,1,0:T(4,128)(2,1)} %bitcast.5, bf16[1,4,2048]{2,1,0:T(4,128)(2,1)} %bitcast.6, bf16[1,4,2048]{2,1,0:T(4,128)(2,1)} %bitcast.7), kind=kLoop, calls=%fused_computation | loop fusion | flops 49152 | bytes 98304 | tf_op jit(solution)/shard_map/stack | solution.py:262
  1.4 0.0 copy-start
  1.4 0.0 copy-start.1
  1.4 4.0 %collective-permute-start.3 = (bf16[3,4,2048]{2,1,0:T(4,128)(2,1)S(1)}, bf16[3,4,2048]{2,1,0:T(4,128)(2,1)S(1)}, u32[]{:S(2)}, u32[]{:S(2)}) collective-permute-start(bf16[3,4,2048]{2,1,0:T(4,128)(2,1)S(1)} %pad_maximum_fusion.packed.refs_0_), channel_id=1, source_target_pairs={{0,24},{4,28},{8,16},{12,20},{16,8},{20,12},{24,0},{28,4},{1,25},{... | collective-permute-start | bytes 147464 | tf_op jit(solution)/shard_map/ppermute | solution.py:273
  5.4 0.5 %collective-permute-start.2 = (bf16[3,4,2048]{2,1,0:T(4,128)(2,1)S(1)}, bf16[3,4,2048]{2,1,0:T(4,128)(2,1)S(1)}, u32[]{:S(2)}, u32[]{:S(2)}) collective-permute-start(bf16[3,4,2048]{2,1,0:T(4,128)(2,1)S(1)} %pad_maximum_fusion.packed.refs_0_), channel_id=1, source_target_pairs={{0,16},{4,20},{8,24},{12,28},{16,0},{20,4},{24,8},{28,12},{1,17},{... | collective-permute-start | bytes 147464 | tf_op jit(solution)/shard_map/ppermute | solution.py:273
  5.9 0.0 collective-permute-start.1
  5.9 0.9 %collective-permute-start = (bf16[3,4,2048]{2,1,0:T(4,128)(2,1)S(1)}, bf16[3,4,2048]{2,1,0:T(4,128)(2,1)S(1)}, u32[]{:S(2)}, u32[]{:S(2)}) collective-permute-start(bf16[3,4,2048]{2,1,0:T(4,128)(2,1)S(1)} %pad_maximum_fusion.packed.refs_0_), channel_id=1, source_target_pairs={{0,8},{4,12},{8,0},{12,4},{16,24},{20,28},{24,16},{28,20},{1,9},{5... | collective-permute-start | bytes 147464 | tf_op jit(solution)/shard_map/ppermute | solution.py:273
  6.8 0.1 inner_products.1.refs_5_
  6.9 1.0 %collective-permute-start.4 = (bf16[3,4,2048]{2,1,0:T(4,128)(2,1)S(1)}, bf16[3,4,2048]{2,1,0:T(4,128)(2,1)S(1)}, u32[]{:S(2)}, u32[]{:S(2)}) collective-permute-start(bf16[3,4,2048]{2,1,0:T(4,128)(2,1)S(1)} %pad_maximum_fusion.packed.refs_0_), channel_id=1, source_target_pairs={{0,4},{4,0},{1,5},{5,1},{2,6},{6,2},{3,7},{7,3},{8,12},{12,8},{9,1... | collective-permute-start | bytes 147464 | tf_op jit(solution)/shard_map/ppermute | solution.py:40
  7.9 0.1 collective-permute-start.6
  8.0 1.5 %collective-permute-done.2.refs_3_ = bf16[3,4,2048]{2,1,0:T(4,128)(2,1)S(1)} collective-permute-done((bf16[3,4,2048]{2,1,0:T(4,128)(2,1)S(1)}, bf16[3,4,2048]{2,1,0:T(4,128)(2,1)S(1)}, u32[]{:S(2)}, u32[]{:S(2)}) %collective-permute-start.2) | collective-permute-done | bytes 49184 | tf_op jit(solution)/shard_map/ppermute | solution.py:273
  9.5 1.0 %collective-permute-done.refs_1_ = bf16[3,4,2048]{2,1,0:T(4,128)(2,1)S(1)} collective-permute-done((bf16[3,4,2048]{2,1,0:T(4,128)(2,1)S(1)}, bf16[3,4,2048]{2,1,0:T(4,128)(2,1)S(1)}, u32[]{:S(2)}, u32[]{:S(2)}) %collective-permute-start) | collective-permute-done | bytes 49184 | tf_op jit(solution)/shard_map/ppermute | solution.py:273
  10.5 0.0 collective-permute-done.6.refs_7_
  10.5 0.2 collective-permute-done.5.refs_6_
  10.7 1.1 %products.1 = (f32[96,128]{1,0:T(8,128)S(1)}, f32[96,128]{1,0:T(8,128)S(1)}, f32[96,128]{1,0:T(8,128)S(1)}, f32[96,128]{1,0:T(8,128)S(1)}) custom-call(bf16[3,4,2048]{2,1,0:T(4,128)(2,1)S(1)} %pad_maximum_fusion.packed.refs_0_, bf16[3,4,2048]{2,1,0:T(4,128)(2,1)S(1)} %collective-permute-done.refs_1_, bf16[3,4,2048]{2,1,0:T(4,128)(2,1)S(1)} %collective-permute-done.1.refs_2_, ...), custom_call_target="tpu_custom_call" | custom-call | tf_op jit(solution)/shard_map/products/pallas_call | solution.py:159
  11.9 3.7 %collective-permute-start.7 = (f32[96,128]{1,0:T(8,128)S(1)}, f32[96,128]{1,0:T(8,128)S(1)}, u32[]{:S(2)}, u32[]{:S(2)}) collective-permute-start(f32[96,128]{1,0:T(8,128)S(1)} %get-tuple-element.10), channel_id=1, source_target_pairs={{0,3},{2,1},{3,0},{1,2},{4,7},{6,5},{7,4},{5,6},{8,11},{10,9},{11,... | collective-permute-start | bytes 147464 | tf_op jit(solution)/shard_map/ppermute | solution.py:31
  15.6 0.0 collective-permute-start.8
  15.6 2.0 %collective-permute-start.9 = (f32[96,128]{1,0:T(8,128)S(1)}, f32[96,128]{1,0:T(8,128)S(1)}, u32[]{:S(2)}, u32[]{:S(2)}) collective-permute-start(f32[96,128]{1,0:T(8,128)S(1)} %get-tuple-element.12), channel_id=1, source_target_pairs={{0,1},{2,0},{3,2},{1,3},{4,5},{6,4},{7,6},{5,7},{8,9},{10,8},{11,1... | collective-permute-start | bytes 147464 | tf_op jit(solution)/shard_map/ppermute | solution.py:31
  17.6 0.3 collective-permute-done.7.refs_1_
  17.9 1.8 %collective-permute-done.8.refs_2_ = f32[96,128]{1,0:T(8,128)S(1)} collective-permute-done((f32[96,128]{1,0:T(8,128)S(1)}, f32[96,128]{1,0:T(8,128)S(1)}, u32[]{:S(2)}, u32[]{:S(2)}) %collective-permute-start.8) | collective-permute-done | bytes 49184 | tf_op jit(solution)/shard_map/ppermute | solution.py:31
  19.7 0.9 %collective-permute-done.9.refs_3_ = f32[96,128]{1,0:T(8,128)S(1)} collective-permute-done((f32[96,128]{1,0:T(8,128)S(1)}, f32[96,128]{1,0:T(8,128)S(1)}, u32[]{:S(2)}, u32[]{:S(2)}) %collective-permute-start.9) | collective-permute-done | bytes 49184 | tf_op jit(solution)/shard_map/ppermute | solution.py:31
  20.5 0.1 attributions.1
  20.7 11.2 %all_to_all.5.arrived = f32[32,2,128]{2,1,0:T(2,128)S(1)} all-to-all(f32[32,2,128]{2,1,0:T(2,128)S(1)} %attributions.1), channel_id=1, replica_groups=mesh['section'=4,'feat'=2,'tensor'=4] {'section','feat','tensor'}, dimensions={0} | all-to-all | bytes 65536 | tf_op jit(solution)/shard_map/all_to_all | solution.py:284
  31.8 0.6 %final.1 = (f32[512]{0:T(512)}, f32[4]{0:T(128)}) custom-call(f32[32,2,128]{2,1,0:T(2,128)S(1)} %all_to_all.5.arrived), custom_call_target="tpu_custom_call" | custom-call | tf_op jit(solution)/shard_map/final/pallas_call | solution.py:239
  (8 shorter events, 0.0 us)
Async XLA Ops:
  1.4 9.3 %copy-start = (bf16[2048,512]{1,0:T(8,128)(2,1)S(1)}, bf16[2048,512]{1,0:T(8,128)(2,1)}, u32[]{:S(2)}) copy-start(bf16[2048,512]{1,0:T(8,128)(2,1)} %refs_8_.1) | copy-start | bytes 6291460
  1.4 9.3 %copy-start.1 = (bf16[512,2048]{1,0:T(8,128)(2,1)S(1)}, bf16[512,2048]{1,0:T(8,128)(2,1)}, u32[]{:S(2)}) copy-start(bf16[512,2048]{1,0:T(8,128)(2,1)} %refs_9_.1) | copy-start | bytes 6291460
  1.4 6.4 %collective-permute-start.3 = (bf16[3,4,2048]{2,1,0:T(4,128)(2,1)S(1)}, bf16[3,4,2048]{2,1,0:T(4,128)(2,1)S(1)}, u32[]{:S(2)}, u32[]{:S(2)}) collective-permute-start(bf16[3,4,2048]{2,1,0:T(4,128)(2,1)S(1)} %pad_maximum_fusion.packed.refs_0_), channel_id=1, source_target_pairs={{0,24},{4,28},{8,16},{12,20},{16,8},{20,12},{24,0},{28,4},{1,25},{... | collective-permute-start | bytes 147464 | tf_op jit(solution)/shard_map/ppermute | solution.py:273
  5.4 4.1 %collective-permute-start.2 = (bf16[3,4,2048]{2,1,0:T(4,128)(2,1)S(1)}, bf16[3,4,2048]{2,1,0:T(4,128)(2,1)S(1)}, u32[]{:S(2)}, u32[]{:S(2)}) collective-permute-start(bf16[3,4,2048]{2,1,0:T(4,128)(2,1)S(1)} %pad_maximum_fusion.packed.refs_0_), channel_id=1, source_target_pairs={{0,16},{4,20},{8,24},{12,28},{16,0},{20,4},{24,8},{28,12},{1,17},{... | collective-permute-start | bytes 147464 | tf_op jit(solution)/shard_map/ppermute | solution.py:273
  5.9 3.6 %collective-permute-start.1 = (bf16[3,4,2048]{2,1,0:T(4,128)(2,1)S(1)}, bf16[3,4,2048]{2,1,0:T(4,128)(2,1)S(1)}, u32[]{:S(2)}, u32[]{:S(2)}) collective-permute-start(bf16[3,4,2048]{2,1,0:T(4,128)(2,1)S(1)} %pad_maximum_fusion.packed.refs_0_), channel_id=1, source_target_pairs={{0,12},{4,8},{8,4},{12,0},{16,28},{20,24},{24,20},{28,16},{1,13},{... | collective-permute-start | bytes 147464 | tf_op jit(solution)/shard_map/ppermute | solution.py:273
  5.9 4.6 %collective-permute-start = (bf16[3,4,2048]{2,1,0:T(4,128)(2,1)S(1)}, bf16[3,4,2048]{2,1,0:T(4,128)(2,1)S(1)}, u32[]{:S(2)}, u32[]{:S(2)}) collective-permute-start(bf16[3,4,2048]{2,1,0:T(4,128)(2,1)S(1)} %pad_maximum_fusion.packed.refs_0_), channel_id=1, source_target_pairs={{0,8},{4,12},{8,0},{12,4},{16,24},{20,28},{24,16},{28,20},{1,9},{5... | collective-permute-start | bytes 147464 | tf_op jit(solution)/shard_map/ppermute | solution.py:273
  6.9 13.6 %copy-start.2 = (f32[512]{0:T(512)S(1)}, f32[512]{0:T(512)}, u32[]{:S(2)}) copy-start(f32[512]{0:T(512)} %param.10) | copy-start | bytes 6148
  6.9 2.6 %collective-permute-start.4 = (bf16[3,4,2048]{2,1,0:T(4,128)(2,1)S(1)}, bf16[3,4,2048]{2,1,0:T(4,128)(2,1)S(1)}, u32[]{:S(2)}, u32[]{:S(2)}) collective-permute-start(bf16[3,4,2048]{2,1,0:T(4,128)(2,1)S(1)} %pad_maximum_fusion.packed.refs_0_), channel_id=1, source_target_pairs={{0,4},{4,0},{1,5},{5,1},{2,6},{6,2},{3,7},{7,3},{8,12},{12,8},{9,1... | collective-permute-start | bytes 147464 | tf_op jit(solution)/shard_map/ppermute | solution.py:40
  7.9 2.6 %collective-permute-start.6 = (bf16[3,4,2048]{2,1,0:T(4,128)(2,1)S(1)}, bf16[3,4,2048]{2,1,0:T(4,128)(2,1)S(1)}, u32[]{:S(2)}, u32[]{:S(2)}) collective-permute-start(bf16[3,4,2048]{2,1,0:T(4,128)(2,1)S(1)} %collective-permute-done.3.refs_4_), channel_id=1, source_target_pairs={{0,4},{4,0},{1,5},{5,1},{2,6},{6,2},{3,7},{7,3},{8,12},{12,8},{9,1... | collective-permute-start | bytes 147464 | tf_op jit(solution)/shard_map/ppermute | solution.py:40
  9.5 1.2 %collective-permute-start.5 = (bf16[3,4,2048]{2,1,0:T(4,128)(2,1)S(1)}, bf16[3,4,2048]{2,1,0:T(4,128)(2,1)S(1)}, u32[]{:S(2)}, u32[]{:S(2)}) collective-permute-start(bf16[3,4,2048]{2,1,0:T(4,128)(2,1)S(1)} %collective-permute-done.2.refs_3_), channel_id=1, source_target_pairs={{0,4},{4,0},{1,5},{5,1},{2,6},{6,2},{3,7},{7,3},{8,12},{12,8},{9,1... | collective-permute-start | bytes 147464 | tf_op jit(solution)/shard_map/ppermute | solution.py:40
  11.9 6.0 %collective-permute-start.7 = (f32[96,128]{1,0:T(8,128)S(1)}, f32[96,128]{1,0:T(8,128)S(1)}, u32[]{:S(2)}, u32[]{:S(2)}) collective-permute-start(f32[96,128]{1,0:T(8,128)S(1)} %get-tuple-element.10), channel_id=1, source_target_pairs={{0,3},{2,1},{3,0},{1,2},{4,7},{6,5},{7,4},{5,6},{8,11},{10,9},{11,... | collective-permute-start | bytes 147464 | tf_op jit(solution)/shard_map/ppermute | solution.py:31
  15.6 4.1 %collective-permute-start.8 = (f32[96,128]{1,0:T(8,128)S(1)}, f32[96,128]{1,0:T(8,128)S(1)}, u32[]{:S(2)}, u32[]{:S(2)}) collective-permute-start(f32[96,128]{1,0:T(8,128)S(1)} %get-tuple-element.11), channel_id=1, source_target_pairs={{0,2},{2,3},{3,1},{1,0},{4,6},{6,7},{7,5},{5,4},{8,10},{10,11},{11... | collective-permute-start | bytes 147464 | tf_op jit(solution)/shard_map/ppermute | solution.py:31
  15.6 5.0 %collective-permute-start.9 = (f32[96,128]{1,0:T(8,128)S(1)}, f32[96,128]{1,0:T(8,128)S(1)}, u32[]{:S(2)}, u32[]{:S(2)}) collective-permute-start(f32[96,128]{1,0:T(8,128)S(1)} %get-tuple-element.12), channel_id=1, source_target_pairs={{0,1},{2,0},{3,2},{1,3},{4,5},{6,4},{7,6},{5,7},{8,9},{10,8},{11,1... | collective-permute-start | bytes 147464 | tf_op jit(solution)/shard_map/ppermute | solution.py:31

commit v12 on v10

--- a/solution.py
+++ b/solution.py
@@ -14,8 +14,12 @@
 EVERY = ("section", "feat", "tensor")
 
 
-def far_first(size):
-    return [0, *reversed(range(1, size))]
+def rotations(size):
+    return sorted(range(1, size), key=lambda r: (r != size // 2, r == 1, -r))
+
+
+def turn(value, axis, size, r):
+    return lax.ppermute(value, axis, [(i, (i + r) % size) for i in range(size)])
 
 
 def row_blocks(sections, feats):
@@ -127,8 +131,8 @@
         held[c, pl.ds(0, 2 * total), :] = encoded[:, c * share : (c + 1) * share]
         held[c, pl.ds(2 * total, total), :] = projected[:, c * share : (c + 1) * share]
     me = lax.axis_index("tensor")
-    for m, out in enumerate(outs):
-        out[...] = held[me ^ m]
+    for r, out in zip([0, *rotations(parts)], outs):
+        out[...] = held[lax.rem(me + r, parts)]
 
 
 def products(parts, blocks, enc_weight, dec_weight):
@@ -161,7 +165,7 @@
 def attribution_kernel(sizes, *refs):
     sections, feats, parts = sizes
     groups = sections * feats
-    terms = [refs[far_first(parts).index(m)] for m in range(parts)]
+    terms = refs[:parts]
     bias, inner, sums = refs[parts:]
     total = terms[0].shape[0] // 3
     tokens = total // groups
@@ -261,7 +265,7 @@
     blocks = [held[place] for place in row_blocks(sections, feats)]
 
     terms = products(parts, blocks, enc_weight, dec_weight)
-    arrived = [exchange(terms[m], "tensor", parts, m) for m in far_first(parts)[1:]]
+    arrived = [turn(term, "tensor", parts, r) for r, term in zip(rotations(parts), terms[1:])]
     sums = attributions(sizes, [terms[0]] + arrived, bias, inner)
     return tuple(final(sizes, tokens, lax.all_to_all(sums, EVERY, 0, 0)))
 

time: 32.2 us -> 32.2 us (level)
  blocking collectives: 10.7 us -> 9.4 us
  waiting for transfers between devices: 6.97 us -> 7.97 us
    ppermute x0 -> x3, waiting for transfers between devices: none -> 5.21 us  [turn(): return lax.ppermute(value, axis, [(i, (i + r) % size) for i in range(size)])]
    ppermute x0 -> x3, starting transfers between devices: none -> 4.68 us  [turn(): return lax.ppermute(value, axis, [(i, (i + r) % size) for i in range(size)])]
    ppermute x6 -> x3, starting transfers between devices: 5.5 us -> 1.04 us  [exchange(): return lax.ppermute(value, axis, [(i, i ^ k) for i in range(size)])]
    ppermute x6 -> x3, waiting for transfers between devices: 4.46 us -> 0.25 us  [exchange(): return lax.ppermute(value, axis, [(i, i ^ k) for i in range(size)])]
    all_to_all x1, blocking collectives: 10.7 us -> 9.4 us  [per_device(): return tuple(final(sizes, tokens, lax.all_to_all(sums, EVERY, 0, 0)))]
  transfers between devices with their start and end apart: 10 -> 10, of which waited for: 5 -> 6; matrix products, arithmetic and copies ran while one was open for 0% -> 0% of each run, Pallas kernels for 0% -> 0%
where the time goes in v12:
time: 32.2 us; the launch traced here: 31.9 us
  starting transfers between devices  11.1 us (34%)
  blocking collectives  9.4 us (29%)
  waiting for transfers between devices  7.97 us (25%)
  Pallas kernels  1.97 us (6%)
  other arithmetic  0.79 us (2%)
  between operations  0.67 us (2%)
    all_to_all x1, blocking collectives, per_device(): return tuple(final(sizes, tokens, lax.all_to_all(sums, EVERY, 0, 0)))  9.4 us
    ppermute x4, starting transfers between devices, per_device(): held[p, q] = lax.ppermute(packed, ('section', 'feat'), pairs)  5.37 us
    ppermute x3, waiting for transfers between devices, turn(): return lax.ppermute(value, axis, [(i, (i + r) % size) for i in range(size)])  5.21 us
    ppermute x3, starting transfers between devices, turn(): return lax.ppermute(value, axis, [(i, (i + r) % size) for i in range(size)])  4.68 us
    ppermute x4, waiting for transfers between devices, per_device(): held[p, q] = lax.ppermute(packed, ('section', 'feat'), pairs)  2.51 us
    pallas_call x1, Pallas kernels, products(): pl.pallas_call(functools.partial(product_kernel, groups, parts), out_shap...  1.16 us
    ppermute x3, starting transfers between devices, exchange(): return lax.ppermute(value, axis, [(i, i ^ k) for i in range(size)])  1.04 us
    another operation x1, other arithmetic, per_device(): packed = jnp.stack([clean_resid, corrupt_resid, metric_grad])  0.79 us
  transfers between devices with their start and end apart: 10, of which 6 were waited for; matrix products, arithmetic and copies ran while one was open for 0% of the time, Pallas kernels for 0%

profile of v12, /device:TPU:0, one launch (start us, length us, event | category | flops | bytes accessed | tf_op | source)
XLA Modules:
  0.0 31.9 jit_solution(11522785936328605461)
XLA Ops:
  0.6 0.8 %pad_maximum_fusion.packed.refs_0_ = bf16[3,4,2048]{2,1,0:T(4,128)(2,1)S(1)} fusion(bf16[1,4,2048]{2,1,0:T(4,128)(2,1)} %bitcast.5, bf16[1,4,2048]{2,1,0:T(4,128)(2,1)} %bitcast.6, bf16[1,4,2048]{2,1,0:T(4,128)(2,1)} %bitcast.7), kind=kLoop, calls=%fused_computation | loop fusion | flops 49152 | bytes 98304 | tf_op jit(solution)/shard_map/stack | solution.py:248
  1.4 0.0 copy-start
  1.4 0.0 copy-start.1
  1.4 4.0 %collective-permute-start.3 = (bf16[3,4,2048]{2,1,0:T(4,128)(2,1)S(1)}, bf16[3,4,2048]{2,1,0:T(4,128)(2,1)S(1)}, u32[]{:S(2)}, u32[]{:S(2)}) collective-permute-start(bf16[3,4,2048]{2,1,0:T(4,128)(2,1)S(1)} %pad_maximum_fusion.packed.refs_0_), channel_id=1, source_target_pairs={{0,24},{4,28},{8,16},{12,20},{16,8},{20,12},{24,0},{28,4},{1,25},{... | collective-permute-start | bytes 147464 | tf_op jit(solution)/shard_map/ppermute | solution.py:259
  5.4 0.5 %collective-permute-start.2 = (bf16[3,4,2048]{2,1,0:T(4,128)(2,1)S(1)}, bf16[3,4,2048]{2,1,0:T(4,128)(2,1)S(1)}, u32[]{:S(2)}, u32[]{:S(2)}) collective-permute-start(bf16[3,4,2048]{2,1,0:T(4,128)(2,1)S(1)} %pad_maximum_fusion.packed.refs_0_), channel_id=1, source_target_pairs={{0,16},{4,20},{8,24},{12,28},{16,0},{20,4},{24,8},{28,12},{1,17},{... | collective-permute-start | bytes 147464 | tf_op jit(solution)/shard_map/ppermute | solution.py:259
  5.9 0.0 collective-permute-start.1
  5.9 0.9 %collective-permute-start = (bf16[3,4,2048]{2,1,0:T(4,128)(2,1)S(1)}, bf16[3,4,2048]{2,1,0:T(4,128)(2,1)S(1)}, u32[]{:S(2)}, u32[]{:S(2)}) collective-permute-start(bf16[3,4,2048]{2,1,0:T(4,128)(2,1)S(1)} %pad_maximum_fusion.packed.refs_0_), channel_id=1, source_target_pairs={{0,8},{4,12},{8,0},{12,4},{16,24},{20,28},{24,16},{28,20},{1,9},{5... | collective-permute-start | bytes 147464 | tf_op jit(solution)/shard_map/ppermute | solution.py:259
  6.8 0.1 inner_products.1.refs_5_
  6.9 1.0 %collective-permute-start.4 = (bf16[3,4,2048]{2,1,0:T(4,128)(2,1)S(1)}, bf16[3,4,2048]{2,1,0:T(4,128)(2,1)S(1)}, u32[]{:S(2)}, u32[]{:S(2)}) collective-permute-start(bf16[3,4,2048]{2,1,0:T(4,128)(2,1)S(1)} %pad_maximum_fusion.packed.refs_0_), channel_id=1, source_target_pairs={{0,4},{4,0},{1,5},{5,1},{2,6},{6,2},{3,7},{7,3},{8,12},{12,8},{9,1... | collective-permute-start | bytes 147464 | tf_op jit(solution)/shard_map/ppermute | solution.py:31
  7.9 0.1 collective-permute-start.6
  8.0 1.5 %collective-permute-done.2.refs_3_ = bf16[3,4,2048]{2,1,0:T(4,128)(2,1)S(1)} collective-permute-done((bf16[3,4,2048]{2,1,0:T(4,128)(2,1)S(1)}, bf16[3,4,2048]{2,1,0:T(4,128)(2,1)S(1)}, u32[]{:S(2)}, u32[]{:S(2)}) %collective-permute-start.2) | collective-permute-done | bytes 49184 | tf_op jit(solution)/shard_map/ppermute | solution.py:259
  9.5 1.0 %collective-permute-done.refs_1_ = bf16[3,4,2048]{2,1,0:T(4,128)(2,1)S(1)} collective-permute-done((bf16[3,4,2048]{2,1,0:T(4,128)(2,1)S(1)}, bf16[3,4,2048]{2,1,0:T(4,128)(2,1)S(1)}, u32[]{:S(2)}, u32[]{:S(2)}) %collective-permute-start) | collective-permute-done | bytes 49184 | tf_op jit(solution)/shard_map/ppermute | solution.py:259
  10.5 0.0 collective-permute-done.6.refs_7_
  10.5 0.2 collective-permute-done.5.refs_6_
  10.7 1.2 %products.1 = (f32[96,128]{1,0:T(8,128)S(1)}, f32[96,128]{1,0:T(8,128)S(1)}, f32[96,128]{1,0:T(8,128)S(1)}, f32[96,128]{1,0:T(8,128)S(1)}) custom-call(bf16[3,4,2048]{2,1,0:T(4,128)(2,1)S(1)} %pad_maximum_fusion.packed.refs_0_, bf16[3,4,2048]{2,1,0:T(4,128)(2,1)S(1)} %collective-permute-done.refs_1_, bf16[3,4,2048]{2,1,0:T(4,128)(2,1)S(1)} %collective-permute-done.1.refs_2_, ...), custom_call_target="tpu_custom_call" | custom-call | tf_op jit(solution)/shard_map/products/pallas_call | solution.py:145
  11.9 2.6 %collective-permute-start.7 = (f32[96,128]{1,0:T(8,128)S(1)}, f32[96,128]{1,0:T(8,128)S(1)}, u32[]{:S(2)}, u32[]{:S(2)}) collective-permute-start(f32[96,128]{1,0:T(8,128)S(1)} %get-tuple-element.10), channel_id=1, source_target_pairs={{0,2},{1,3},{2,0},{3,1},{4,6},{5,7},{6,4},{7,5},{8,10},{9,11},{10,... | collective-permute-start | bytes 147464 | tf_op jit(solution)/shard_map/ppermute | solution.py:22
  14.5 1.3 %collective-permute-start.8 = (f32[96,128]{1,0:T(8,128)S(1)}, f32[96,128]{1,0:T(8,128)S(1)}, u32[]{:S(2)}, u32[]{:S(2)}) collective-permute-start(f32[96,128]{1,0:T(8,128)S(1)} %get-tuple-element.11), channel_id=1, source_target_pairs={{0,3},{1,0},{2,1},{3,2},{4,7},{5,4},{6,5},{7,6},{8,11},{9,8},{10,9... | collective-permute-start | bytes 147464 | tf_op jit(solution)/shard_map/ppermute | solution.py:22
  15.9 0.7 %collective-permute-start.9 = (f32[96,128]{1,0:T(8,128)S(1)}, f32[96,128]{1,0:T(8,128)S(1)}, u32[]{:S(2)}, u32[]{:S(2)}) collective-permute-start(f32[96,128]{1,0:T(8,128)S(1)} %get-tuple-element.12), channel_id=1, source_target_pairs={{0,1},{1,2},{2,3},{3,0},{4,5},{5,6},{6,7},{7,4},{8,9},{9,10},{10,1... | collective-permute-start | bytes 147464 | tf_op jit(solution)/shard_map/ppermute | solution.py:22
  16.6 1.0 %collective-permute-done.7.refs_1_ = f32[96,128]{1,0:T(8,128)S(1)} collective-permute-done((f32[96,128]{1,0:T(8,128)S(1)}, f32[96,128]{1,0:T(8,128)S(1)}, u32[]{:S(2)}, u32[]{:S(2)}) %collective-permute-start.7) | collective-permute-done | bytes 49184 | tf_op jit(solution)/shard_map/ppermute | solution.py:22
  17.6 1.1 %collective-permute-done.8.refs_2_ = f32[96,128]{1,0:T(8,128)S(1)} collective-permute-done((f32[96,128]{1,0:T(8,128)S(1)}, f32[96,128]{1,0:T(8,128)S(1)}, u32[]{:S(2)}, u32[]{:S(2)}) %collective-permute-start.8) | collective-permute-done | bytes 49184 | tf_op jit(solution)/shard_map/ppermute | solution.py:22
  18.6 3.1 %collective-permute-done.9.refs_3_ = f32[96,128]{1,0:T(8,128)S(1)} collective-permute-done((f32[96,128]{1,0:T(8,128)S(1)}, f32[96,128]{1,0:T(8,128)S(1)}, u32[]{:S(2)}, u32[]{:S(2)}) %collective-permute-start.9) | collective-permute-done | bytes 49184 | tf_op jit(solution)/shard_map/ppermute | solution.py:22
  21.8 0.1 attributions.1
  21.9 9.4 %all_to_all.5.arrived = f32[32,2,128]{2,1,0:T(2,128)S(1)} all-to-all(f32[32,2,128]{2,1,0:T(2,128)S(1)} %attributions.1), channel_id=1, replica_groups=mesh['section'=4,'feat'=2,'tensor'=4] {'section','feat','tensor'}, dimensions={0} | all-to-all | bytes 65536 | tf_op jit(solution)/shard_map/all_to_all | solution.py:270
  31.3 0.6 %final.1 = (f32[512]{0:T(512)}, f32[4]{0:T(128)}) custom-call(f32[32,2,128]{2,1,0:T(2,128)S(1)} %all_to_all.5.arrived), custom_call_target="tpu_custom_call" | custom-call | tf_op jit(solution)/shard_map/final/pallas_call | solution.py:225
  (8 shorter events, 0.0 us)
Async XLA Ops:
  1.4 9.3 %copy-start = (bf16[2048,512]{1,0:T(8,128)(2,1)S(1)}, bf16[2048,512]{1,0:T(8,128)(2,1)}, u32[]{:S(2)}) copy-start(bf16[2048,512]{1,0:T(8,128)(2,1)} %refs_8_.1) | copy-start | bytes 6291460
  1.4 9.3 %copy-start.1 = (bf16[512,2048]{1,0:T(8,128)(2,1)S(1)}, bf16[512,2048]{1,0:T(8,128)(2,1)}, u32[]{:S(2)}) copy-start(bf16[512,2048]{1,0:T(8,128)(2,1)} %refs_9_.1) | copy-start | bytes 6291460
  1.4 6.4 %collective-permute-start.3 = (bf16[3,4,2048]{2,1,0:T(4,128)(2,1)S(1)}, bf16[3,4,2048]{2,1,0:T(4,128)(2,1)S(1)}, u32[]{:S(2)}, u32[]{:S(2)}) collective-permute-start(bf16[3,4,2048]{2,1,0:T(4,128)(2,1)S(1)} %pad_maximum_fusion.packed.refs_0_), channel_id=1, source_target_pairs={{0,24},{4,28},{8,16},{12,20},{16,8},{20,12},{24,0},{28,4},{1,25},{... | collective-permute-start | bytes 147464 | tf_op jit(solution)/shard_map/ppermute | solution.py:259
  5.4 4.1 %collective-permute-start.2 = (bf16[3,4,2048]{2,1,0:T(4,128)(2,1)S(1)}, bf16[3,4,2048]{2,1,0:T(4,128)(2,1)S(1)}, u32[]{:S(2)}, u32[]{:S(2)}) collective-permute-start(bf16[3,4,2048]{2,1,0:T(4,128)(2,1)S(1)} %pad_maximum_fusion.packed.refs_0_), channel_id=1, source_target_pairs={{0,16},{4,20},{8,24},{12,28},{16,0},{20,4},{24,8},{28,12},{1,17},{... | collective-permute-start | bytes 147464 | tf_op jit(solution)/shard_map/ppermute | solution.py:259
  5.9 3.6 %collective-permute-start.1 = (bf16[3,4,2048]{2,1,0:T(4,128)(2,1)S(1)}, bf16[3,4,2048]{2,1,0:T(4,128)(2,1)S(1)}, u32[]{:S(2)}, u32[]{:S(2)}) collective-permute-start(bf16[3,4,2048]{2,1,0:T(4,128)(2,1)S(1)} %pad_maximum_fusion.packed.refs_0_), channel_id=1, source_target_pairs={{0,12},{4,8},{8,4},{12,0},{16,28},{20,24},{24,20},{28,16},{1,13},{... | collective-permute-start | bytes 147464 | tf_op jit(solution)/shard_map/ppermute | solution.py:259
  5.9 4.6 %collective-permute-start = (bf16[3,4,2048]{2,1,0:T(4,128)(2,1)S(1)}, bf16[3,4,2048]{2,1,0:T(4,128)(2,1)S(1)}, u32[]{:S(2)}, u32[]{:S(2)}) collective-permute-start(bf16[3,4,2048]{2,1,0:T(4,128)(2,1)S(1)} %pad_maximum_fusion.packed.refs_0_), channel_id=1, source_target_pairs={{0,8},{4,12},{8,0},{12,4},{16,24},{20,28},{24,16},{28,20},{1,9},{5... | collective-permute-start | bytes 147464 | tf_op jit(solution)/shard_map/ppermute | solution.py:259
  6.9 14.9 %copy-start.2 = (f32[512]{0:T(512)S(1)}, f32[512]{0:T(512)}, u32[]{:S(2)}) copy-start(f32[512]{0:T(512)} %param.10) | copy-start | bytes 6148
  6.9 2.6 %collective-permute-start.4 = (bf16[3,4,2048]{2,1,0:T(4,128)(2,1)S(1)}, bf16[3,4,2048]{2,1,0:T(4,128)(2,1)S(1)}, u32[]{:S(2)}, u32[]{:S(2)}) collective-permute-start(bf16[3,4,2048]{2,1,0:T(4,128)(2,1)S(1)} %pad_maximum_fusion.packed.refs_0_), channel_id=1, source_target_pairs={{0,4},{4,0},{1,5},{5,1},{2,6},{6,2},{3,7},{7,3},{8,12},{12,8},{9,1... | collective-permute-start | bytes 147464 | tf_op jit(solution)/shard_map/ppermute | solution.py:31
  7.9 2.6 %collective-permute-start.6 = (bf16[3,4,2048]{2,1,0:T(4,128)(2,1)S(1)}, bf16[3,4,2048]{2,1,0:T(4,128)(2,1)S(1)}, u32[]{:S(2)}, u32[]{:S(2)}) collective-permute-start(bf16[3,4,2048]{2,1,0:T(4,128)(2,1)S(1)} %collective-permute-done.3.refs_4_), channel_id=1, source_target_pairs={{0,4},{4,0},{1,5},{5,1},{2,6},{6,2},{3,7},{7,3},{8,12},{12,8},{9,1... | collective-permute-start | bytes 147464 | tf_op jit(solution)/shard_map/ppermute | solution.py:31
  9.5 1.2 %collective-permute-start.5 = (bf16[3,4,2048]{2,1,0:T(4,128)(2,1)S(1)}, bf16[3,4,2048]{2,1,0:T(4,128)(2,1)S(1)}, u32[]{:S(2)}, u32[]{:S(2)}) collective-permute-start(bf16[3,4,2048]{2,1,0:T(4,128)(2,1)S(1)} %collective-permute-done.2.refs_3_), channel_id=1, source_target_pairs={{0,4},{4,0},{1,5},{5,1},{2,6},{6,2},{3,7},{7,3},{8,12},{12,8},{9,1... | collective-permute-start | bytes 147464 | tf_op jit(solution)/shard_map/ppermute | solution.py:31
  11.9 5.7 %collective-permute-start.7 = (f32[96,128]{1,0:T(8,128)S(1)}, f32[96,128]{1,0:T(8,128)S(1)}, u32[]{:S(2)}, u32[]{:S(2)}) collective-permute-start(f32[96,128]{1,0:T(8,128)S(1)} %get-tuple-element.10), channel_id=1, source_target_pairs={{0,2},{1,3},{2,0},{3,1},{4,6},{5,7},{6,4},{7,5},{8,10},{9,11},{10,... | collective-permute-start | bytes 147464 | tf_op jit(solution)/shard_map/ppermute | solution.py:22
  14.5 4.1 %collective-permute-start.8 = (f32[96,128]{1,0:T(8,128)S(1)}, f32[96,128]{1,0:T(8,128)S(1)}, u32[]{:S(2)}, u32[]{:S(2)}) collective-permute-start(f32[96,128]{1,0:T(8,128)S(1)} %get-tuple-element.11), channel_id=1, source_target_pairs={{0,3},{1,0},{2,1},{3,2},{4,7},{5,4},{6,5},{7,6},{8,11},{9,8},{10,9... | collective-permute-start | bytes 147464 | tf_op jit(solution)/shard_map/ppermute | solution.py:22
  15.9 5.9 %collective-permute-start.9 = (f32[96,128]{1,0:T(8,128)S(1)}, f32[96,128]{1,0:T(8,128)S(1)}, u32[]{:S(2)}, u32[]{:S(2)}) collective-permute-start(f32[96,128]{1,0:T(8,128)S(1)} %get-tuple-element.12), channel_id=1, source_target_pairs={{0,1},{1,2},{2,3},{3,0},{4,5},{5,6},{6,7},{7,4},{8,9},{9,10},{10,1... | collective-permute-start | bytes 147464 | tf_op jit(solution)/shard_map/ppermute | solution.py:22

commit v13 on v10

--- a/solution.py
+++ b/solution.py
@@ -14,13 +14,9 @@
 EVERY = ("section", "feat", "tensor")
 
 
-def far_first(size):
-    return [0, *reversed(range(1, size))]
-
-
 def row_blocks(sections, feats):
     places = [(p, q) for p in range(feats) for q in range(sections)]
-    return sorted(places, key=lambda place: (place[0] > 0 and place[1] != 1, place[1], place[0]))
+    return sorted(places, key=lambda place: (place[0] > 0 and place[1] != 1, place[1], -place[0]))
 
 
 def exchange(value, axis, size, k):
@@ -103,9 +99,9 @@
 
 def product_kernel(groups, parts, *refs):
     blocks = refs[:groups]
-    enc, dec = refs[groups : groups + 2]
-    outs = refs[groups + 2 : groups + 2 + parts]
-    rows, held = refs[groups + 2 + parts :]
+    enc, dec, bias = refs[groups : groups + 3]
+    outs = refs[groups + 3 : groups + 3 + parts]
+    rows, held = refs[groups + 3 + parts :]
     tokens = blocks[0].shape[1]
     total = groups * tokens
     share = LANES
@@ -129,9 +125,10 @@
     me = lax.axis_index("tensor")
     for m, out in enumerate(outs):
         out[...] = held[me ^ m]
-
-
-def products(parts, blocks, enc_weight, dec_weight):
+    outs[0][pl.ds(0, 2 * total), :] += bias[pl.ds(me, 1), :]
+
+
+def products(parts, blocks, enc_weight, dec_weight, bias):
     groups = len(blocks)
     _, tokens, width = blocks[0].shape
     features = enc_weight.shape[1]
@@ -141,7 +138,7 @@
     return pl.pallas_call(
         functools.partial(product_kernel, groups, parts),
         out_shape=[part] * parts,
-        in_specs=[vmem] * (groups + 2),
+        in_specs=[vmem] * (groups + 3),
         out_specs=[vmem] * parts,
         scratch_shapes=[
             pltpu.VMEM((rows, width), jnp.float32),
@@ -149,7 +146,7 @@
         ],
         compiler_params=pltpu.CompilerParams(vmem_limit_bytes=48 * 2**20),
         name="products",
-    )(*blocks, enc_weight, dec_weight)
+    )(*blocks, enc_weight, dec_weight, bias)
 
 
 def add_up(values):
@@ -161,15 +158,14 @@
 def attribution_kernel(sizes, *refs):
     sections, feats, parts = sizes
     groups = sections * feats
-    terms = [refs[far_first(parts).index(m)] for m in range(parts)]
-    bias, inner, sums = refs[parts:]
+    terms = refs[:parts]
+    inner, sums = refs[parts:]
     total = terms[0].shape[0] // 3
     tokens = total // groups
     preact = add_up([term[...] for term in terms])
     section, feat = lax.axis_index("section"), lax.axis_index("feat")
-    b = bias[pl.ds(lax.axis_index("tensor"), 1), :]
-    act_clean = jnp.maximum(preact[:total] + b, 0.0)
-    act_corrupt = jnp.maximum(preact[total : 2 * total] + b, 0.0)
+    act_clean = jnp.maximum(preact[:total], 0.0)
+    act_corrupt = jnp.maximum(preact[total : 2 * total], 0.0)
     attribution = (act_corrupt - act_clean) * preact[2 * total :]
 
     devices = groups * parts
@@ -180,29 +176,29 @@
     place = lane == lax.broadcasted_iota(jnp.int32, (tokens, LANES), 0)
     for k, (p, q) in enumerate(row_blocks(sections, feats)):
         column = jnp.broadcast_to(token_part[k * tokens : (k + 1) * tokens], (tokens, LANES))
-        if k == 0:
+        if (p, q) == (1, 0):
             column = column - inner[pl.ds(0, tokens), :]
         row = jnp.sum(jnp.where(place, column, 0.0), axis=0, keepdims=True)
-        owner = (section ^ q) * feats + (feat ^ p)
+        owner = (section ^ q) * feats + (feat ^ 1 ^ p)
         sums[pl.ds(owner * parts, parts), 1, :] = jnp.broadcast_to(row, (parts, LANES))
 
 
-def attributions(sizes, terms, bias, inner):
+def attributions(sizes, terms, inner):
     sections, feats, parts = sizes
     vmem = pl.BlockSpec(memory_space=pltpu.VMEM)
     return pl.pallas_call(
         functools.partial(attribution_kernel, sizes),
         out_shape=jax.ShapeDtypeStruct((sections * feats * parts, 2, LANES), jnp.float32),
-        in_specs=[vmem] * (parts + 2),
+        in_specs=[vmem] * (parts + 1),
         out_specs=vmem,
         compiler_params=pltpu.CompilerParams(vmem_limit_bytes=16 * 2**20),
         name="attributions",
-    )(*terms, bias, inner)
+    )(*terms, inner)
 
 
 def final_kernel(sizes, arrived, feature_out, error_out, features, errors, sems):
     sections, feats, parts = sizes
-    group = lax.axis_index("section") * feats + lax.axis_index("feat")
+    group = lax.axis_index("section") * feats + (lax.axis_index("feat") ^ 1)
     mine = arrived[pl.ds(group * parts, parts), 0, :]
     for i in range(parts):
         features[pl.ds(i * LANES, LANES)] = mine[i]
@@ -260,9 +256,16 @@
             held[p, q] = exchange(block, "feat", feats, p)
     blocks = [held[place] for place in row_blocks(sections, feats)]
 
-    terms = products(parts, blocks, enc_weight, dec_weight)
-    arrived = [exchange(terms[m], "tensor", parts, m) for m in far_first(parts)[1:]]
-    sums = attributions(sizes, [terms[0]] + arrived, bias, inner)
+    terms = products(parts, blocks, enc_weight, dec_weight, bias)
+    arrived = [
+        lax.ppermute(
+            terms[m],
+            ("feat", "tensor"),
+            [(f * parts + t, (f ^ 1) * parts + (t ^ m)) for f in range(feats) for t in range(parts)],
+        )
+        for m in reversed(range(parts))
+    ]
+    sums = attributions(sizes, arrived, inner)
     return tuple(final(sizes, tokens, lax.all_to_all(sums, EVERY, 0, 0)))
 
 

time: 32.2 us -> 32.2 us (level)
  waiting for transfers between devices: 6.97 us -> 6.3 us
  blocking collectives: 10.7 us -> 11.1 us
    ppermute x0 -> x4, starting transfers between devices: none -> 4.29 us  [per_device(): lax.ppermute(terms[m], ('feat', 'tensor'), [(f * parts + t, (f ^ 1) * par...]
    ppermute x6 -> x3, starting transfers between devices: 5.5 us -> 1.59 us  [exchange(): return lax.ppermute(value, axis, [(i, i ^ k) for i in range(size)])]
    ppermute x6 -> x3, waiting for transfers between devices: 4.46 us -> 0.63 us  [exchange(): return lax.ppermute(value, axis, [(i, i ^ k) for i in range(size)])]
    ppermute x0 -> x4, waiting for transfers between devices: none -> 3.81 us  [per_device(): lax.ppermute(terms[m], ('feat', 'tensor'), [(f * parts + t, (f ^ 1) * par...]
    ppermute x4, waiting for transfers between devices: 2.51 us -> 1.86 us  [per_device(): held[p, q] = lax.ppermute(packed, ('section', 'feat'), pairs)]
    all_to_all x1, blocking collectives: 10.7 us -> 11.1 us  [per_device(): return tuple(final(sizes, tokens, lax.all_to_all(sums, EVERY, 0, 0)))]
  transfers between devices with their start and end apart: 10 -> 11, of which waited for: 5 -> 5; matrix products, arithmetic and copies ran while one was open for 0% -> 0% of each run, Pallas kernels for 0% -> 0%
where the time goes in v13:
time: 32.2 us; the launch traced here: 31.9 us
  blocking collectives  11.1 us (34%)
  starting transfers between devices  11 us (34%)
  waiting for transfers between devices  6.3 us (20%)
  Pallas kernels  1.96 us (6%)
  other arithmetic  0.79 us (2%)
  between operations  0.69 us (2%)
    all_to_all x1, blocking collectives, per_device(): return tuple(final(sizes, tokens, lax.all_to_all(sums, EVERY, 0, 0)))  11.1 us
    ppermute x4, starting transfers between devices, per_device(): held[p, q] = lax.ppermute(packed, ('section', 'feat'), pairs)  5.09 us
    ppermute x4, starting transfers between devices, per_device(): lax.ppermute(terms[m], ('feat', 'tensor'), [(f * parts + t, (f ^ 1) * par...  4.29 us
    ppermute x4, waiting for transfers between devices, per_device(): lax.ppermute(terms[m], ('feat', 'tensor'), [(f * parts + t, (f ^ 1) * par...  3.81 us
    ppermute x4, waiting for transfers between devices, per_device(): held[p, q] = lax.ppermute(packed, ('section', 'feat'), pairs)  1.86 us
    ppermute x3, starting transfers between devices, exchange(): return lax.ppermute(value, axis, [(i, i ^ k) for i in range(size)])  1.59 us
    pallas_call x1, Pallas kernels, products(): pl.pallas_call(functools.partial(product_kernel, groups, parts), out_shap...  1.15 us
    another operation x1, other arithmetic, per_device(): packed = jnp.stack([clean_resid, corrupt_resid, metric_grad])  0.79 us
  transfers between devices with their start and end apart: 11, of which 5 were waited for; matrix products, arithmetic and copies ran while one was open for 0% of the time, Pallas kernels for 0%

profile of v13, /device:TPU:0, one launch (start us, length us, event | category | flops | bytes accessed | tf_op | source)
XLA Modules:
  0.0 31.9 jit_solution(3506710336737817036)
XLA Ops:
  0.6 0.8 %pad_maximum_fusion.packed.refs_0_ = bf16[3,4,2048]{2,1,0:T(4,128)(2,1)S(1)} fusion(bf16[1,4,2048]{2,1,0:T(4,128)(2,1)} %bitcast.5, bf16[1,4,2048]{2,1,0:T(4,128)(2,1)} %bitcast.6, bf16[1,4,2048]{2,1,0:T(4,128)(2,1)} %bitcast.7), kind=kLoop, calls=%fused_computation | loop fusion | flops 49152 | bytes 98304 | tf_op jit(solution)/shard_map/stack | solution.py:240
  1.4 0.0 copy-start
  1.4 0.0 copy-start.1
  1.4 0.0 copy-start.2
  1.5 4.0 %collective-permute-start.3 = (bf16[3,4,2048]{2,1,0:T(4,128)(2,1)S(1)}, bf16[3,4,2048]{2,1,0:T(4,128)(2,1)S(1)}, u32[]{:S(2)}, u32[]{:S(2)}) collective-permute-start(bf16[3,4,2048]{2,1,0:T(4,128)(2,1)S(1)} %pad_maximum_fusion.packed.refs_0_), channel_id=1, source_target_pairs={{0,24},{4,28},{8,16},{12,20},{16,8},{20,12},{24,0},{28,4},{1,25},{... | collective-permute-start | bytes 147464 | tf_op jit(solution)/shard_map/ppermute | solution.py:251
  5.4 0.5 %collective-permute-start.2 = (bf16[3,4,2048]{2,1,0:T(4,128)(2,1)S(1)}, bf16[3,4,2048]{2,1,0:T(4,128)(2,1)S(1)}, u32[]{:S(2)}, u32[]{:S(2)}) collective-permute-start(bf16[3,4,2048]{2,1,0:T(4,128)(2,1)S(1)} %pad_maximum_fusion.packed.refs_0_), channel_id=1, source_target_pairs={{0,16},{4,20},{8,24},{12,28},{16,0},{20,4},{24,8},{28,12},{1,17},{... | collective-permute-start | bytes 147464 | tf_op jit(solution)/shard_map/ppermute | solution.py:251
  5.9 0.1 collective-permute-start.1
  6.1 0.5 %collective-permute-start = (bf16[3,4,2048]{2,1,0:T(4,128)(2,1)S(1)}, bf16[3,4,2048]{2,1,0:T(4,128)(2,1)S(1)}, u32[]{:S(2)}, u32[]{:S(2)}) collective-permute-start(bf16[3,4,2048]{2,1,0:T(4,128)(2,1)S(1)} %pad_maximum_fusion.packed.refs_0_), channel_id=1, source_target_pairs={{0,12},{4,8},{8,4},{12,0},{16,28},{20,24},{24,20},{28,16},{1,13},{... | collective-permute-start | bytes 147464 | tf_op jit(solution)/shard_map/ppermute | solution.py:251
  6.6 0.1 inner_products.1.refs_4_
  6.7 1.5 %collective-permute-start.4 = (bf16[3,4,2048]{2,1,0:T(4,128)(2,1)S(1)}, bf16[3,4,2048]{2,1,0:T(4,128)(2,1)S(1)}, u32[]{:S(2)}, u32[]{:S(2)}) collective-permute-start(bf16[3,4,2048]{2,1,0:T(4,128)(2,1)S(1)} %pad_maximum_fusion.packed.refs_0_), channel_id=1, source_target_pairs={{0,4},{4,0},{1,5},{5,1},{2,6},{6,2},{3,7},{7,3},{8,12},{12,8},{9,1... | collective-permute-start | bytes 147464 | tf_op jit(solution)/shard_map/ppermute | solution.py:23
  8.2 0.1 collective-permute-start.6
  8.2 1.3 %collective-permute-done.2.refs_3_ = bf16[3,4,2048]{2,1,0:T(4,128)(2,1)S(1)} collective-permute-done((bf16[3,4,2048]{2,1,0:T(4,128)(2,1)S(1)}, bf16[3,4,2048]{2,1,0:T(4,128)(2,1)S(1)}, u32[]{:S(2)}, u32[]{:S(2)}) %collective-permute-start.2) | collective-permute-done | bytes 49184 | tf_op jit(solution)/shard_map/ppermute | solution.py:251
  9.5 0.0 collective-permute-start.5
  9.5 0.6 %collective-permute-done.1.refs_2_ = bf16[3,4,2048]{2,1,0:T(4,128)(2,1)S(1)} collective-permute-done((bf16[3,4,2048]{2,1,0:T(4,128)(2,1)S(1)}, bf16[3,4,2048]{2,1,0:T(4,128)(2,1)S(1)}, u32[]{:S(2)}, u32[]{:S(2)}) %collective-permute-start.1) | collective-permute-done | bytes 49184 | tf_op jit(solution)/shard_map/ppermute | solution.py:251
  10.1 0.6 %collective-permute-done.5.refs_6_ = bf16[3,4,2048]{2,1,0:T(4,128)(2,1)S(1)} collective-permute-done((bf16[3,4,2048]{2,1,0:T(4,128)(2,1)S(1)}, bf16[3,4,2048]{2,1,0:T(4,128)(2,1)S(1)}, u32[]{:S(2)}, u32[]{:S(2)}) %collective-permute-start.5) | collective-permute-done | bytes 49184 | tf_op jit(solution)/shard_map/ppermute | solution.py:23
  10.8 1.1 %products.1 = (f32[96,128]{1,0:T(8,128)S(1)}, f32[96,128]{1,0:T(8,128)S(1)}, f32[96,128]{1,0:T(8,128)S(1)}, f32[96,128]{1,0:T(8,128)S(1)}) custom-call(bf16[3,4,2048]{2,1,0:T(4,128)(2,1)S(1)} %pad_maximum_fusion.packed.refs_0_, bf16[3,4,2048]{2,1,0:T(4,128)(2,1)S(1)} %collective-permute-done.refs_1_, bf16[3,4,2048]{2,1,0:T(4,128)(2,1)S(1)} %collective-permute-done.1.refs_2_, ...), custom_call_target="tpu_custom_call" | custom-call | tf_op jit(solution)/shard_map/products/pallas_call | solution.py:138
  11.9 3.4 %collective-permute-start.7 = (f32[96,128]{1,0:T(8,128)S(1)}, f32[96,128]{1,0:T(8,128)S(1)}, u32[]{:S(2)}, u32[]{:S(2)}) collective-permute-start(f32[96,128]{1,0:T(8,128)S(1)} %get-tuple-element.9), channel_id=1, source_target_pairs={{0,7},{1,6},{2,5},{3,4},{4,3},{5,2},{6,1},{7,0},{8,15},{9,14},{10,... | collective-permute-start | bytes 147464 | tf_op jit(solution)/shard_map/ppermute | solution.py:261
  15.3 0.6 %collective-permute-start.9 = (f32[96,128]{1,0:T(8,128)S(1)}, f32[96,128]{1,0:T(8,128)S(1)}, u32[]{:S(2)}, u32[]{:S(2)}) collective-permute-start(f32[96,128]{1,0:T(8,128)S(1)} %get-tuple-element.11), channel_id=1, source_target_pairs={{0,5},{1,4},{2,7},{3,6},{4,1},{5,0},{6,3},{7,2},{8,13},{9,12},{10,... | collective-permute-start | bytes 147464 | tf_op jit(solution)/shard_map/ppermute | solution.py:261
  15.9 0.3 collective-permute-start.10
  16.2 1.4 %collective-permute-done.7.refs_0_ = f32[96,128]{1,0:T(8,128)S(1)} collective-permute-done((f32[96,128]{1,0:T(8,128)S(1)}, f32[96,128]{1,0:T(8,128)S(1)}, u32[]{:S(2)}, u32[]{:S(2)}) %collective-permute-start.7) | collective-permute-done | bytes 49184 | tf_op jit(solution)/shard_map/ppermute | solution.py:261
  17.6 2.4 %collective-permute-done.8.refs_1_ = f32[96,128]{1,0:T(8,128)S(1)} collective-permute-done((f32[96,128]{1,0:T(8,128)S(1)}, f32[96,128]{1,0:T(8,128)S(1)}, u32[]{:S(2)}, u32[]{:S(2)}) %collective-permute-start.8) | collective-permute-done | bytes 49184 | tf_op jit(solution)/shard_map/ppermute | solution.py:261
  20.0 0.1 attributions.1
  20.1 11.1 %all_to_all.5.arrived = f32[32,2,128]{2,1,0:T(2,128)S(1)} all-to-all(f32[32,2,128]{2,1,0:T(2,128)S(1)} %attributions.1), channel_id=1, replica_groups=mesh['section'=4,'feat'=2,'tensor'=4] {'section','feat','tensor'}, dimensions={0} | all-to-all | bytes 65536 | tf_op jit(solution)/shard_map/all_to_all | solution.py:269
  31.3 0.6 %final.1 = (f32[512]{0:T(512)}, f32[4]{0:T(128)}) custom-call(f32[32,2,128]{2,1,0:T(2,128)S(1)} %all_to_all.5.arrived), custom_call_target="tpu_custom_call" | custom-call | tf_op jit(solution)/shard_map/final/pallas_call | solution.py:217
  (10 shorter events, 0.0 us)
Async XLA Ops:
  1.4 9.3 %copy-start = (bf16[2048,512]{1,0:T(8,128)(2,1)S(1)}, bf16[2048,512]{1,0:T(8,128)(2,1)}, u32[]{:S(2)}) copy-start(bf16[2048,512]{1,0:T(8,128)(2,1)} %refs_8_.1) | copy-start | bytes 6291460
  1.4 9.3 %copy-start.1 = (bf16[512,2048]{1,0:T(8,128)(2,1)S(1)}, bf16[512,2048]{1,0:T(8,128)(2,1)}, u32[]{:S(2)}) copy-start(bf16[512,2048]{1,0:T(8,128)(2,1)} %refs_9_.1) | copy-start | bytes 6291460
  1.4 9.3 %copy-start.2 = (f32[512]{0:T(512)S(1)}, f32[512]{0:T(512)}, u32[]{:S(2)}) copy-start(f32[512]{0:T(512)} %param.10) | copy-start | bytes 6148
  1.5 6.7 %collective-permute-start.3 = (bf16[3,4,2048]{2,1,0:T(4,128)(2,1)S(1)}, bf16[3,4,2048]{2,1,0:T(4,128)(2,1)S(1)}, u32[]{:S(2)}, u32[]{:S(2)}) collective-permute-start(bf16[3,4,2048]{2,1,0:T(4,128)(2,1)S(1)} %pad_maximum_fusion.packed.refs_0_), channel_id=1, source_target_pairs={{0,24},{4,28},{8,16},{12,20},{16,8},{20,12},{24,0},{28,4},{1,25},{... | collective-permute-start | bytes 147464 | tf_op jit(solution)/shard_map/ppermute | solution.py:251
  5.4 4.1 %collective-permute-start.2 = (bf16[3,4,2048]{2,1,0:T(4,128)(2,1)S(1)}, bf16[3,4,2048]{2,1,0:T(4,128)(2,1)S(1)}, u32[]{:S(2)}, u32[]{:S(2)}) collective-permute-start(bf16[3,4,2048]{2,1,0:T(4,128)(2,1)S(1)} %pad_maximum_fusion.packed.refs_0_), channel_id=1, source_target_pairs={{0,16},{4,20},{8,24},{12,28},{16,0},{20,4},{24,8},{28,12},{1,17},{... | collective-permute-start | bytes 147464 | tf_op jit(solution)/shard_map/ppermute | solution.py:251
  5.9 4.2 %collective-permute-start.1 = (bf16[3,4,2048]{2,1,0:T(4,128)(2,1)S(1)}, bf16[3,4,2048]{2,1,0:T(4,128)(2,1)S(1)}, u32[]{:S(2)}, u32[]{:S(2)}) collective-permute-start(bf16[3,4,2048]{2,1,0:T(4,128)(2,1)S(1)} %pad_maximum_fusion.packed.refs_0_), channel_id=1, source_target_pairs={{0,8},{4,12},{8,0},{12,4},{16,24},{20,28},{24,16},{28,20},{1,9},{5... | collective-permute-start | bytes 147464 | tf_op jit(solution)/shard_map/ppermute | solution.py:251
  6.1 4.0 %collective-permute-start = (bf16[3,4,2048]{2,1,0:T(4,128)(2,1)S(1)}, bf16[3,4,2048]{2,1,0:T(4,128)(2,1)S(1)}, u32[]{:S(2)}, u32[]{:S(2)}) collective-permute-start(bf16[3,4,2048]{2,1,0:T(4,128)(2,1)S(1)} %pad_maximum_fusion.packed.refs_0_), channel_id=1, source_target_pairs={{0,12},{4,8},{8,4},{12,0},{16,28},{20,24},{24,20},{28,16},{1,13},{... | collective-permute-start | bytes 147464 | tf_op jit(solution)/shard_map/ppermute | solution.py:251
  6.7 2.9 %collective-permute-start.4 = (bf16[3,4,2048]{2,1,0:T(4,128)(2,1)S(1)}, bf16[3,4,2048]{2,1,0:T(4,128)(2,1)S(1)}, u32[]{:S(2)}, u32[]{:S(2)}) collective-permute-start(bf16[3,4,2048]{2,1,0:T(4,128)(2,1)S(1)} %pad_maximum_fusion.packed.refs_0_), channel_id=1, source_target_pairs={{0,4},{4,0},{1,5},{5,1},{2,6},{6,2},{3,7},{7,3},{8,12},{12,8},{9,1... | collective-permute-start | bytes 147464 | tf_op jit(solution)/shard_map/ppermute | solution.py:23
  8.2 1.9 %collective-permute-start.6 = (bf16[3,4,2048]{2,1,0:T(4,128)(2,1)S(1)}, bf16[3,4,2048]{2,1,0:T(4,128)(2,1)S(1)}, u32[]{:S(2)}, u32[]{:S(2)}) collective-permute-start(bf16[3,4,2048]{2,1,0:T(4,128)(2,1)S(1)} %collective-permute-done.3.refs_4_), channel_id=1, source_target_pairs={{0,4},{4,0},{1,5},{5,1},{2,6},{6,2},{3,7},{7,3},{8,12},{12,8},{9,1... | collective-permute-start | bytes 147464 | tf_op jit(solution)/shard_map/ppermute | solution.py:23
  9.5 1.2 %collective-permute-start.5 = (bf16[3,4,2048]{2,1,0:T(4,128)(2,1)S(1)}, bf16[3,4,2048]{2,1,0:T(4,128)(2,1)S(1)}, u32[]{:S(2)}, u32[]{:S(2)}) collective-permute-start(bf16[3,4,2048]{2,1,0:T(4,128)(2,1)S(1)} %collective-permute-done.2.refs_3_), channel_id=1, source_target_pairs={{0,4},{4,0},{1,5},{5,1},{2,6},{6,2},{3,7},{7,3},{8,12},{12,8},{9,1... | collective-permute-start | bytes 147464 | tf_op jit(solution)/shard_map/ppermute | solution.py:23
  11.9 5.7 %collective-permute-start.7 = (f32[96,128]{1,0:T(8,128)S(1)}, f32[96,128]{1,0:T(8,128)S(1)}, u32[]{:S(2)}, u32[]{:S(2)}) collective-permute-start(f32[96,128]{1,0:T(8,128)S(1)} %get-tuple-element.9), channel_id=1, source_target_pairs={{0,7},{1,6},{2,5},{3,4},{4,3},{5,2},{6,1},{7,0},{8,15},{9,14},{10,... | collective-permute-start | bytes 147464 | tf_op jit(solution)/shard_map/ppermute | solution.py:261
  15.3 4.7 %collective-permute-start.8 = (f32[96,128]{1,0:T(8,128)S(1)}, f32[96,128]{1,0:T(8,128)S(1)}, u32[]{:S(2)}, u32[]{:S(2)}) collective-permute-start(f32[96,128]{1,0:T(8,128)S(1)} %get-tuple-element.10), channel_id=1, source_target_pairs={{0,6},{1,7},{2,4},{3,5},{4,2},{5,3},{6,0},{7,1},{8,14},{9,15},{10,... | collective-permute-start | bytes 147464 | tf_op jit(solution)/shard_map/ppermute | solution.py:261
  15.3 4.7 %collective-permute-start.9 = (f32[96,128]{1,0:T(8,128)S(1)}, f32[96,128]{1,0:T(8,128)S(1)}, u32[]{:S(2)}, u32[]{:S(2)}) collective-permute-start(f32[96,128]{1,0:T(8,128)S(1)} %get-tuple-element.11), channel_id=1, source_target_pairs={{0,5},{1,4},{2,7},{3,6},{4,1},{5,0},{6,3},{7,2},{8,13},{9,12},{10,... | collective-permute-start | bytes 147464 | tf_op jit(solution)/shard_map/ppermute | solution.py:261
  15.9 4.1 %collective-permute-start.10 = (f32[96,128]{1,0:T(8,128)S(1)}, f32[96,128]{1,0:T(8,128)S(1)}, u32[]{:S(2)}, u32[]{:S(2)}) collective-permute-start(f32[96,128]{1,0:T(8,128)S(1)} %get-tuple-element.12), channel_id=1, source_target_pairs={{0,4},{1,5},{2,6},{3,7},{4,0},{5,1},{6,2},{7,3},{8,12},{9,13},{10,... | collective-permute-start | bytes 147464 | tf_op jit(solution)/shard_map/ppermute | solution.py:261

commit v14 on v13

--- a/solution.py
+++ b/solution.py
@@ -16,7 +16,7 @@
 
 def row_blocks(sections, feats):
     places = [(p, q) for p in range(feats) for q in range(sections)]
-    return sorted(places, key=lambda place: (place[0] > 0 and place[1] != 1, place[1], -place[0]))
+    return sorted(places, key=lambda place: (place[0] > 0 and place[1] != 1, place[1], place[0]))
 
 
 def exchange(value, axis, size, k):

time: 32.2 us -> 32.2 us (level)
    ppermute x4, waiting for transfers between devices: 1.86 us -> 2.52 us  [per_device(): held[p, q] = lax.ppermute(packed, ('section', 'feat'), pairs)]
    ppermute x3, starting transfers between devices: 1.59 us -> 1.03 us  [exchange(): return lax.ppermute(value, axis, [(i, i ^ k) for i in range(size)])]
    ppermute x3, waiting for transfers between devices: 0.63 us -> 0.25 us  [exchange(): return lax.ppermute(value, axis, [(i, i ^ k) for i in range(size)])]
where the time goes in v14:
time: 32.2 us; the launch traced here: 31.9 us
  blocking collectives  11.2 us (35%)
  starting transfers between devices  10.7 us (33%)
  waiting for transfers between devices  6.58 us (20%)
  Pallas kernels  1.96 us (6%)
  other arithmetic  0.79 us (2%)
  between operations  0.69 us (2%)
    all_to_all x1, blocking collectives, per_device(): return tuple(final(sizes, tokens, lax.all_to_all(sums, EVERY, 0, 0)))  11.2 us
    ppermute x4, starting transfers between devices, per_device(): held[p, q] = lax.ppermute(packed, ('section', 'feat'), pairs)  5.37 us
    ppermute x4, starting transfers between devices, per_device(): lax.ppermute(terms[m], ('feat', 'tensor'), [(f * parts + t, (f ^ 1) * par...  4.29 us
    ppermute x4, waiting for transfers between devices, per_device(): lax.ppermute(terms[m], ('feat', 'tensor'), [(f * parts + t, (f ^ 1) * par...  3.81 us
    ppermute x4, waiting for transfers between devices, per_device(): held[p, q] = lax.ppermute(packed, ('section', 'feat'), pairs)  2.52 us
    pallas_call x1, Pallas kernels, products(): pl.pallas_call(functools.partial(product_kernel, groups, parts), out_shap...  1.15 us
    ppermute x3, starting transfers between devices, exchange(): return lax.ppermute(value, axis, [(i, i ^ k) for i in range(size)])  1.03 us
    another operation x1, other arithmetic, per_device(): packed = jnp.stack([clean_resid, corrupt_resid, metric_grad])  0.79 us
  transfers between devices with their start and end apart: 11, of which 5 were waited for; matrix products, arithmetic and copies ran while one was open for 0% of the time, Pallas kernels for 0%

profile of v14, /device:TPU:0, one launch (start us, length us, event | category | flops | bytes accessed | tf_op | source)
XLA Modules:
  0.0 31.9 jit_solution(12921444045722245477)
XLA Ops:
  0.6 0.8 %pad_maximum_fusion.packed.refs_0_ = bf16[3,4,2048]{2,1,0:T(4,128)(2,1)S(1)} fusion(bf16[1,4,2048]{2,1,0:T(4,128)(2,1)} %bitcast.5, bf16[1,4,2048]{2,1,0:T(4,128)(2,1)} %bitcast.6, bf16[1,4,2048]{2,1,0:T(4,128)(2,1)} %bitcast.7), kind=kLoop, calls=%fused_computation | loop fusion | flops 49152 | bytes 98304 | tf_op jit(solution)/shard_map/stack | solution.py:240
  1.4 0.0 copy-start
  1.4 0.0 copy-start.1
  1.4 0.0 copy-start.2
  1.5 4.0 %collective-permute-start.3 = (bf16[3,4,2048]{2,1,0:T(4,128)(2,1)S(1)}, bf16[3,4,2048]{2,1,0:T(4,128)(2,1)S(1)}, u32[]{:S(2)}, u32[]{:S(2)}) collective-permute-start(bf16[3,4,2048]{2,1,0:T(4,128)(2,1)S(1)} %pad_maximum_fusion.packed.refs_0_), channel_id=1, source_target_pairs={{0,24},{4,28},{8,16},{12,20},{16,8},{20,12},{24,0},{28,4},{1,25},{... | collective-permute-start | bytes 147464 | tf_op jit(solution)/shard_map/ppermute | solution.py:251
  5.4 0.5 %collective-permute-start.2 = (bf16[3,4,2048]{2,1,0:T(4,128)(2,1)S(1)}, bf16[3,4,2048]{2,1,0:T(4,128)(2,1)S(1)}, u32[]{:S(2)}, u32[]{:S(2)}) collective-permute-start(bf16[3,4,2048]{2,1,0:T(4,128)(2,1)S(1)} %pad_maximum_fusion.packed.refs_0_), channel_id=1, source_target_pairs={{0,16},{4,20},{8,24},{12,28},{16,0},{20,4},{24,8},{28,12},{1,17},{... | collective-permute-start | bytes 147464 | tf_op jit(solution)/shard_map/ppermute | solution.py:251
  5.9 0.9 %collective-permute-start = (bf16[3,4,2048]{2,1,0:T(4,128)(2,1)S(1)}, bf16[3,4,2048]{2,1,0:T(4,128)(2,1)S(1)}, u32[]{:S(2)}, u32[]{:S(2)}) collective-permute-start(bf16[3,4,2048]{2,1,0:T(4,128)(2,1)S(1)} %pad_maximum_fusion.packed.refs_0_), channel_id=1, source_target_pairs={{0,8},{4,12},{8,0},{12,4},{16,24},{20,28},{24,16},{28,20},{1,9},{5... | collective-permute-start | bytes 147464 | tf_op jit(solution)/shard_map/ppermute | solution.py:251
  6.8 0.1 inner_products.1.refs_4_
  6.9 1.0 %collective-permute-start.4 = (bf16[3,4,2048]{2,1,0:T(4,128)(2,1)S(1)}, bf16[3,4,2048]{2,1,0:T(4,128)(2,1)S(1)}, u32[]{:S(2)}, u32[]{:S(2)}) collective-permute-start(bf16[3,4,2048]{2,1,0:T(4,128)(2,1)S(1)} %pad_maximum_fusion.packed.refs_0_), channel_id=1, source_target_pairs={{0,4},{4,0},{1,5},{5,1},{2,6},{6,2},{3,7},{7,3},{8,12},{12,8},{9,1... | collective-permute-start | bytes 147464 | tf_op jit(solution)/shard_map/ppermute | solution.py:23
  7.9 0.1 collective-permute-start.6
  8.0 1.5 %collective-permute-done.2.refs_3_ = bf16[3,4,2048]{2,1,0:T(4,128)(2,1)S(1)} collective-permute-done((bf16[3,4,2048]{2,1,0:T(4,128)(2,1)S(1)}, bf16[3,4,2048]{2,1,0:T(4,128)(2,1)S(1)}, u32[]{:S(2)}, u32[]{:S(2)}) %collective-permute-start.2) | collective-permute-done | bytes 49184 | tf_op jit(solution)/shard_map/ppermute | solution.py:251
  9.5 0.0 collective-permute-start.5
  9.5 0.0 collective-permute-done.4.refs_5_
  9.5 1.0 %collective-permute-done.refs_1_ = bf16[3,4,2048]{2,1,0:T(4,128)(2,1)S(1)} collective-permute-done((bf16[3,4,2048]{2,1,0:T(4,128)(2,1)S(1)}, bf16[3,4,2048]{2,1,0:T(4,128)(2,1)S(1)}, u32[]{:S(2)}, u32[]{:S(2)}) %collective-permute-start) | collective-permute-done | bytes 49184 | tf_op jit(solution)/shard_map/ppermute | solution.py:251
  10.5 0.2 collective-permute-done.5.refs_6_
  10.8 1.1 %products.1 = (f32[96,128]{1,0:T(8,128)S(1)}, f32[96,128]{1,0:T(8,128)S(1)}, f32[96,128]{1,0:T(8,128)S(1)}, f32[96,128]{1,0:T(8,128)S(1)}) custom-call(bf16[3,4,2048]{2,1,0:T(4,128)(2,1)S(1)} %pad_maximum_fusion.packed.refs_0_, bf16[3,4,2048]{2,1,0:T(4,128)(2,1)S(1)} %collective-permute-done.refs_1_, bf16[3,4,2048]{2,1,0:T(4,128)(2,1)S(1)} %collective-permute-done.1.refs_2_, ...), custom_call_target="tpu_custom_call" | custom-call | tf_op jit(solution)/shard_map/products/pallas_call | solution.py:138
  11.9 3.4 %collective-permute-start.7 = (f32[96,128]{1,0:T(8,128)S(1)}, f32[96,128]{1,0:T(8,128)S(1)}, u32[]{:S(2)}, u32[]{:S(2)}) collective-permute-start(f32[96,128]{1,0:T(8,128)S(1)} %get-tuple-element.9), channel_id=1, source_target_pairs={{0,7},{1,6},{2,5},{3,4},{4,3},{5,2},{6,1},{7,0},{8,15},{9,14},{10,... | collective-permute-start | bytes 147464 | tf_op jit(solution)/shard_map/ppermute | solution.py:261
  15.3 0.6 %collective-permute-start.9 = (f32[96,128]{1,0:T(8,128)S(1)}, f32[96,128]{1,0:T(8,128)S(1)}, u32[]{:S(2)}, u32[]{:S(2)}) collective-permute-start(f32[96,128]{1,0:T(8,128)S(1)} %get-tuple-element.11), channel_id=1, source_target_pairs={{0,5},{1,4},{2,7},{3,6},{4,1},{5,0},{6,3},{7,2},{8,13},{9,12},{10,... | collective-permute-start | bytes 147464 | tf_op jit(solution)/shard_map/ppermute | solution.py:261
  15.9 0.3 collective-permute-start.10
  16.2 1.4 %collective-permute-done.7.refs_0_ = f32[96,128]{1,0:T(8,128)S(1)} collective-permute-done((f32[96,128]{1,0:T(8,128)S(1)}, f32[96,128]{1,0:T(8,128)S(1)}, u32[]{:S(2)}, u32[]{:S(2)}) %collective-permute-start.7) | collective-permute-done | bytes 49184 | tf_op jit(solution)/shard_map/ppermute | solution.py:261
  17.6 2.4 %collective-permute-done.8.refs_1_ = f32[96,128]{1,0:T(8,128)S(1)} collective-permute-done((f32[96,128]{1,0:T(8,128)S(1)}, f32[96,128]{1,0:T(8,128)S(1)}, u32[]{:S(2)}, u32[]{:S(2)}) %collective-permute-start.8) | collective-permute-done | bytes 49184 | tf_op jit(solution)/shard_map/ppermute | solution.py:261
  20.0 0.1 attributions.1
  20.1 11.2 %all_to_all.5.arrived = f32[32,2,128]{2,1,0:T(2,128)S(1)} all-to-all(f32[32,2,128]{2,1,0:T(2,128)S(1)} %attributions.1), channel_id=1, replica_groups=mesh['section'=4,'feat'=2,'tensor'=4] {'section','feat','tensor'}, dimensions={0} | all-to-all | bytes 65536 | tf_op jit(solution)/shard_map/all_to_all | solution.py:269
  31.3 0.6 %final.1 = (f32[512]{0:T(512)}, f32[4]{0:T(128)}) custom-call(f32[32,2,128]{2,1,0:T(2,128)S(1)} %all_to_all.5.arrived), custom_call_target="tpu_custom_call" | custom-call | tf_op jit(solution)/shard_map/final/pallas_call | solution.py:217
  (10 shorter events, 0.0 us)
Async XLA Ops:
  1.4 9.3 %copy-start = (bf16[2048,512]{1,0:T(8,128)(2,1)S(1)}, bf16[2048,512]{1,0:T(8,128)(2,1)}, u32[]{:S(2)}) copy-start(bf16[2048,512]{1,0:T(8,128)(2,1)} %refs_8_.1) | copy-start | bytes 6291460
  1.4 9.3 %copy-start.1 = (bf16[512,2048]{1,0:T(8,128)(2,1)S(1)}, bf16[512,2048]{1,0:T(8,128)(2,1)}, u32[]{:S(2)}) copy-start(bf16[512,2048]{1,0:T(8,128)(2,1)} %refs_9_.1) | copy-start | bytes 6291460
  1.4 9.3 %copy-start.2 = (f32[512]{0:T(512)S(1)}, f32[512]{0:T(512)}, u32[]{:S(2)}) copy-start(f32[512]{0:T(512)} %param.10) | copy-start | bytes 6148
  1.5 6.4 %collective-permute-start.3 = (bf16[3,4,2048]{2,1,0:T(4,128)(2,1)S(1)}, bf16[3,4,2048]{2,1,0:T(4,128)(2,1)S(1)}, u32[]{:S(2)}, u32[]{:S(2)}) collective-permute-start(bf16[3,4,2048]{2,1,0:T(4,128)(2,1)S(1)} %pad_maximum_fusion.packed.refs_0_), channel_id=1, source_target_pairs={{0,24},{4,28},{8,16},{12,20},{16,8},{20,12},{24,0},{28,4},{1,25},{... | collective-permute-start | bytes 147464 | tf_op jit(solution)/shard_map/ppermute | solution.py:251
  5.4 4.1 %collective-permute-start.2 = (bf16[3,4,2048]{2,1,0:T(4,128)(2,1)S(1)}, bf16[3,4,2048]{2,1,0:T(4,128)(2,1)S(1)}, u32[]{:S(2)}, u32[]{:S(2)}) collective-permute-start(bf16[3,4,2048]{2,1,0:T(4,128)(2,1)S(1)} %pad_maximum_fusion.packed.refs_0_), channel_id=1, source_target_pairs={{0,16},{4,20},{8,24},{12,28},{16,0},{20,4},{24,8},{28,12},{1,17},{... | collective-permute-start | bytes 147464 | tf_op jit(solution)/shard_map/ppermute | solution.py:251
  5.9 3.6 %collective-permute-start.1 = (bf16[3,4,2048]{2,1,0:T(4,128)(2,1)S(1)}, bf16[3,4,2048]{2,1,0:T(4,128)(2,1)S(1)}, u32[]{:S(2)}, u32[]{:S(2)}) collective-permute-start(bf16[3,4,2048]{2,1,0:T(4,128)(2,1)S(1)} %pad_maximum_fusion.packed.refs_0_), channel_id=1, source_target_pairs={{0,12},{4,8},{8,4},{12,0},{16,28},{20,24},{24,20},{28,16},{1,13},{... | collective-permute-start | bytes 147464 | tf_op jit(solution)/shard_map/ppermute | solution.py:251
  5.9 4.6 %collective-permute-start = (bf16[3,4,2048]{2,1,0:T(4,128)(2,1)S(1)}, bf16[3,4,2048]{2,1,0:T(4,128)(2,1)S(1)}, u32[]{:S(2)}, u32[]{:S(2)}) collective-permute-start(bf16[3,4,2048]{2,1,0:T(4,128)(2,1)S(1)} %pad_maximum_fusion.packed.refs_0_), channel_id=1, source_target_pairs={{0,8},{4,12},{8,0},{12,4},{16,24},{20,28},{24,16},{28,20},{1,9},{5... | collective-permute-start | bytes 147464 | tf_op jit(solution)/shard_map/ppermute | solution.py:251
  6.9 2.6 %collective-permute-start.4 = (bf16[3,4,2048]{2,1,0:T(4,128)(2,1)S(1)}, bf16[3,4,2048]{2,1,0:T(4,128)(2,1)S(1)}, u32[]{:S(2)}, u32[]{:S(2)}) collective-permute-start(bf16[3,4,2048]{2,1,0:T(4,128)(2,1)S(1)} %pad_maximum_fusion.packed.refs_0_), channel_id=1, source_target_pairs={{0,4},{4,0},{1,5},{5,1},{2,6},{6,2},{3,7},{7,3},{8,12},{12,8},{9,1... | collective-permute-start | bytes 147464 | tf_op jit(solution)/shard_map/ppermute | solution.py:23
  7.9 2.6 %collective-permute-start.6 = (bf16[3,4,2048]{2,1,0:T(4,128)(2,1)S(1)}, bf16[3,4,2048]{2,1,0:T(4,128)(2,1)S(1)}, u32[]{:S(2)}, u32[]{:S(2)}) collective-permute-start(bf16[3,4,2048]{2,1,0:T(4,128)(2,1)S(1)} %collective-permute-done.3.refs_4_), channel_id=1, source_target_pairs={{0,4},{4,0},{1,5},{5,1},{2,6},{6,2},{3,7},{7,3},{8,12},{12,8},{9,1... | collective-permute-start | bytes 147464 | tf_op jit(solution)/shard_map/ppermute | solution.py:23
  9.5 1.2 %collective-permute-start.5 = (bf16[3,4,2048]{2,1,0:T(4,128)(2,1)S(1)}, bf16[3,4,2048]{2,1,0:T(4,128)(2,1)S(1)}, u32[]{:S(2)}, u32[]{:S(2)}) collective-permute-start(bf16[3,4,2048]{2,1,0:T(4,128)(2,1)S(1)} %collective-permute-done.2.refs_3_), channel_id=1, source_target_pairs={{0,4},{4,0},{1,5},{5,1},{2,6},{6,2},{3,7},{7,3},{8,12},{12,8},{9,1... | collective-permute-start | bytes 147464 | tf_op jit(solution)/shard_map/ppermute | solution.py:23
  11.9 5.7 %collective-permute-start.7 = (f32[96,128]{1,0:T(8,128)S(1)}, f32[96,128]{1,0:T(8,128)S(1)}, u32[]{:S(2)}, u32[]{:S(2)}) collective-permute-start(f32[96,128]{1,0:T(8,128)S(1)} %get-tuple-element.9), channel_id=1, source_target_pairs={{0,7},{1,6},{2,5},{3,4},{4,3},{5,2},{6,1},{7,0},{8,15},{9,14},{10,... | collective-permute-start | bytes 147464 | tf_op jit(solution)/shard_map/ppermute | solution.py:261
  15.3 4.7 %collective-permute-start.8 = (f32[96,128]{1,0:T(8,128)S(1)}, f32[96,128]{1,0:T(8,128)S(1)}, u32[]{:S(2)}, u32[]{:S(2)}) collective-permute-start(f32[96,128]{1,0:T(8,128)S(1)} %get-tuple-element.10), channel_id=1, source_target_pairs={{0,6},{1,7},{2,4},{3,5},{4,2},{5,3},{6,0},{7,1},{8,14},{9,15},{10,... | collective-permute-start | bytes 147464 | tf_op jit(solution)/shard_map/ppermute | solution.py:261
  15.3 4.7 %collective-permute-start.9 = (f32[96,128]{1,0:T(8,128)S(1)}, f32[96,128]{1,0:T(8,128)S(1)}, u32[]{:S(2)}, u32[]{:S(2)}) collective-permute-start(f32[96,128]{1,0:T(8,128)S(1)} %get-tuple-element.11), channel_id=1, source_target_pairs={{0,5},{1,4},{2,7},{3,6},{4,1},{5,0},{6,3},{7,2},{8,13},{9,12},{10,... | collective-permute-start | bytes 147464 | tf_op jit(solution)/shard_map/ppermute | solution.py:261
  15.9 4.1 %collective-permute-start.10 = (f32[96,128]{1,0:T(8,128)S(1)}, f32[96,128]{1,0:T(8,128)S(1)}, u32[]{:S(2)}, u32[]{:S(2)}) collective-permute-start(f32[96,128]{1,0:T(8,128)S(1)} %get-tuple-element.12), channel_id=1, source_target_pairs={{0,4},{1,5},{2,6},{3,7},{4,0},{5,1},{6,2},{7,3},{8,12},{9,13},{10,... | collective-permute-start | bytes 147464 | tf_op jit(solution)/shard_map/ppermute | solution.py:261

commit v15 on v14

--- a/solution.py
+++ b/solution.py
@@ -168,27 +168,30 @@
     act_corrupt = jnp.maximum(preact[total : 2 * total], 0.0)
     attribution = (act_corrupt - act_clean) * preact[2 * total :]
 
-    devices = groups * parts
-    feature_part = jnp.sum(attribution, axis=0, keepdims=True)
-    sums[:, 0, :] = jnp.broadcast_to(feature_part, (devices, LANES))
+    sums[pl.ds(0, 1), :] = jnp.sum(attribution, axis=0, keepdims=True)
     token_part = jnp.sum(attribution, axis=1, keepdims=True)
     lane = lax.broadcasted_iota(jnp.int32, (tokens, LANES), 1)
-    place = lane == lax.broadcasted_iota(jnp.int32, (tokens, LANES), 0)
+    token = lax.broadcasted_iota(jnp.int32, (tokens, LANES), 0)
+    held = [jnp.zeros((1, LANES), jnp.float32) for _ in range(sums.shape[0] - 1)]
     for k, (p, q) in enumerate(row_blocks(sections, feats)):
         column = jnp.broadcast_to(token_part[k * tokens : (k + 1) * tokens], (tokens, LANES))
         if (p, q) == (1, 0):
             column = column - inner[pl.ds(0, tokens), :]
-        row = jnp.sum(jnp.where(place, column, 0.0), axis=0, keepdims=True)
-        owner = (section ^ q) * feats + (feat ^ 1 ^ p)
-        sums[pl.ds(owner * parts, parts), 1, :] = jnp.broadcast_to(row, (parts, LANES))
+        first = ((section ^ q) * feats + (feat ^ 1 ^ p)) * tokens
+        for i in range(len(held)):
+            place = lane == token + (first - i * LANES)
+            held[i] = held[i] + jnp.sum(jnp.where(place, column, 0.0), axis=0, keepdims=True)
+    for i, row in enumerate(held):
+        sums[pl.ds(1 + i, 1), :] = row
 
 
 def attributions(sizes, terms, inner):
-    sections, feats, parts = sizes
+    parts = sizes[2]
+    token_rows = -(-terms[0].shape[0] // 3 // LANES)
     vmem = pl.BlockSpec(memory_space=pltpu.VMEM)
     return pl.pallas_call(
         functools.partial(attribution_kernel, sizes),
-        out_shape=jax.ShapeDtypeStruct((sections * feats * parts, 2, LANES), jnp.float32),
+        out_shape=jax.ShapeDtypeStruct((1 + token_rows, LANES), jnp.float32),
         in_specs=[vmem] * (parts + 1),
         out_specs=vmem,
         compiler_params=pltpu.CompilerParams(vmem_limit_bytes=16 * 2**20),
@@ -204,8 +207,11 @@
         features[pl.ds(i * LANES, LANES)] = mine[i]
     feature_copy = pltpu.make_async_copy(features, feature_out, sems.at[0])
     feature_copy.start()
-    owed = add_up([arrived[i, 1:2, :] for i in range(sections * feats * parts)])
-    errors[...] = -owed[0, : errors.shape[0]]
+    tokens = errors.shape[0]
+    own = lax.axis_index("section") * feats + lax.axis_index("feat")
+    row, first = own * tokens // LANES, lax.rem(own * tokens, LANES)
+    owed = add_up([arrived[i, pl.ds(1 + row, 1), :] for i in range(sections * feats * parts)])
+    errors[...] = -pltpu.roll(owed, lax.rem(LANES - first, LANES), 1)[0, :tokens]
     error_copy = pltpu.make_async_copy(errors, error_out, sems.at[1])
     error_copy.start()
     feature_copy.wait()
@@ -266,7 +272,7 @@
         for m in reversed(range(parts))
     ]
     sums = attributions(sizes, arrived, inner)
-    return tuple(final(sizes, tokens, lax.all_to_all(sums, EVERY, 0, 0)))
+    return tuple(final(sizes, tokens, lax.all_gather(sums, EVERY)))
 
 
 def solution(mesh):

time: 32.2 us -> 87.9 us (2.73)
  blocking collectives: 11.2 us -> 66.8 us
    all_gather x0 -> x1, blocking collectives: none -> 66.8 us  [per_device(): return tuple(final(sizes, tokens, lax.all_gather(sums, EVERY)))]
    all_to_all x1 -> x0, blocking collectives: 11.2 us -> none  [per_device(): return tuple(final(sizes, tokens, lax.all_to_all(sums, EVERY, 0, 0)))]
where the time goes in v15:
time: 87.9 us; the launch traced here: 87.6 us
  blocking collectives  66.8 us (76%)
  starting transfers between devices  10.7 us (12%)
  waiting for transfers between devices  6.58 us (7%)
  Pallas kernels  1.96 us (2%)
    all_gather x1, blocking collectives, per_device(): return tuple(final(sizes, tokens, lax.all_gather(sums, EVERY)))  66.8 us
    ppermute x4, starting transfers between devices, per_device(): held[p, q] = lax.ppermute(packed, ('section', 'feat'), pairs)  5.37 us
    ppermute x4, starting transfers between devices, per_device(): lax.ppermute(terms[m], ('feat', 'tensor'), [(f * parts + t, (f ^ 1) * par...  4.29 us
    ppermute x4, waiting for transfers between devices, per_device(): lax.ppermute(terms[m], ('feat', 'tensor'), [(f * parts + t, (f ^ 1) * par...  3.81 us
    ppermute x4, waiting for transfers between devices, per_device(): held[p, q] = lax.ppermute(packed, ('section', 'feat'), pairs)  2.52 us
  transfers between devices with their start and end apart: 11, of which 5 were waited for; matrix products, arithmetic and copies ran while one was open for 0% of the time, Pallas kernels for 0%

profile of v15, /device:TPU:0, one launch (start us, length us, event | category | flops | bytes accessed | tf_op | source)
XLA Modules:
  0.0 87.6 jit_solution(14240571685763589906)
XLA Ops:
  0.6 0.8 pad_maximum_fusion.packed.refs_0_
  1.4 0.0 copy-start
  1.4 0.0 copy-start.1
  1.4 0.0 copy-start.2
  1.5 4.0 %collective-permute-start.3 = (bf16[3,4,2048]{2,1,0:T(4,128)(2,1)S(1)}, bf16[3,4,2048]{2,1,0:T(4,128)(2,1)S(1)}, u32[]{:S(2)}, u32[]{:S(2)}) collective-permute-start(bf16[3,4,2048]{2,1,0:T(4,128)(2,1)S(1)} %pad_maximum_fusion.packed.refs_0_), channel_id=1, source_target_pairs={{0,24},{4,28},{8,16},{12,20},{16,8},{20,12},{24,0},{28,4},{1,25},{... | collective-permute-start | bytes 147464 | tf_op jit(solution)/shard_map/ppermute | solution.py:257
  5.4 0.5 collective-permute-start.2
  5.9 0.9 %collective-permute-start = (bf16[3,4,2048]{2,1,0:T(4,128)(2,1)S(1)}, bf16[3,4,2048]{2,1,0:T(4,128)(2,1)S(1)}, u32[]{:S(2)}, u32[]{:S(2)}) collective-permute-start(bf16[3,4,2048]{2,1,0:T(4,128)(2,1)S(1)} %pad_maximum_fusion.packed.refs_0_), channel_id=1, source_target_pairs={{0,8},{4,12},{8,0},{12,4},{16,24},{20,28},{24,16},{28,20},{1,9},{5... | collective-permute-start | bytes 147464 | tf_op jit(solution)/shard_map/ppermute | solution.py:257
  6.8 0.1 inner_products.1.refs_4_
  6.9 1.0 %collective-permute-start.4 = (bf16[3,4,2048]{2,1,0:T(4,128)(2,1)S(1)}, bf16[3,4,2048]{2,1,0:T(4,128)(2,1)S(1)}, u32[]{:S(2)}, u32[]{:S(2)}) collective-permute-start(bf16[3,4,2048]{2,1,0:T(4,128)(2,1)S(1)} %pad_maximum_fusion.packed.refs_0_), channel_id=1, source_target_pairs={{0,4},{4,0},{1,5},{5,1},{2,6},{6,2},{3,7},{7,3},{8,12},{12,8},{9,1... | collective-permute-start | bytes 147464 | tf_op jit(solution)/shard_map/ppermute | solution.py:23
  7.9 0.1 collective-permute-start.6
  8.0 1.5 %collective-permute-done.2.refs_3_ = bf16[3,4,2048]{2,1,0:T(4,128)(2,1)S(1)} collective-permute-done((bf16[3,4,2048]{2,1,0:T(4,128)(2,1)S(1)}, bf16[3,4,2048]{2,1,0:T(4,128)(2,1)S(1)}, u32[]{:S(2)}, u32[]{:S(2)}) %collective-permute-start.2) | collective-permute-done | bytes 49184 | tf_op jit(solution)/shard_map/ppermute | solution.py:257
  9.5 0.0 collective-permute-start.5
  9.5 0.0 collective-permute-done.4.refs_5_
  9.5 1.0 %collective-permute-done.refs_1_ = bf16[3,4,2048]{2,1,0:T(4,128)(2,1)S(1)} collective-permute-done((bf16[3,4,2048]{2,1,0:T(4,128)(2,1)S(1)}, bf16[3,4,2048]{2,1,0:T(4,128)(2,1)S(1)}, u32[]{:S(2)}, u32[]{:S(2)}) %collective-permute-start) | collective-permute-done | bytes 49184 | tf_op jit(solution)/shard_map/ppermute | solution.py:257
  10.5 0.2 collective-permute-done.5.refs_6_
  10.8 1.1 %products.1 = (f32[96,128]{1,0:T(8,128)S(1)}, f32[96,128]{1,0:T(8,128)S(1)}, f32[96,128]{1,0:T(8,128)S(1)}, f32[96,128]{1,0:T(8,128)S(1)}) custom-call(bf16[3,4,2048]{2,1,0:T(4,128)(2,1)S(1)} %pad_maximum_fusion.packed.refs_0_, bf16[3,4,2048]{2,1,0:T(4,128)(2,1)S(1)} %collective-permute-done.refs_1_, bf16[3,4,2048]{2,1,0:T(4,128)(2,1)S(1)} %collective-permute-done.1.refs_2_, ...), custom_call_target="tpu_custom_call" | custom-call | tf_op jit(solution)/shard_map/products/pallas_call | solution.py:138
  11.9 3.4 %collective-permute-start.7 = (f32[96,128]{1,0:T(8,128)S(1)}, f32[96,128]{1,0:T(8,128)S(1)}, u32[]{:S(2)}, u32[]{:S(2)}) collective-permute-start(f32[96,128]{1,0:T(8,128)S(1)} %get-tuple-element.9), channel_id=1, source_target_pairs={{0,7},{1,6},{2,5},{3,4},{4,3},{5,2},{6,1},{7,0},{8,15},{9,14},{10,... | collective-permute-start | bytes 147464 | tf_op jit(solution)/shard_map/ppermute | solution.py:267
  15.3 0.6 collective-permute-start.9
  15.9 0.3 collective-permute-start.10
  16.2 1.4 %collective-permute-done.7.refs_0_ = f32[96,128]{1,0:T(8,128)S(1)} collective-permute-done((f32[96,128]{1,0:T(8,128)S(1)}, f32[96,128]{1,0:T(8,128)S(1)}, u32[]{:S(2)}, u32[]{:S(2)}) %collective-permute-start.7) | collective-permute-done | bytes 49184 | tf_op jit(solution)/shard_map/ppermute | solution.py:267
  17.6 2.4 %collective-permute-done.8.refs_1_ = f32[96,128]{1,0:T(8,128)S(1)} collective-permute-done((f32[96,128]{1,0:T(8,128)S(1)}, f32[96,128]{1,0:T(8,128)S(1)}, u32[]{:S(2)}, u32[]{:S(2)}) %collective-permute-start.8) | collective-permute-done | bytes 49184 | tf_op jit(solution)/shard_map/ppermute | solution.py:267
  20.0 0.1 attributions.1
  20.1 66.8 %all-gather.1.arrived = f32[32,2,128]{2,1,0:T(2,128)S(1)} all-gather(f32[1,2,128]{2,1,0:T(2,128)S(1)} %bitcast.5), channel_id=2, replica_groups=mesh['section'=4,'feat'=2,'tensor'=4] {'section','feat','tensor'}, dimensions={0}, use_global_device_ids=true | all-gather | bytes 33792 | tf_op jit(solution)/shard_map/all_gather | solution.py:275
  87.0 0.6 final.1
  (10 shorter events, 0.0 us)
Async XLA Ops:
  1.4 9.3 %copy-start = (bf16[2048,512]{1,0:T(8,128)(2,1)S(1)}, bf16[2048,512]{1,0:T(8,128)(2,1)}, u32[]{:S(2)}) copy-start(bf16[2048,512]{1,0:T(8,128)(2,1)} %refs_8_.1) | copy-start | bytes 6291460
  1.4 9.3 %copy-start.1 = (bf16[512,2048]{1,0:T(8,128)(2,1)S(1)}, bf16[512,2048]{1,0:T(8,128)(2,1)}, u32[]{:S(2)}) copy-start(bf16[512,2048]{1,0:T(8,128)(2,1)} %refs_9_.1) | copy-start | bytes 6291460
  1.4 9.3 %copy-start.2 = (f32[512]{0:T(512)S(1)}, f32[512]{0:T(512)}, u32[]{:S(2)}) copy-start(f32[512]{0:T(512)} %param.10) | copy-start | bytes 6148
  1.5 6.4 %collective-permute-start.3 = (bf16[3,4,2048]{2,1,0:T(4,128)(2,1)S(1)}, bf16[3,4,2048]{2,1,0:T(4,128)(2,1)S(1)}, u32[]{:S(2)}, u32[]{:S(2)}) collective-permute-start(bf16[3,4,2048]{2,1,0:T(4,128)(2,1)S(1)} %pad_maximum_fusion.packed.refs_0_), channel_id=1, source_target_pairs={{0,24},{4,28},{8,16},{12,20},{16,8},{20,12},{24,0},{28,4},{1,25},{... | collective-permute-start | bytes 147464 | tf_op jit(solution)/shard_map/ppermute | solution.py:257
  5.4 4.1 %collective-permute-start.2 = (bf16[3,4,2048]{2,1,0:T(4,128)(2,1)S(1)}, bf16[3,4,2048]{2,1,0:T(4,128)(2,1)S(1)}, u32[]{:S(2)}, u32[]{:S(2)}) collective-permute-start(bf16[3,4,2048]{2,1,0:T(4,128)(2,1)S(1)} %pad_maximum_fusion.packed.refs_0_), channel_id=1, source_target_pairs={{0,16},{4,20},{8,24},{12,28},{16,0},{20,4},{24,8},{28,12},{1,17},{... | collective-permute-start | bytes 147464 | tf_op jit(solution)/shard_map/ppermute | solution.py:257
  5.9 3.6 %collective-permute-start.1 = (bf16[3,4,2048]{2,1,0:T(4,128)(2,1)S(1)}, bf16[3,4,2048]{2,1,0:T(4,128)(2,1)S(1)}, u32[]{:S(2)}, u32[]{:S(2)}) collective-permute-start(bf16[3,4,2048]{2,1,0:T(4,128)(2,1)S(1)} %pad_maximum_fusion.packed.refs_0_), channel_id=1, source_target_pairs={{0,12},{4,8},{8,4},{12,0},{16,28},{20,24},{24,20},{28,16},{1,13},{... | collective-permute-start | bytes 147464 | tf_op jit(solution)/shard_map/ppermute | solution.py:257
  5.9 4.6 %collective-permute-start = (bf16[3,4,2048]{2,1,0:T(4,128)(2,1)S(1)}, bf16[3,4,2048]{2,1,0:T(4,128)(2,1)S(1)}, u32[]{:S(2)}, u32[]{:S(2)}) collective-permute-start(bf16[3,4,2048]{2,1,0:T(4,128)(2,1)S(1)} %pad_maximum_fusion.packed.refs_0_), channel_id=1, source_target_pairs={{0,8},{4,12},{8,0},{12,4},{16,24},{20,28},{24,16},{28,20},{1,9},{5... | collective-permute-start | bytes 147464 | tf_op jit(solution)/shard_map/ppermute | solution.py:257
  6.9 2.6 %collective-permute-start.4 = (bf16[3,4,2048]{2,1,0:T(4,128)(2,1)S(1)}, bf16[3,4,2048]{2,1,0:T(4,128)(2,1)S(1)}, u32[]{:S(2)}, u32[]{:S(2)}) collective-permute-start(bf16[3,4,2048]{2,1,0:T(4,128)(2,1)S(1)} %pad_maximum_fusion.packed.refs_0_), channel_id=1, source_target_pairs={{0,4},{4,0},{1,5},{5,1},{2,6},{6,2},{3,7},{7,3},{8,12},{12,8},{9,1... | collective-permute-start | bytes 147464 | tf_op jit(solution)/shard_map/ppermute | solution.py:23
  7.9 2.6 %collective-permute-start.6 = (bf16[3,4,2048]{2,1,0:T(4,128)(2,1)S(1)}, bf16[3,4,2048]{2,1,0:T(4,128)(2,1)S(1)}, u32[]{:S(2)}, u32[]{:S(2)}) collective-permute-start(bf16[3,4,2048]{2,1,0:T(4,128)(2,1)S(1)} %collective-permute-done.3.refs_4_), channel_id=1, source_target_pairs={{0,4},{4,0},{1,5},{5,1},{2,6},{6,2},{3,7},{7,3},{8,12},{12,8},{9,1... | collective-permute-start | bytes 147464 | tf_op jit(solution)/shard_map/ppermute | solution.py:23
  9.5 1.2 %collective-permute-start.5 = (bf16[3,4,2048]{2,1,0:T(4,128)(2,1)S(1)}, bf16[3,4,2048]{2,1,0:T(4,128)(2,1)S(1)}, u32[]{:S(2)}, u32[]{:S(2)}) collective-permute-start(bf16[3,4,2048]{2,1,0:T(4,128)(2,1)S(1)} %collective-permute-done.2.refs_3_), channel_id=1, source_target_pairs={{0,4},{4,0},{1,5},{5,1},{2,6},{6,2},{3,7},{7,3},{8,12},{12,8},{9,1... | collective-permute-start | bytes 147464 | tf_op jit(solution)/shard_map/ppermute | solution.py:23
  11.9 5.7 %collective-permute-start.7 = (f32[96,128]{1,0:T(8,128)S(1)}, f32[96,128]{1,0:T(8,128)S(1)}, u32[]{:S(2)}, u32[]{:S(2)}) collective-permute-start(f32[96,128]{1,0:T(8,128)S(1)} %get-tuple-element.9), channel_id=1, source_target_pairs={{0,7},{1,6},{2,5},{3,4},{4,3},{5,2},{6,1},{7,0},{8,15},{9,14},{10,... | collective-permute-start | bytes 147464 | tf_op jit(solution)/shard_map/ppermute | solution.py:267
  15.3 4.7 %collective-permute-start.8 = (f32[96,128]{1,0:T(8,128)S(1)}, f32[96,128]{1,0:T(8,128)S(1)}, u32[]{:S(2)}, u32[]{:S(2)}) collective-permute-start(f32[96,128]{1,0:T(8,128)S(1)} %get-tuple-element.10), channel_id=1, source_target_pairs={{0,6},{1,7},{2,4},{3,5},{4,2},{5,3},{6,0},{7,1},{8,14},{9,15},{10,... | collective-permute-start | bytes 147464 | tf_op jit(solution)/shard_map/ppermute | solution.py:267
  15.3 4.7 %collective-permute-start.9 = (f32[96,128]{1,0:T(8,128)S(1)}, f32[96,128]{1,0:T(8,128)S(1)}, u32[]{:S(2)}, u32[]{:S(2)}) collective-permute-start(f32[96,128]{1,0:T(8,128)S(1)} %get-tuple-element.11), channel_id=1, source_target_pairs={{0,5},{1,4},{2,7},{3,6},{4,1},{5,0},{6,3},{7,2},{8,13},{9,12},{10,... | collective-permute-start | bytes 147464 | tf_op jit(solution)/shard_map/ppermute | solution.py:267
  15.9 4.1 %collective-permute-start.10 = (f32[96,128]{1,0:T(8,128)S(1)}, f32[96,128]{1,0:T(8,128)S(1)}, u32[]{:S(2)}, u32[]{:S(2)}) collective-permute-start(f32[96,128]{1,0:T(8,128)S(1)} %get-tuple-element.12), channel_id=1, source_target_pairs={{0,4},{1,5},{2,6},{3,7},{4,0},{5,1},{6,2},{7,3},{8,12},{9,13},{10,... | collective-permute-start | bytes 147464 | tf_op jit(solution)/shard_map/ppermute | solution.py:267

commit v16 on v14

--- a/solution.py
+++ b/solution.py
@@ -12,6 +12,10 @@
 
 
 EVERY = ("section", "feat", "tensor")
+
+
+def rotations(size):
+    return sorted(range(size), key=lambda r: (r != size // 2, r == 0, r == 1, -r))
 
 
 def row_blocks(sections, feats):
@@ -123,9 +127,10 @@
         held[c, pl.ds(0, 2 * total), :] = encoded[:, c * share : (c + 1) * share]
         held[c, pl.ds(2 * total, total), :] = projected[:, c * share : (c + 1) * share]
     me = lax.axis_index("tensor")
-    for m, out in enumerate(outs):
-        out[...] = held[me ^ m]
-    outs[0][pl.ds(0, 2 * total), :] += bias[pl.ds(me, 1), :]
+    for r, out in zip(rotations(parts), outs):
+        out[...] = held[lax.rem(me + r, parts)]
+        if r == 0:
+            out[pl.ds(0, 2 * total), :] += bias[pl.ds(me, 1), :]
 
 
 def products(parts, blocks, enc_weight, dec_weight, bias):
@@ -257,14 +262,14 @@
     blocks = [held[place] for place in row_blocks(sections, feats)]
 
     terms = products(parts, blocks, enc_weight, dec_weight, bias)
-    arrived = [
-        lax.ppermute(
-            terms[m],
-            ("feat", "tensor"),
-            [(f * parts + t, (f ^ 1) * parts + (t ^ m)) for f in range(feats) for t in range(parts)],
-        )
-        for m in reversed(range(parts))
-    ]
+    arrived = []
+    for r, term in zip(rotations(parts), terms):
+        pairs = [
+            (f * parts + t, (f ^ 1) * parts + (t + r) % parts)
+            for f in range(feats)
+            for t in range(parts)
+        ]
+        arrived.append(lax.ppermute(term, ("feat", "tensor"), pairs))
     sums = attributions(sizes, arrived, inner)
     return tuple(final(sizes, tokens, lax.all_to_all(sums, EVERY, 0, 0)))
 

time: 32.2 us -> 32.2 us (level)
  blocking collectives: 11.2 us -> 10.1 us
  waiting for transfers between devices: 6.58 us -> 7.48 us
    all_to_all x1, blocking collectives: 11.2 us -> 10.1 us  [per_device(): return tuple(final(sizes, tokens, lax.all_to_all(sums, EVERY, 0, 0)))]
    ppermute x4, waiting for transfers between devices: 3.81 us -> 4.71 us  [per_device(): arrived.append(lax.ppermute(term, ('feat', 'tensor'), pairs))]
  transfers between devices with their start and end apart: 11 -> 11, of which waited for: 5 -> 6; matrix products, arithmetic and copies ran while one was open for 0% -> 0% of each run, Pallas kernels for 0% -> 0%
where the time goes in v16:
time: 32.2 us; the launch traced here: 31.9 us
  starting transfers between devices  10.9 us (34%)
  blocking collectives  10.1 us (31%)
  waiting for transfers between devices  7.48 us (23%)
  Pallas kernels  1.97 us (6%)
  other arithmetic  0.79 us (2%)
  between operations  0.69 us (2%)
    all_to_all x1, blocking collectives, per_device(): return tuple(final(sizes, tokens, lax.all_to_all(sums, EVERY, 0, 0)))  10.1 us
    ppermute x4, starting transfers between devices, per_device(): held[p, q] = lax.ppermute(packed, ('section', 'feat'), pairs)  5.37 us
    ppermute x4, waiting for transfers between devices, per_device(): arrived.append(lax.ppermute(term, ('feat', 'tensor'), pairs))  4.71 us
    ppermute x4, starting transfers between devices, per_device(): arrived.append(lax.ppermute(term, ('feat', 'tensor'), pairs))  4.52 us
    ppermute x4, waiting for transfers between devices, per_device(): held[p, q] = lax.ppermute(packed, ('section', 'feat'), pairs)  2.52 us
    pallas_call x1, Pallas kernels, products(): pl.pallas_call(functools.partial(product_kernel, groups, parts), out_shap...  1.15 us
    ppermute x3, starting transfers between devices, exchange(): return lax.ppermute(value, axis, [(i, i ^ k) for i in range(size)])  1.03 us
    another operation x1, other arithmetic, per_device(): packed = jnp.stack([clean_resid, corrupt_resid, metric_grad])  0.79 us
  transfers between devices with their start and end apart: 11, of which 6 were waited for; matrix products, arithmetic and copies ran while one was open for 0% of the time, Pallas kernels for 0%

profile of v16, /device:TPU:0, one launch (start us, length us, event | category | flops | bytes accessed | tf_op | source)
XLA Modules:
  0.0 31.9 jit_solution(11310821325352176258)
XLA Ops:
  0.6 0.8 %pad_maximum_fusion.packed.refs_0_ = bf16[3,4,2048]{2,1,0:T(4,128)(2,1)S(1)} fusion(bf16[1,4,2048]{2,1,0:T(4,128)(2,1)} %bitcast.5, bf16[1,4,2048]{2,1,0:T(4,128)(2,1)} %bitcast.6, bf16[1,4,2048]{2,1,0:T(4,128)(2,1)} %bitcast.7), kind=kLoop, calls=%fused_computation | loop fusion | flops 49152 | bytes 98304 | tf_op jit(solution)/shard_map/stack | solution.py:245
  1.4 0.0 copy-start
  1.4 0.0 copy-start.1
  1.4 0.0 copy-start.2
  1.5 4.0 %collective-permute-start.3 = (bf16[3,4,2048]{2,1,0:T(4,128)(2,1)S(1)}, bf16[3,4,2048]{2,1,0:T(4,128)(2,1)S(1)}, u32[]{:S(2)}, u32[]{:S(2)}) collective-permute-start(bf16[3,4,2048]{2,1,0:T(4,128)(2,1)S(1)} %pad_maximum_fusion.packed.refs_0_), channel_id=1, source_target_pairs={{0,24},{4,28},{8,16},{12,20},{16,8},{20,12},{24,0},{28,4},{1,25},{... | collective-permute-start | bytes 147464 | tf_op jit(solution)/shard_map/ppermute | solution.py:256
  5.4 0.5 %collective-permute-start.2 = (bf16[3,4,2048]{2,1,0:T(4,128)(2,1)S(1)}, bf16[3,4,2048]{2,1,0:T(4,128)(2,1)S(1)}, u32[]{:S(2)}, u32[]{:S(2)}) collective-permute-start(bf16[3,4,2048]{2,1,0:T(4,128)(2,1)S(1)} %pad_maximum_fusion.packed.refs_0_), channel_id=1, source_target_pairs={{0,16},{4,20},{8,24},{12,28},{16,0},{20,4},{24,8},{28,12},{1,17},{... | collective-permute-start | bytes 147464 | tf_op jit(solution)/shard_map/ppermute | solution.py:256
  5.9 0.9 %collective-permute-start = (bf16[3,4,2048]{2,1,0:T(4,128)(2,1)S(1)}, bf16[3,4,2048]{2,1,0:T(4,128)(2,1)S(1)}, u32[]{:S(2)}, u32[]{:S(2)}) collective-permute-start(bf16[3,4,2048]{2,1,0:T(4,128)(2,1)S(1)} %pad_maximum_fusion.packed.refs_0_), channel_id=1, source_target_pairs={{0,8},{4,12},{8,0},{12,4},{16,24},{20,28},{24,16},{28,20},{1,9},{5... | collective-permute-start | bytes 147464 | tf_op jit(solution)/shard_map/ppermute | solution.py:256
  6.8 0.1 inner_products.1.refs_4_
  6.9 1.0 %collective-permute-start.4 = (bf16[3,4,2048]{2,1,0:T(4,128)(2,1)S(1)}, bf16[3,4,2048]{2,1,0:T(4,128)(2,1)S(1)}, u32[]{:S(2)}, u32[]{:S(2)}) collective-permute-start(bf16[3,4,2048]{2,1,0:T(4,128)(2,1)S(1)} %pad_maximum_fusion.packed.refs_0_), channel_id=1, source_target_pairs={{0,4},{4,0},{1,5},{5,1},{2,6},{6,2},{3,7},{7,3},{8,12},{12,8},{9,1... | collective-permute-start | bytes 147464 | tf_op jit(solution)/shard_map/ppermute | solution.py:27
  7.9 0.1 collective-permute-start.6
  8.0 1.5 %collective-permute-done.2.refs_3_ = bf16[3,4,2048]{2,1,0:T(4,128)(2,1)S(1)} collective-permute-done((bf16[3,4,2048]{2,1,0:T(4,128)(2,1)S(1)}, bf16[3,4,2048]{2,1,0:T(4,128)(2,1)S(1)}, u32[]{:S(2)}, u32[]{:S(2)}) %collective-permute-start.2) | collective-permute-done | bytes 49184 | tf_op jit(solution)/shard_map/ppermute | solution.py:256
  9.5 1.0 %collective-permute-done.refs_1_ = bf16[3,4,2048]{2,1,0:T(4,128)(2,1)S(1)} collective-permute-done((bf16[3,4,2048]{2,1,0:T(4,128)(2,1)S(1)}, bf16[3,4,2048]{2,1,0:T(4,128)(2,1)S(1)}, u32[]{:S(2)}, u32[]{:S(2)}) %collective-permute-start) | collective-permute-done | bytes 49184 | tf_op jit(solution)/shard_map/ppermute | solution.py:256
  10.5 0.2 collective-permute-done.5.refs_6_
  10.8 1.2 %products.1 = (f32[96,128]{1,0:T(8,128)S(1)}, f32[96,128]{1,0:T(8,128)S(1)}, f32[96,128]{1,0:T(8,128)S(1)}, f32[96,128]{1,0:T(8,128)S(1)}) custom-call(bf16[3,4,2048]{2,1,0:T(4,128)(2,1)S(1)} %pad_maximum_fusion.packed.refs_0_, bf16[3,4,2048]{2,1,0:T(4,128)(2,1)S(1)} %collective-permute-done.refs_1_, bf16[3,4,2048]{2,1,0:T(4,128)(2,1)S(1)} %collective-permute-done.1.refs_2_, ...), custom_call_target="tpu_custom_call" | custom-call | tf_op jit(solution)/shard_map/products/pallas_call | solution.py:143
  11.9 2.4 %collective-permute-start.7 = (f32[96,128]{1,0:T(8,128)S(1)}, f32[96,128]{1,0:T(8,128)S(1)}, u32[]{:S(2)}, u32[]{:S(2)}) collective-permute-start(f32[96,128]{1,0:T(8,128)S(1)} %get-tuple-element.9), channel_id=1, source_target_pairs={{0,6},{1,7},{2,4},{3,5},{4,2},{5,3},{6,0},{7,1},{8,14},{9,15},{10,... | collective-permute-start | bytes 147464 | tf_op jit(solution)/shard_map/ppermute | solution.py:272
  14.3 1.3 %collective-permute-start.8 = (f32[96,128]{1,0:T(8,128)S(1)}, f32[96,128]{1,0:T(8,128)S(1)}, u32[]{:S(2)}, u32[]{:S(2)}) collective-permute-start(f32[96,128]{1,0:T(8,128)S(1)} %get-tuple-element.10), channel_id=1, source_target_pairs={{0,7},{1,4},{2,5},{3,6},{4,3},{5,0},{6,1},{7,2},{8,15},{9,12},{10,... | collective-permute-start | bytes 147464 | tf_op jit(solution)/shard_map/ppermute | solution.py:272
  15.6 0.4 %collective-permute-start.9 = (f32[96,128]{1,0:T(8,128)S(1)}, f32[96,128]{1,0:T(8,128)S(1)}, u32[]{:S(2)}, u32[]{:S(2)}) collective-permute-start(f32[96,128]{1,0:T(8,128)S(1)} %get-tuple-element.11), channel_id=1, source_target_pairs={{0,5},{1,6},{2,7},{3,4},{4,1},{5,2},{6,3},{7,0},{8,13},{9,14},{10,... | collective-permute-start | bytes 147464 | tf_op jit(solution)/shard_map/ppermute | solution.py:272
  16.1 0.3 %collective-permute-start.10 = (f32[96,128]{1,0:T(8,128)S(1)}, f32[96,128]{1,0:T(8,128)S(1)}, u32[]{:S(2)}, u32[]{:S(2)}) collective-permute-start(f32[96,128]{1,0:T(8,128)S(1)} %get-tuple-element.12), channel_id=1, source_target_pairs={{0,4},{1,5},{2,6},{3,7},{4,0},{5,1},{6,2},{7,3},{8,12},{9,13},{10,... | collective-permute-start | bytes 147464 | tf_op jit(solution)/shard_map/ppermute | solution.py:272
  16.4 0.1 collective-permute-done.7.refs_0_
  16.6 1.3 %collective-permute-done.8.refs_1_ = f32[96,128]{1,0:T(8,128)S(1)} collective-permute-done((f32[96,128]{1,0:T(8,128)S(1)}, f32[96,128]{1,0:T(8,128)S(1)}, u32[]{:S(2)}, u32[]{:S(2)}) %collective-permute-start.8) | collective-permute-done | bytes 49184 | tf_op jit(solution)/shard_map/ppermute | solution.py:272
  17.9 3.3 %collective-permute-done.9.refs_2_ = f32[96,128]{1,0:T(8,128)S(1)} collective-permute-done((f32[96,128]{1,0:T(8,128)S(1)}, f32[96,128]{1,0:T(8,128)S(1)}, u32[]{:S(2)}, u32[]{:S(2)}) %collective-permute-start.9) | collective-permute-done | bytes 49184 | tf_op jit(solution)/shard_map/ppermute | solution.py:272
  21.1 0.1 attributions.1
  21.3 10.1 %all_to_all.5.arrived = f32[32,2,128]{2,1,0:T(2,128)S(1)} all-to-all(f32[32,2,128]{2,1,0:T(2,128)S(1)} %attributions.1), channel_id=1, replica_groups=mesh['section'=4,'feat'=2,'tensor'=4] {'section','feat','tensor'}, dimensions={0} | all-to-all | bytes 65536 | tf_op jit(solution)/shard_map/all_to_all | solution.py:274
  31.3 0.6 %final.1 = (f32[512]{0:T(512)}, f32[4]{0:T(128)}) custom-call(f32[32,2,128]{2,1,0:T(2,128)S(1)} %all_to_all.5.arrived), custom_call_target="tpu_custom_call" | custom-call | tf_op jit(solution)/shard_map/final/pallas_call | solution.py:222
  (10 shorter events, 0.0 us)
Async XLA Ops:
  1.4 9.3 %copy-start = (bf16[2048,512]{1,0:T(8,128)(2,1)S(1)}, bf16[2048,512]{1,0:T(8,128)(2,1)}, u32[]{:S(2)}) copy-start(bf16[2048,512]{1,0:T(8,128)(2,1)} %refs_8_.1) | copy-start | bytes 6291460
  1.4 9.3 %copy-start.1 = (bf16[512,2048]{1,0:T(8,128)(2,1)S(1)}, bf16[512,2048]{1,0:T(8,128)(2,1)}, u32[]{:S(2)}) copy-start(bf16[512,2048]{1,0:T(8,128)(2,1)} %refs_9_.1) | copy-start | bytes 6291460
  1.4 9.3 %copy-start.2 = (f32[512]{0:T(512)S(1)}, f32[512]{0:T(512)}, u32[]{:S(2)}) copy-start(f32[512]{0:T(512)} %param.10) | copy-start | bytes 6148
  1.5 6.4 %collective-permute-start.3 = (bf16[3,4,2048]{2,1,0:T(4,128)(2,1)S(1)}, bf16[3,4,2048]{2,1,0:T(4,128)(2,1)S(1)}, u32[]{:S(2)}, u32[]{:S(2)}) collective-permute-start(bf16[3,4,2048]{2,1,0:T(4,128)(2,1)S(1)} %pad_maximum_fusion.packed.refs_0_), channel_id=1, source_target_pairs={{0,24},{4,28},{8,16},{12,20},{16,8},{20,12},{24,0},{28,4},{1,25},{... | collective-permute-start | bytes 147464 | tf_op jit(solution)/shard_map/ppermute | solution.py:256
  5.4 4.1 %collective-permute-start.2 = (bf16[3,4,2048]{2,1,0:T(4,128)(2,1)S(1)}, bf16[3,4,2048]{2,1,0:T(4,128)(2,1)S(1)}, u32[]{:S(2)}, u32[]{:S(2)}) collective-permute-start(bf16[3,4,2048]{2,1,0:T(4,128)(2,1)S(1)} %pad_maximum_fusion.packed.refs_0_), channel_id=1, source_target_pairs={{0,16},{4,20},{8,24},{12,28},{16,0},{20,4},{24,8},{28,12},{1,17},{... | collective-permute-start | bytes 147464 | tf_op jit(solution)/shard_map/ppermute | solution.py:256
  5.9 3.6 %collective-permute-start.1 = (bf16[3,4,2048]{2,1,0:T(4,128)(2,1)S(1)}, bf16[3,4,2048]{2,1,0:T(4,128)(2,1)S(1)}, u32[]{:S(2)}, u32[]{:S(2)}) collective-permute-start(bf16[3,4,2048]{2,1,0:T(4,128)(2,1)S(1)} %pad_maximum_fusion.packed.refs_0_), channel_id=1, source_target_pairs={{0,12},{4,8},{8,4},{12,0},{16,28},{20,24},{24,20},{28,16},{1,13},{... | collective-permute-start | bytes 147464 | tf_op jit(solution)/shard_map/ppermute | solution.py:256
  5.9 4.6 %collective-permute-start = (bf16[3,4,2048]{2,1,0:T(4,128)(2,1)S(1)}, bf16[3,4,2048]{2,1,0:T(4,128)(2,1)S(1)}, u32[]{:S(2)}, u32[]{:S(2)}) collective-permute-start(bf16[3,4,2048]{2,1,0:T(4,128)(2,1)S(1)} %pad_maximum_fusion.packed.refs_0_), channel_id=1, source_target_pairs={{0,8},{4,12},{8,0},{12,4},{16,24},{20,28},{24,16},{28,20},{1,9},{5... | collective-permute-start | bytes 147464 | tf_op jit(solution)/shard_map/ppermute | solution.py:256
  6.9 2.6 %collective-permute-start.4 = (bf16[3,4,2048]{2,1,0:T(4,128)(2,1)S(1)}, bf16[3,4,2048]{2,1,0:T(4,128)(2,1)S(1)}, u32[]{:S(2)}, u32[]{:S(2)}) collective-permute-start(bf16[3,4,2048]{2,1,0:T(4,128)(2,1)S(1)} %pad_maximum_fusion.packed.refs_0_), channel_id=1, source_target_pairs={{0,4},{4,0},{1,5},{5,1},{2,6},{6,2},{3,7},{7,3},{8,12},{12,8},{9,1... | collective-permute-start | bytes 147464 | tf_op jit(solution)/shard_map/ppermute | solution.py:27
  7.9 2.6 %collective-permute-start.6 = (bf16[3,4,2048]{2,1,0:T(4,128)(2,1)S(1)}, bf16[3,4,2048]{2,1,0:T(4,128)(2,1)S(1)}, u32[]{:S(2)}, u32[]{:S(2)}) collective-permute-start(bf16[3,4,2048]{2,1,0:T(4,128)(2,1)S(1)} %collective-permute-done.3.refs_4_), channel_id=1, source_target_pairs={{0,4},{4,0},{1,5},{5,1},{2,6},{6,2},{3,7},{7,3},{8,12},{12,8},{9,1... | collective-permute-start | bytes 147464 | tf_op jit(solution)/shard_map/ppermute | solution.py:27
  9.5 1.2 %collective-permute-start.5 = (bf16[3,4,2048]{2,1,0:T(4,128)(2,1)S(1)}, bf16[3,4,2048]{2,1,0:T(4,128)(2,1)S(1)}, u32[]{:S(2)}, u32[]{:S(2)}) collective-permute-start(bf16[3,4,2048]{2,1,0:T(4,128)(2,1)S(1)} %collective-permute-done.2.refs_3_), channel_id=1, source_target_pairs={{0,4},{4,0},{1,5},{5,1},{2,6},{6,2},{3,7},{7,3},{8,12},{12,8},{9,1... | collective-permute-start | bytes 147464 | tf_op jit(solution)/shard_map/ppermute | solution.py:27
  11.9 4.7 %collective-permute-start.7 = (f32[96,128]{1,0:T(8,128)S(1)}, f32[96,128]{1,0:T(8,128)S(1)}, u32[]{:S(2)}, u32[]{:S(2)}) collective-permute-start(f32[96,128]{1,0:T(8,128)S(1)} %get-tuple-element.9), channel_id=1, source_target_pairs={{0,6},{1,7},{2,4},{3,5},{4,2},{5,3},{6,0},{7,1},{8,14},{9,15},{10,... | collective-permute-start | bytes 147464 | tf_op jit(solution)/shard_map/ppermute | solution.py:272
  14.3 3.5 %collective-permute-start.8 = (f32[96,128]{1,0:T(8,128)S(1)}, f32[96,128]{1,0:T(8,128)S(1)}, u32[]{:S(2)}, u32[]{:S(2)}) collective-permute-start(f32[96,128]{1,0:T(8,128)S(1)} %get-tuple-element.10), channel_id=1, source_target_pairs={{0,7},{1,4},{2,5},{3,6},{4,3},{5,0},{6,1},{7,2},{8,15},{9,12},{10,... | collective-permute-start | bytes 147464 | tf_op jit(solution)/shard_map/ppermute | solution.py:272
  15.6 5.5 %collective-permute-start.9 = (f32[96,128]{1,0:T(8,128)S(1)}, f32[96,128]{1,0:T(8,128)S(1)}, u32[]{:S(2)}, u32[]{:S(2)}) collective-permute-start(f32[96,128]{1,0:T(8,128)S(1)} %get-tuple-element.11), channel_id=1, source_target_pairs={{0,5},{1,6},{2,7},{3,4},{4,1},{5,2},{6,3},{7,0},{8,13},{9,14},{10,... | collective-permute-start | bytes 147464 | tf_op jit(solution)/shard_map/ppermute | solution.py:272
  16.1 5.1 %collective-permute-start.10 = (f32[96,128]{1,0:T(8,128)S(1)}, f32[96,128]{1,0:T(8,128)S(1)}, u32[]{:S(2)}, u32[]{:S(2)}) collective-permute-start(f32[96,128]{1,0:T(8,128)S(1)} %get-tuple-element.12), channel_id=1, source_target_pairs={{0,4},{1,5},{2,6},{3,7},{4,0},{5,1},{6,2},{7,3},{8,12},{9,13},{10,... | collective-permute-start | bytes 147464 | tf_op jit(solution)/shard_map/ppermute | solution.py:272

commit v17 on v10

--- a/solution.py
+++ b/solution.py
@@ -105,30 +105,32 @@
     blocks = refs[:groups]
     enc, dec = refs[groups : groups + 2]
     outs = refs[groups + 2 : groups + 2 + parts]
-    rows, held = refs[groups + 2 + parts :]
+    rows = refs[groups + 2 + parts]
     tokens = blocks[0].shape[1]
     total = groups * tokens
-    share = LANES
     for k, block in enumerate(blocks):
         for a in range(3):
             rows[pl.ds(a * total + k * tokens, tokens), :] = block[a].astype(jnp.float32)
-    encoded = jnp.dot(
-        rows[pl.ds(0, 2 * total), :].astype(jnp.bfloat16),
-        enc[...],
-        preferred_element_type=jnp.float32,
-    )
-    projected = lax.dot_general(
-        rows[pl.ds(2 * total, total), :].astype(jnp.bfloat16),
-        dec[...],
-        (((1,), (1,)), ((), ())),
-        preferred_element_type=jnp.float32,
-    )
-    for c in range(parts):
-        held[c, pl.ds(0, 2 * total), :] = encoded[:, c * share : (c + 1) * share]
-        held[c, pl.ds(2 * total, total), :] = projected[:, c * share : (c + 1) * share]
     me = lax.axis_index("tensor")
-    for m, out in enumerate(outs):
-        out[...] = held[me ^ m]
+    low = me % 2 == 0
+    for upper in range(parts // 2):
+        pair = pl.ds(pl.multiple_of((me // 2 ^ upper) * 2 * LANES, 2 * LANES), 2 * LANES)
+        encoded = jnp.dot(
+            rows[pl.ds(0, 2 * total), :].astype(jnp.bfloat16),
+            enc[:, pair],
+            preferred_element_type=jnp.float32,
+        )
+        projected = lax.dot_general(
+            rows[pl.ds(2 * total, total), :].astype(jnp.bfloat16),
+            dec[pair, :],
+            (((1,), (1,)), ((), ())),
+            preferred_element_type=jnp.float32,
+        )
+        for start, value in ((0, encoded), (2 * total, projected)):
+            first, second = value[:, :LANES], value[:, LANES:]
+            place = pl.ds(start, value.shape[0])
+            outs[2 * upper][place, :] = jnp.where(low, first, second)
+            outs[2 * upper + 1][place, :] = jnp.where(low, second, first)
 
 
 def products(parts, blocks, enc_weight, dec_weight):
@@ -145,7 +147,6 @@
         out_specs=[vmem] * parts,
         scratch_shapes=[
             pltpu.VMEM((rows, width), jnp.float32),
-            pltpu.VMEM((parts, rows, features // parts), jnp.float32),
         ],
         compiler_params=pltpu.CompilerParams(vmem_limit_bytes=48 * 2**20),
         name="products",

time: 32.2 us -> 32.2 us (level)
  no operation moved by 1% of the time
where the time goes in v17:
time: 32.2 us; the launch traced here: 31.9 us
  starting transfers between devices  10.9 us (34%)
  blocking collectives  10.7 us (33%)
  waiting for transfers between devices  6.96 us (22%)
  Pallas kernels  1.92 us (6%)
  other arithmetic  0.79 us (2%)
  between operations  0.67 us (2%)
    all_to_all x1, blocking collectives, per_device(): return tuple(final(sizes, tokens, lax.all_to_all(sums, EVERY, 0, 0)))  10.7 us
    ppermute x6, starting transfers between devices, exchange(): return lax.ppermute(value, axis, [(i, i ^ k) for i in range(size)])  5.49 us
    ppermute x4, starting transfers between devices, per_device(): held[p, q] = lax.ppermute(packed, ('section', 'feat'), pairs)  5.37 us
    ppermute x6, waiting for transfers between devices, exchange(): return lax.ppermute(value, axis, [(i, i ^ k) for i in range(size)])  4.46 us
    ppermute x4, waiting for transfers between devices, per_device(): held[p, q] = lax.ppermute(packed, ('section', 'feat'), pairs)  2.51 us
    pallas_call x1, Pallas kernels, products(): pl.pallas_call(functools.partial(product_kernel, groups, parts), out_shap...  1.11 us
    another operation x1, other arithmetic, per_device(): packed = jnp.stack([clean_resid, corrupt_resid, metric_grad])  0.79 us
  transfers between devices with their start and end apart: 10, of which 5 were waited for; matrix products, arithmetic and copies ran while one was open for 0% of the time, Pallas kernels for 0%

profile of v17, /device:TPU:0, one launch (start us, length us, event | category | flops | bytes accessed | tf_op | source)
XLA Modules:
  0.0 31.9 jit_solution(13480210381327160826)
XLA Ops:
  0.6 0.8 %pad_maximum_fusion.packed.refs_0_ = bf16[3,4,2048]{2,1,0:T(4,128)(2,1)S(1)} fusion(bf16[1,4,2048]{2,1,0:T(4,128)(2,1)} %bitcast.5, bf16[1,4,2048]{2,1,0:T(4,128)(2,1)} %bitcast.6, bf16[1,4,2048]{2,1,0:T(4,128)(2,1)} %bitcast.7), kind=kLoop, calls=%fused_computation | loop fusion | flops 49152 | bytes 98304 | tf_op jit(solution)/shard_map/stack | solution.py:245
  1.4 0.0 copy-start
  1.4 0.0 copy-start.1
  1.4 4.0 %collective-permute-start.3 = (bf16[3,4,2048]{2,1,0:T(4,128)(2,1)S(1)}, bf16[3,4,2048]{2,1,0:T(4,128)(2,1)S(1)}, u32[]{:S(2)}, u32[]{:S(2)}) collective-permute-start(bf16[3,4,2048]{2,1,0:T(4,128)(2,1)S(1)} %pad_maximum_fusion.packed.refs_0_), channel_id=1, source_target_pairs={{0,24},{4,28},{8,16},{12,20},{16,8},{20,12},{24,0},{28,4},{1,25},{... | collective-permute-start | bytes 147464 | tf_op jit(solution)/shard_map/ppermute | solution.py:256
  5.4 0.5 %collective-permute-start.2 = (bf16[3,4,2048]{2,1,0:T(4,128)(2,1)S(1)}, bf16[3,4,2048]{2,1,0:T(4,128)(2,1)S(1)}, u32[]{:S(2)}, u32[]{:S(2)}) collective-permute-start(bf16[3,4,2048]{2,1,0:T(4,128)(2,1)S(1)} %pad_maximum_fusion.packed.refs_0_), channel_id=1, source_target_pairs={{0,16},{4,20},{8,24},{12,28},{16,0},{20,4},{24,8},{28,12},{1,17},{... | collective-permute-start | bytes 147464 | tf_op jit(solution)/shard_map/ppermute | solution.py:256
  5.9 0.0 collective-permute-start.1
  5.9 0.9 %collective-permute-start = (bf16[3,4,2048]{2,1,0:T(4,128)(2,1)S(1)}, bf16[3,4,2048]{2,1,0:T(4,128)(2,1)S(1)}, u32[]{:S(2)}, u32[]{:S(2)}) collective-permute-start(bf16[3,4,2048]{2,1,0:T(4,128)(2,1)S(1)} %pad_maximum_fusion.packed.refs_0_), channel_id=1, source_target_pairs={{0,8},{4,12},{8,0},{12,4},{16,24},{20,28},{24,16},{28,20},{1,9},{5... | collective-permute-start | bytes 147464 | tf_op jit(solution)/shard_map/ppermute | solution.py:256
  6.8 0.1 inner_products.1.refs_5_
  6.9 1.0 %collective-permute-start.4 = (bf16[3,4,2048]{2,1,0:T(4,128)(2,1)S(1)}, bf16[3,4,2048]{2,1,0:T(4,128)(2,1)S(1)}, u32[]{:S(2)}, u32[]{:S(2)}) collective-permute-start(bf16[3,4,2048]{2,1,0:T(4,128)(2,1)S(1)} %pad_maximum_fusion.packed.refs_0_), channel_id=1, source_target_pairs={{0,4},{4,0},{1,5},{5,1},{2,6},{6,2},{3,7},{7,3},{8,12},{12,8},{9,1... | collective-permute-start | bytes 147464 | tf_op jit(solution)/shard_map/ppermute | solution.py:27
  7.9 0.1 collective-permute-start.6
  8.0 1.5 %collective-permute-done.2.refs_3_ = bf16[3,4,2048]{2,1,0:T(4,128)(2,1)S(1)} collective-permute-done((bf16[3,4,2048]{2,1,0:T(4,128)(2,1)S(1)}, bf16[3,4,2048]{2,1,0:T(4,128)(2,1)S(1)}, u32[]{:S(2)}, u32[]{:S(2)}) %collective-permute-start.2) | collective-permute-done | bytes 49184 | tf_op jit(solution)/shard_map/ppermute | solution.py:256
  9.5 1.0 %collective-permute-done.refs_1_ = bf16[3,4,2048]{2,1,0:T(4,128)(2,1)S(1)} collective-permute-done((bf16[3,4,2048]{2,1,0:T(4,128)(2,1)S(1)}, bf16[3,4,2048]{2,1,0:T(4,128)(2,1)S(1)}, u32[]{:S(2)}, u32[]{:S(2)}) %collective-permute-start) | collective-permute-done | bytes 49184 | tf_op jit(solution)/shard_map/ppermute | solution.py:256
  10.5 0.0 collective-permute-done.6.refs_7_
  10.5 0.2 collective-permute-done.5.refs_6_
  10.7 1.1 %products.1 = (f32[96,128]{1,0:T(8,128)S(1)}, f32[96,128]{1,0:T(8,128)S(1)}, f32[96,128]{1,0:T(8,128)S(1)}, f32[96,128]{1,0:T(8,128)S(1)}) custom-call(bf16[3,4,2048]{2,1,0:T(4,128)(2,1)S(1)} %pad_maximum_fusion.packed.refs_0_, bf16[3,4,2048]{2,1,0:T(4,128)(2,1)S(1)} %collective-permute-done.refs_1_, bf16[3,4,2048]{2,1,0:T(4,128)(2,1)S(1)} %collective-permute-done.1.refs_2_, ...), custom_call_target="tpu_custom_call" | custom-call | tf_op jit(solution)/shard_map/products/pallas_call | solution.py:143
  11.8 3.7 %collective-permute-start.7 = (f32[96,128]{1,0:T(8,128)S(1)}, f32[96,128]{1,0:T(8,128)S(1)}, u32[]{:S(2)}, u32[]{:S(2)}) collective-permute-start(f32[96,128]{1,0:T(8,128)S(1)} %get-tuple-element.10), channel_id=1, source_target_pairs={{0,3},{1,2},{2,1},{3,0},{4,7},{5,6},{6,5},{7,4},{8,11},{9,10},{10,... | collective-permute-start | bytes 147464 | tf_op jit(solution)/shard_map/ppermute | solution.py:27
  15.5 0.0 collective-permute-start.8
  15.5 0.8 %collective-permute-start.9 = (f32[96,128]{1,0:T(8,128)S(1)}, f32[96,128]{1,0:T(8,128)S(1)}, u32[]{:S(2)}, u32[]{:S(2)}) collective-permute-start(f32[96,128]{1,0:T(8,128)S(1)} %get-tuple-element.12), channel_id=1, source_target_pairs={{0,1},{1,0},{2,3},{3,2},{4,5},{5,4},{6,7},{7,6},{8,9},{9,8},{10,11... | collective-permute-start | bytes 147464 | tf_op jit(solution)/shard_map/ppermute | solution.py:27
  16.3 1.6 %collective-permute-done.7.refs_1_ = f32[96,128]{1,0:T(8,128)S(1)} collective-permute-done((f32[96,128]{1,0:T(8,128)S(1)}, f32[96,128]{1,0:T(8,128)S(1)}, u32[]{:S(2)}, u32[]{:S(2)}) %collective-permute-start.7) | collective-permute-done | bytes 49184 | tf_op jit(solution)/shard_map/ppermute | solution.py:27
  17.9 2.6 %collective-permute-done.8.refs_2_ = f32[96,128]{1,0:T(8,128)S(1)} collective-permute-done((f32[96,128]{1,0:T(8,128)S(1)}, f32[96,128]{1,0:T(8,128)S(1)}, u32[]{:S(2)}, u32[]{:S(2)}) %collective-permute-start.8) | collective-permute-done | bytes 49184 | tf_op jit(solution)/shard_map/ppermute | solution.py:27
  20.5 0.0 collective-permute-done.9.refs_3_
  20.5 0.1 attributions.1
  20.6 10.7 %all_to_all.5.arrived = f32[32,2,128]{2,1,0:T(2,128)S(1)} all-to-all(f32[32,2,128]{2,1,0:T(2,128)S(1)} %attributions.1), channel_id=1, replica_groups=mesh['section'=4,'feat'=2,'tensor'=4] {'section','feat','tensor'}, dimensions={0} | all-to-all | bytes 65536 | tf_op jit(solution)/shard_map/all_to_all | solution.py:267
  31.3 0.6 %final.1 = (f32[512]{0:T(512)}, f32[4]{0:T(128)}) custom-call(f32[32,2,128]{2,1,0:T(2,128)S(1)} %all_to_all.5.arrived), custom_call_target="tpu_custom_call" | custom-call | tf_op jit(solution)/shard_map/final/pallas_call | solution.py:222
  (8 shorter events, 0.0 us)
Async XLA Ops:
  1.4 9.3 %copy-start = (bf16[2048,512]{1,0:T(8,128)(2,1)S(1)}, bf16[2048,512]{1,0:T(8,128)(2,1)}, u32[]{:S(2)}) copy-start(bf16[2048,512]{1,0:T(8,128)(2,1)} %refs_8_.1) | copy-start | bytes 6291460
  1.4 9.3 %copy-start.1 = (bf16[512,2048]{1,0:T(8,128)(2,1)S(1)}, bf16[512,2048]{1,0:T(8,128)(2,1)}, u32[]{:S(2)}) copy-start(bf16[512,2048]{1,0:T(8,128)(2,1)} %refs_9_.1) | copy-start | bytes 6291460
  1.4 6.4 %collective-permute-start.3 = (bf16[3,4,2048]{2,1,0:T(4,128)(2,1)S(1)}, bf16[3,4,2048]{2,1,0:T(4,128)(2,1)S(1)}, u32[]{:S(2)}, u32[]{:S(2)}) collective-permute-start(bf16[3,4,2048]{2,1,0:T(4,128)(2,1)S(1)} %pad_maximum_fusion.packed.refs_0_), channel_id=1, source_target_pairs={{0,24},{4,28},{8,16},{12,20},{16,8},{20,12},{24,0},{28,4},{1,25},{... | collective-permute-start | bytes 147464 | tf_op jit(solution)/shard_map/ppermute | solution.py:256
  5.4 4.1 %collective-permute-start.2 = (bf16[3,4,2048]{2,1,0:T(4,128)(2,1)S(1)}, bf16[3,4,2048]{2,1,0:T(4,128)(2,1)S(1)}, u32[]{:S(2)}, u32[]{:S(2)}) collective-permute-start(bf16[3,4,2048]{2,1,0:T(4,128)(2,1)S(1)} %pad_maximum_fusion.packed.refs_0_), channel_id=1, source_target_pairs={{0,16},{4,20},{8,24},{12,28},{16,0},{20,4},{24,8},{28,12},{1,17},{... | collective-permute-start | bytes 147464 | tf_op jit(solution)/shard_map/ppermute | solution.py:256
  5.9 3.6 %collective-permute-start.1 = (bf16[3,4,2048]{2,1,0:T(4,128)(2,1)S(1)}, bf16[3,4,2048]{2,1,0:T(4,128)(2,1)S(1)}, u32[]{:S(2)}, u32[]{:S(2)}) collective-permute-start(bf16[3,4,2048]{2,1,0:T(4,128)(2,1)S(1)} %pad_maximum_fusion.packed.refs_0_), channel_id=1, source_target_pairs={{0,12},{4,8},{8,4},{12,0},{16,28},{20,24},{24,20},{28,16},{1,13},{... | collective-permute-start | bytes 147464 | tf_op jit(solution)/shard_map/ppermute | solution.py:256
  5.9 4.6 %collective-permute-start = (bf16[3,4,2048]{2,1,0:T(4,128)(2,1)S(1)}, bf16[3,4,2048]{2,1,0:T(4,128)(2,1)S(1)}, u32[]{:S(2)}, u32[]{:S(2)}) collective-permute-start(bf16[3,4,2048]{2,1,0:T(4,128)(2,1)S(1)} %pad_maximum_fusion.packed.refs_0_), channel_id=1, source_target_pairs={{0,8},{4,12},{8,0},{12,4},{16,24},{20,28},{24,16},{28,20},{1,9},{5... | collective-permute-start | bytes 147464 | tf_op jit(solution)/shard_map/ppermute | solution.py:256
  6.9 13.6 %copy-start.2 = (f32[512]{0:T(512)S(1)}, f32[512]{0:T(512)}, u32[]{:S(2)}) copy-start(f32[512]{0:T(512)} %param.10) | copy-start | bytes 6148
  6.9 2.6 %collective-permute-start.4 = (bf16[3,4,2048]{2,1,0:T(4,128)(2,1)S(1)}, bf16[3,4,2048]{2,1,0:T(4,128)(2,1)S(1)}, u32[]{:S(2)}, u32[]{:S(2)}) collective-permute-start(bf16[3,4,2048]{2,1,0:T(4,128)(2,1)S(1)} %pad_maximum_fusion.packed.refs_0_), channel_id=1, source_target_pairs={{0,4},{4,0},{1,5},{5,1},{2,6},{6,2},{3,7},{7,3},{8,12},{12,8},{9,1... | collective-permute-start | bytes 147464 | tf_op jit(solution)/shard_map/ppermute | solution.py:27
  7.9 2.6 %collective-permute-start.6 = (bf16[3,4,2048]{2,1,0:T(4,128)(2,1)S(1)}, bf16[3,4,2048]{2,1,0:T(4,128)(2,1)S(1)}, u32[]{:S(2)}, u32[]{:S(2)}) collective-permute-start(bf16[3,4,2048]{2,1,0:T(4,128)(2,1)S(1)} %collective-permute-done.3.refs_4_), channel_id=1, source_target_pairs={{0,4},{4,0},{1,5},{5,1},{2,6},{6,2},{3,7},{7,3},{8,12},{12,8},{9,1... | collective-permute-start | bytes 147464 | tf_op jit(solution)/shard_map/ppermute | solution.py:27
  9.5 1.2 %collective-permute-start.5 = (bf16[3,4,2048]{2,1,0:T(4,128)(2,1)S(1)}, bf16[3,4,2048]{2,1,0:T(4,128)(2,1)S(1)}, u32[]{:S(2)}, u32[]{:S(2)}) collective-permute-start(bf16[3,4,2048]{2,1,0:T(4,128)(2,1)S(1)} %collective-permute-done.2.refs_3_), channel_id=1, source_target_pairs={{0,4},{4,0},{1,5},{5,1},{2,6},{6,2},{3,7},{7,3},{8,12},{12,8},{9,1... | collective-permute-start | bytes 147464 | tf_op jit(solution)/shard_map/ppermute | solution.py:27
  11.8 6.0 %collective-permute-start.7 = (f32[96,128]{1,0:T(8,128)S(1)}, f32[96,128]{1,0:T(8,128)S(1)}, u32[]{:S(2)}, u32[]{:S(2)}) collective-permute-start(f32[96,128]{1,0:T(8,128)S(1)} %get-tuple-element.10), channel_id=1, source_target_pairs={{0,3},{1,2},{2,1},{3,0},{4,7},{5,6},{6,5},{7,4},{8,11},{9,10},{10,... | collective-permute-start | bytes 147464 | tf_op jit(solution)/shard_map/ppermute | solution.py:27
  15.5 5.0 %collective-permute-start.8 = (f32[96,128]{1,0:T(8,128)S(1)}, f32[96,128]{1,0:T(8,128)S(1)}, u32[]{:S(2)}, u32[]{:S(2)}) collective-permute-start(f32[96,128]{1,0:T(8,128)S(1)} %get-tuple-element.11), channel_id=1, source_target_pairs={{0,2},{1,3},{2,0},{3,1},{4,6},{5,7},{6,4},{7,5},{8,10},{9,11},{10,... | collective-permute-start | bytes 147464 | tf_op jit(solution)/shard_map/ppermute | solution.py:27
  15.5 5.0 %collective-permute-start.9 = (f32[96,128]{1,0:T(8,128)S(1)}, f32[96,128]{1,0:T(8,128)S(1)}, u32[]{:S(2)}, u32[]{:S(2)}) collective-permute-start(f32[96,128]{1,0:T(8,128)S(1)} %get-tuple-element.12), channel_id=1, source_target_pairs={{0,1},{1,0},{2,3},{3,2},{4,5},{5,4},{6,7},{7,6},{8,9},{9,8},{10,11... | collective-permute-start | bytes 147464 | tf_op jit(solution)/shard_map/ppermute | solution.py:27

commit v18 on v17

--- a/solution.py
+++ b/solution.py
@@ -15,7 +15,7 @@
 
 
 def far_first(size):
-    return [0, *reversed(range(1, size))]
+    return sorted(range(size), key=lambda m: (m > 0, m < size // 2, m))
 
 
 def row_blocks(sections, feats):
@@ -45,13 +45,6 @@
         cost_estimate=pl.CostEstimate(flops=2**32, bytes_accessed=2**24, transcendentals=0),
         name="inner_products",
     )(packed)
-
-
-def inner_kernel(packed, inner):
-    tokens = packed.shape[1]
-    clean, corrupt, grad = [packed[a].astype(jnp.float32) for a in range(3)]
-    part = jnp.sum((corrupt - clean) * grad, axis=1, keepdims=True)
-    inner[pl.ds(0, tokens), :] = jnp.broadcast_to(part, (tokens, LANES))
 
 
 def inner_products(packed):

time: 32.2 us -> 32.7 us (1.016)
  blocking collectives: 10.7 us -> 11.2 us
    all_to_all x1, blocking collectives: 10.7 us -> 11.2 us  [per_device(): return tuple(final(sizes, tokens, lax.all_to_all(sums, EVERY, 0, 0)))]
where the time goes in v18:
time: 32.7 us; the launch traced here: 32.4 us
  blocking collectives  11.2 us (34%)
  starting transfers between devices  10.6 us (32%)
  waiting for transfers between devices  7.14 us (22%)
  Pallas kernels  1.92 us (6%)
  other arithmetic  0.79 us (2%)
  between operations  0.67 us (2%)
    all_to_all x1, blocking collectives, per_device(): return tuple(final(sizes, tokens, lax.all_to_all(sums, EVERY, 0, 0)))  11.2 us
    ppermute x4, starting transfers between devices, per_device(): held[p, q] = lax.ppermute(packed, ('section', 'feat'), pairs)  5.37 us
    ppermute x6, starting transfers between devices, exchange(): return lax.ppermute(value, axis, [(i, i ^ k) for i in range(size)])  5.27 us
    ppermute x6, waiting for transfers between devices, exchange(): return lax.ppermute(value, axis, [(i, i ^ k) for i in range(size)])  4.63 us
    ppermute x4, waiting for transfers between devices, per_device(): held[p, q] = lax.ppermute(packed, ('section', 'feat'), pairs)  2.51 us
    pallas_call x1, Pallas kernels, products(): pl.pallas_call(functools.partial(product_kernel, groups, parts), out_shap...  1.11 us
    another operation x1, other arithmetic, per_device(): packed = jnp.stack([clean_resid, corrupt_resid, metric_grad])  0.79 us
  transfers between devices with their start and end apart: 10, of which 5 were waited for; matrix products, arithmetic and copies ran while one was open for 0% of the time, Pallas kernels for 0%

profile of v18, /device:TPU:0, one launch (start us, length us, event | category | flops | bytes accessed | tf_op | source)
XLA Modules:
  0.0 32.4 jit_solution(17659530092647944747)
XLA Ops:
  0.6 0.8 %pad_maximum_fusion.packed.refs_0_ = bf16[3,4,2048]{2,1,0:T(4,128)(2,1)S(1)} fusion(bf16[1,4,2048]{2,1,0:T(4,128)(2,1)} %bitcast.5, bf16[1,4,2048]{2,1,0:T(4,128)(2,1)} %bitcast.6, bf16[1,4,2048]{2,1,0:T(4,128)(2,1)} %bitcast.7), kind=kLoop, calls=%fused_computation | loop fusion | flops 49152 | bytes 98304 | tf_op jit(solution)/shard_map/stack | solution.py:238
  1.4 0.0 copy-start
  1.4 0.0 copy-start.1
  1.4 4.0 %collective-permute-start.3 = (bf16[3,4,2048]{2,1,0:T(4,128)(2,1)S(1)}, bf16[3,4,2048]{2,1,0:T(4,128)(2,1)S(1)}, u32[]{:S(2)}, u32[]{:S(2)}) collective-permute-start(bf16[3,4,2048]{2,1,0:T(4,128)(2,1)S(1)} %pad_maximum_fusion.packed.refs_0_), channel_id=1, source_target_pairs={{0,24},{4,28},{8,16},{12,20},{16,8},{20,12},{24,0},{28,4},{1,25},{... | collective-permute-start | bytes 147464 | tf_op jit(solution)/shard_map/ppermute | solution.py:249
  5.4 0.5 %collective-permute-start.2 = (bf16[3,4,2048]{2,1,0:T(4,128)(2,1)S(1)}, bf16[3,4,2048]{2,1,0:T(4,128)(2,1)S(1)}, u32[]{:S(2)}, u32[]{:S(2)}) collective-permute-start(bf16[3,4,2048]{2,1,0:T(4,128)(2,1)S(1)} %pad_maximum_fusion.packed.refs_0_), channel_id=1, source_target_pairs={{0,16},{4,20},{8,24},{12,28},{16,0},{20,4},{24,8},{28,12},{1,17},{... | collective-permute-start | bytes 147464 | tf_op jit(solution)/shard_map/ppermute | solution.py:249
  5.9 0.0 collective-permute-start.1
  5.9 0.9 %collective-permute-start = (bf16[3,4,2048]{2,1,0:T(4,128)(2,1)S(1)}, bf16[3,4,2048]{2,1,0:T(4,128)(2,1)S(1)}, u32[]{:S(2)}, u32[]{:S(2)}) collective-permute-start(bf16[3,4,2048]{2,1,0:T(4,128)(2,1)S(1)} %pad_maximum_fusion.packed.refs_0_), channel_id=1, source_target_pairs={{0,8},{4,12},{8,0},{12,4},{16,24},{20,28},{24,16},{28,20},{1,9},{5... | collective-permute-start | bytes 147464 | tf_op jit(solution)/shard_map/ppermute | solution.py:249
  6.8 0.1 inner_products.1.refs_5_
  6.9 1.0 %collective-permute-start.4 = (bf16[3,4,2048]{2,1,0:T(4,128)(2,1)S(1)}, bf16[3,4,2048]{2,1,0:T(4,128)(2,1)S(1)}, u32[]{:S(2)}, u32[]{:S(2)}) collective-permute-start(bf16[3,4,2048]{2,1,0:T(4,128)(2,1)S(1)} %pad_maximum_fusion.packed.refs_0_), channel_id=1, source_target_pairs={{0,4},{4,0},{1,5},{5,1},{2,6},{6,2},{3,7},{7,3},{8,12},{12,8},{9,1... | collective-permute-start | bytes 147464 | tf_op jit(solution)/shard_map/ppermute | solution.py:27
  7.9 0.0 collective-permute-done.3.refs_4_
  7.9 0.1 collective-permute-start.6
  8.0 1.5 %collective-permute-done.2.refs_3_ = bf16[3,4,2048]{2,1,0:T(4,128)(2,1)S(1)} collective-permute-done((bf16[3,4,2048]{2,1,0:T(4,128)(2,1)S(1)}, bf16[3,4,2048]{2,1,0:T(4,128)(2,1)S(1)}, u32[]{:S(2)}, u32[]{:S(2)}) %collective-permute-start.2) | collective-permute-done | bytes 49184 | tf_op jit(solution)/shard_map/ppermute | solution.py:249
  9.5 1.0 %collective-permute-done.refs_1_ = bf16[3,4,2048]{2,1,0:T(4,128)(2,1)S(1)} collective-permute-done((bf16[3,4,2048]{2,1,0:T(4,128)(2,1)S(1)}, bf16[3,4,2048]{2,1,0:T(4,128)(2,1)S(1)}, u32[]{:S(2)}, u32[]{:S(2)}) %collective-permute-start) | collective-permute-done | bytes 49184 | tf_op jit(solution)/shard_map/ppermute | solution.py:249
  10.5 0.0 collective-permute-done.6.refs_7_
  10.5 0.2 collective-permute-done.5.refs_6_
  10.7 1.1 %products.1 = (f32[96,128]{1,0:T(8,128)S(1)}, f32[96,128]{1,0:T(8,128)S(1)}, f32[96,128]{1,0:T(8,128)S(1)}, f32[96,128]{1,0:T(8,128)S(1)}) custom-call(bf16[3,4,2048]{2,1,0:T(4,128)(2,1)S(1)} %pad_maximum_fusion.packed.refs_0_, bf16[3,4,2048]{2,1,0:T(4,128)(2,1)S(1)} %collective-permute-done.refs_1_, bf16[3,4,2048]{2,1,0:T(4,128)(2,1)S(1)} %collective-permute-done.1.refs_2_, ...), custom_call_target="tpu_custom_call" | custom-call | tf_op jit(solution)/shard_map/products/pallas_call | solution.py:136
  11.8 2.6 %collective-permute-start.7 = (f32[96,128]{1,0:T(8,128)S(1)}, f32[96,128]{1,0:T(8,128)S(1)}, u32[]{:S(2)}, u32[]{:S(2)}) collective-permute-start(f32[96,128]{1,0:T(8,128)S(1)} %get-tuple-element.10), channel_id=1, source_target_pairs={{0,2},{1,3},{2,0},{3,1},{4,6},{5,7},{6,4},{7,5},{8,10},{9,11},{10,... | collective-permute-start | bytes 147464 | tf_op jit(solution)/shard_map/ppermute | solution.py:27
  14.5 1.3 %collective-permute-start.8 = (f32[96,128]{1,0:T(8,128)S(1)}, f32[96,128]{1,0:T(8,128)S(1)}, u32[]{:S(2)}, u32[]{:S(2)}) collective-permute-start(f32[96,128]{1,0:T(8,128)S(1)} %get-tuple-element.11), channel_id=1, source_target_pairs={{0,3},{1,2},{2,1},{3,0},{4,7},{5,6},{6,5},{7,4},{8,11},{9,10},{10,... | collective-permute-start | bytes 147464 | tf_op jit(solution)/shard_map/ppermute | solution.py:27
  15.8 0.2 collective-permute-start.9
  16.1 1.9 %collective-permute-done.7.refs_1_ = f32[96,128]{1,0:T(8,128)S(1)} collective-permute-done((f32[96,128]{1,0:T(8,128)S(1)}, f32[96,128]{1,0:T(8,128)S(1)}, u32[]{:S(2)}, u32[]{:S(2)}) %collective-permute-start.7) | collective-permute-done | bytes 49184 | tf_op jit(solution)/shard_map/ppermute | solution.py:27
  17.9 2.5 %collective-permute-done.8.refs_2_ = f32[96,128]{1,0:T(8,128)S(1)} collective-permute-done((f32[96,128]{1,0:T(8,128)S(1)}, f32[96,128]{1,0:T(8,128)S(1)}, u32[]{:S(2)}, u32[]{:S(2)}) %collective-permute-start.8) | collective-permute-done | bytes 49184 | tf_op jit(solution)/shard_map/ppermute | solution.py:27
  20.5 0.1 attributions.1
  20.6 11.2 %all_to_all.5.arrived = f32[32,2,128]{2,1,0:T(2,128)S(1)} all-to-all(f32[32,2,128]{2,1,0:T(2,128)S(1)} %attributions.1), channel_id=1, replica_groups=mesh['section'=4,'feat'=2,'tensor'=4] {'section','feat','tensor'}, dimensions={0} | all-to-all | bytes 65536 | tf_op jit(solution)/shard_map/all_to_all | solution.py:260
  31.7 0.6 %final.1 = (f32[512]{0:T(512)}, f32[4]{0:T(128)}) custom-call(f32[32,2,128]{2,1,0:T(2,128)S(1)} %all_to_all.5.arrived), custom_call_target="tpu_custom_call" | custom-call | tf_op jit(solution)/shard_map/final/pallas_call | solution.py:215
  (8 shorter events, 0.0 us)
Async XLA Ops:
  1.4 9.3 %copy-start = (bf16[2048,512]{1,0:T(8,128)(2,1)S(1)}, bf16[2048,512]{1,0:T(8,128)(2,1)}, u32[]{:S(2)}) copy-start(bf16[2048,512]{1,0:T(8,128)(2,1)} %refs_8_.1) | copy-start | bytes 6291460
  1.4 9.3 %copy-start.1 = (bf16[512,2048]{1,0:T(8,128)(2,1)S(1)}, bf16[512,2048]{1,0:T(8,128)(2,1)}, u32[]{:S(2)}) copy-start(bf16[512,2048]{1,0:T(8,128)(2,1)} %refs_9_.1) | copy-start | bytes 6291460
  1.4 6.4 %collective-permute-start.3 = (bf16[3,4,2048]{2,1,0:T(4,128)(2,1)S(1)}, bf16[3,4,2048]{2,1,0:T(4,128)(2,1)S(1)}, u32[]{:S(2)}, u32[]{:S(2)}) collective-permute-start(bf16[3,4,2048]{2,1,0:T(4,128)(2,1)S(1)} %pad_maximum_fusion.packed.refs_0_), channel_id=1, source_target_pairs={{0,24},{4,28},{8,16},{12,20},{16,8},{20,12},{24,0},{28,4},{1,25},{... | collective-permute-start | bytes 147464 | tf_op jit(solution)/shard_map/ppermute | solution.py:249
  5.4 4.1 %collective-permute-start.2 = (bf16[3,4,2048]{2,1,0:T(4,128)(2,1)S(1)}, bf16[3,4,2048]{2,1,0:T(4,128)(2,1)S(1)}, u32[]{:S(2)}, u32[]{:S(2)}) collective-permute-start(bf16[3,4,2048]{2,1,0:T(4,128)(2,1)S(1)} %pad_maximum_fusion.packed.refs_0_), channel_id=1, source_target_pairs={{0,16},{4,20},{8,24},{12,28},{16,0},{20,4},{24,8},{28,12},{1,17},{... | collective-permute-start | bytes 147464 | tf_op jit(solution)/shard_map/ppermute | solution.py:249
  5.9 3.6 %collective-permute-start.1 = (bf16[3,4,2048]{2,1,0:T(4,128)(2,1)S(1)}, bf16[3,4,2048]{2,1,0:T(4,128)(2,1)S(1)}, u32[]{:S(2)}, u32[]{:S(2)}) collective-permute-start(bf16[3,4,2048]{2,1,0:T(4,128)(2,1)S(1)} %pad_maximum_fusion.packed.refs_0_), channel_id=1, source_target_pairs={{0,12},{4,8},{8,4},{12,0},{16,28},{20,24},{24,20},{28,16},{1,13},{... | collective-permute-start | bytes 147464 | tf_op jit(solution)/shard_map/ppermute | solution.py:249
  5.9 4.6 %collective-permute-start = (bf16[3,4,2048]{2,1,0:T(4,128)(2,1)S(1)}, bf16[3,4,2048]{2,1,0:T(4,128)(2,1)S(1)}, u32[]{:S(2)}, u32[]{:S(2)}) collective-permute-start(bf16[3,4,2048]{2,1,0:T(4,128)(2,1)S(1)} %pad_maximum_fusion.packed.refs_0_), channel_id=1, source_target_pairs={{0,8},{4,12},{8,0},{12,4},{16,24},{20,28},{24,16},{28,20},{1,9},{5... | collective-permute-start | bytes 147464 | tf_op jit(solution)/shard_map/ppermute | solution.py:249
  6.9 13.5 %copy-start.2 = (f32[512]{0:T(512)S(1)}, f32[512]{0:T(512)}, u32[]{:S(2)}) copy-start(f32[512]{0:T(512)} %param.10) | copy-start | bytes 6148
  6.9 2.6 %collective-permute-start.4 = (bf16[3,4,2048]{2,1,0:T(4,128)(2,1)S(1)}, bf16[3,4,2048]{2,1,0:T(4,128)(2,1)S(1)}, u32[]{:S(2)}, u32[]{:S(2)}) collective-permute-start(bf16[3,4,2048]{2,1,0:T(4,128)(2,1)S(1)} %pad_maximum_fusion.packed.refs_0_), channel_id=1, source_target_pairs={{0,4},{4,0},{1,5},{5,1},{2,6},{6,2},{3,7},{7,3},{8,12},{12,8},{9,1... | collective-permute-start | bytes 147464 | tf_op jit(solution)/shard_map/ppermute | solution.py:27
  7.9 2.6 %collective-permute-start.6 = (bf16[3,4,2048]{2,1,0:T(4,128)(2,1)S(1)}, bf16[3,4,2048]{2,1,0:T(4,128)(2,1)S(1)}, u32[]{:S(2)}, u32[]{:S(2)}) collective-permute-start(bf16[3,4,2048]{2,1,0:T(4,128)(2,1)S(1)} %collective-permute-done.3.refs_4_), channel_id=1, source_target_pairs={{0,4},{4,0},{1,5},{5,1},{2,6},{6,2},{3,7},{7,3},{8,12},{12,8},{9,1... | collective-permute-start | bytes 147464 | tf_op jit(solution)/shard_map/ppermute | solution.py:27
  9.5 1.2 %collective-permute-start.5 = (bf16[3,4,2048]{2,1,0:T(4,128)(2,1)S(1)}, bf16[3,4,2048]{2,1,0:T(4,128)(2,1)S(1)}, u32[]{:S(2)}, u32[]{:S(2)}) collective-permute-start(bf16[3,4,2048]{2,1,0:T(4,128)(2,1)S(1)} %collective-permute-done.2.refs_3_), channel_id=1, source_target_pairs={{0,4},{4,0},{1,5},{5,1},{2,6},{6,2},{3,7},{7,3},{8,12},{12,8},{9,1... | collective-permute-start | bytes 147464 | tf_op jit(solution)/shard_map/ppermute | solution.py:27
  11.8 6.1 %collective-permute-start.7 = (f32[96,128]{1,0:T(8,128)S(1)}, f32[96,128]{1,0:T(8,128)S(1)}, u32[]{:S(2)}, u32[]{:S(2)}) collective-permute-start(f32[96,128]{1,0:T(8,128)S(1)} %get-tuple-element.10), channel_id=1, source_target_pairs={{0,2},{1,3},{2,0},{3,1},{4,6},{5,7},{6,4},{7,5},{8,10},{9,11},{10,... | collective-permute-start | bytes 147464 | tf_op jit(solution)/shard_map/ppermute | solution.py:27
  14.5 6.0 %collective-permute-start.8 = (f32[96,128]{1,0:T(8,128)S(1)}, f32[96,128]{1,0:T(8,128)S(1)}, u32[]{:S(2)}, u32[]{:S(2)}) collective-permute-start(f32[96,128]{1,0:T(8,128)S(1)} %get-tuple-element.11), channel_id=1, source_target_pairs={{0,3},{1,2},{2,1},{3,0},{4,7},{5,6},{6,5},{7,4},{8,11},{9,10},{10,... | collective-permute-start | bytes 147464 | tf_op jit(solution)/shard_map/ppermute | solution.py:27
  15.8 4.6 %collective-permute-start.9 = (f32[96,128]{1,0:T(8,128)S(1)}, f32[96,128]{1,0:T(8,128)S(1)}, u32[]{:S(2)}, u32[]{:S(2)}) collective-permute-start(f32[96,128]{1,0:T(8,128)S(1)} %get-tuple-element.12), channel_id=1, source_target_pairs={{0,1},{1,0},{2,3},{3,2},{4,5},{5,4},{6,7},{7,6},{8,9},{9,8},{10,11... | collective-permute-start | bytes 147464 | tf_op jit(solution)/shard_map/ppermute | solution.py:27

commit v19 on v10

--- a/solution.py
+++ b/solution.py
@@ -19,8 +19,18 @@
 
 
 def row_blocks(sections, feats):
+    direct = sections // 2
     places = [(p, q) for p in range(feats) for q in range(sections)]
-    return sorted(places, key=lambda place: (place[0] > 0 and place[1] != 1, place[1], place[0]))
+    return sorted(
+        places,
+        key=lambda place: (
+            place[0] > 0 and place[1] != direct,
+            place[1] != 0,
+            place[1] != direct,
+            place[1],
+            place[0],
+        ),
+    )
 
 
 def exchange(value, axis, size, k):
@@ -246,7 +256,7 @@
     bias = enc_bias.reshape(parts, features // parts)
     held = {(0, 0): packed}
     for p, q in row_blocks(sections, feats):
-        if q > 0 and (p == 0 or q == 1):
+        if q > 0 and (p == 0 or q == sections // 2):
             pairs = [
                 (s * feats + f, (s ^ q) * feats + (f ^ p))
                 for s in range(sections)

time: 32.2 us -> 32.3 us (level)
  no operation moved by 1% of the time
where the time goes in v19:
time: 32.3 us; the launch traced here: 31.9 us
  starting transfers between devices  10.9 us (34%)
  blocking collectives  10.7 us (33%)
  waiting for transfers between devices  6.94 us (21%)
  Pallas kernels  1.95 us (6%)
  other arithmetic  0.79 us (2%)
  between operations  0.68 us (2%)
    all_to_all x1, blocking collectives, per_device(): return tuple(final(sizes, tokens, lax.all_to_all(sums, EVERY, 0, 0)))  10.7 us
    ppermute x6, starting transfers between devices, exchange(): return lax.ppermute(value, axis, [(i, i ^ k) for i in range(size)])  5.5 us
    ppermute x4, starting transfers between devices, per_device(): held[p, q] = lax.ppermute(packed, ('section', 'feat'), pairs)  5.4 us
    ppermute x6, waiting for transfers between devices, exchange(): return lax.ppermute(value, axis, [(i, i ^ k) for i in range(size)])  4.43 us
    ppermute x4, waiting for transfers between devices, per_device(): held[p, q] = lax.ppermute(packed, ('section', 'feat'), pairs)  2.51 us
    pallas_call x1, Pallas kernels, products(): pl.pallas_call(functools.partial(product_kernel, groups, parts), out_shap...  1.14 us
    another operation x1, other arithmetic, per_device(): packed = jnp.stack([clean_resid, corrupt_resid, metric_grad])  0.79 us
  transfers between devices with their start and end apart: 10, of which 5 were waited for; matrix products, arithmetic and copies ran while one was open for 0% of the time, Pallas kernels for 0%

profile of v19, /device:TPU:0, one launch (start us, length us, event | category | flops | bytes accessed | tf_op | source)
XLA Modules:
  0.0 31.9 jit_solution(5884720269980838827)
XLA Ops:
  0.6 0.8 %pad_maximum_fusion.packed.refs_0_ = bf16[3,4,2048]{2,1,0:T(4,128)(2,1)S(1)} fusion(bf16[1,4,2048]{2,1,0:T(4,128)(2,1)} %bitcast.5, bf16[1,4,2048]{2,1,0:T(4,128)(2,1)} %bitcast.6, bf16[1,4,2048]{2,1,0:T(4,128)(2,1)} %bitcast.7), kind=kLoop, calls=%fused_computation | loop fusion | flops 49152 | bytes 98304 | tf_op jit(solution)/shard_map/stack | solution.py:254
  1.4 0.0 copy-start
  1.4 0.0 copy-start.1
  1.4 4.0 %collective-permute-start.3 = (bf16[3,4,2048]{2,1,0:T(4,128)(2,1)S(1)}, bf16[3,4,2048]{2,1,0:T(4,128)(2,1)S(1)}, u32[]{:S(2)}, u32[]{:S(2)}) collective-permute-start(bf16[3,4,2048]{2,1,0:T(4,128)(2,1)S(1)} %pad_maximum_fusion.packed.refs_0_), channel_id=1, source_target_pairs={{0,24},{4,28},{8,16},{12,20},{16,8},{20,12},{24,0},{28,4},{1,25},{... | collective-permute-start | bytes 147464 | tf_op jit(solution)/shard_map/ppermute | solution.py:265
  5.4 0.5 %collective-permute-start.2 = (bf16[3,4,2048]{2,1,0:T(4,128)(2,1)S(1)}, bf16[3,4,2048]{2,1,0:T(4,128)(2,1)S(1)}, u32[]{:S(2)}, u32[]{:S(2)}) collective-permute-start(bf16[3,4,2048]{2,1,0:T(4,128)(2,1)S(1)} %pad_maximum_fusion.packed.refs_0_), channel_id=1, source_target_pairs={{0,8},{4,12},{8,0},{12,4},{16,24},{20,28},{24,16},{28,20},{1,9},{5... | collective-permute-start | bytes 147464 | tf_op jit(solution)/shard_map/ppermute | solution.py:265
  5.9 0.0 collective-permute-start.1
  5.9 0.9 %collective-permute-start = (bf16[3,4,2048]{2,1,0:T(4,128)(2,1)S(1)}, bf16[3,4,2048]{2,1,0:T(4,128)(2,1)S(1)}, u32[]{:S(2)}, u32[]{:S(2)}) collective-permute-start(bf16[3,4,2048]{2,1,0:T(4,128)(2,1)S(1)} %pad_maximum_fusion.packed.refs_0_), channel_id=1, source_target_pairs={{0,16},{4,20},{8,24},{12,28},{16,0},{20,4},{24,8},{28,12},{1,17},{... | collective-permute-start | bytes 147464 | tf_op jit(solution)/shard_map/ppermute | solution.py:265
  6.9 0.1 inner_products.1.refs_5_
  7.0 1.0 %collective-permute-start.4 = (bf16[3,4,2048]{2,1,0:T(4,128)(2,1)S(1)}, bf16[3,4,2048]{2,1,0:T(4,128)(2,1)S(1)}, u32[]{:S(2)}, u32[]{:S(2)}) collective-permute-start(bf16[3,4,2048]{2,1,0:T(4,128)(2,1)S(1)} %pad_maximum_fusion.packed.refs_0_), channel_id=1, source_target_pairs={{0,4},{4,0},{1,5},{5,1},{2,6},{6,2},{3,7},{7,3},{8,12},{12,8},{9,1... | collective-permute-start | bytes 147464 | tf_op jit(solution)/shard_map/ppermute | solution.py:37
  7.9 0.0 collective-permute-done.3.refs_4_
  7.9 0.1 collective-permute-start.6
  8.0 1.5 %collective-permute-done.2.refs_3_ = bf16[3,4,2048]{2,1,0:T(4,128)(2,1)S(1)} collective-permute-done((bf16[3,4,2048]{2,1,0:T(4,128)(2,1)S(1)}, bf16[3,4,2048]{2,1,0:T(4,128)(2,1)S(1)}, u32[]{:S(2)}, u32[]{:S(2)}) %collective-permute-start.2) | collective-permute-done | bytes 49184 | tf_op jit(solution)/shard_map/ppermute | solution.py:265
  9.5 1.0 %collective-permute-done.refs_1_ = bf16[3,4,2048]{2,1,0:T(4,128)(2,1)S(1)} collective-permute-done((bf16[3,4,2048]{2,1,0:T(4,128)(2,1)S(1)}, bf16[3,4,2048]{2,1,0:T(4,128)(2,1)S(1)}, u32[]{:S(2)}, u32[]{:S(2)}) %collective-permute-start) | collective-permute-done | bytes 49184 | tf_op jit(solution)/shard_map/ppermute | solution.py:265
  10.5 0.0 collective-permute-done.6.refs_7_
  10.5 0.2 collective-permute-done.5.refs_6_
  10.7 1.1 %products.1 = (f32[96,128]{1,0:T(8,128)S(1)}, f32[96,128]{1,0:T(8,128)S(1)}, f32[96,128]{1,0:T(8,128)S(1)}, f32[96,128]{1,0:T(8,128)S(1)}) custom-call(bf16[3,4,2048]{2,1,0:T(4,128)(2,1)S(1)} %pad_maximum_fusion.packed.refs_0_, bf16[3,4,2048]{2,1,0:T(4,128)(2,1)S(1)} %collective-permute-done.refs_1_, bf16[3,4,2048]{2,1,0:T(4,128)(2,1)S(1)} %collective-permute-done.1.refs_2_, ...), custom_call_target="tpu_custom_call" | custom-call | tf_op jit(solution)/shard_map/products/pallas_call | solution.py:151
  11.9 3.7 %collective-permute-start.7 = (f32[96,128]{1,0:T(8,128)S(1)}, f32[96,128]{1,0:T(8,128)S(1)}, u32[]{:S(2)}, u32[]{:S(2)}) collective-permute-start(f32[96,128]{1,0:T(8,128)S(1)} %get-tuple-element.10), channel_id=1, source_target_pairs={{0,3},{1,2},{2,1},{3,0},{4,7},{5,6},{6,5},{7,4},{8,11},{9,10},{10,... | collective-permute-start | bytes 147464 | tf_op jit(solution)/shard_map/ppermute | solution.py:37
  15.6 0.8 %collective-permute-start.9 = (f32[96,128]{1,0:T(8,128)S(1)}, f32[96,128]{1,0:T(8,128)S(1)}, u32[]{:S(2)}, u32[]{:S(2)}) collective-permute-start(f32[96,128]{1,0:T(8,128)S(1)} %get-tuple-element.12), channel_id=1, source_target_pairs={{0,1},{1,0},{2,3},{3,2},{4,5},{5,4},{6,7},{7,6},{8,9},{9,8},{10,11... | collective-permute-start | bytes 147464 | tf_op jit(solution)/shard_map/ppermute | solution.py:37
  16.3 1.6 %collective-permute-done.7.refs_1_ = f32[96,128]{1,0:T(8,128)S(1)} collective-permute-done((f32[96,128]{1,0:T(8,128)S(1)}, f32[96,128]{1,0:T(8,128)S(1)}, u32[]{:S(2)}, u32[]{:S(2)}) %collective-permute-start.7) | collective-permute-done | bytes 49184 | tf_op jit(solution)/shard_map/ppermute | solution.py:37
  17.9 2.7 %collective-permute-done.8.refs_2_ = f32[96,128]{1,0:T(8,128)S(1)} collective-permute-done((f32[96,128]{1,0:T(8,128)S(1)}, f32[96,128]{1,0:T(8,128)S(1)}, u32[]{:S(2)}, u32[]{:S(2)}) %collective-permute-start.8) | collective-permute-done | bytes 49184 | tf_op jit(solution)/shard_map/ppermute | solution.py:37
  20.5 0.0 collective-permute-done.9.refs_3_
  20.5 0.1 attributions.1
  20.7 10.7 %all_to_all.5.arrived = f32[32,2,128]{2,1,0:T(2,128)S(1)} all-to-all(f32[32,2,128]{2,1,0:T(2,128)S(1)} %attributions.1), channel_id=1, replica_groups=mesh['section'=4,'feat'=2,'tensor'=4] {'section','feat','tensor'}, dimensions={0} | all-to-all | bytes 65536 | tf_op jit(solution)/shard_map/all_to_all | solution.py:276
  31.3 0.6 %final.1 = (f32[512]{0:T(512)}, f32[4]{0:T(128)}) custom-call(f32[32,2,128]{2,1,0:T(2,128)S(1)} %all_to_all.5.arrived), custom_call_target="tpu_custom_call" | custom-call | tf_op jit(solution)/shard_map/final/pallas_call | solution.py:231
  (8 shorter events, 0.0 us)
Async XLA Ops:
  1.4 9.3 %copy-start = (bf16[2048,512]{1,0:T(8,128)(2,1)S(1)}, bf16[2048,512]{1,0:T(8,128)(2,1)}, u32[]{:S(2)}) copy-start(bf16[2048,512]{1,0:T(8,128)(2,1)} %refs_8_.1) | copy-start | bytes 6291460
  1.4 9.3 %copy-start.1 = (bf16[512,2048]{1,0:T(8,128)(2,1)S(1)}, bf16[512,2048]{1,0:T(8,128)(2,1)}, u32[]{:S(2)}) copy-start(bf16[512,2048]{1,0:T(8,128)(2,1)} %refs_9_.1) | copy-start | bytes 6291460
  1.4 6.5 %collective-permute-start.3 = (bf16[3,4,2048]{2,1,0:T(4,128)(2,1)S(1)}, bf16[3,4,2048]{2,1,0:T(4,128)(2,1)S(1)}, u32[]{:S(2)}, u32[]{:S(2)}) collective-permute-start(bf16[3,4,2048]{2,1,0:T(4,128)(2,1)S(1)} %pad_maximum_fusion.packed.refs_0_), channel_id=1, source_target_pairs={{0,24},{4,28},{8,16},{12,20},{16,8},{20,12},{24,0},{28,4},{1,25},{... | collective-permute-start | bytes 147464 | tf_op jit(solution)/shard_map/ppermute | solution.py:265
  5.4 4.1 %collective-permute-start.2 = (bf16[3,4,2048]{2,1,0:T(4,128)(2,1)S(1)}, bf16[3,4,2048]{2,1,0:T(4,128)(2,1)S(1)}, u32[]{:S(2)}, u32[]{:S(2)}) collective-permute-start(bf16[3,4,2048]{2,1,0:T(4,128)(2,1)S(1)} %pad_maximum_fusion.packed.refs_0_), channel_id=1, source_target_pairs={{0,8},{4,12},{8,0},{12,4},{16,24},{20,28},{24,16},{28,20},{1,9},{5... | collective-permute-start | bytes 147464 | tf_op jit(solution)/shard_map/ppermute | solution.py:265
  5.9 3.6 %collective-permute-start.1 = (bf16[3,4,2048]{2,1,0:T(4,128)(2,1)S(1)}, bf16[3,4,2048]{2,1,0:T(4,128)(2,1)S(1)}, u32[]{:S(2)}, u32[]{:S(2)}) collective-permute-start(bf16[3,4,2048]{2,1,0:T(4,128)(2,1)S(1)} %pad_maximum_fusion.packed.refs_0_), channel_id=1, source_target_pairs={{0,20},{4,16},{8,28},{12,24},{16,4},{20,0},{24,12},{28,8},{1,21},{... | collective-permute-start | bytes 147464 | tf_op jit(solution)/shard_map/ppermute | solution.py:265
  5.9 4.6 %collective-permute-start = (bf16[3,4,2048]{2,1,0:T(4,128)(2,1)S(1)}, bf16[3,4,2048]{2,1,0:T(4,128)(2,1)S(1)}, u32[]{:S(2)}, u32[]{:S(2)}) collective-permute-start(bf16[3,4,2048]{2,1,0:T(4,128)(2,1)S(1)} %pad_maximum_fusion.packed.refs_0_), channel_id=1, source_target_pairs={{0,16},{4,20},{8,24},{12,28},{16,0},{20,4},{24,8},{28,12},{1,17},{... | collective-permute-start | bytes 147464 | tf_op jit(solution)/shard_map/ppermute | solution.py:265
  7.0 13.6 %copy-start.2 = (f32[512]{0:T(512)S(1)}, f32[512]{0:T(512)}, u32[]{:S(2)}) copy-start(f32[512]{0:T(512)} %param.10) | copy-start | bytes 6148
  7.0 2.6 %collective-permute-start.4 = (bf16[3,4,2048]{2,1,0:T(4,128)(2,1)S(1)}, bf16[3,4,2048]{2,1,0:T(4,128)(2,1)S(1)}, u32[]{:S(2)}, u32[]{:S(2)}) collective-permute-start(bf16[3,4,2048]{2,1,0:T(4,128)(2,1)S(1)} %pad_maximum_fusion.packed.refs_0_), channel_id=1, source_target_pairs={{0,4},{4,0},{1,5},{5,1},{2,6},{6,2},{3,7},{7,3},{8,12},{12,8},{9,1... | collective-permute-start | bytes 147464 | tf_op jit(solution)/shard_map/ppermute | solution.py:37
  7.9 2.6 %collective-permute-start.6 = (bf16[3,4,2048]{2,1,0:T(4,128)(2,1)S(1)}, bf16[3,4,2048]{2,1,0:T(4,128)(2,1)S(1)}, u32[]{:S(2)}, u32[]{:S(2)}) collective-permute-start(bf16[3,4,2048]{2,1,0:T(4,128)(2,1)S(1)} %collective-permute-done.3.refs_4_), channel_id=1, source_target_pairs={{0,4},{4,0},{1,5},{5,1},{2,6},{6,2},{3,7},{7,3},{8,12},{12,8},{9,1... | collective-permute-start | bytes 147464 | tf_op jit(solution)/shard_map/ppermute | solution.py:37
  9.5 1.2 %collective-permute-start.5 = (bf16[3,4,2048]{2,1,0:T(4,128)(2,1)S(1)}, bf16[3,4,2048]{2,1,0:T(4,128)(2,1)S(1)}, u32[]{:S(2)}, u32[]{:S(2)}) collective-permute-start(bf16[3,4,2048]{2,1,0:T(4,128)(2,1)S(1)} %collective-permute-done.2.refs_3_), channel_id=1, source_target_pairs={{0,4},{4,0},{1,5},{5,1},{2,6},{6,2},{3,7},{7,3},{8,12},{12,8},{9,1... | collective-permute-start | bytes 147464 | tf_op jit(solution)/shard_map/ppermute | solution.py:37
  11.9 6.0 %collective-permute-start.7 = (f32[96,128]{1,0:T(8,128)S(1)}, f32[96,128]{1,0:T(8,128)S(1)}, u32[]{:S(2)}, u32[]{:S(2)}) collective-permute-start(f32[96,128]{1,0:T(8,128)S(1)} %get-tuple-element.10), channel_id=1, source_target_pairs={{0,3},{1,2},{2,1},{3,0},{4,7},{5,6},{6,5},{7,4},{8,11},{9,10},{10,... | collective-permute-start | bytes 147464 | tf_op jit(solution)/shard_map/ppermute | solution.py:37
  15.6 5.0 %collective-permute-start.8 = (f32[96,128]{1,0:T(8,128)S(1)}, f32[96,128]{1,0:T(8,128)S(1)}, u32[]{:S(2)}, u32[]{:S(2)}) collective-permute-start(f32[96,128]{1,0:T(8,128)S(1)} %get-tuple-element.11), channel_id=1, source_target_pairs={{0,2},{1,3},{2,0},{3,1},{4,6},{5,7},{6,4},{7,5},{8,10},{9,11},{10,... | collective-permute-start | bytes 147464 | tf_op jit(solution)/shard_map/ppermute | solution.py:37
  15.6 5.0 %collective-permute-start.9 = (f32[96,128]{1,0:T(8,128)S(1)}, f32[96,128]{1,0:T(8,128)S(1)}, u32[]{:S(2)}, u32[]{:S(2)}) collective-permute-start(f32[96,128]{1,0:T(8,128)S(1)} %get-tuple-element.12), channel_id=1, source_target_pairs={{0,1},{1,0},{2,3},{3,2},{4,5},{5,4},{6,7},{7,6},{8,9},{9,8},{10,11... | collective-permute-start | bytes 147464 | tf_op jit(solution)/shard_map/ppermute | solution.py:37

commit v20 on v18

--- a/solution.py
+++ b/solution.py
@@ -15,12 +15,22 @@
 
 
 def far_first(size):
-    return sorted(range(size), key=lambda m: (m > 0, m < size // 2, m))
+    return [0, *reversed(range(1, size))]
 
 
 def row_blocks(sections, feats):
+    direct = sections // 2
     places = [(p, q) for p in range(feats) for q in range(sections)]
-    return sorted(places, key=lambda place: (place[0] > 0 and place[1] != 1, place[1], place[0]))
+    return sorted(
+        places,
+        key=lambda place: (
+            place[0] > 0 and place[1] != direct,
+            place[1] != 0,
+            place[1] != direct,
+            place[1],
+            place[0],
+        ),
+    )
 
 
 def exchange(value, axis, size, k):
@@ -45,53 +55,6 @@
         cost_estimate=pl.CostEstimate(flops=2**32, bytes_accessed=2**24, transcendentals=0),
         name="inner_products",
     )(packed)
-
-
-def inner_products(packed):
-    vmem = pl.BlockSpec(memory_space=pltpu.VMEM)
-    return pl.pallas_call(
-        inner_kernel,
-        out_shape=jax.ShapeDtypeStruct((TILE, LANES), jnp.float32),
-        in_specs=[vmem],
-        out_specs=vmem,
-        compiler_params=pltpu.CompilerParams(vmem_limit_bytes=4 * 2**20),
-        cost_estimate=pl.CostEstimate(flops=2**32, bytes_accessed=2**24, transcendentals=0),
-        name="inner_products",
-    )(packed)
-
-
-def load_kernel(pieces, *refs):
-    count = (len(refs) - 2) // 2
-    sems = refs[-1]
-    copies = []
-    for i in range(count):
-        source, target = refs[1 + i], refs[1 + count + i]
-        count_here = min(pieces, source.shape[0] // 16) or 1
-        step = source.shape[0] // count_here
-        for j in range(count_here):
-            part = pl.ds(j * step, step)
-            copies.append(
-                pltpu.make_async_copy(source.at[part], target.at[part], sems.at[i, j])
-            )
-    for copy in copies:
-        copy.start()
-    for copy in copies:
-        copy.wait()
-
-
-def load(after, *arrays, pieces=4):
-    size = sum(array.size * array.dtype.itemsize for array in arrays)
-    return pl.pallas_call(
-        functools.partial(load_kernel, pieces),
-        out_shape=[jax.ShapeDtypeStruct(array.shape, array.dtype) for array in arrays],
-        in_specs=[pl.BlockSpec(memory_space=pltpu.VMEM)]
-        + [pl.BlockSpec(memory_space=pltpu.HBM)] * len(arrays),
-        out_specs=[pl.BlockSpec(memory_space=pltpu.VMEM)] * len(arrays),
-        scratch_shapes=[pltpu.SemaphoreType.DMA((len(arrays), pieces))],
-        compiler_params=pltpu.CompilerParams(vmem_limit_bytes=16 * 2**20),
-        cost_estimate=pl.CostEstimate(flops=0, bytes_accessed=2 * size, transcendentals=0),
-        name="load_weights",
-    )(after, *arrays)
 
 
 def product_kernel(groups, parts, *refs):
@@ -240,7 +203,7 @@
     bias = enc_bias.reshape(parts, features // parts)
     held = {(0, 0): packed}
     for p, q in row_blocks(sections, feats):
-        if q > 0 and (p == 0 or q == 1):
+        if q > 0 and (p == 0 or q == sections // 2):
             pairs = [
                 (s * feats + f, (s ^ q) * feats + (f ^ p))
                 for s in range(sections)

time: 32.7 us -> 32.2 us (0.985)
  blocking collectives: 11.2 us -> 10.7 us
    all_to_all x1, blocking collectives: 11.2 us -> 10.7 us  [per_device(): return tuple(final(sizes, tokens, lax.all_to_all(sums, EVERY, 0, 0)))]
where the time goes in v20:
time: 32.2 us; the launch traced here: 31.9 us
  starting transfers between devices  10.9 us (34%)
  blocking collectives  10.7 us (33%)
  waiting for transfers between devices  6.94 us (22%)
  Pallas kernels  1.92 us (6%)
  other arithmetic  0.79 us (2%)
  between operations  0.67 us (2%)
    all_to_all x1, blocking collectives, per_device(): return tuple(final(sizes, tokens, lax.all_to_all(sums, EVERY, 0, 0)))  10.7 us
    ppermute x6, starting transfers between devices, exchange(): return lax.ppermute(value, axis, [(i, i ^ k) for i in range(size)])  5.49 us
    ppermute x4, starting transfers between devices, per_device(): held[p, q] = lax.ppermute(packed, ('section', 'feat'), pairs)  5.4 us
    ppermute x6, waiting for transfers between devices, exchange(): return lax.ppermute(value, axis, [(i, i ^ k) for i in range(size)])  4.43 us
    ppermute x4, waiting for transfers between devices, per_device(): held[p, q] = lax.ppermute(packed, ('section', 'feat'), pairs)  2.51 us
    pallas_call x1, Pallas kernels, products(): pl.pallas_call(functools.partial(product_kernel, groups, parts), out_shap...  1.11 us
    another operation x1, other arithmetic, per_device(): packed = jnp.stack([clean_resid, corrupt_resid, metric_grad])  0.79 us
  transfers between devices with their start and end apart: 10, of which 5 were waited for; matrix products, arithmetic and copies ran while one was open for 0% of the time, Pallas kernels for 0%

profile of v20, /device:TPU:0, one launch (start us, length us, event | category | flops | bytes accessed | tf_op | source)
XLA Modules:
  0.0 31.9 jit_solution(10496636110157733339)
XLA Ops:
  0.6 0.8 %pad_maximum_fusion.packed.refs_0_ = bf16[3,4,2048]{2,1,0:T(4,128)(2,1)S(1)} fusion(bf16[1,4,2048]{2,1,0:T(4,128)(2,1)} %bitcast.5, bf16[1,4,2048]{2,1,0:T(4,128)(2,1)} %bitcast.6, bf16[1,4,2048]{2,1,0:T(4,128)(2,1)} %bitcast.7), kind=kLoop, calls=%fused_computation | loop fusion | flops 49152 | bytes 98304 | tf_op jit(solution)/shard_map/stack | solution.py:201
  1.4 0.0 copy-start
  1.4 0.0 copy-start.1
  1.4 4.0 %collective-permute-start.3 = (bf16[3,4,2048]{2,1,0:T(4,128)(2,1)S(1)}, bf16[3,4,2048]{2,1,0:T(4,128)(2,1)S(1)}, u32[]{:S(2)}, u32[]{:S(2)}) collective-permute-start(bf16[3,4,2048]{2,1,0:T(4,128)(2,1)S(1)} %pad_maximum_fusion.packed.refs_0_), channel_id=1, source_target_pairs={{0,24},{4,28},{8,16},{12,20},{16,8},{20,12},{24,0},{28,4},{1,25},{... | collective-permute-start | bytes 147464 | tf_op jit(solution)/shard_map/ppermute | solution.py:212
  5.4 0.5 %collective-permute-start.2 = (bf16[3,4,2048]{2,1,0:T(4,128)(2,1)S(1)}, bf16[3,4,2048]{2,1,0:T(4,128)(2,1)S(1)}, u32[]{:S(2)}, u32[]{:S(2)}) collective-permute-start(bf16[3,4,2048]{2,1,0:T(4,128)(2,1)S(1)} %pad_maximum_fusion.packed.refs_0_), channel_id=1, source_target_pairs={{0,8},{4,12},{8,0},{12,4},{16,24},{20,28},{24,16},{28,20},{1,9},{5... | collective-permute-start | bytes 147464 | tf_op jit(solution)/shard_map/ppermute | solution.py:212
  5.9 0.0 collective-permute-start.1
  5.9 0.9 %collective-permute-start = (bf16[3,4,2048]{2,1,0:T(4,128)(2,1)S(1)}, bf16[3,4,2048]{2,1,0:T(4,128)(2,1)S(1)}, u32[]{:S(2)}, u32[]{:S(2)}) collective-permute-start(bf16[3,4,2048]{2,1,0:T(4,128)(2,1)S(1)} %pad_maximum_fusion.packed.refs_0_), channel_id=1, source_target_pairs={{0,16},{4,20},{8,24},{12,28},{16,0},{20,4},{24,8},{28,12},{1,17},{... | collective-permute-start | bytes 147464 | tf_op jit(solution)/shard_map/ppermute | solution.py:212
  6.9 0.1 inner_products.1.refs_5_
  7.0 1.0 %collective-permute-start.4 = (bf16[3,4,2048]{2,1,0:T(4,128)(2,1)S(1)}, bf16[3,4,2048]{2,1,0:T(4,128)(2,1)S(1)}, u32[]{:S(2)}, u32[]{:S(2)}) collective-permute-start(bf16[3,4,2048]{2,1,0:T(4,128)(2,1)S(1)} %pad_maximum_fusion.packed.refs_0_), channel_id=1, source_target_pairs={{0,4},{4,0},{1,5},{5,1},{2,6},{6,2},{3,7},{7,3},{8,12},{12,8},{9,1... | collective-permute-start | bytes 147464 | tf_op jit(solution)/shard_map/ppermute | solution.py:37
  7.9 0.1 collective-permute-start.6
  8.0 1.5 %collective-permute-done.2.refs_3_ = bf16[3,4,2048]{2,1,0:T(4,128)(2,1)S(1)} collective-permute-done((bf16[3,4,2048]{2,1,0:T(4,128)(2,1)S(1)}, bf16[3,4,2048]{2,1,0:T(4,128)(2,1)S(1)}, u32[]{:S(2)}, u32[]{:S(2)}) %collective-permute-start.2) | collective-permute-done | bytes 49184 | tf_op jit(solution)/shard_map/ppermute | solution.py:212
  9.5 1.0 %collective-permute-done.refs_1_ = bf16[3,4,2048]{2,1,0:T(4,128)(2,1)S(1)} collective-permute-done((bf16[3,4,2048]{2,1,0:T(4,128)(2,1)S(1)}, bf16[3,4,2048]{2,1,0:T(4,128)(2,1)S(1)}, u32[]{:S(2)}, u32[]{:S(2)}) %collective-permute-start) | collective-permute-done | bytes 49184 | tf_op jit(solution)/shard_map/ppermute | solution.py:212
  10.5 0.0 collective-permute-done.6.refs_7_
  10.5 0.2 collective-permute-done.5.refs_6_
  10.7 1.1 %products.1 = (f32[96,128]{1,0:T(8,128)S(1)}, f32[96,128]{1,0:T(8,128)S(1)}, f32[96,128]{1,0:T(8,128)S(1)}, f32[96,128]{1,0:T(8,128)S(1)}) custom-call(bf16[3,4,2048]{2,1,0:T(4,128)(2,1)S(1)} %pad_maximum_fusion.packed.refs_0_, bf16[3,4,2048]{2,1,0:T(4,128)(2,1)S(1)} %collective-permute-done.refs_1_, bf16[3,4,2048]{2,1,0:T(4,128)(2,1)S(1)} %collective-permute-done.1.refs_2_, ...), custom_call_target="tpu_custom_call" | custom-call | tf_op jit(solution)/shard_map/products/pallas_call | solution.py:99
  11.8 3.7 %collective-permute-start.7 = (f32[96,128]{1,0:T(8,128)S(1)}, f32[96,128]{1,0:T(8,128)S(1)}, u32[]{:S(2)}, u32[]{:S(2)}) collective-permute-start(f32[96,128]{1,0:T(8,128)S(1)} %get-tuple-element.10), channel_id=1, source_target_pairs={{0,3},{1,2},{2,1},{3,0},{4,7},{5,6},{6,5},{7,4},{8,11},{9,10},{10,... | collective-permute-start | bytes 147464 | tf_op jit(solution)/shard_map/ppermute | solution.py:37
  15.5 0.0 collective-permute-start.8
  15.5 0.8 %collective-permute-start.9 = (f32[96,128]{1,0:T(8,128)S(1)}, f32[96,128]{1,0:T(8,128)S(1)}, u32[]{:S(2)}, u32[]{:S(2)}) collective-permute-start(f32[96,128]{1,0:T(8,128)S(1)} %get-tuple-element.12), channel_id=1, source_target_pairs={{0,1},{1,0},{2,3},{3,2},{4,5},{5,4},{6,7},{7,6},{8,9},{9,8},{10,11... | collective-permute-start | bytes 147464 | tf_op jit(solution)/shard_map/ppermute | solution.py:37
  16.3 1.6 %collective-permute-done.7.refs_1_ = f32[96,128]{1,0:T(8,128)S(1)} collective-permute-done((f32[96,128]{1,0:T(8,128)S(1)}, f32[96,128]{1,0:T(8,128)S(1)}, u32[]{:S(2)}, u32[]{:S(2)}) %collective-permute-start.7) | collective-permute-done | bytes 49184 | tf_op jit(solution)/shard_map/ppermute | solution.py:37
  17.9 2.6 %collective-permute-done.8.refs_2_ = f32[96,128]{1,0:T(8,128)S(1)} collective-permute-done((f32[96,128]{1,0:T(8,128)S(1)}, f32[96,128]{1,0:T(8,128)S(1)}, u32[]{:S(2)}, u32[]{:S(2)}) %collective-permute-start.8) | collective-permute-done | bytes 49184 | tf_op jit(solution)/shard_map/ppermute | solution.py:37
  20.5 0.0 collective-permute-done.9.refs_3_
  20.5 0.1 attributions.1
  20.6 10.7 %all_to_all.5.arrived = f32[32,2,128]{2,1,0:T(2,128)S(1)} all-to-all(f32[32,2,128]{2,1,0:T(2,128)S(1)} %attributions.1), channel_id=1, replica_groups=mesh['section'=4,'feat'=2,'tensor'=4] {'section','feat','tensor'}, dimensions={0} | all-to-all | bytes 65536 | tf_op jit(solution)/shard_map/all_to_all | solution.py:223
  31.3 0.6 %final.1 = (f32[512]{0:T(512)}, f32[4]{0:T(128)}) custom-call(f32[32,2,128]{2,1,0:T(2,128)S(1)} %all_to_all.5.arrived), custom_call_target="tpu_custom_call" | custom-call | tf_op jit(solution)/shard_map/final/pallas_call | solution.py:178
  (8 shorter events, 0.0 us)
Async XLA Ops:
  1.4 9.3 %copy-start = (bf16[2048,512]{1,0:T(8,128)(2,1)S(1)}, bf16[2048,512]{1,0:T(8,128)(2,1)}, u32[]{:S(2)}) copy-start(bf16[2048,512]{1,0:T(8,128)(2,1)} %refs_8_.1) | copy-start | bytes 6291460
  1.4 9.3 %copy-start.1 = (bf16[512,2048]{1,0:T(8,128)(2,1)S(1)}, bf16[512,2048]{1,0:T(8,128)(2,1)}, u32[]{:S(2)}) copy-start(bf16[512,2048]{1,0:T(8,128)(2,1)} %refs_9_.1) | copy-start | bytes 6291460
  1.4 6.5 %collective-permute-start.3 = (bf16[3,4,2048]{2,1,0:T(4,128)(2,1)S(1)}, bf16[3,4,2048]{2,1,0:T(4,128)(2,1)S(1)}, u32[]{:S(2)}, u32[]{:S(2)}) collective-permute-start(bf16[3,4,2048]{2,1,0:T(4,128)(2,1)S(1)} %pad_maximum_fusion.packed.refs_0_), channel_id=1, source_target_pairs={{0,24},{4,28},{8,16},{12,20},{16,8},{20,12},{24,0},{28,4},{1,25},{... | collective-permute-start | bytes 147464 | tf_op jit(solution)/shard_map/ppermute | solution.py:212
  5.4 4.1 %collective-permute-start.2 = (bf16[3,4,2048]{2,1,0:T(4,128)(2,1)S(1)}, bf16[3,4,2048]{2,1,0:T(4,128)(2,1)S(1)}, u32[]{:S(2)}, u32[]{:S(2)}) collective-permute-start(bf16[3,4,2048]{2,1,0:T(4,128)(2,1)S(1)} %pad_maximum_fusion.packed.refs_0_), channel_id=1, source_target_pairs={{0,8},{4,12},{8,0},{12,4},{16,24},{20,28},{24,16},{28,20},{1,9},{5... | collective-permute-start | bytes 147464 | tf_op jit(solution)/shard_map/ppermute | solution.py:212
  5.9 3.6 %collective-permute-start.1 = (bf16[3,4,2048]{2,1,0:T(4,128)(2,1)S(1)}, bf16[3,4,2048]{2,1,0:T(4,128)(2,1)S(1)}, u32[]{:S(2)}, u32[]{:S(2)}) collective-permute-start(bf16[3,4,2048]{2,1,0:T(4,128)(2,1)S(1)} %pad_maximum_fusion.packed.refs_0_), channel_id=1, source_target_pairs={{0,20},{4,16},{8,28},{12,24},{16,4},{20,0},{24,12},{28,8},{1,21},{... | collective-permute-start | bytes 147464 | tf_op jit(solution)/shard_map/ppermute | solution.py:212
  5.9 4.6 %collective-permute-start = (bf16[3,4,2048]{2,1,0:T(4,128)(2,1)S(1)}, bf16[3,4,2048]{2,1,0:T(4,128)(2,1)S(1)}, u32[]{:S(2)}, u32[]{:S(2)}) collective-permute-start(bf16[3,4,2048]{2,1,0:T(4,128)(2,1)S(1)} %pad_maximum_fusion.packed.refs_0_), channel_id=1, source_target_pairs={{0,16},{4,20},{8,24},{12,28},{16,0},{20,4},{24,8},{28,12},{1,17},{... | collective-permute-start | bytes 147464 | tf_op jit(solution)/shard_map/ppermute | solution.py:212
  7.0 13.6 %copy-start.2 = (f32[512]{0:T(512)S(1)}, f32[512]{0:T(512)}, u32[]{:S(2)}) copy-start(f32[512]{0:T(512)} %param.10) | copy-start | bytes 6148
  7.0 2.6 %collective-permute-start.4 = (bf16[3,4,2048]{2,1,0:T(4,128)(2,1)S(1)}, bf16[3,4,2048]{2,1,0:T(4,128)(2,1)S(1)}, u32[]{:S(2)}, u32[]{:S(2)}) collective-permute-start(bf16[3,4,2048]{2,1,0:T(4,128)(2,1)S(1)} %pad_maximum_fusion.packed.refs_0_), channel_id=1, source_target_pairs={{0,4},{4,0},{1,5},{5,1},{2,6},{6,2},{3,7},{7,3},{8,12},{12,8},{9,1... | collective-permute-start | bytes 147464 | tf_op jit(solution)/shard_map/ppermute | solution.py:37
  7.9 2.6 %collective-permute-start.6 = (bf16[3,4,2048]{2,1,0:T(4,128)(2,1)S(1)}, bf16[3,4,2048]{2,1,0:T(4,128)(2,1)S(1)}, u32[]{:S(2)}, u32[]{:S(2)}) collective-permute-start(bf16[3,4,2048]{2,1,0:T(4,128)(2,1)S(1)} %collective-permute-done.3.refs_4_), channel_id=1, source_target_pairs={{0,4},{4,0},{1,5},{5,1},{2,6},{6,2},{3,7},{7,3},{8,12},{12,8},{9,1... | collective-permute-start | bytes 147464 | tf_op jit(solution)/shard_map/ppermute | solution.py:37
  9.5 1.2 %collective-permute-start.5 = (bf16[3,4,2048]{2,1,0:T(4,128)(2,1)S(1)}, bf16[3,4,2048]{2,1,0:T(4,128)(2,1)S(1)}, u32[]{:S(2)}, u32[]{:S(2)}) collective-permute-start(bf16[3,4,2048]{2,1,0:T(4,128)(2,1)S(1)} %collective-permute-done.2.refs_3_), channel_id=1, source_target_pairs={{0,4},{4,0},{1,5},{5,1},{2,6},{6,2},{3,7},{7,3},{8,12},{12,8},{9,1... | collective-permute-start | bytes 147464 | tf_op jit(solution)/shard_map/ppermute | solution.py:37
  11.8 6.0 %collective-permute-start.7 = (f32[96,128]{1,0:T(8,128)S(1)}, f32[96,128]{1,0:T(8,128)S(1)}, u32[]{:S(2)}, u32[]{:S(2)}) collective-permute-start(f32[96,128]{1,0:T(8,128)S(1)} %get-tuple-element.10), channel_id=1, source_target_pairs={{0,3},{1,2},{2,1},{3,0},{4,7},{5,6},{6,5},{7,4},{8,11},{9,10},{10,... | collective-permute-start | bytes 147464 | tf_op jit(solution)/shard_map/ppermute | solution.py:37
  15.5 5.0 %collective-permute-start.8 = (f32[96,128]{1,0:T(8,128)S(1)}, f32[96,128]{1,0:T(8,128)S(1)}, u32[]{:S(2)}, u32[]{:S(2)}) collective-permute-start(f32[96,128]{1,0:T(8,128)S(1)} %get-tuple-element.11), channel_id=1, source_target_pairs={{0,2},{1,3},{2,0},{3,1},{4,6},{5,7},{6,4},{7,5},{8,10},{9,11},{10,... | collective-permute-start | bytes 147464 | tf_op jit(solution)/shard_map/ppermute | solution.py:37
  15.5 5.0 %collective-permute-start.9 = (f32[96,128]{1,0:T(8,128)S(1)}, f32[96,128]{1,0:T(8,128)S(1)}, u32[]{:S(2)}, u32[]{:S(2)}) collective-permute-start(f32[96,128]{1,0:T(8,128)S(1)} %get-tuple-element.12), channel_id=1, source_target_pairs={{0,1},{1,0},{2,3},{3,2},{4,5},{5,4},{6,7},{7,6},{8,9},{9,8},{10,11... | collective-permute-start | bytes 147464 | tf_op jit(solution)/shard_map/ppermute | solution.py:37

commit v21 on v20

--- a/solution.py
+++ b/solution.py
@@ -165,7 +165,7 @@
         features[pl.ds(i * LANES, LANES)] = mine[i]
     feature_copy = pltpu.make_async_copy(features, feature_out, sems.at[0])
     feature_copy.start()
-    owed = add_up([arrived[i, 1:2, :] for i in range(sections * feats * parts)])
+    owed = jnp.sum(arrived[:, 1, :], axis=0, keepdims=True)
     errors[...] = -owed[0, : errors.shape[0]]
     error_copy = pltpu.make_async_copy(errors, error_out, sems.at[1])
     error_copy.start()

time: 32.2 us -> 32.2 us (level)
  no operation moved by 1% of the time
where the time goes in v21:
time: 32.2 us; the launch traced here: 31.9 us
  starting transfers between devices  10.9 us (34%)
  blocking collectives  10.7 us (33%)
  waiting for transfers between devices  6.94 us (22%)
  Pallas kernels  1.92 us (6%)
  other arithmetic  0.79 us (2%)
  between operations  0.67 us (2%)
    all_to_all x1, blocking collectives, per_device(): return tuple(final(sizes, tokens, lax.all_to_all(sums, EVERY, 0, 0)))  10.7 us
    ppermute x6, starting transfers between devices, exchange(): return lax.ppermute(value, axis, [(i, i ^ k) for i in range(size)])  5.49 us
    ppermute x4, starting transfers between devices, per_device(): held[p, q] = lax.ppermute(packed, ('section', 'feat'), pairs)  5.4 us
    ppermute x6, waiting for transfers between devices, exchange(): return lax.ppermute(value, axis, [(i, i ^ k) for i in range(size)])  4.43 us
    ppermute x4, waiting for transfers between devices, per_device(): held[p, q] = lax.ppermute(packed, ('section', 'feat'), pairs)  2.51 us
    pallas_call x1, Pallas kernels, products(): pl.pallas_call(functools.partial(product_kernel, groups, parts), out_shap...  1.11 us
    another operation x1, other arithmetic, per_device(): packed = jnp.stack([clean_resid, corrupt_resid, metric_grad])  0.79 us
  transfers between devices with their start and end apart: 10, of which 5 were waited for; matrix products, arithmetic and copies ran while one was open for 0% of the time, Pallas kernels for 0%

profile of v21, /device:TPU:0, one launch (start us, length us, event | category | flops | bytes accessed | tf_op | source)
XLA Modules:
  0.0 31.9 jit_solution(16642706961928400680)
XLA Ops:
  0.6 0.8 %pad_maximum_fusion.packed.refs_0_ = bf16[3,4,2048]{2,1,0:T(4,128)(2,1)S(1)} fusion(bf16[1,4,2048]{2,1,0:T(4,128)(2,1)} %bitcast.5, bf16[1,4,2048]{2,1,0:T(4,128)(2,1)} %bitcast.6, bf16[1,4,2048]{2,1,0:T(4,128)(2,1)} %bitcast.7), kind=kLoop, calls=%fused_computation | loop fusion | flops 49152 | bytes 98304 | tf_op jit(solution)/shard_map/stack | solution.py:201
  1.4 0.0 copy-start
  1.4 0.0 copy-start.1
  1.4 4.0 %collective-permute-start.3 = (bf16[3,4,2048]{2,1,0:T(4,128)(2,1)S(1)}, bf16[3,4,2048]{2,1,0:T(4,128)(2,1)S(1)}, u32[]{:S(2)}, u32[]{:S(2)}) collective-permute-start(bf16[3,4,2048]{2,1,0:T(4,128)(2,1)S(1)} %pad_maximum_fusion.packed.refs_0_), channel_id=1, source_target_pairs={{0,24},{4,28},{8,16},{12,20},{16,8},{20,12},{24,0},{28,4},{1,25},{... | collective-permute-start | bytes 147464 | tf_op jit(solution)/shard_map/ppermute | solution.py:212
  5.4 0.5 %collective-permute-start.2 = (bf16[3,4,2048]{2,1,0:T(4,128)(2,1)S(1)}, bf16[3,4,2048]{2,1,0:T(4,128)(2,1)S(1)}, u32[]{:S(2)}, u32[]{:S(2)}) collective-permute-start(bf16[3,4,2048]{2,1,0:T(4,128)(2,1)S(1)} %pad_maximum_fusion.packed.refs_0_), channel_id=1, source_target_pairs={{0,8},{4,12},{8,0},{12,4},{16,24},{20,28},{24,16},{28,20},{1,9},{5... | collective-permute-start | bytes 147464 | tf_op jit(solution)/shard_map/ppermute | solution.py:212
  5.9 0.0 collective-permute-start.1
  5.9 0.9 %collective-permute-start = (bf16[3,4,2048]{2,1,0:T(4,128)(2,1)S(1)}, bf16[3,4,2048]{2,1,0:T(4,128)(2,1)S(1)}, u32[]{:S(2)}, u32[]{:S(2)}) collective-permute-start(bf16[3,4,2048]{2,1,0:T(4,128)(2,1)S(1)} %pad_maximum_fusion.packed.refs_0_), channel_id=1, source_target_pairs={{0,16},{4,20},{8,24},{12,28},{16,0},{20,4},{24,8},{28,12},{1,17},{... | collective-permute-start | bytes 147464 | tf_op jit(solution)/shard_map/ppermute | solution.py:212
  6.9 0.1 inner_products.1.refs_5_
  7.0 1.0 %collective-permute-start.4 = (bf16[3,4,2048]{2,1,0:T(4,128)(2,1)S(1)}, bf16[3,4,2048]{2,1,0:T(4,128)(2,1)S(1)}, u32[]{:S(2)}, u32[]{:S(2)}) collective-permute-start(bf16[3,4,2048]{2,1,0:T(4,128)(2,1)S(1)} %pad_maximum_fusion.packed.refs_0_), channel_id=1, source_target_pairs={{0,4},{4,0},{1,5},{5,1},{2,6},{6,2},{3,7},{7,3},{8,12},{12,8},{9,1... | collective-permute-start | bytes 147464 | tf_op jit(solution)/shard_map/ppermute | solution.py:37
  7.9 0.1 collective-permute-start.6
  8.0 1.5 %collective-permute-done.2.refs_3_ = bf16[3,4,2048]{2,1,0:T(4,128)(2,1)S(1)} collective-permute-done((bf16[3,4,2048]{2,1,0:T(4,128)(2,1)S(1)}, bf16[3,4,2048]{2,1,0:T(4,128)(2,1)S(1)}, u32[]{:S(2)}, u32[]{:S(2)}) %collective-permute-start.2) | collective-permute-done | bytes 49184 | tf_op jit(solution)/shard_map/ppermute | solution.py:212
  9.5 1.0 %collective-permute-done.refs_1_ = bf16[3,4,2048]{2,1,0:T(4,128)(2,1)S(1)} collective-permute-done((bf16[3,4,2048]{2,1,0:T(4,128)(2,1)S(1)}, bf16[3,4,2048]{2,1,0:T(4,128)(2,1)S(1)}, u32[]{:S(2)}, u32[]{:S(2)}) %collective-permute-start) | collective-permute-done | bytes 49184 | tf_op jit(solution)/shard_map/ppermute | solution.py:212
  10.5 0.0 collective-permute-done.6.refs_7_
  10.5 0.2 collective-permute-done.5.refs_6_
  10.7 1.1 %products.1 = (f32[96,128]{1,0:T(8,128)S(1)}, f32[96,128]{1,0:T(8,128)S(1)}, f32[96,128]{1,0:T(8,128)S(1)}, f32[96,128]{1,0:T(8,128)S(1)}) custom-call(bf16[3,4,2048]{2,1,0:T(4,128)(2,1)S(1)} %pad_maximum_fusion.packed.refs_0_, bf16[3,4,2048]{2,1,0:T(4,128)(2,1)S(1)} %collective-permute-done.refs_1_, bf16[3,4,2048]{2,1,0:T(4,128)(2,1)S(1)} %collective-permute-done.1.refs_2_, ...), custom_call_target="tpu_custom_call" | custom-call | tf_op jit(solution)/shard_map/products/pallas_call | solution.py:99
  11.8 3.7 %collective-permute-start.7 = (f32[96,128]{1,0:T(8,128)S(1)}, f32[96,128]{1,0:T(8,128)S(1)}, u32[]{:S(2)}, u32[]{:S(2)}) collective-permute-start(f32[96,128]{1,0:T(8,128)S(1)} %get-tuple-element.10), channel_id=1, source_target_pairs={{0,3},{1,2},{2,1},{3,0},{4,7},{5,6},{6,5},{7,4},{8,11},{9,10},{10,... | collective-permute-start | bytes 147464 | tf_op jit(solution)/shard_map/ppermute | solution.py:37
  15.5 0.0 collective-permute-start.8
  15.5 0.8 %collective-permute-start.9 = (f32[96,128]{1,0:T(8,128)S(1)}, f32[96,128]{1,0:T(8,128)S(1)}, u32[]{:S(2)}, u32[]{:S(2)}) collective-permute-start(f32[96,128]{1,0:T(8,128)S(1)} %get-tuple-element.12), channel_id=1, source_target_pairs={{0,1},{1,0},{2,3},{3,2},{4,5},{5,4},{6,7},{7,6},{8,9},{9,8},{10,11... | collective-permute-start | bytes 147464 | tf_op jit(solution)/shard_map/ppermute | solution.py:37
  16.3 1.6 %collective-permute-done.7.refs_1_ = f32[96,128]{1,0:T(8,128)S(1)} collective-permute-done((f32[96,128]{1,0:T(8,128)S(1)}, f32[96,128]{1,0:T(8,128)S(1)}, u32[]{:S(2)}, u32[]{:S(2)}) %collective-permute-start.7) | collective-permute-done | bytes 49184 | tf_op jit(solution)/shard_map/ppermute | solution.py:37
  17.9 2.6 %collective-permute-done.8.refs_2_ = f32[96,128]{1,0:T(8,128)S(1)} collective-permute-done((f32[96,128]{1,0:T(8,128)S(1)}, f32[96,128]{1,0:T(8,128)S(1)}, u32[]{:S(2)}, u32[]{:S(2)}) %collective-permute-start.8) | collective-permute-done | bytes 49184 | tf_op jit(solution)/shard_map/ppermute | solution.py:37
  20.5 0.0 collective-permute-done.9.refs_3_
  20.5 0.1 attributions.1
  20.6 10.7 %all_to_all.5.arrived = f32[32,2,128]{2,1,0:T(2,128)S(1)} all-to-all(f32[32,2,128]{2,1,0:T(2,128)S(1)} %attributions.1), channel_id=1, replica_groups=mesh['section'=4,'feat'=2,'tensor'=4] {'section','feat','tensor'}, dimensions={0} | all-to-all | bytes 65536 | tf_op jit(solution)/shard_map/all_to_all | solution.py:223
  31.3 0.6 %final.1 = (f32[512]{0:T(512)}, f32[4]{0:T(128)}) custom-call(f32[32,2,128]{2,1,0:T(2,128)S(1)} %all_to_all.5.arrived), custom_call_target="tpu_custom_call" | custom-call | tf_op jit(solution)/shard_map/final/pallas_call | solution.py:178
  (8 shorter events, 0.0 us)
Async XLA Ops:
  1.4 9.3 %copy-start = (bf16[2048,512]{1,0:T(8,128)(2,1)S(1)}, bf16[2048,512]{1,0:T(8,128)(2,1)}, u32[]{:S(2)}) copy-start(bf16[2048,512]{1,0:T(8,128)(2,1)} %refs_8_.1) | copy-start | bytes 6291460
  1.4 9.3 %copy-start.1 = (bf16[512,2048]{1,0:T(8,128)(2,1)S(1)}, bf16[512,2048]{1,0:T(8,128)(2,1)}, u32[]{:S(2)}) copy-start(bf16[512,2048]{1,0:T(8,128)(2,1)} %refs_9_.1) | copy-start | bytes 6291460
  1.4 6.5 %collective-permute-start.3 = (bf16[3,4,2048]{2,1,0:T(4,128)(2,1)S(1)}, bf16[3,4,2048]{2,1,0:T(4,128)(2,1)S(1)}, u32[]{:S(2)}, u32[]{:S(2)}) collective-permute-start(bf16[3,4,2048]{2,1,0:T(4,128)(2,1)S(1)} %pad_maximum_fusion.packed.refs_0_), channel_id=1, source_target_pairs={{0,24},{4,28},{8,16},{12,20},{16,8},{20,12},{24,0},{28,4},{1,25},{... | collective-permute-start | bytes 147464 | tf_op jit(solution)/shard_map/ppermute | solution.py:212
  5.4 4.1 %collective-permute-start.2 = (bf16[3,4,2048]{2,1,0:T(4,128)(2,1)S(1)}, bf16[3,4,2048]{2,1,0:T(4,128)(2,1)S(1)}, u32[]{:S(2)}, u32[]{:S(2)}) collective-permute-start(bf16[3,4,2048]{2,1,0:T(4,128)(2,1)S(1)} %pad_maximum_fusion.packed.refs_0_), channel_id=1, source_target_pairs={{0,8},{4,12},{8,0},{12,4},{16,24},{20,28},{24,16},{28,20},{1,9},{5... | collective-permute-start | bytes 147464 | tf_op jit(solution)/shard_map/ppermute | solution.py:212
  5.9 3.6 %collective-permute-start.1 = (bf16[3,4,2048]{2,1,0:T(4,128)(2,1)S(1)}, bf16[3,4,2048]{2,1,0:T(4,128)(2,1)S(1)}, u32[]{:S(2)}, u32[]{:S(2)}) collective-permute-start(bf16[3,4,2048]{2,1,0:T(4,128)(2,1)S(1)} %pad_maximum_fusion.packed.refs_0_), channel_id=1, source_target_pairs={{0,20},{4,16},{8,28},{12,24},{16,4},{20,0},{24,12},{28,8},{1,21},{... | collective-permute-start | bytes 147464 | tf_op jit(solution)/shard_map/ppermute | solution.py:212
  5.9 4.6 %collective-permute-start = (bf16[3,4,2048]{2,1,0:T(4,128)(2,1)S(1)}, bf16[3,4,2048]{2,1,0:T(4,128)(2,1)S(1)}, u32[]{:S(2)}, u32[]{:S(2)}) collective-permute-start(bf16[3,4,2048]{2,1,0:T(4,128)(2,1)S(1)} %pad_maximum_fusion.packed.refs_0_), channel_id=1, source_target_pairs={{0,16},{4,20},{8,24},{12,28},{16,0},{20,4},{24,8},{28,12},{1,17},{... | collective-permute-start | bytes 147464 | tf_op jit(solution)/shard_map/ppermute | solution.py:212
  7.0 13.6 %copy-start.2 = (f32[512]{0:T(512)S(1)}, f32[512]{0:T(512)}, u32[]{:S(2)}) copy-start(f32[512]{0:T(512)} %param.10) | copy-start | bytes 6148
  7.0 2.6 %collective-permute-start.4 = (bf16[3,4,2048]{2,1,0:T(4,128)(2,1)S(1)}, bf16[3,4,2048]{2,1,0:T(4,128)(2,1)S(1)}, u32[]{:S(2)}, u32[]{:S(2)}) collective-permute-start(bf16[3,4,2048]{2,1,0:T(4,128)(2,1)S(1)} %pad_maximum_fusion.packed.refs_0_), channel_id=1, source_target_pairs={{0,4},{4,0},{1,5},{5,1},{2,6},{6,2},{3,7},{7,3},{8,12},{12,8},{9,1... | collective-permute-start | bytes 147464 | tf_op jit(solution)/shard_map/ppermute | solution.py:37
  7.9 2.6 %collective-permute-start.6 = (bf16[3,4,2048]{2,1,0:T(4,128)(2,1)S(1)}, bf16[3,4,2048]{2,1,0:T(4,128)(2,1)S(1)}, u32[]{:S(2)}, u32[]{:S(2)}) collective-permute-start(bf16[3,4,2048]{2,1,0:T(4,128)(2,1)S(1)} %collective-permute-done.3.refs_4_), channel_id=1, source_target_pairs={{0,4},{4,0},{1,5},{5,1},{2,6},{6,2},{3,7},{7,3},{8,12},{12,8},{9,1... | collective-permute-start | bytes 147464 | tf_op jit(solution)/shard_map/ppermute | solution.py:37
  9.5 1.2 %collective-permute-start.5 = (bf16[3,4,2048]{2,1,0:T(4,128)(2,1)S(1)}, bf16[3,4,2048]{2,1,0:T(4,128)(2,1)S(1)}, u32[]{:S(2)}, u32[]{:S(2)}) collective-permute-start(bf16[3,4,2048]{2,1,0:T(4,128)(2,1)S(1)} %collective-permute-done.2.refs_3_), channel_id=1, source_target_pairs={{0,4},{4,0},{1,5},{5,1},{2,6},{6,2},{3,7},{7,3},{8,12},{12,8},{9,1... | collective-permute-start | bytes 147464 | tf_op jit(solution)/shard_map/ppermute | solution.py:37
  11.8 6.0 %collective-permute-start.7 = (f32[96,128]{1,0:T(8,128)S(1)}, f32[96,128]{1,0:T(8,128)S(1)}, u32[]{:S(2)}, u32[]{:S(2)}) collective-permute-start(f32[96,128]{1,0:T(8,128)S(1)} %get-tuple-element.10), channel_id=1, source_target_pairs={{0,3},{1,2},{2,1},{3,0},{4,7},{5,6},{6,5},{7,4},{8,11},{9,10},{10,... | collective-permute-start | bytes 147464 | tf_op jit(solution)/shard_map/ppermute | solution.py:37
  15.5 5.0 %collective-permute-start.8 = (f32[96,128]{1,0:T(8,128)S(1)}, f32[96,128]{1,0:T(8,128)S(1)}, u32[]{:S(2)}, u32[]{:S(2)}) collective-permute-start(f32[96,128]{1,0:T(8,128)S(1)} %get-tuple-element.11), channel_id=1, source_target_pairs={{0,2},{1,3},{2,0},{3,1},{4,6},{5,7},{6,4},{7,5},{8,10},{9,11},{10,... | collective-permute-start | bytes 147464 | tf_op jit(solution)/shard_map/ppermute | solution.py:37
  15.5 5.0 %collective-permute-start.9 = (f32[96,128]{1,0:T(8,128)S(1)}, f32[96,128]{1,0:T(8,128)S(1)}, u32[]{:S(2)}, u32[]{:S(2)}) collective-permute-start(f32[96,128]{1,0:T(8,128)S(1)} %get-tuple-element.12), channel_id=1, source_target_pairs={{0,1},{1,0},{2,3},{3,2},{4,5},{5,4},{6,7},{7,6},{8,9},{9,8},{10,11... | collective-permute-start | bytes 147464 | tf_op jit(solution)/shard_map/ppermute | solution.py:37
